TPU v7x, 32 devices: a whole 2x2x4 slice. The times are simulated.
32 devices in a mesh: groups: 2 (over x), tokens: 16 (over z, y, core).
Axes of the slice: x: 2, y: 2, z: 4, core: 2. Of those that a mesh axis runs over, the one named last changes fastest.
Arguments:
- update_keys: bfloat16 [16384, 2048], P(('groups', 'tokens')), parts along dimension 0, may hold values from -6 to 6
- update_values: bfloat16 [16384, 2048], P(('groups', 'tokens')), parts along dimension 0, may hold values from -6 to 6
- update_rates: float32 [16384, 4], P(('groups', 'tokens')), parts along dimension 0, may hold values from 0.05 to 1
- update_mask: int32 [16384], P(('groups', 'tokens')), parts along dimension 0, may hold values 0 or 1
- fast_weights: bfloat16 [4, 3, 512, 512], replicated, may hold values from -0.25 to 0.25
- step_sizes: float32 [4], replicated, may hold values from 0.02 to 0.08
- target_queries: bfloat16 [4096, 2048], P(('groups', 'tokens')), parts along dimension 0, may hold values from -8 to 8
- target_keys: bfloat16 [4096, 2048], P(('groups', 'tokens')), parts along dimension 0, may hold values from -8 to 8
- target_values: bfloat16 [4096, 2048], P(('groups', 'tokens')), parts along dimension 0, may hold values from -6 to 6
- target_views: int32 [4096], P(('groups', 'tokens')), parts along dimension 0, may hold values from 0 to 15, as said below
Outputs:
- mixed: bfloat16 [4096, 2048], P(('groups', 'tokens')), parts along dimension 0
There are 2 independent parts, one for each index of `groups`. A program takes and returns all parts, laid end to end along the dimension named above; an argument that names none is the same for every part. Nothing has to cross between parts.
Inputs may be any that keep to these rules, and one draw needn't show every extreme that they name: `target_views`: every view id names exactly 128 rows. Owner o holds view o; of the 128 rows of one device, either none or exactly 16 belong to the view of one owner.
All inputs are finite; a program needn't handle non-finite values. No bound on the sum of `update_mask` on one device may be relied on, other than what follows from the above.
Results may differ from a plain program's by a relative error of at most 0.0083.
Values may be sent and summed in bfloat16 or wider, within the bound.
No kernel may reach another device: no remote copies, remote signals or barrier semaphores. Data moves between devices by JAX's collectives and lax.ppermute only.
A program may use at most 128 MiB of HBM per device.

v0:
```python
import jax
import jax.numpy as jnp
from jax import lax
from jax.sharding import PartitionSpec as P

VIEW_ROWS = 128
VIEWS_DEV = 1


epsilon = 1e-05


def swish_parts(pre_gate):
    sigma = jax.nn.sigmoid(pre_gate)
    return (pre_gate * sigma, sigma * (1.0 + pre_gate * (1.0 - sigma)))


def row_normalize(matrix):
    return matrix * lax.rsqrt(jnp.mean(matrix * matrix, axis=-1, keepdims=True) + epsilon)


def local_gradient(update_keys, update_values, update_rates, update_mask, fast_weights):
    row_count = update_keys.shape[0]
    head_count = fast_weights.shape[0]
    head_width = fast_weights.shape[2]
    key_rows = update_keys.reshape(row_count, head_count, head_width)
    rate_rows = update_mask.astype(jnp.float32)[:, None] * update_rates
    value_rows = update_values.reshape(row_count, head_count, head_width).astype(jnp.float32)
    target_grad = (-rate_rows[:, :, None] * value_rows).astype(jnp.bfloat16)
    pre_gate = jnp.einsum(
        "rhi,hij->rhj", key_rows, fast_weights[:, 0], preferred_element_type=jnp.float32
    )
    pre_up = jnp.einsum(
        "rhi,hij->rhj", key_rows, fast_weights[:, 1], preferred_element_type=jnp.float32
    )
    activated, slope = swish_parts(pre_gate)
    hidden = (activated * pre_up).astype(jnp.bfloat16)
    back = jnp.einsum(
        "rho,hjo->rhj", target_grad, fast_weights[:, 2], preferred_element_type=jnp.float32
    )
    grad_gate = (back * pre_up * slope).astype(jnp.bfloat16)
    grad_up = (back * activated).astype(jnp.bfloat16)
    gate_term = jnp.einsum("rhi,rhj->hij", key_rows, grad_gate, preferred_element_type=jnp.float32)
    up_term = jnp.einsum("rhi,rhj->hij", key_rows, grad_up, preferred_element_type=jnp.float32)
    down_term = jnp.einsum("rhj,rho->hjo", hidden, target_grad, preferred_element_type=jnp.float32)
    return jnp.stack([gate_term, up_term, down_term], axis=1)


def update_weights(update_keys, update_values, update_rates, update_mask, fast_weights, step_sizes):
    grad_local = local_gradient(update_keys, update_values, update_rates, update_mask, fast_weights)
    head_count = fast_weights.shape[0]
    head_width = fast_weights.shape[2]
    flat_rows = 3 * head_count * head_width
    grad_share = lax.psum_scatter(
        grad_local.reshape(flat_rows, head_width), "tokens", scatter_dimension=0, tiled=True
    )
    share_rows = grad_share.shape[0]
    first_row = lax.axis_index("tokens") * share_rows
    own_rows = lax.dynamic_slice_in_dim(
        fast_weights.reshape(flat_rows, head_width), first_row, share_rows, 0
    )
    head_of_row = (first_row + jnp.arange(share_rows, dtype=jnp.int32)) // (3 * head_width)
    head_match = head_of_row[:, None] == jnp.arange(head_count, dtype=jnp.int32)[None, :]
    step_rows = jnp.sum(jnp.where(head_match, step_sizes[None, :], 0.0), axis=1)
    fresh_share = (
        own_rows.astype(jnp.float32) - step_rows[:, None] * row_normalize(grad_share)
    ).astype(jnp.bfloat16)
    fresh = lax.all_gather(fresh_share, "tokens", axis=0, tiled=True).reshape(
        head_count, 3, head_width, head_width
    )
    return fresh


def regroup_rows(target_queries, target_keys, target_values, target_views):
    row_count = target_views.shape[0]
    dev_count = lax.axis_size("tokens")
    capacity = 2 * row_count // dev_count
    owner_dev = target_views // VIEWS_DEV
    hit_int = (owner_dev[:, None] == jnp.arange(dev_count, dtype=jnp.int32)[None, :]).astype(
        jnp.int32
    )
    dev_rank = jnp.sum(hit_int * (jnp.cumsum(hit_int, axis=0) - 1), axis=1)
    slot_index = owner_dev * capacity + dev_rank
    pick_hit = jnp.arange(dev_count * capacity, dtype=jnp.int32)[:, None] == slot_index[None, :]
    pick_table = pick_hit.astype(jnp.bfloat16)
    sent_queries = jnp.dot(pick_table, target_queries, preferred_element_type=jnp.float32).astype(
        jnp.bfloat16
    )
    sent_keys = jnp.dot(pick_table, target_keys, preferred_element_type=jnp.float32).astype(
        jnp.bfloat16
    )
    sent_values = jnp.dot(pick_table, target_values, preferred_element_type=jnp.float32).astype(
        jnp.bfloat16
    )
    sent_views = jnp.sum(jnp.where(pick_hit, target_views[None, :] + 1, 0), axis=1) - 1
    got_queries, got_keys, got_values, got_views = (
        lax.all_to_all(sent_queries, "tokens", split_axis=0, concat_axis=0, tiled=True),
        lax.all_to_all(sent_keys, "tokens", split_axis=0, concat_axis=0, tiled=True),
        lax.all_to_all(sent_values, "tokens", split_axis=0, concat_axis=0, tiled=True),
        lax.all_to_all(sent_views, "tokens", split_axis=0, concat_axis=0, tiled=True),
    )
    is_valid = got_views >= 0
    local_view = jnp.where(is_valid, got_views % VIEWS_DEV, 0)
    view_match = is_valid[:, None] & (
        local_view[:, None] == jnp.arange(VIEWS_DEV, dtype=jnp.int32)[None, :]
    )
    view_hit = view_match.astype(jnp.int32)
    view_rank = jnp.sum(view_hit * (jnp.cumsum(view_hit, axis=0) - 1), axis=1)
    placed_at = jnp.where(is_valid, local_view * VIEW_ROWS + view_rank, -1)
    place_table = (jnp.arange(row_count, dtype=jnp.int32)[:, None] == placed_at[None, :]).astype(
        jnp.bfloat16
    )
    return tuple(
        (
            jnp.dot(place_table, got_rows, preferred_element_type=jnp.float32).astype(jnp.bfloat16)
            for got_rows in (got_queries, got_keys, got_values)
        )
    )


def attend_views(arranged, head_count, head_width):
    row_count = arranged[0].shape[0]
    view_shape = (row_count // VIEW_ROWS, VIEW_ROWS, head_count, head_width)
    scores = jnp.einsum(
        "vqhd,vkhd->vhqk",
        arranged[0].reshape(view_shape),
        arranged[1].reshape(view_shape),
        preferred_element_type=jnp.float32,
    ) * head_width ** (-0.5)
    probs = jax.nn.softmax(scores, axis=-1).astype(jnp.bfloat16)
    attended = jnp.einsum(
        "vhqk,vkhd->vqhd",
        probs,
        arranged[2].reshape(view_shape),
        preferred_element_type=jnp.float32,
    )
    return attended.reshape(row_count, head_count, head_width)


def finish_rows(fresh, arranged_queries, attended):
    row_count = arranged_queries.shape[0]
    head_count = fresh.shape[0]
    head_width = fresh.shape[2]
    query_rows = arranged_queries.reshape(row_count, head_count, head_width)
    pre_gate = jnp.einsum(
        "rhi,hij->rhj", query_rows, fresh[:, 0], preferred_element_type=jnp.float32
    )
    pre_up = jnp.einsum("rhi,hij->rhj", query_rows, fresh[:, 1], preferred_element_type=jnp.float32)
    activated, slope = swish_parts(pre_gate)
    target_hidden = (activated * pre_up).astype(jnp.bfloat16)
    fast_out = jnp.einsum(
        "rhj,hjo->rho", target_hidden, fresh[:, 2], preferred_element_type=jnp.float32
    )
    mixed = row_normalize(fast_out) + attended
    return mixed.reshape(row_count, head_count * head_width).astype(jnp.bfloat16)


def on_device(
    update_keys,
    update_values,
    update_rates,
    update_mask,
    fast_weights,
    step_sizes,
    target_queries,
    target_keys,
    target_values,
    target_views,
):
    head_count = fast_weights.shape[0]
    head_width = fast_weights.shape[2]
    fresh = update_weights(
        update_keys, update_values, update_rates, update_mask, fast_weights, step_sizes
    )
    arranged = regroup_rows(target_queries, target_keys, target_values, target_views)
    attended = attend_views(arranged, head_count, head_width)
    return finish_rows(fresh, arranged[0], attended)


def solution(mesh):
    return jax.shard_map(
        on_device,
        mesh=mesh,
        in_specs=(
            P(("groups", "tokens"), None),
            P(("groups", "tokens"), None),
            P(("groups", "tokens"), None),
            P(("groups", "tokens")),
            P(),
            P(),
            P(("groups", "tokens"), None),
            P(("groups", "tokens"), None),
            P(("groups", "tokens"), None),
            P(("groups", "tokens")),
        ),
        out_specs=P(("groups", "tokens"), None),
        check_vma=False,
    )
```

profile of v0, /device:TPU:0, one launch (start us, length us, event | category | flops | bytes accessed | tf_op | source)
XLA Modules:
  0.0 328.3 jit_solution(13886927430357881111)
XLA Ops:
  6.5 0.0 copy-start
  6.5 0.0 reduce-scatter.2.cloned.1.call-start
  6.5 2.9 copy.131
  9.5 0.0 copy-start.1
  9.5 3.0 fusion.16
  12.5 0.4 copy-done.1
  12.9 1.3 fusion.18
  14.2 0.0 copy-done.7
  14.2 0.0 copy-start.5
  14.2 0.3 copy-done.2
  14.5 0.5 convert_element_type.100
  15.0 0.0 copy-done.5
  15.1 1.6 fusion.20
  16.6 3.5 %convolution_bitcast_fusion.2 = f32[4,1,512,512]{3,2,0,1:T(8,128)} fusion(f32[4,512,512]{1,2,0:T(8,128)S(1)} %fusion.18, f32[4,512,512]{1,2,0:T(8,128)S(1)} %fusion.16, f32[64,4,8,512]{3,2,1,0:T(8,128)S(1)} %bitcast.183, f32[512,4]{0,1:T(4,128)S(1)} %multiply_negate_fusion), kind=kOutput, calls=%fused_computation.27 | convolution fusion | flops 1082130432 | bytes 16785408 | tf_op jit(solution)/shard_map/rhj,rho->hjo/dot_general | solution.py:45
  20.1 4.0 %convolution_bitcast_fusion.1 = f32[4,1,512,512]{3,2,0,1:T(8,128)} fusion(bf16[512,4,512]{0,2,1:T(8,128)(2,1)S(1)} %bitcast.180, f32[4,512,512]{1,2,0:T(8,128)S(1)} %fusion.16, f32[4,512,512]{1,2,0:T(8,128)S(1)} %fusion.18, f32[4,512,512]{2,1,0:T(8,128)S(1)} %fusion.20), kind=kOutput, calls=%fused_computation.26 | convolution fusion | flops 1084227584 | bytes 18874368 | tf_op jit(solution)/shard_map/rhi,rhj->hij/dot_general | solution.py:43
  24.1 3.4 %convolution_bitcast_fusion = f32[4,1,512,512]{3,2,0,1:T(8,128)} fusion(bf16[512,4,512]{0,2,1:T(8,128)(2,1)S(1)} %bitcast.181, f32[4,512,512]{2,1,0:T(8,128)S(1)} %fusion.20, f32[4,512,512]{1,2,0:T(8,128)S(1)} %fusion.16), kind=kOutput, calls=%fused_computation.25 | convolution fusion | flops 1080033280 | bytes 14680064 | tf_op jit(solution)/shard_map/rhi,rhj->hij/dot_general | solution.py:44
  27.5 10.7 %pad_maximum_fusion = f32[4,3,512,512]{3,2,0,1:T(8,128)} fusion(f32[4,1,512,512]{3,2,0,1:T(8,128)} %convolution_bitcast_fusion.2, f32[4,1,512,512]{3,2,0,1:T(8,128)} %convolution_bitcast_fusion, f32[4,1,512,512]{3,2,0,1:T(8,128)} %convolution_bitcast_fusion.1), kind=kLoop, calls=%fused_computation.1 | loop fusion | flops 6291456 | bytes 25165824 | tf_op jit(solution)/shard_map/stack | solution.py:46
  38.2 10.6 %copy.107 = f32[4,3,512,512]{3,2,1,0:T(8,128)} copy(f32[4,3,512,512]{3,2,0,1:T(8,128)} %pad_maximum_fusion) | data formatting | bytes 25165824 | tf_op jit(solution)/shard_map/stack | solution.py:46
  48.8 0.0 reduce-scatter.2.cloned.1.call-update
  48.8 0.0 copy-start.3
  48.9 0.0 all-gather.2.cloned.1.call-start
  48.9 0.5 copy-done.8
  49.5 0.1 select_reduce_fusion.2
  49.5 136.9 %reduce-scatter.2.cloned.1.call-done = f32[384,512]{1,0:T(8,128)} async-done(((f32[6144,512]{1,0:T(8,128)}), f32[384,512]{1,0:T(8,128)}) %reduce-scatter.2.cloned.1.call-update) | async-done | bytes 786448 | tf_op jit(solution)/shard_map/reduce_scatter | solution.py:54
  186.4 1.3 multiply_reduce_fusion.1
  187.7 2.2 subtract_convert_fusion
  189.9 0.0 all-gather.2.cloned.1.call-update
  189.9 0.0 copy-done.6
  189.9 0.1 fusion.60
  190.0 0.2 reduce_window_sum.32
  190.2 0.2 select_reduce_fusion.1
  190.4 0.1 select_reduce_fusion
  190.5 0.7 sub.44
  191.2 4.0 %all-to-all-start = ((s32[16,16,1]{1,2,0:T(1,128)}), s32[16,16,1]{1,2,0:T(1,128)S(1)}, u32[]{:S(2)}, u32[]{:S(2)}) async-start(s32[16,16,1]{1,2,0:T(1,128)} %sub.44), calls=%async_computation.1 | async-start | bytes 16384 | tf_op jit(solution)/shard_map/all_to_all | solution.py:100
  195.2 0.0 copy-done
  195.2 1.4 convolution_convert_fusion
  196.6 5.0 %all-to-all-done = s32[16,16,1]{1,2,0:T(1,128)S(1)} async-done(((s32[16,16,1]{1,2,0:T(1,128)}), s32[16,16,1]{1,2,0:T(1,128)S(1)}, u32[]{:S(2)}, u32[]{:S(2)}) %all-to-all-start) | async-done | bytes 1056 | tf_op jit(solution)/shard_map/all_to_all | solution.py:100
  201.7 3.7 %all-to-all-start.3 = ((bf16[16,16,2048]{2,1,0:T(8,128)(2,1)}), bf16[16,16,2048]{2,1,0:T(8,128)(2,1)S(1)}, u32[]{:S(2)}, u32[]{:S(2)}) async-start(bf16[16,16,2048]{2,1,0:T(8,128)(2,1)} %bitcast.28), calls=%async_computation.4 | async-start | bytes 2097152 | tf_op jit(solution)/shard_map/all_to_all | solution.py:98
  205.3 0.0 copy-done.3
  205.3 1.4 convolution_convert_fusion.1
  206.8 31.1 %all-to-all-done.3 = bf16[16,16,2048]{2,1,0:T(8,128)(2,1)S(1)} async-done(((bf16[16,16,2048]{2,1,0:T(8,128)(2,1)}), bf16[16,16,2048]{2,1,0:T(8,128)(2,1)S(1)}, u32[]{:S(2)}, u32[]{:S(2)}) %all-to-all-start.3) | async-done | bytes 1048608 | tf_op jit(solution)/shard_map/all_to_all | solution.py:98
  237.8 16.5 %all-to-all-start.2 = ((bf16[16,16,2048]{2,1,0:T(8,128)(2,1)}), bf16[16,16,2048]{2,1,0:T(8,128)(2,1)S(1)}, u32[]{:S(2)}, u32[]{:S(2)}) async-start(bf16[16,16,2048]{2,1,0:T(8,128)(2,1)} %bitcast.188), calls=%async_computation.3 | async-start | bytes 2097152 | tf_op jit(solution)/shard_map/all_to_all | solution.py:99
  254.3 0.0 copy-done.4
  254.3 1.4 convolution_convert_fusion.2
  255.8 25.2 %all-to-all-done.2 = bf16[16,16,2048]{2,1,0:T(8,128)(2,1)S(1)} async-done(((bf16[16,16,2048]{2,1,0:T(8,128)(2,1)}), bf16[16,16,2048]{2,1,0:T(8,128)(2,1)S(1)}, u32[]{:S(2)}, u32[]{:S(2)}) %all-to-all-start.2) | async-done | bytes 1048608 | tf_op jit(solution)/shard_map/all_to_all | solution.py:99
  281.0 6.6 %all-to-all-start.1 = ((bf16[16,16,2048]{2,1,0:T(8,128)(2,1)}), bf16[16,16,2048]{2,1,0:T(8,128)(2,1)}, u32[]{:S(2)}, u32[]{:S(2)}) async-start(bf16[16,16,2048]{2,1,0:T(8,128)(2,1)} %bitcast.187), calls=%async_computation.2 | async-start | bytes 2097152 | tf_op jit(solution)/shard_map/all_to_all | solution.py:97
  287.6 0.1 ge.29
  287.7 0.1 reshape.215
  287.8 0.3 reduce-window.6
  288.1 0.2 slice_reduce_fusion
  288.3 0.2 reduce-window.9
  288.5 0.1 broadcast.224
  288.6 0.3 convolution_convert_fusion.4
  288.9 0.3 copy.124
  289.2 0.3 convolution_convert_fusion.3
  289.5 21.1 %all-to-all-done.1 = bf16[16,16,2048]{2,1,0:T(8,128)(2,1)} async-done(((bf16[16,16,2048]{2,1,0:T(8,128)(2,1)}), bf16[16,16,2048]{2,1,0:T(8,128)(2,1)}, u32[]{:S(2)}, u32[]{:S(2)}) %all-to-all-start.1) | async-done | bytes 1048608 | tf_op jit(solution)/shard_map/all_to_all | solution.py:97
  310.6 1.5 convolution_convert_fusion.5
  312.1 0.3 convolution_multiply_fusion
  312.4 0.1 fusion.71
  312.5 0.0 all-gather.2.cloned.1.call-done
  312.5 3.5 %fusion.27 = f32[128,4,512]{0,2,1:T(8,128)} fusion(bf16[4,3,512,512]{3,2,1,0:T(8,128)(2,1)} %bitcast.196, bf16[16,4,8,512]{3,2,1,0:T(8,128)(2,1)S(1)} %bitcast.192), kind=kOutput, calls=%fused_computation.44 | convolution fusion | flops 268435456 | bytes 3670016 | tf_op jit(solution)/shard_map/rhi,hij->rhj/dot_general | solution.py:145
  316.0 4.1 %multiply_reduce_fusion = (f32[128,4]{0,1:T(4,128)S(1)}, f32[128,4,512]{0,2,1:T(8,128)S(1)}) fusion(bf16[4,3,512,512]{3,2,1,0:T(8,128)(2,1)} %bitcast.197, f32[128,4,512]{0,2,1:T(8,128)} %fusion.27, bf16[16,4,8,512]{3,2,1,0:T(8,128)(2,1)S(1)} %bitcast.193), kind=kOutput, calls=%fused_computation.54 | convolution fusion | flops 538967552 | bytes 6817792 | tf_op jit(solution)/shard_map/rhj,hjo->rho/dot_general | solution.py:151
  320.1 0.3 fusion.32
  320.4 1.0 copy.118
  (16 shorter events, 0.1 us)
Async XLA Ops:
  6.5 188.7 %copy-start = (bf16[128,2048]{1,0:T(8,128)(2,1)S(1)}, bf16[128,2048]{1,0:T(8,128)(2,1)}, u32[]{:S(2)}) copy-start(bf16[128,2048]{1,0:T(8,128)(2,1)} %param.17) | copy-start | bytes 1572868
  6.5 179.9 %reduce-scatter.2.cloned.1.call-start = ((), (), s32[]{:S(2)}) async-start(), calls=%async_computation.5 | async-start | bytes 13369344 | tf_op jit(solution)/shard_map/reduce_scatter | solution.py:54
  9.5 3.4 %copy-start.1 = (bf16[4,3,512,512]{3,2,1,0:T(8,128)(2,1)S(1)}, bf16[4,3,512,512]{3,2,1,0:T(8,128)(2,1)}, u32[]{:S(2)}) copy-start(bf16[4,3,512,512]{3,2,1,0:T(8,128)(2,1)} %param.14) | copy-start | bytes 18874372
  12.9 1.3 copy-start.7
  12.9 1.6 copy-start.2
  14.2 0.8 copy-start.5
  48.8 0.7 copy-start.8
  48.8 141.1 %copy-start.6 = (s32[128]{0:T(128)S(1)}, s32[128]{0:T(128)}, u32[]{:S(2)}) copy-start(s32[128]{0:T(128)} %param.19) | copy-start | bytes 1540
  48.8 156.5 %copy-start.3 = (bf16[128,2048]{1,0:T(8,128)(2,1)S(1)}, bf16[128,2048]{1,0:T(8,128)(2,1)}, u32[]{:S(2)}) copy-start(bf16[128,2048]{1,0:T(8,128)(2,1)} %param.18) | copy-start | bytes 1572868
  48.9 263.7 %all-gather.2.cloned.1.call-start = ((), (), s32[]{:S(2)}) async-start(), calls=%async_computation.6 | async-start | bytes 6684672 | tf_op jit(solution)/shard_map/all_gather | solution.py:68
  189.9 64.5 %copy-start.4 = (bf16[128,2048]{1,0:T(8,128)(2,1)S(1)}, bf16[128,2048]{1,0:T(8,128)(2,1)}, u32[]{:S(2)}) copy-start(bf16[128,2048]{1,0:T(8,128)(2,1)} %param.16) | copy-start | bytes 1572868
  191.2 10.5 %all-to-all-start = ((s32[16,16,1]{1,2,0:T(1,128)}), s32[16,16,1]{1,2,0:T(1,128)S(1)}, u32[]{:S(2)}, u32[]{:S(2)}) async-start(s32[16,16,1]{1,2,0:T(1,128)} %sub.44), calls=%async_computation.1 | async-start | bytes 16384 | tf_op jit(solution)/shard_map/all_to_all | solution.py:100
  201.7 36.2 %all-to-all-start.3 = ((bf16[16,16,2048]{2,1,0:T(8,128)(2,1)}), bf16[16,16,2048]{2,1,0:T(8,128)(2,1)S(1)}, u32[]{:S(2)}, u32[]{:S(2)}) async-start(bf16[16,16,2048]{2,1,0:T(8,128)(2,1)} %bitcast.28), calls=%async_computation.4 | async-start | bytes 2097152 | tf_op jit(solution)/shard_map/all_to_all | solution.py:98
  237.8 43.1 %all-to-all-start.2 = ((bf16[16,16,2048]{2,1,0:T(8,128)(2,1)}), bf16[16,16,2048]{2,1,0:T(8,128)(2,1)S(1)}, u32[]{:S(2)}, u32[]{:S(2)}) async-start(bf16[16,16,2048]{2,1,0:T(8,128)(2,1)} %bitcast.188), calls=%async_computation.3 | async-start | bytes 2097152 | tf_op jit(solution)/shard_map/all_to_all | solution.py:99
  281.0 29.6 %all-to-all-start.1 = ((bf16[16,16,2048]{2,1,0:T(8,128)(2,1)}), bf16[16,16,2048]{2,1,0:T(8,128)(2,1)}, u32[]{:S(2)}, u32[]{:S(2)}) async-start(bf16[16,16,2048]{2,1,0:T(8,128)(2,1)} %bitcast.187), calls=%async_computation.2 | async-start | bytes 2097152 | tf_op jit(solution)/shard_map/all_to_all | solution.py:97
Sparse Core Ops, SparseCore 0:
  49.0 137.4 reduce-scatter.1
  190.0 87.6 all-gather.1
where the time goes:
time: 330 us; the launch traced here: 328 us
  waiting for transfers between devices  219 us (66%)
  matrix products  31.3 us (9%)
  starting transfers between devices  30.8 us (9%)
  local copies, waits for them, and re-layouts  17.1 us (5%)
  other arithmetic  16.1 us (5%)
  between operations  13.7 us (4%)
    reduce_scatter x1, waiting for transfers between devices, update_weights(): lax.psum_scatter(grad_local.reshape(flat_rows, head_width), 'tokens', sca...  137 us
    all_to_all x1, waiting for transfers between devices, regroup_rows(): lax.all_to_all(sent_keys, 'tokens', split_axis=0, concat_axis=0, tiled=True)  31.1 us
    all_to_all x1, waiting for transfers between devices, regroup_rows(): lax.all_to_all(sent_values, 'tokens', split_axis=0, concat_axis=0, tiled=...  25.2 us
    all_to_all x1, waiting for transfers between devices, regroup_rows(): lax.all_to_all(sent_queries, 'tokens', split_axis=0, concat_axis=0, tiled...  21.1 us
    all_to_all x1, starting transfers between devices, regroup_rows(): lax.all_to_all(sent_values, 'tokens', split_axis=0, concat_axis=0, tiled=...  16.5 us
    another operation x1, other arithmetic, local_gradient(): return jnp.stack([gate_term, up_term, down_term], axis=1)  10.7 us
    another operation x1, local copies, waits for them, and re-layouts, local_gradient(): return jnp.stack([gate_term, up_term, down_term], axis=1)  10.6 us
  transfers between devices with their start and end apart: 6, of which 5 were waited for; matrix products, arithmetic and copies ran while one was open for 3% of the time, Pallas kernels for 0%

commit v1 on v0

v1 whole, which is shorter than its diff:
```python
import jax
import jax.numpy as jnp
from jax import lax
from jax.sharding import PartitionSpec as P

VIEW_ROWS = 128
AXIS = "tokens"
epsilon = 1e-05
f32 = jnp.float32
bf16 = jnp.bfloat16


def row_normalize(matrix):
    return matrix * lax.rsqrt(jnp.mean(matrix * matrix, axis=-1, keepdims=True) + epsilon)


def swap(value, mask, senders=None):
    count = lax.axis_size(AXIS)
    pairs = [(t, t ^ mask) for t in range(count) if senders is None or senders(t)]
    return lax.ppermute(value, AXIS, pairs)


def head_of(plane, head_count):
    half = head_count // 2
    return (plane % 2) * half + plane // 2


def head_partials(keys, grads, weights, bit):
    pre_gate = jnp.dot(keys, weights[0], preferred_element_type=f32)
    pre_up = jnp.dot(keys, weights[1], preferred_element_type=f32)
    back = lax.dot_general(grads, weights[2], (((1,), (1,)), ((), ())), preferred_element_type=f32)
    sigma = jax.nn.sigmoid(pre_gate)
    activated = pre_gate * sigma
    hidden = (activated * pre_up).astype(bf16)
    grad_gate = (back * pre_up * (sigma * (1.0 + pre_gate * (1.0 - sigma)))).astype(bf16)
    grad_up = (back * activated).astype(bf16)
    out = []
    for left, right in ((keys, grad_gate), (keys, grad_up), (hidden, grads)):
        full = lax.dot_general(
            left, right, (((0,), (0,)), ((), ())), preferred_element_type=f32
        ).astype(bf16)
        rows = full.shape[0] // 2
        keep = lax.dynamic_slice_in_dim(full, bit * rows, rows, 0)
        send = lax.dynamic_slice_in_dim(full, (1 - bit) * rows, rows, 0)
        out.append((send, keep))
    return out


def on_device(
    update_keys,
    update_values,
    update_rates,
    update_mask,
    fast_weights,
    step_sizes,
    target_queries,
    target_keys,
    target_values,
    target_views,
):
    heads, _, width, _ = fast_weights.shape
    count = lax.axis_size(AXIS)
    me = lax.axis_index(AXIS)
    span = count // heads
    plane, inner = me // span, me % span
    core = inner % 2
    half = heads // 2
    inner_bits = [b for b in range(1, span.bit_length() - 1)]
    my_head = head_of(plane, heads)
    bit_of = lambda b: (me >> b) & 1
    first_bit = bit_of(1)

    rates = -(update_mask.astype(f32)[:, None] * update_rates)

    def grads_of(which):
        cols = lax.dynamic_slice_in_dim(update_values, which * half * width, half * width, 1)
        rate = lax.dynamic_slice_in_dim(rates, which * half, half, 1)
        rows = cols.shape[0]
        scaled = rate[:, :, None] * cols.reshape(rows, half, width).astype(f32)
        return scaled.reshape(rows, half * width).astype(bf16)

    def keys_of(which):
        return lax.dynamic_slice_in_dim(update_keys, which * half * width, half * width, 1)

    keys_in = swap(keys_of(1 - core), 1)
    grads_in = swap(grads_of(1 - core), 1)
    keys_all = jnp.concatenate([keys_of(core), keys_in], axis=0)
    grads_all = jnp.concatenate([grads_of(core), grads_in], axis=0)

    def rows_for(dest):
        head = head_of(dest, heads)
        return jnp.stack(
            [
                lax.dynamic_slice_in_dim(x, head * width, width, 1)
                for x in (target_queries, target_keys, target_values)
            ]
        )

    pieces = []
    for step in range(heads):
        piece = rows_for(plane ^ step)
        if step:
            piece = swap(piece, step * span)
        group = [(0, piece)]
        for b in reversed([0] + inner_bits):
            group = group + [(e | (1 << b), swap(x, 1 << b)) for e, x in group]
        pieces.append([x for _, x in sorted(group, key=lambda item: item[0])])

    views = lax.all_gather(target_views, AXIS, axis=0, tiled=True)
    mine = (views % span) == inner
    view_hit = (
        mine[:, None] & ((views // span)[:, None] == jnp.arange(heads, dtype=jnp.int32)[None, :])
    ).astype(jnp.int32)
    rank = jnp.sum(view_hit * (jnp.cumsum(view_hit, axis=0) - 1), axis=1)
    place = jnp.where(mine, (views // span) * VIEW_ROWS + rank, -1)
    bits = count.bit_length() - 1
    place = place.reshape((2,) * bits + (-1,))
    for b in range(bits):
        place = jnp.where(bit_of(b) == 1, jnp.flip(place, axis=bits - 1 - b), place)
    place = place.reshape(-1)
    pick = (
        jnp.arange(heads * VIEW_ROWS, dtype=jnp.int32)[:, None] == place[None, :]
    ).astype(bf16)
    gathered = jnp.concatenate([x for group in pieces for x in group], axis=1)
    arranged = [
        jnp.dot(pick, gathered[i], preferred_element_type=f32).astype(bf16) for i in range(3)
    ]

    fresh_parts = []
    reduced = {}
    for j in range(half):
        head = core * half + j
        weights = lax.dynamic_index_in_dim(fast_weights, head, 0, keepdims=False)
        cols = slice(j * width, (j + 1) * width)
        parts = head_partials(keys_all[:, cols], grads_all[:, cols], weights, first_bit)
        for i in (2, 0, 1):
            send, keep = parts[i]
            total = keep.astype(f32) + swap(send, 2).astype(f32)
            for b in inner_bits[1:]:
                rows = total.shape[0] // 2
                send = lax.dynamic_slice_in_dim(total, (1 - bit_of(b)) * rows, rows, 0)
                keep = lax.dynamic_slice_in_dim(total, bit_of(b) * rows, rows, 0)
                total = keep + swap(send.astype(bf16), 1 << b).astype(f32)
            total = total + swap(
                total.astype(bf16), span, lambda t: (t // span) % 2 != t % 2
            ).astype(f32)
            for b in range(1, heads.bit_length() - 1):
                mask = 1 << (b - 1)
                total = total + swap(
                    total.astype(bf16),
                    span << b,
                    lambda t: (t // span) % 2 == t % 2
                    and ((t // span) // 2 % (2 * mask)) == ((j % (2 * mask)) ^ mask),
                ).astype(f32)
            reduced[j, i] = total

    share_rows = reduced[0, 0].shape[0]
    first_row = jnp.int32(0)
    for b in inner_bits:
        first_row = first_row * 2 + bit_of(b)
    first_row = first_row * share_rows
    owner = lambda t: (t // span) % 2 == t % 2
    is_owner = (plane % 2) == core
    step_size = lax.dynamic_index_in_dim(step_sizes, my_head, 0, keepdims=False)
    fresh = []
    for i in range(3):
        total = reduced[0, i]
        for j in range(1, half):
            total = jnp.where(plane // 2 == j, reduced[j, i], total)
        old = lax.dynamic_slice(
            fast_weights, (my_head, i, first_row, 0), (1, 1, share_rows, width)
        ).reshape(share_rows, width)
        new = (old.astype(f32) - step_size * row_normalize(total)).astype(bf16)
        for b in reversed(inner_bits):
            other = swap(new, 1 << b, owner)
            new = jnp.where(
                bit_of(b) == 1,
                jnp.concatenate([other, new], axis=0),
                jnp.concatenate([new, other], axis=0),
            )
        other = swap(new, 1, owner)
        fresh.append(jnp.where(is_owner, new, other))

    view_shape = (heads, VIEW_ROWS, width)
    scores = jnp.einsum(
        "vqd,vkd->vqk",
        arranged[0].reshape(view_shape),
        arranged[1].reshape(view_shape),
        preferred_element_type=f32,
    ) * width ** (-0.5)
    probs = jax.nn.softmax(scores, axis=-1).astype(bf16)
    attended = jnp.einsum(
        "vqk,vkd->vqd", probs, arranged[2].reshape(view_shape), preferred_element_type=f32
    ).reshape(heads * VIEW_ROWS, width)
    pre_gate = jnp.dot(arranged[0], fresh[0], preferred_element_type=f32)
    pre_up = jnp.dot(arranged[0], fresh[1], preferred_element_type=f32)
    hidden = (jax.nn.sigmoid(pre_gate) * pre_gate * pre_up).astype(bf16)
    fast_out = jnp.dot(hidden, fresh[2], preferred_element_type=f32)
    mixed = (row_normalize(fast_out) + attended).astype(bf16).reshape(view_shape)

    got = []
    for step in range(heads):
        block = lax.dynamic_index_in_dim(mixed, plane ^ step, 0, keepdims=False)
        got.append(swap(block, step * span) if step else block)
    columns = []
    for head in range(heads):
        source = (head % half) * 2 + head // half
        column = got[0]
        for step in range(1, heads):
            column = jnp.where((plane ^ step) == source, got[step], column)
        columns.append(column)
    return jnp.concatenate(columns, axis=1)


def solution(mesh):
    rows = P(("groups", "tokens"), None)
    return jax.shard_map(
        on_device,
        mesh=mesh,
        in_specs=(
            rows,
            rows,
            rows,
            P(("groups", "tokens")),
            P(),
            P(),
            rows,
            rows,
            rows,
            P(("groups", "tokens")),
        ),
        out_specs=rows,
        check_vma=False,
    )
```

time: 330 us -> 212 us (0.64)
  waiting for transfers between devices: 219 us -> 52.1 us
  starting transfers between devices: 30.8 us -> 66.3 us
  blocking collectives: 0 us -> 29.4 us
  between operations: 13.7 us -> 0.95 us
  matrix products: 31.3 us -> 19 us
  other arithmetic: 16.1 us -> 21.3 us
  local copies, waits for them, and re-layouts: 17.1 us -> 21.7 us
    reduce_scatter x1 -> x0, waiting for transfers between devices: 137 us -> none  [update_weights(): lax.psum_scatter(grad_local.reshape(flat_rows, head_width), 'tokens', sca...]
    all_to_all x4 -> x0, waiting for transfers between devices: 82.4 us -> none  [the longest x1 31.1 us: regroup_rows(): lax.all_to_all(sent_keys, 'tokens', split_axis=0, concat_axis=0, tiled=True)]
    ppermute x0 -> x44, starting transfers between devices: none -> 66.3 us  [swap(): return lax.ppermute(value, AXIS, pairs)]
    ppermute x0 -> x44, waiting for transfers between devices: none -> 52.1 us  [swap(): return lax.ppermute(value, AXIS, pairs)]
    all_to_all x4 -> x0, starting transfers between devices: 30.8 us -> none  [the longest x1 16.5 us: regroup_rows(): lax.all_to_all(sent_values, 'tokens', split_axis=0, concat_axis=0, tiled=...]
    all_gather x0 -> x1, blocking collectives: none -> 29.4 us  [on_device(): views = lax.all_gather(target_views, AXIS, axis=0, tiled=True)]
    dot_general x16 -> x19, matrix products: 31.3 us -> 19 us  [the longest x6 5.48 us: head_partials(): lax.dot_general(left, right, (((0,), (0,)), ((), ())), preferred_element_...]
    unnamed x18 -> x52, local copies, waits for them, and re-layouts: 1.19 us -> 12.3 us
  transfers between devices with their start and end apart: 6 -> 44, of which waited for: 5 -> 15; matrix products, arithmetic and copies ran while one was open for 3% -> 23% of each run, Pallas kernels for 0% -> 0%
where the time goes in v1:
time: 212 us; the launch traced here: 211 us
  starting transfers between devices  66.3 us (31%)
  waiting for transfers between devices  52.1 us (25%)
  blocking collectives  29.4 us (14%)
  local copies, waits for them, and re-layouts  21.7 us (10%)
  other arithmetic  21.3 us (10%)
  matrix products  19 us (9%)
    ppermute x44, starting transfers between devices, swap(): return lax.ppermute(value, AXIS, pairs)  66.3 us
    ppermute x44, waiting for transfers between devices, swap(): return lax.ppermute(value, AXIS, pairs)  52.1 us
    all_gather x1, blocking collectives, on_device(): views = lax.all_gather(target_views, AXIS, axis=0, tiled=True)  29.4 us
    unnamed x52, local copies, waits for them, and re-layouts  12.3 us
    dot_general x6, matrix products, head_partials(): lax.dot_general(left, right, (((0,), (0,)), ((), ())), preferred_element_...  5.48 us
    convert_element_type x1, other arithmetic, grads_of(): return scaled.reshape(rows, half * width).astype(bf16)  4.44 us
  transfers between devices with their start and end apart: 44, of which 15 were waited for; matrix products, arithmetic and copies ran while one was open for 23% of the time, Pallas kernels for 0%

profile of v1, /device:TPU:0, one launch (start us, length us, event | category | flops | bytes accessed | tf_op | source)
XLA Modules:
  0.0 210.7 jit_solution(10577225888726591850)
XLA Ops:
  0.0 2.0 dynamic-slice_bitcast_fusion.17
  2.0 2.1 dynamic-slice_bitcast_fusion.15
  4.1 1.0 pad_maximum_fusion.6
  5.5 2.5 %collective-permute-start.1 = (bf16[3,128,512]{2,1,0:T(8,128)(2,1)}, bf16[3,128,512]{2,1,0:T(8,128)(2,1)}, u32[]{:S(2)}, u32[]{:S(2)}) collective-permute-start(bf16[3,128,512]{2,1,0:T(8,128)(2,1)} %get-tuple-element.39), channel_id=1, source_target_pairs={{0,2},{1,3},{2,0},{3,1},{4,6},{5,7},{6,4},{7,5},{8,10},{9,11},{10,... | collective-permute-start | bytes 1179656 | tf_op jit(solution)/shard_map/ppermute | solution.py:20
  8.1 1.2 constant_dynamic-slice_fusion.9
  10.3 1.6 collective-permute-start.3
  12.7 2.6 %collective-permute-start.7 = (bf16[3,128,512]{2,1,0:T(8,128)(2,1)}, bf16[3,128,512]{2,1,0:T(8,128)(2,1)}, u32[]{:S(2)}, u32[]{:S(2)}) collective-permute-start(bf16[3,128,512]{2,1,0:T(8,128)(2,1)} %pad_maximum_fusion.4), channel_id=1, source_target_pairs={{0,8},{1,9},{2,10},{3,11},{4,12},{5,13},{6,14},{7,15},{8,0},{9,1},... | collective-permute-start | bytes 1179656 | tf_op jit(solution)/shard_map/ppermute | solution.py:20
  15.3 29.4 %all-gather = s32[16,1,128]{2,1,0:T(1,128)S(1)} all-gather(s32[1,1,128]{2,1,0:T(1,128)S(1)} %bitcast.168), channel_id=1, replica_groups=mesh['groups'=2,'tokens'=16] {'tokens'}, dimensions={0}, use_global_device_ids=true | all-gather | bytes 8704 | tf_op jit(solution)/shard_map/all_gather | solution.py:109
  51.3 1.9 copy.23
  53.2 1.3 reduce-window.6
  55.1 4.4 %multiply_convert_fusion.7 = (bf16[512,1024]{1,0:T(8,128)(2,1)}, bf16[512,1024]{1,0:T(8,128)(2,1)}) fusion(f32[512,1024]{1,0:T(8,128)S(1)} %bitcast.144, bf16[512,2048]{1,0:T(8,128)(2,1)} %param.11, s32[]{:T(128)S(6)} %select_n.323, f32[512,1024]{1,0:T(8,128)} %bitcast.145, s32[]{:T(128)S(6)} %select_n.324), kind=kLoop, calls=%fused_computation.23 | loop fusion | flops 3145728 | bytes 8388616 | tf_op jit(solution)/shard_map/convert_element_type | solution.py:80
  61.1 1.8 constant_dynamic-update-slice_fusion.14
  63.0 1.8 constant_dynamic-update-slice_fusion.13
  65.6 1.9 constant_dynamic-update-slice_fusion.11
  68.8 5.2 %collective-permute-done.11 = bf16[3,128,512]{2,1,0:T(8,128)(2,1)S(1)} collective-permute-done((bf16[3,128,512]{2,1,0:T(8,128)(2,1)S(1)}, bf16[3,128,512]{2,1,0:T(8,128)(2,1)S(1)}, u32[]{:S(2)}, u32[]{:S(2)}) %collective-permute-start.11) | collective-permute-done | bytes 393248 | tf_op jit(solution)/shard_map/ppermute | solution.py:20
  75.2 1.6 collective-permute-start.13
  76.8 1.5 fusion.15
  78.3 1.7 fusion.20
  82.2 4.0 %collective-permute-done.9 = bf16[3,128,512]{2,1,0:T(8,128)(2,1)S(1)} collective-permute-done((bf16[3,128,512]{2,1,0:T(8,128)(2,1)}, bf16[3,128,512]{2,1,0:T(8,128)(2,1)S(1)}, u32[]{:S(2)}, u32[]{:S(2)}) %collective-permute-start.9) | collective-permute-done | bytes 393248 | tf_op jit(solution)/shard_map/ppermute | solution.py:20
  86.2 6.7 %collective-permute-done.13 = bf16[3,128,512]{2,1,0:T(8,128)(2,1)S(1)} collective-permute-done((bf16[3,128,512]{2,1,0:T(8,128)(2,1)S(1)}, bf16[3,128,512]{2,1,0:T(8,128)(2,1)S(1)}, u32[]{:S(2)}, u32[]{:S(2)}) %collective-permute-start.13) | collective-permute-done | bytes 393248 | tf_op jit(solution)/shard_map/ppermute | solution.py:20
  95.0 1.1 convolution_convert_fusion.5
  97.7 1.1 convolution_convert_fusion.4
  102.0 1.0 constant_dynamic-update-slice_fusion.7
  103.0 0.9 collective-permute-start.36
  104.0 1.2 collective-permute-start.17
  105.3 0.9 collective-permute-start.20
  106.3 1.2 collective-permute-start.25
  107.6 1.5 fusion.9
  109.1 1.3 fusion.10
  110.4 0.9 collective-permute-start.28
  111.4 4.2 %collective-permute-done.36 = bf16[256,512]{1,0:T(8,128)(2,1)S(1)} collective-permute-done((bf16[256,512]{1,0:T(8,128)(2,1)S(1)}, bf16[256,512]{1,0:T(8,128)(2,1)S(1)}, u32[]{:S(2)}, u32[]{:S(2)}) %collective-permute-start.36) | collective-permute-done | bytes 262176 | tf_op jit(solution)/shard_map/ppermute | solution.py:20
  115.6 1.3 collective-permute-start.34
  116.9 4.2 %collective-permute-done.17 = bf16[256,512]{1,0:T(8,128)(2,1)S(1)} collective-permute-done((bf16[256,512]{1,0:T(8,128)(2,1)S(1)}, bf16[256,512]{1,0:T(8,128)(2,1)S(1)}, u32[]{:S(2)}, u32[]{:S(2)}) %collective-permute-start.17) | collective-permute-done | bytes 262176 | tf_op jit(solution)/shard_map/ppermute | solution.py:20
  121.2 1.3 collective-permute-start.37
  122.5 4.2 %collective-permute-done.20 = bf16[256,512]{1,0:T(8,128)(2,1)S(1)} collective-permute-done((bf16[256,512]{1,0:T(8,128)(2,1)S(1)}, bf16[256,512]{1,0:T(8,128)(2,1)S(1)}, u32[]{:S(2)}, u32[]{:S(2)}) %collective-permute-start.20) | collective-permute-done | bytes 262176 | tf_op jit(solution)/shard_map/ppermute | solution.py:20
  126.8 1.3 collective-permute-start.18
  128.2 4.2 %collective-permute-done.25 = bf16[256,512]{1,0:T(8,128)(2,1)S(1)} collective-permute-done((bf16[256,512]{1,0:T(8,128)(2,1)S(1)}, bf16[256,512]{1,0:T(8,128)(2,1)S(1)}, u32[]{:S(2)}, u32[]{:S(2)}) %collective-permute-start.25) | collective-permute-done | bytes 262176 | tf_op jit(solution)/shard_map/ppermute | solution.py:20
  132.4 1.3 collective-permute-start.21
  133.8 3.3 %collective-permute-done.28 = bf16[256,512]{1,0:T(8,128)(2,1)S(1)} collective-permute-done((bf16[256,512]{1,0:T(8,128)(2,1)S(1)}, bf16[256,512]{1,0:T(8,128)(2,1)S(1)}, u32[]{:S(2)}, u32[]{:S(2)}) %collective-permute-start.28) | collective-permute-done | bytes 262176 | tf_op jit(solution)/shard_map/ppermute | solution.py:20
  137.1 1.3 collective-permute-start.26
  138.5 1.3 collective-permute-start.29
  139.9 8.3 %collective-permute-start.35 = (bf16[256,512]{1,0:T(8,128)(2,1)S(1)}, bf16[256,512]{1,0:T(8,128)(2,1)S(1)}, u32[]{:S(2)}, u32[]{:S(2)}) collective-permute-start(bf16[256,512]{1,0:T(8,128)(2,1)S(1)} %fusion.54), channel_id=1, source_target_pairs={{0,8},{2,10},{5,13},{7,15},{16,24},{18,26},{21,29},{23,31}} | collective-permute-start | bytes 786440 | tf_op jit(solution)/shard_map/ppermute | solution.py:20
  148.3 1.3 collective-permute-start.38
  149.8 5.5 %collective-permute-start.19 = (bf16[256,512]{1,0:T(8,128)(2,1)S(1)}, bf16[256,512]{1,0:T(8,128)(2,1)S(1)}, u32[]{:S(2)}, u32[]{:S(2)}) collective-permute-start(bf16[256,512]{1,0:T(8,128)(2,1)S(1)} %fusion.50), channel_id=1, source_target_pairs={{0,8},{2,10},{5,13},{7,15},{16,24},{18,26},{21,29},{23,31}} | collective-permute-start | bytes 786440 | tf_op jit(solution)/shard_map/ppermute | solution.py:20
  155.4 1.3 collective-permute-start.22
  156.8 5.5 %collective-permute-start.27 = (bf16[256,512]{1,0:T(8,128)(2,1)S(1)}, bf16[256,512]{1,0:T(8,128)(2,1)S(1)}, u32[]{:S(2)}, u32[]{:S(2)}) collective-permute-start(bf16[256,512]{1,0:T(8,128)(2,1)S(1)} %fusion.52), channel_id=1, source_target_pairs={{0,8},{2,10},{5,13},{7,15},{16,24},{18,26},{21,29},{23,31}} | collective-permute-start | bytes 786440 | tf_op jit(solution)/shard_map/ppermute | solution.py:20
  162.4 1.3 collective-permute-start.30
  164.1 3.2 %collective-permute-done.22 = bf16[256,512]{1,0:T(8,128)(2,1)S(1)} collective-permute-done((bf16[256,512]{1,0:T(8,128)(2,1)S(1)}, bf16[256,512]{1,0:T(8,128)(2,1)S(1)}, u32[]{:S(2)}, u32[]{:S(2)}) %collective-permute-start.22) | collective-permute-done | bytes 262176 | tf_op jit(solution)/shard_map/ppermute | solution.py:20
  167.8 3.8 %collective-permute-done.30 = bf16[256,512]{1,0:T(8,128)(2,1)S(1)} collective-permute-done((bf16[256,512]{1,0:T(8,128)(2,1)S(1)}, bf16[256,512]{1,0:T(8,128)(2,1)S(1)}, u32[]{:S(2)}, u32[]{:S(2)}) %collective-permute-start.30) | collective-permute-done | bytes 262176 | tf_op jit(solution)/shard_map/ppermute | solution.py:20
  172.0 0.9 fusion.24
  172.9 2.5 %collective-permute-start.23 = (bf16[256,512]{1,0:T(8,128)(2,1)S(1)}, bf16[256,512]{1,0:T(8,128)(2,1)S(1)}, u32[]{:S(2)}, u32[]{:S(2)}) collective-permute-start(bf16[256,512]{1,0:T(8,128)(2,1)S(1)} %get-tuple-element.12), channel_id=1, source_target_pairs={{0,2},{2,0},{5,7},{7,5},{8,10},{10,8},{13,15},{15,13},{16,18},{18,... | collective-permute-start | bytes 786440 | tf_op jit(solution)/shard_map/ppermute | solution.py:20
  175.5 1.3 fusion.11
  176.7 3.3 %collective-permute-start.31 = (bf16[256,512]{1,0:T(8,128)(2,1)S(1)}, bf16[256,512]{1,0:T(8,128)(2,1)S(1)}, u32[]{:S(2)}, u32[]{:S(2)}) collective-permute-start(bf16[256,512]{1,0:T(8,128)(2,1)S(1)} %get-tuple-element.11), channel_id=1, source_target_pairs={{0,2},{2,0},{5,7},{7,5},{8,10},{10,8},{13,15},{15,13},{16,18},{18,... | collective-permute-start | bytes 786440 | tf_op jit(solution)/shard_map/ppermute | solution.py:20
  180.3 2.5 %collective-permute-start.39 = (bf16[256,512]{1,0:T(8,128)(2,1)S(1)}, bf16[256,512]{1,0:T(8,128)(2,1)S(1)}, u32[]{:S(2)}, u32[]{:S(2)}) collective-permute-start(bf16[256,512]{1,0:T(8,128)(2,1)S(1)} %get-tuple-element.13), channel_id=1, source_target_pairs={{0,2},{2,0},{5,7},{7,5},{8,10},{10,8},{13,15},{15,13},{16,18},{18,... | collective-permute-start | bytes 786440 | tf_op jit(solution)/shard_map/ppermute | solution.py:20
  183.1 2.1 collective-permute-start.24
  185.3 1.0 maximum_select_fusion.1
  186.3 2.1 collective-permute-start.32
  188.6 1.0 maximum_select_fusion.2
  189.6 2.1 collective-permute-start.40
  192.8 3.0 %multiply_reduce_fusion = (f32[512]{0:T(512)S(1)}, f32[512,512]{1,0:T(8,128)}) fusion(bf16[512,512]{1,0:T(8,128)(2,1)} %maximum_select_fusion.2, bf16[512,512]{1,0:T(8,128)(2,1)} %collective-permute-done.40, pred[]{:T(512)S(6)} %eq.132, f32[512,512]{1,0:T(8,128)S(1)} %fusion.34, bf16[512,512]{1,0:T(8,128)(2,1)S(1)} %fusion.9, ...), kind=kOutput, calls=%fused_computation.45 | convolution fusion | flops 539491840 | bytes 4720641 | tf_op jit(solution)/shard_map/dot_general | solution.py:198
  195.8 1.5 fusion.16
  197.5 4.3 %collective-permute-start.43 = (bf16[128,512]{1,0:T(8,128)(2,1)S(1)}, bf16[128,512]{1,0:T(8,128)(2,1)S(1)}, u32[]{:S(2)}, u32[]{:S(2)}) collective-permute-start(bf16[128,512]{1,0:T(8,128)(2,1)S(1)} %get-tuple-element.24), channel_id=1, source_target_pairs={{0,4},{1,5},{2,6},{3,7},{4,0},{5,1},{6,2},{7,3},{8,12},{9,13},{10,... | collective-permute-start | bytes 393224 | tf_op jit(solution)/shard_map/ppermute | solution.py:20
  201.8 3.9 %collective-permute-done.41 = bf16[128,512]{1,0:T(8,128)(2,1)S(1)} collective-permute-done((bf16[128,512]{1,0:T(8,128)(2,1)S(1)}, bf16[128,512]{1,0:T(8,128)(2,1)S(1)}, u32[]{:S(2)}, u32[]{:S(2)}) %collective-permute-start.41) | collective-permute-done | bytes 131104 | tf_op jit(solution)/shard_map/ppermute | solution.py:20
  205.7 4.1 %collective-permute-done.42 = bf16[128,512]{1,0:T(8,128)(2,1)S(1)} collective-permute-done((bf16[128,512]{1,0:T(8,128)(2,1)S(1)}, bf16[128,512]{1,0:T(8,128)(2,1)S(1)}, u32[]{:S(2)}, u32[]{:S(2)}) %collective-permute-start.42) | collective-permute-done | bytes 131104 | tf_op jit(solution)/shard_map/ppermute | solution.py:20
  (166 shorter events, 28.6 us)
Async XLA Ops:
  0.0 8.0 %copy-start.1 = (bf16[512,2048]{1,0:T(8,128)(2,1)S(1)}, bf16[512,2048]{1,0:T(8,128)(2,1)}, u32[]{:S(2)}) copy-start(bf16[512,2048]{1,0:T(8,128)(2,1)} %param.10) | copy-start | bytes 6291460
  5.1 55.7 %collective-permute-start = (bf16[3,128,512]{2,1,0:T(8,128)(2,1)}, bf16[3,128,512]{2,1,0:T(8,128)(2,1)}, u32[]{:S(2)}, u32[]{:S(2)}) collective-permute-start(bf16[3,128,512]{2,1,0:T(8,128)(2,1)} %get-tuple-element.39), channel_id=1, source_target_pairs={{0,1},{1,0},{2,3},{3,2},{4,5},{5,4},{6,7},{7,6},{8,9},{9,8},{10,11... | collective-permute-start | bytes 1179656 | tf_op jit(solution)/shard_map/ppermute | solution.py:20
  5.5 54.1 %collective-permute-start.1 = (bf16[3,128,512]{2,1,0:T(8,128)(2,1)}, bf16[3,128,512]{2,1,0:T(8,128)(2,1)}, u32[]{:S(2)}, u32[]{:S(2)}) collective-permute-start(bf16[3,128,512]{2,1,0:T(8,128)(2,1)} %get-tuple-element.39), channel_id=1, source_target_pairs={{0,2},{1,3},{2,0},{3,1},{4,6},{5,7},{6,4},{7,5},{8,10},{9,11},{10,... | collective-permute-start | bytes 1179656 | tf_op jit(solution)/shard_map/ppermute | solution.py:20
  8.0 1.4 copy-start.4
  8.0 1.4 copy-start.5
  8.0 1.4 copy-start.8
  8.1 3.8 %copy-start.7 = (bf16[1,128,512]{2,1,0:T(8,128)(2,1)S(1)}, bf16[1,128,512]{2,1,0:T(8,128)(2,1)}, u32[]{:S(2)}) copy-start(bf16[1,128,512]{2,1,0:T(8,128)(2,1)} %get-tuple-element.30) | copy-start | bytes 393220
  8.1 7.2 %copy-start.12 = (s32[128]{0:T(128)S(1)}, s32[128]{0:T(128)}, u32[]{:S(2)}) copy-start(s32[128]{0:T(128)} %param.19) | copy-start | bytes 1540
  9.3 65.9 %collective-permute-start.15 = (bf16[512,1024]{1,0:T(8,128)(2,1)}, bf16[512,1024]{1,0:T(8,128)(2,1)}, u32[]{:S(2)}, u32[]{:S(2)}) collective-permute-start(bf16[512,1024]{1,0:T(8,128)(2,1)} %get-tuple-element.19), channel_id=1, source_target_pairs={{0,1},{1,0},{2,3},{3,2},{4,5},{5,4},{6,7},{7,6},{8,9},{9,8},{10,11... | collective-permute-start | bytes 3145736 | tf_op jit(solution)/shard_map/ppermute | solution.py:20
  10.3 50.5 %collective-permute-start.3 = (bf16[3,128,512]{2,1,0:T(8,128)(2,1)}, bf16[3,128,512]{2,1,0:T(8,128)(2,1)}, u32[]{:S(2)}, u32[]{:S(2)}) collective-permute-start(bf16[3,128,512]{2,1,0:T(8,128)(2,1)} %pad_maximum_fusion.3), channel_id=1, source_target_pairs={{0,4},{1,5},{2,6},{3,7},{4,0},{5,1},{6,2},{7,3},{8,12},{9,13},{10,... | collective-permute-start | bytes 1179656 | tf_op jit(solution)/shard_map/ppermute | solution.py:20
  12.7 54.8 %collective-permute-start.7 = (bf16[3,128,512]{2,1,0:T(8,128)(2,1)}, bf16[3,128,512]{2,1,0:T(8,128)(2,1)}, u32[]{:S(2)}, u32[]{:S(2)}) collective-permute-start(bf16[3,128,512]{2,1,0:T(8,128)(2,1)} %pad_maximum_fusion.4), channel_id=1, source_target_pairs={{0,8},{1,9},{2,10},{3,11},{4,12},{5,13},{6,14},{7,15},{8,0},{9,1},... | collective-permute-start | bytes 1179656 | tf_op jit(solution)/shard_map/ppermute | solution.py:20
  51.3 1.9 copy-start.9
  51.3 1.9 copy-start.11
  51.3 3.7 %copy-start.10 = (pred[2048]{0:T(1024)(128)(4,1)S(1)}, pred[2048]{0:T(1024)(128)(4,1)}, u32[]{:S(2)}) copy-start(pred[2048]{0:T(1024)(128)(4,1)} %fusion.77) | copy-start | bytes 6148
  55.1 4.9 %copy-start.3 = (bf16[1,128,512]{2,1,0:T(8,128)(2,1)S(1)}, bf16[1,128,512]{2,1,0:T(8,128)(2,1)}, u32[]{:S(2)}) copy-start(bf16[1,128,512]{2,1,0:T(8,128)(2,1)} %get-tuple-element.48) | copy-start | bytes 393220
  55.1 4.9 %copy-start.6 = (bf16[1,128,512]{2,1,0:T(8,128)(2,1)S(1)}, bf16[1,128,512]{2,1,0:T(8,128)(2,1)}, u32[]{:S(2)}) copy-start(bf16[1,128,512]{2,1,0:T(8,128)(2,1)} %get-tuple-element.27) | copy-start | bytes 393220
  55.1 5.0 %copy-start.13 = (f32[4]{0:T(128)S(1)}, f32[4]{0:T(128)}, u32[]{:S(2)}) copy-start(f32[4]{0:T(128)} %param.15) | copy-start | bytes 52
  59.6 7.9 %copy-start.2 = (bf16[512,1024]{1,0:T(8,128)(2,1)S(1)}, bf16[512,1024]{1,0:T(8,128)(2,1)}, u32[]{:S(2)}) copy-start(bf16[512,1024]{1,0:T(8,128)(2,1)} %get-tuple-element.17) | copy-start | bytes 3145732
  59.6 3.3 %collective-permute-start.2 = (bf16[3,128,512]{2,1,0:T(8,128)(2,1)}, bf16[3,128,512]{2,1,0:T(8,128)(2,1)S(1)}, u32[]{:S(2)}, u32[]{:S(2)}) collective-permute-start(bf16[3,128,512]{2,1,0:T(8,128)(2,1)} %collective-permute-done.1), channel_id=1, source_target_pairs={{0,1},{1,0},{2,3},{3,2},{4,5},{5,4},{6,7},{7,6},{8,9},{9,8},{10,11... | collective-permute-start | bytes 1179656 | tf_op jit(solution)/shard_map/ppermute | solution.py:20
  60.7 13.2 %collective-permute-start.11 = (bf16[3,128,512]{2,1,0:T(8,128)(2,1)S(1)}, bf16[3,128,512]{2,1,0:T(8,128)(2,1)S(1)}, u32[]{:S(2)}, u32[]{:S(2)}) collective-permute-start(bf16[3,128,512]{2,1,0:T(8,128)(2,1)S(1)} %pad_maximum_fusion.5), channel_id=1, source_target_pairs={{0,12},{1,13},{2,14},{3,15},{4,8},{5,9},{6,10},{7,11},{8,4},{9,5},... | collective-permute-start | bytes 1179656 | tf_op jit(solution)/shard_map/ppermute | solution.py:20
  60.8 6.9 %collective-permute-start.4 = (bf16[3,128,512]{2,1,0:T(8,128)(2,1)}, bf16[3,128,512]{2,1,0:T(8,128)(2,1)S(1)}, u32[]{:S(2)}, u32[]{:S(2)}) collective-permute-start(bf16[3,128,512]{2,1,0:T(8,128)(2,1)} %collective-permute-done.3), channel_id=1, source_target_pairs={{0,1},{1,0},{2,3},{3,2},{4,5},{5,4},{6,7},{7,6},{8,9},{9,8},{10,11... | collective-permute-start | bytes 1179656 | tf_op jit(solution)/shard_map/ppermute | solution.py:20
  62.9 11.5 %collective-permute-start.5 = (bf16[3,128,512]{2,1,0:T(8,128)(2,1)}, bf16[3,128,512]{2,1,0:T(8,128)(2,1)S(1)}, u32[]{:S(2)}, u32[]{:S(2)}) collective-permute-start(bf16[3,128,512]{2,1,0:T(8,128)(2,1)} %collective-permute-done.3), channel_id=1, source_target_pairs={{0,2},{1,3},{2,0},{3,1},{4,6},{5,7},{6,4},{7,5},{8,10},{9,11},{10,... | collective-permute-start | bytes 1179656 | tf_op jit(solution)/shard_map/ppermute | solution.py:20
  65.6 14.4 %slice-start = ((s8[6291456]{0:T(1024)(128)(4,1)}), s8[4194304]{0:T(1024)(128)(4,1)S(1)}, s32[]{:S(2)}) async-start(s8[6291456]{0:T(1024)(128)(4,1)} %bitcast.151), calls=%async_computation | async-start | bytes 8388608
  67.5 25.4 %collective-permute-start.16 = (bf16[512,1024]{1,0:T(8,128)(2,1)S(1)}, bf16[512,1024]{1,0:T(8,128)(2,1)S(1)}, u32[]{:S(2)}, u32[]{:S(2)}) collective-permute-start(bf16[512,1024]{1,0:T(8,128)(2,1)S(1)} %copy-done.2), channel_id=1, source_target_pairs={{0,1},{1,0},{2,3},{3,2},{4,5},{5,4},{6,7},{7,6},{8,9},{9,8},{10,11... | collective-permute-start | bytes 3145736 | tf_op jit(solution)/shard_map/ppermute | solution.py:20
  67.7 35.3 %collective-permute-start.8 = (bf16[3,128,512]{2,1,0:T(8,128)(2,1)}, bf16[3,128,512]{2,1,0:T(8,128)(2,1)S(1)}, u32[]{:S(2)}, u32[]{:S(2)}) collective-permute-start(bf16[3,128,512]{2,1,0:T(8,128)(2,1)} %collective-permute-done.7), channel_id=1, source_target_pairs={{0,1},{1,0},{2,3},{3,2},{4,5},{5,4},{6,7},{7,6},{8,9},{9,8},{10,11... | collective-permute-start | bytes 1179656 | tf_op jit(solution)/shard_map/ppermute | solution.py:20
  73.9 12.3 %collective-permute-start.9 = (bf16[3,128,512]{2,1,0:T(8,128)(2,1)}, bf16[3,128,512]{2,1,0:T(8,128)(2,1)S(1)}, u32[]{:S(2)}, u32[]{:S(2)}) collective-permute-start(bf16[3,128,512]{2,1,0:T(8,128)(2,1)} %collective-permute-done.7), channel_id=1, source_target_pairs={{0,2},{1,3},{2,0},{3,1},{4,6},{5,7},{6,4},{7,5},{8,10},{9,11},{10,... | collective-permute-start | bytes 1179656 | tf_op jit(solution)/shard_map/ppermute | solution.py:20
  74.4 30.9 %collective-permute-start.12 = (bf16[3,128,512]{2,1,0:T(8,128)(2,1)S(1)}, bf16[3,128,512]{2,1,0:T(8,128)(2,1)S(1)}, u32[]{:S(2)}, u32[]{:S(2)}) collective-permute-start(bf16[3,128,512]{2,1,0:T(8,128)(2,1)S(1)} %collective-permute-done.11), channel_id=1, source_target_pairs={{0,1},{1,0},{2,3},{3,2},{4,5},{5,4},{6,7},{7,6},{8,9},{9,8},{10,11... | collective-permute-start | bytes 1179656 | tf_op jit(solution)/shard_map/ppermute | solution.py:20
  75.2 17.7 %collective-permute-start.13 = (bf16[3,128,512]{2,1,0:T(8,128)(2,1)S(1)}, bf16[3,128,512]{2,1,0:T(8,128)(2,1)S(1)}, u32[]{:S(2)}, u32[]{:S(2)}) collective-permute-start(bf16[3,128,512]{2,1,0:T(8,128)(2,1)S(1)} %collective-permute-done.11), channel_id=1, source_target_pairs={{0,2},{1,3},{2,0},{3,1},{4,6},{5,7},{6,4},{7,5},{8,10},{9,11},{10,... | collective-permute-start | bytes 1179656 | tf_op jit(solution)/shard_map/ppermute | solution.py:20
  76.8 3.3 %slice-start.1 = ((s8[6291456]{0:T(1024)(128)(4,1)}), s8[2097152]{0:T(1024)(128)(4,1)S(1)}, s32[]{:S(2)}) async-start(s8[6291456]{0:T(1024)(128)(4,1)} %bitcast.151), calls=%async_computation.1 | async-start | bytes 4194304
  81.5 12.0 %copy-start = (bf16[512,1024]{1,0:T(8,128)(2,1)S(1)}, bf16[512,1024]{1,0:T(8,128)(2,1)}, u32[]{:S(2)}) copy-start(bf16[512,1024]{1,0:T(8,128)(2,1)} %get-tuple-element.16) | copy-start | bytes 3145732
  86.2 14.5 %collective-permute-start.6 = (bf16[3,128,512]{2,1,0:T(8,128)(2,1)S(1)}, bf16[3,128,512]{2,1,0:T(8,128)(2,1)S(1)}, u32[]{:S(2)}, u32[]{:S(2)}) collective-permute-start(bf16[3,128,512]{2,1,0:T(8,128)(2,1)S(1)} %collective-permute-done.5), channel_id=1, source_target_pairs={{0,1},{1,0},{2,3},{3,2},{4,5},{5,4},{6,7},{7,6},{8,9},{9,8},{10,11... | collective-permute-start | bytes 1179656 | tf_op jit(solution)/shard_map/ppermute | solution.py:20
  92.9 11.1 %collective-permute-start.10 = (bf16[3,128,512]{2,1,0:T(8,128)(2,1)S(1)}, bf16[3,128,512]{2,1,0:T(8,128)(2,1)S(1)}, u32[]{:S(2)}, u32[]{:S(2)}) collective-permute-start(bf16[3,128,512]{2,1,0:T(8,128)(2,1)S(1)} %collective-permute-done.9), channel_id=1, source_target_pairs={{0,1},{1,0},{2,3},{3,2},{4,5},{5,4},{6,7},{7,6},{8,9},{9,8},{10,11... | collective-permute-start | bytes 1179656 | tf_op jit(solution)/shard_map/ppermute | solution.py:20
  92.9 13.4 %collective-permute-start.14 = (bf16[3,128,512]{2,1,0:T(8,128)(2,1)S(1)}, bf16[3,128,512]{2,1,0:T(8,128)(2,1)S(1)}, u32[]{:S(2)}, u32[]{:S(2)}) collective-permute-start(bf16[3,128,512]{2,1,0:T(8,128)(2,1)S(1)} %collective-permute-done.13), channel_id=1, source_target_pairs={{0,1},{1,0},{2,3},{3,2},{4,5},{5,4},{6,7},{7,6},{8,9},{9,8},{10,11... | collective-permute-start | bytes 1179656 | tf_op jit(solution)/shard_map/ppermute | solution.py:20
  98.9 2.2 %slice-start.2 = ((s8[6291456]{0:T(1024)(128)(4,1)}), s8[4194304]{0:T(1024)(128)(4,1)S(1)}, s32[]{:S(2)}) async-start(s8[6291456]{0:T(1024)(128)(4,1)} %bitcast.162), calls=%async_computation.2 | async-start | bytes 8388608
  99.7 2.2 %slice-start.3 = ((s8[6291456]{0:T(1024)(128)(4,1)}), s8[2097152]{0:T(1024)(128)(4,1)S(1)}, s32[]{:S(2)}) async-start(s8[6291456]{0:T(1024)(128)(4,1)} %bitcast.162), calls=%async_computation.3 | async-start | bytes 4194304
  100.7 9.6 %collective-permute-start.33 = (bf16[256,512]{1,0:T(8,128)(2,1)S(1)}, bf16[256,512]{1,0:T(8,128)(2,1)S(1)}, u32[]{:S(2)}, u32[]{:S(2)}) collective-permute-start(bf16[256,512]{1,0:T(8,128)(2,1)S(1)} %constant_dynamic-slice_fusion.1), channel_id=1, source_target_pairs={{0,2},{1,3},{2,0},{3,1},{4,6},{5,7},{6,4},{7,5},{8,10},{9,11},{10,... | collective-permute-start | bytes 786440 | tf_op jit(solution)/shard_map/ppermute | solution.py:20
  103.0 12.6 %collective-permute-start.36 = (bf16[256,512]{1,0:T(8,128)(2,1)S(1)}, bf16[256,512]{1,0:T(8,128)(2,1)S(1)}, u32[]{:S(2)}, u32[]{:S(2)}) collective-permute-start(bf16[256,512]{1,0:T(8,128)(2,1)S(1)} %constant_dynamic-slice_fusion), channel_id=1, source_target_pairs={{0,2},{1,3},{2,0},{3,1},{4,6},{5,7},{6,4},{7,5},{8,10},{9,11},{10,... | collective-permute-start | bytes 786440 | tf_op jit(solution)/shard_map/ppermute | solution.py:20
  104.0 17.2 %collective-permute-start.17 = (bf16[256,512]{1,0:T(8,128)(2,1)S(1)}, bf16[256,512]{1,0:T(8,128)(2,1)S(1)}, u32[]{:S(2)}, u32[]{:S(2)}) collective-permute-start(bf16[256,512]{1,0:T(8,128)(2,1)S(1)} %constant_dynamic-slice_fusion.5), channel_id=1, source_target_pairs={{0,2},{1,3},{2,0},{3,1},{4,6},{5,7},{6,4},{7,5},{8,10},{9,11},{10,... | collective-permute-start | bytes 786440 | tf_op jit(solution)/shard_map/ppermute | solution.py:20
  105.3 21.5 %collective-permute-start.20 = (bf16[256,512]{1,0:T(8,128)(2,1)S(1)}, bf16[256,512]{1,0:T(8,128)(2,1)S(1)}, u32[]{:S(2)}, u32[]{:S(2)}) collective-permute-start(bf16[256,512]{1,0:T(8,128)(2,1)S(1)} %constant_dynamic-slice_fusion.4), channel_id=1, source_target_pairs={{0,2},{1,3},{2,0},{3,1},{4,6},{5,7},{6,4},{7,5},{8,10},{9,11},{10,... | collective-permute-start | bytes 786440 | tf_op jit(solution)/shard_map/ppermute | solution.py:20
  106.3 26.1 %collective-permute-start.25 = (bf16[256,512]{1,0:T(8,128)(2,1)S(1)}, bf16[256,512]{1,0:T(8,128)(2,1)S(1)}, u32[]{:S(2)}, u32[]{:S(2)}) collective-permute-start(bf16[256,512]{1,0:T(8,128)(2,1)S(1)} %constant_dynamic-slice_fusion.3), channel_id=1, source_target_pairs={{0,2},{1,3},{2,0},{3,1},{4,6},{5,7},{6,4},{7,5},{8,10},{9,11},{10,... | collective-permute-start | bytes 786440 | tf_op jit(solution)/shard_map/ppermute | solution.py:20
  110.4 26.7 %collective-permute-start.28 = (bf16[256,512]{1,0:T(8,128)(2,1)S(1)}, bf16[256,512]{1,0:T(8,128)(2,1)S(1)}, u32[]{:S(2)}, u32[]{:S(2)}) collective-permute-start(bf16[256,512]{1,0:T(8,128)(2,1)S(1)} %constant_dynamic-slice_fusion.2), channel_id=1, source_target_pairs={{0,2},{1,3},{2,0},{3,1},{4,6},{5,7},{6,4},{7,5},{8,10},{9,11},{10,... | collective-permute-start | bytes 786440 | tf_op jit(solution)/shard_map/ppermute | solution.py:20
  115.6 22.9 %collective-permute-start.34 = (bf16[256,512]{1,0:T(8,128)(2,1)S(1)}, bf16[256,512]{1,0:T(8,128)(2,1)S(1)}, u32[]{:S(2)}, u32[]{:S(2)}) collective-permute-start(bf16[256,512]{1,0:T(8,128)(2,1)S(1)} %fusion.44), channel_id=1, source_target_pairs={{1,5},{3,7},{4,0},{6,2},{9,13},{11,15},{12,8},{14,10},{17,21},{19,... | collective-permute-start | bytes 786440 | tf_op jit(solution)/shard_map/ppermute | solution.py:20
  121.2 18.7 %collective-permute-start.37 = (bf16[256,512]{1,0:T(8,128)(2,1)S(1)}, bf16[256,512]{1,0:T(8,128)(2,1)S(1)}, u32[]{:S(2)}, u32[]{:S(2)}) collective-permute-start(bf16[256,512]{1,0:T(8,128)(2,1)S(1)} %fusion.45), channel_id=1, source_target_pairs={{1,5},{3,7},{4,0},{6,2},{9,13},{11,15},{12,8},{14,10},{17,21},{19,... | collective-permute-start | bytes 786440 | tf_op jit(solution)/shard_map/ppermute | solution.py:20
  126.8 21.5 %collective-permute-start.18 = (bf16[256,512]{1,0:T(8,128)(2,1)S(1)}, bf16[256,512]{1,0:T(8,128)(2,1)S(1)}, u32[]{:S(2)}, u32[]{:S(2)}) collective-permute-start(bf16[256,512]{1,0:T(8,128)(2,1)S(1)} %fusion.40), channel_id=1, source_target_pairs={{1,5},{3,7},{4,0},{6,2},{9,13},{11,15},{12,8},{14,10},{17,21},{19,... | collective-permute-start | bytes 786440 | tf_op jit(solution)/shard_map/ppermute | solution.py:20
  132.4 17.3 %collective-permute-start.21 = (bf16[256,512]{1,0:T(8,128)(2,1)S(1)}, bf16[256,512]{1,0:T(8,128)(2,1)S(1)}, u32[]{:S(2)}, u32[]{:S(2)}) collective-permute-start(bf16[256,512]{1,0:T(8,128)(2,1)S(1)} %fusion.41), channel_id=1, source_target_pairs={{1,5},{3,7},{4,0},{6,2},{9,13},{11,15},{12,8},{14,10},{17,21},{19,... | collective-permute-start | bytes 786440 | tf_op jit(solution)/shard_map/ppermute | solution.py:20
  137.1 18.3 %collective-permute-start.26 = (bf16[256,512]{1,0:T(8,128)(2,1)S(1)}, bf16[256,512]{1,0:T(8,128)(2,1)S(1)}, u32[]{:S(2)}, u32[]{:S(2)}) collective-permute-start(bf16[256,512]{1,0:T(8,128)(2,1)S(1)} %fusion.42), channel_id=1, source_target_pairs={{1,5},{3,7},{4,0},{6,2},{9,13},{11,15},{12,8},{14,10},{17,21},{19,... | collective-permute-start | bytes 786440 | tf_op jit(solution)/shard_map/ppermute | solution.py:20
  138.5 18.3 %collective-permute-start.29 = (bf16[256,512]{1,0:T(8,128)(2,1)S(1)}, bf16[256,512]{1,0:T(8,128)(2,1)S(1)}, u32[]{:S(2)}, u32[]{:S(2)}) collective-permute-start(bf16[256,512]{1,0:T(8,128)(2,1)S(1)} %fusion.43), channel_id=1, source_target_pairs={{1,5},{3,7},{4,0},{6,2},{9,13},{11,15},{12,8},{14,10},{17,21},{19,... | collective-permute-start | bytes 786440 | tf_op jit(solution)/shard_map/ppermute | solution.py:20
  139.9 22.5 %collective-permute-start.35 = (bf16[256,512]{1,0:T(8,128)(2,1)S(1)}, bf16[256,512]{1,0:T(8,128)(2,1)S(1)}, u32[]{:S(2)}, u32[]{:S(2)}) collective-permute-start(bf16[256,512]{1,0:T(8,128)(2,1)S(1)} %fusion.54), channel_id=1, source_target_pairs={{0,8},{2,10},{5,13},{7,15},{16,24},{18,26},{21,29},{23,31}} | collective-permute-start | bytes 786440 | tf_op jit(solution)/shard_map/ppermute | solution.py:20
  148.3 15.4 %collective-permute-start.38 = (bf16[256,512]{1,0:T(8,128)(2,1)S(1)}, bf16[256,512]{1,0:T(8,128)(2,1)S(1)}, u32[]{:S(2)}, u32[]{:S(2)}) collective-permute-start(bf16[256,512]{1,0:T(8,128)(2,1)S(1)} %fusion.55), channel_id=1, source_target_pairs={{8,0},{10,2},{13,5},{15,7},{24,16},{26,18},{29,21},{31,23}} | collective-permute-start | bytes 786440 | tf_op jit(solution)/shard_map/ppermute | solution.py:20
  149.8 14.4 %collective-permute-start.19 = (bf16[256,512]{1,0:T(8,128)(2,1)S(1)}, bf16[256,512]{1,0:T(8,128)(2,1)S(1)}, u32[]{:S(2)}, u32[]{:S(2)}) collective-permute-start(bf16[256,512]{1,0:T(8,128)(2,1)S(1)} %fusion.50), channel_id=1, source_target_pairs={{0,8},{2,10},{5,13},{7,15},{16,24},{18,26},{21,29},{23,31}} | collective-permute-start | bytes 786440 | tf_op jit(solution)/shard_map/ppermute | solution.py:20
  155.4 12.0 %collective-permute-start.22 = (bf16[256,512]{1,0:T(8,128)(2,1)S(1)}, bf16[256,512]{1,0:T(8,128)(2,1)S(1)}, u32[]{:S(2)}, u32[]{:S(2)}) collective-permute-start(bf16[256,512]{1,0:T(8,128)(2,1)S(1)} %fusion.51), channel_id=1, source_target_pairs={{8,0},{10,2},{13,5},{15,7},{24,16},{26,18},{29,21},{31,23}} | collective-permute-start | bytes 786440 | tf_op jit(solution)/shard_map/ppermute | solution.py:20
  156.8 10.9 %collective-permute-start.27 = (bf16[256,512]{1,0:T(8,128)(2,1)S(1)}, bf16[256,512]{1,0:T(8,128)(2,1)S(1)}, u32[]{:S(2)}, u32[]{:S(2)}) collective-permute-start(bf16[256,512]{1,0:T(8,128)(2,1)S(1)} %fusion.52), channel_id=1, source_target_pairs={{0,8},{2,10},{5,13},{7,15},{16,24},{18,26},{21,29},{23,31}} | collective-permute-start | bytes 786440 | tf_op jit(solution)/shard_map/ppermute | solution.py:20
  162.4 9.2 %collective-permute-start.30 = (bf16[256,512]{1,0:T(8,128)(2,1)S(1)}, bf16[256,512]{1,0:T(8,128)(2,1)S(1)}, u32[]{:S(2)}, u32[]{:S(2)}) collective-permute-start(bf16[256,512]{1,0:T(8,128)(2,1)S(1)} %fusion.53), channel_id=1, source_target_pairs={{8,0},{10,2},{13,5},{15,7},{24,16},{26,18},{29,21},{31,23}} | collective-permute-start | bytes 786440 | tf_op jit(solution)/shard_map/ppermute | solution.py:20
  172.9 10.0 %collective-permute-start.23 = (bf16[256,512]{1,0:T(8,128)(2,1)S(1)}, bf16[256,512]{1,0:T(8,128)(2,1)S(1)}, u32[]{:S(2)}, u32[]{:S(2)}) collective-permute-start(bf16[256,512]{1,0:T(8,128)(2,1)S(1)} %get-tuple-element.12), channel_id=1, source_target_pairs={{0,2},{2,0},{5,7},{7,5},{8,10},{10,8},{13,15},{15,13},{16,18},{18,... | collective-permute-start | bytes 786440 | tf_op jit(solution)/shard_map/ppermute | solution.py:20
  176.7 8.6 %collective-permute-start.31 = (bf16[256,512]{1,0:T(8,128)(2,1)S(1)}, bf16[256,512]{1,0:T(8,128)(2,1)S(1)}, u32[]{:S(2)}, u32[]{:S(2)}) collective-permute-start(bf16[256,512]{1,0:T(8,128)(2,1)S(1)} %get-tuple-element.11), channel_id=1, source_target_pairs={{0,2},{2,0},{5,7},{7,5},{8,10},{10,8},{13,15},{15,13},{16,18},{18,... | collective-permute-start | bytes 786440 | tf_op jit(solution)/shard_map/ppermute | solution.py:20
  180.3 8.3 %collective-permute-start.39 = (bf16[256,512]{1,0:T(8,128)(2,1)S(1)}, bf16[256,512]{1,0:T(8,128)(2,1)S(1)}, u32[]{:S(2)}, u32[]{:S(2)}) collective-permute-start(bf16[256,512]{1,0:T(8,128)(2,1)S(1)} %get-tuple-element.13), channel_id=1, source_target_pairs={{0,2},{2,0},{5,7},{7,5},{8,10},{10,8},{13,15},{15,13},{16,18},{18,... | collective-permute-start | bytes 786440 | tf_op jit(solution)/shard_map/ppermute | solution.py:20
  183.1 9.0 %collective-permute-start.24 = (bf16[512,512]{1,0:T(8,128)(2,1)S(1)}, bf16[512,512]{1,0:T(8,128)(2,1)}, u32[]{:S(2)}, u32[]{:S(2)}) collective-permute-start(bf16[512,512]{1,0:T(8,128)(2,1)S(1)} %maximum_select_fusion), channel_id=1, source_target_pairs={{0,1},{2,3},{5,4},{7,6},{8,9},{10,11},{13,12},{15,14},{16,17},{18,... | collective-permute-start | bytes 1572872 | tf_op jit(solution)/shard_map/ppermute | solution.py:20
  186.3 6.2 %collective-permute-start.32 = (bf16[512,512]{1,0:T(8,128)(2,1)}, bf16[512,512]{1,0:T(8,128)(2,1)}, u32[]{:S(2)}, u32[]{:S(2)}) collective-permute-start(bf16[512,512]{1,0:T(8,128)(2,1)} %maximum_select_fusion.1), channel_id=1, source_target_pairs={{0,1},{2,3},{5,4},{7,6},{8,9},{10,11},{13,12},{15,14},{16,17},{18,... | collective-permute-start | bytes 1572872 | tf_op jit(solution)/shard_map/ppermute | solution.py:20
  189.6 3.1 %collective-permute-start.40 = (bf16[512,512]{1,0:T(8,128)(2,1)}, bf16[512,512]{1,0:T(8,128)(2,1)}, u32[]{:S(2)}, u32[]{:S(2)}) collective-permute-start(bf16[512,512]{1,0:T(8,128)(2,1)} %maximum_select_fusion.2), channel_id=1, source_target_pairs={{0,1},{2,3},{5,4},{7,6},{8,9},{10,11},{13,12},{15,14},{16,17},{18,... | collective-permute-start | bytes 1572872 | tf_op jit(solution)/shard_map/ppermute | solution.py:20
  197.3 8.3 %collective-permute-start.41 = (bf16[128,512]{1,0:T(8,128)(2,1)S(1)}, bf16[128,512]{1,0:T(8,128)(2,1)S(1)}, u32[]{:S(2)}, u32[]{:S(2)}) collective-permute-start(bf16[128,512]{1,0:T(8,128)(2,1)S(1)} %get-tuple-element.26), channel_id=1, source_target_pairs={{0,12},{1,13},{2,14},{3,15},{4,8},{5,9},{6,10},{7,11},{8,4},{9,5},... | collective-permute-start | bytes 393224 | tf_op jit(solution)/shard_map/ppermute | solution.py:20
  197.4 12.4 %collective-permute-start.42 = (bf16[128,512]{1,0:T(8,128)(2,1)S(1)}, bf16[128,512]{1,0:T(8,128)(2,1)S(1)}, u32[]{:S(2)}, u32[]{:S(2)}) collective-permute-start(bf16[128,512]{1,0:T(8,128)(2,1)S(1)} %get-tuple-element.25), channel_id=1, source_target_pairs={{0,8},{1,9},{2,10},{3,11},{4,12},{5,13},{6,14},{7,15},{8,0},{9,1},... | collective-permute-start | bytes 393224 | tf_op jit(solution)/shard_map/ppermute | solution.py:20
  197.5 12.3 %collective-permute-start.43 = (bf16[128,512]{1,0:T(8,128)(2,1)S(1)}, bf16[128,512]{1,0:T(8,128)(2,1)S(1)}, u32[]{:S(2)}, u32[]{:S(2)}) collective-permute-start(bf16[128,512]{1,0:T(8,128)(2,1)S(1)} %get-tuple-element.24), channel_id=1, source_target_pairs={{0,4},{1,5},{2,6},{3,7},{4,0},{5,1},{6,2},{7,3},{8,12},{9,13},{10,... | collective-permute-start | bytes 393224 | tf_op jit(solution)/shard_map/ppermute | solution.py:20

commit v2 on v1

v2 whole, which is shorter than its diff:
```python
import functools

import jax
import jax.numpy as jnp
from jax import lax
from jax.experimental import pallas as pl
from jax.experimental.pallas import tpu as pltpu
from jax.sharding import PartitionSpec as P

VIEW_ROWS = 128
AXIS = "tokens"
epsilon = 1e-05
f32 = jnp.float32
bf16 = jnp.bfloat16
i32 = jnp.int32
TAG_ROWS = 16
VMEM_LIMIT = 48 * 1024 * 1024


def swap(value, mask, senders=None):
    count = lax.axis_size(AXIS)
    pairs = [(t, t ^ mask) for t in range(count) if senders is None or senders(t)]
    return lax.ppermute(value, AXIS, pairs)


def head_of(plane, head_count):
    half = head_count // 2
    return (plane % 2) * half + plane // 2


def whole(shape):
    return pl.BlockSpec(shape, lambda *_: (0,) * len(shape))


def call(body, name, scalars, inputs, specs, outs, grid=(1,), out_specs=None, scratch=(), flops=0):
    moved = sum(x.size * x.dtype.itemsize for x in inputs) + sum(
        x.size * x.dtype.itemsize for x in outs
    )
    return pl.pallas_call(
        body,
        name=name,
        grid_spec=pltpu.PrefetchScalarGridSpec(
            num_scalar_prefetch=1,
            grid=grid,
            in_specs=specs,
            out_specs=out_specs or [whole(o.shape) for o in outs],
            scratch_shapes=list(scratch),
        ),
        out_shape=list(outs),
        cost_estimate=pl.CostEstimate(flops=flops, bytes_accessed=moved, transcendentals=0),
        compiler_params=pltpu.CompilerParams(vmem_limit_bytes=VMEM_LIMIT),
    )(scalars, *inputs)


def lane_pick(table, lane):
    at = lax.broadcasted_iota(i32, table.shape, 1) == lane
    return jnp.sum(jnp.where(at, table, 0.0), axis=1, keepdims=True)


def pack_update_body(half, width, where, keys, values, rates, out):
    other = 1 - where[1]
    out[0] = keys[...]
    for j in range(half):
        cols = pl.ds(j * width, width)
        rate = lane_pick(rates[...], other * half + j)
        out[1, :, cols] = (rate * values[:, cols].astype(f32)).astype(bf16)


def pack_update(where, keys, values, rates, half, width):
    rows, cols = keys.shape[0], half * width
    block = min(128, rows)
    spec = pl.BlockSpec((block, cols), lambda i, w: (i, 1 - w[1]))
    return call(
        functools.partial(pack_update_body, half, width),
        "pack_update",
        where,
        (keys, values, rates),
        [spec, spec, pl.BlockSpec((block, rates.shape[1]), lambda i, w: (i, 0))],
        [jax.ShapeDtypeStruct((2, rows, cols), bf16)],
        grid=(rows // block,),
        out_specs=[pl.BlockSpec((2, block, cols), lambda i, w: (0, i, 0))],
    )[0]


def pack_target_body(heads, width, where, queries, keys, values, tags, *outs):
    rows = queries.shape[0]
    for step in range(heads):
        head = head_of(where[0] ^ step, heads)
        cols = pl.ds(pl.multiple_of(head * width, width), width)
        for i, source in enumerate((queries, keys, values)):
            outs[step][pl.ds(i * rows, rows), :] = source[:, cols]
        outs[step][pl.ds(3 * rows, TAG_ROWS), :] = jnp.zeros((TAG_ROWS, width), bf16)
        outs[step][pl.ds(3 * rows, TAG_ROWS), pl.ds(0, rows)] = tags[...]


def pack_target(where, queries, keys, values, tags, heads, width):
    rows = queries.shape[0]
    out = jax.ShapeDtypeStruct((3 * rows + TAG_ROWS, width), bf16)
    inputs = (queries, keys, values, tags)
    return call(
        functools.partial(pack_target_body, heads, width),
        "pack_target",
        where,
        inputs,
        [whole(x.shape) for x in inputs],
        [out] * heads,
    )


def head_grad_body(lane, half, where, keys, values, rates, other, weights, *refs):
    sends, keeps = refs[:2], refs[2:4]
    hidden_s, gate_s, up_s, grads_s, full = refs[4:]
    rows, width = keys.shape
    head = where[1] * half + lane
    chunk = 256
    for at in range(0, 2 * rows, chunk):
        span = pl.ds(at, chunk)
        if at < rows:
            k = keys[span, :]
            rate = lane_pick(rates[span, :], head)
            tg = (rate * values[span, :].astype(f32)).astype(bf16)
        else:
            k = other[0, pl.ds(at - rows, chunk), :]
            tg = other[1, pl.ds(at - rows, chunk), :]
        grads_s[span, :] = tg
        pre_gate = jnp.dot(k, weights[0, 0], preferred_element_type=f32)
        pre_up = jnp.dot(k, weights[0, 1], preferred_element_type=f32)
        back = lax.dot_general(
            tg, weights[0, 2], (((1,), (1,)), ((), ())), preferred_element_type=f32
        )
        sigma = jax.nn.sigmoid(pre_gate)
        activated = pre_gate * sigma
        hidden_s[span, :] = (activated * pre_up).astype(bf16)
        gate_s[span, :] = (back * pre_up * (sigma * (1.0 + pre_gate * (1.0 - sigma)))).astype(bf16)
        up_s[span, :] = (back * activated).astype(bf16)
    outer = (((0,), (0,)), ((), ()))
    upper = pl.ds(0, rows)
    lower = pl.ds(rows, rows)
    for i, right in enumerate((gate_s, up_s)):
        full[i] = lax.dot_general(
            keys[...], right[upper, :], outer, preferred_element_type=f32
        ) + lax.dot_general(other[0], right[lower, :], outer, preferred_element_type=f32)
    full[2] = lax.dot_general(hidden_s[...], grads_s[...], outer, preferred_element_type=f32)
    quarter = width // 4
    bit = where[2]
    for g in range(2):
        for i in range(3):
            kept = pl.ds(pl.multiple_of(bit * 2 * quarter + g * quarter, quarter), quarter)
            sent = pl.ds(pl.multiple_of((1 - bit) * 2 * quarter + g * quarter, quarter), quarter)
            keeps[g][i] = full[i, kept, :]
            sends[g][i] = full[i, sent, :].astype(bf16)


def head_grad(where, keys, values, rates, other, weights, lane, half, width):
    rows = keys.shape[0]
    own = pl.BlockSpec((rows, width), lambda i, w: (0, w[1] * half + lane))
    shape = (3, width // 4, width)
    both = pltpu.VMEM((2 * rows, width), bf16)
    outs = call(
        functools.partial(head_grad_body, lane, half),
        "head_grad_%d" % lane,
        where,
        (keys, values, rates, other, weights),
        [
            own,
            own,
            whole(rates.shape),
            pl.BlockSpec((2, rows, width), lambda i, w: (0, 0, lane)),
            pl.BlockSpec((1, 3, width, width), lambda i, w: (w[1] * half + lane, 0, 0, 0)),
        ],
        [jax.ShapeDtypeStruct(shape, bf16)] * 2 + [jax.ShapeDtypeStruct(shape, f32)] * 2,
        scratch=[both] * 4 + [pltpu.VMEM((3, width, width), f32)],
        flops=24 * rows * width * width,
    )
    return outs[:2], outs[2:]


def arrange_body(count, span, where, *refs):
    pieces, outs = refs[:-2], refs[-2:]
    me = where[3]
    inner = where[4]
    rows = (pieces[0].shape[0] - TAG_ROWS) // 3
    heads = count // span
    core = inner % 2
    tags = [p[pl.ds(3 * rows, TAG_ROWS), pl.ds(0, rows)].astype(f32) for p in pieces]
    ids = jnp.concatenate(
        [t[0:1, :] * 256.0 + t[1:2, :] for t in tags]
        + [t[2:3, :] * 256.0 + t[3:4, :] for t in tags],
        axis=0,
    ).astype(i32)
    own = len(pieces)

    def source_of(shape, axis):
        index = lax.broadcasted_iota(i32, shape, axis)
        diff = jnp.where(index < own, 2 * index, 2 * (index - own) + 1)
        return me ^ diff

    earlier = (source_of((count, count), 1) < source_of((count, count), 0)).astype(f32)
    before = (
        lax.broadcasted_iota(i32, (rows, rows), 0) < lax.broadcasted_iota(i32, (rows, rows), 1)
    ).astype(f32)
    for which, out in enumerate(outs):
        target = inner - core + (core if which == 0 else 1 - core)
        place = jnp.full((count, rows), -1.0, f32)
        for j in range(heads):
            hit = (ids == j * span + target).astype(f32)
            rank = jnp.dot(hit, before, preferred_element_type=f32) + jnp.sum(
                jnp.dot(earlier, hit, preferred_element_type=f32), axis=1, keepdims=True
            )
            place = jnp.where(hit > 0.0, rank + float(j * VIEW_ROWS), place)
        place = place.astype(i32)
        group = 4
        totals = [None] * 3
        for first in range(0, own, group):
            row_at = lax.broadcasted_iota(i32, (heads * VIEW_ROWS, rows), 0)
            pick = jnp.concatenate(
                [
                    (row_at == place[n : n + 1, :]).astype(f32).astype(bf16)
                    for n in range(first, first + group)
                ],
                axis=1,
            )
            for i in range(3):
                source = jnp.concatenate(
                    [pieces[n][pl.ds(i * rows, rows), :] for n in range(first, first + group)],
                    axis=0,
                )
                part = jnp.dot(pick, source, preferred_element_type=f32)
                totals[i] = part if totals[i] is None else totals[i] + part
        for i in range(3):
            out[i] = totals[i].astype(bf16)


def arrange(where, pieces, count, span, heads, width):
    shape = jax.ShapeDtypeStruct((3, heads * VIEW_ROWS, width), bf16)
    return call(
        functools.partial(arrange_body, count, span),
        "arrange",
        where,
        tuple(pieces),
        [whole(x.shape) for x in pieces],
        [shape] * 2,
        flops=12 * VIEW_ROWS * heads * width * VIEW_ROWS * len(pieces),
    )


def attend_body(where, own, other, queries, attended):
    width = queries.shape[1]
    q = own[0] + other[0]
    queries[...] = q
    for v in range(q.shape[0] // VIEW_ROWS):
        at = pl.ds(v * VIEW_ROWS, VIEW_ROWS)
        k = own[1, at, :] + other[1, at, :]
        scores = lax.dot_general(
            own[0, at, :] + other[0, at, :],
            k,
            (((1,), (1,)), ((), ())),
            preferred_element_type=f32,
        ) * width ** (-0.5)
        top = jnp.max(scores, axis=1, keepdims=True)
        raised = jnp.exp(scores - top)
        probs = (raised / jnp.sum(raised, axis=1, keepdims=True)).astype(bf16)
        attended[at, :] = jnp.dot(
            probs, own[2, at, :] + other[2, at, :], preferred_element_type=f32
        )


def attend(where, own, other):
    _, rows, width = own.shape
    return call(
        attend_body,
        "attend",
        where,
        (own, other),
        [whole(own.shape)] * 2,
        [jax.ShapeDtypeStruct((rows, width), bf16), jax.ShapeDtypeStruct((rows, width), f32)],
        flops=4 * rows * VIEW_ROWS * width,
    )


def renew_body(where, keep, got, old, steps, fresh):
    total = keep[...] + got[...].astype(f32)
    scale = lax.rsqrt(jnp.mean(total * total, axis=-1, keepdims=True) + epsilon)
    step = steps[where[5]]
    fresh[...] = (old[0].astype(f32) - step * (total * scale)).astype(bf16)


def renew(where, keep, got, weights, steps, group, groups):
    parts, rows, width = keep.shape
    return call(
        renew_body,
        "renew",
        where,
        (keep, got, weights, steps),
        [
            whole(keep.shape),
            whole(got.shape),
            pl.BlockSpec(
                (1, parts, rows, width), lambda i, w: (w[5], 0, w[6 + group], 0)
            ),
            pl.BlockSpec(memory_space=pltpu.SMEM),
        ],
        [jax.ShapeDtypeStruct(keep.shape, bf16)],
    )[0]


def finish_body(where, queries, attended, *refs):
    weights = refs[:8]
    outs, full = refs[8:-1], refs[-1]
    bit, is_owner = where[2], where[8]
    quarter = weights[0].shape[1]

    def place(blocks):
        for side in range(2):
            half = bit if side == 0 else 1 - bit
            for g in range(2):
                at = pl.ds(pl.multiple_of(half * 2 * quarter + g * quarter, quarter), quarter)
                for i in range(3):
                    full[i, at, :] = blocks[2 * side + g][i]

    @pl.when(is_owner == 1)
    def _():
        place(weights[:4])

    @pl.when(is_owner == 0)
    def _():
        place(weights[4:])

    for step, out in enumerate(outs):
        at = pl.ds(pl.multiple_of((where[0] ^ step) * VIEW_ROWS, VIEW_ROWS), VIEW_ROWS)
        q = queries[at, :]
        pre_gate = jnp.dot(q, full[0], preferred_element_type=f32)
        pre_up = jnp.dot(q, full[1], preferred_element_type=f32)
        hidden = (pre_gate * jax.nn.sigmoid(pre_gate) * pre_up).astype(bf16)
        fast = jnp.dot(hidden, full[2], preferred_element_type=f32)
        scale = lax.rsqrt(jnp.mean(fast * fast, axis=-1, keepdims=True) + epsilon)
        out[...] = (fast * scale + attended[at, :]).astype(bf16)


def finish(where, queries, attended, weights, heads):
    width = queries.shape[1]
    inputs = (queries, attended, *weights)
    return call(
        finish_body,
        "finish",
        where,
        inputs,
        [whole(x.shape) for x in inputs],
        [jax.ShapeDtypeStruct((VIEW_ROWS, width), bf16)] * heads,
        scratch=[pltpu.VMEM((3, width, width), bf16)],
        flops=6 * queries.shape[0] * width * width,
    )


def join_body(heads, width, where, *refs):
    out = refs[-1]
    for step in range(heads):
        head = head_of(where[0] ^ step, heads)
        out[:, pl.ds(pl.multiple_of(head * width, width), width)] = refs[step][...]


def join(where, blocks, heads, width):
    rows = blocks[0].shape[0]
    return call(
        functools.partial(join_body, heads, width),
        "join",
        where,
        tuple(blocks),
        [whole(x.shape) for x in blocks],
        [jax.ShapeDtypeStruct((rows, heads * width), bf16)],
    )[0]


def on_device(
    update_keys,
    update_values,
    update_rates,
    update_mask,
    fast_weights,
    step_sizes,
    target_queries,
    target_keys,
    target_values,
    target_views,
):
    heads, _, width, _ = fast_weights.shape
    half = heads // 2
    count = lax.axis_size(AXIS)
    me = lax.axis_index(AXIS)
    span = count // heads
    plane, inner = me // span, me % span
    core = inner % 2
    inner_bits = list(range(1, span.bit_length() - 1))
    bit_of = lambda b: (me >> b) & 1
    matched = lambda t: (t // span) % 2 == t % 2

    share = width // 4 // 2 ** (len(inner_bits) - 1)
    first = [bit_of(1) * 2 + g for g in range(2)]
    for b in inner_bits[1:]:
        first = [2 * f + bit_of(b) for f in first]
    is_owner = (plane % 2 == core).astype(i32)
    where = jnp.stack(
        [plane, core, bit_of(1), me, inner, head_of(plane, heads), first[0], first[1], is_owner]
    ).astype(i32)

    rates = -(update_mask.astype(f32)[:, None] * update_rates)
    tag = jnp.stack([target_views // 256, target_views % 256]).astype(bf16)
    tag = jnp.concatenate([tag, jnp.zeros((TAG_ROWS - 2, tag.shape[1]), bf16)])
    tag_in = swap(tag, 1)
    other = swap(pack_update(where, update_keys, update_values, rates, half, width), 1)
    tags = jnp.concatenate([tag[:2], tag_in[:2], jnp.zeros((TAG_ROWS - 4, tag.shape[1]), bf16)])

    sent = pack_target(where, target_queries, target_keys, target_values, tags, heads, width)
    pieces = {}
    for step in range(heads):
        group = {step * span: swap(sent[step], step * span) if step else sent[0]}
        for b in reversed(inner_bits):
            group.update({n | (1 << b): swap(x, 1 << b) for n, x in list(group.items())})
        pieces.update(group)
    own, given = arrange(
        where, [pieces[n] for n in sorted(pieces)], count, span, heads, width
    )
    queries, attended = attend(where, own, swap(given, 1))

    sums = []
    for j in range(half):
        sends, keeps = head_grad(
            where, update_keys, update_values, rates, other, fast_weights, j, half, width
        )
        for g in range(2):
            total = keeps[g] + swap(sends[g], 2).astype(f32)
            for b in inner_bits[1:]:
                rows = total.shape[1] // 2
                send = lax.dynamic_slice_in_dim(total, (1 - bit_of(b)) * rows, rows, 1)
                keep = lax.dynamic_slice_in_dim(total, bit_of(b) * rows, rows, 1)
                total = keep + swap(send.astype(bf16), 1 << b).astype(f32)
            total = total + swap(total.astype(bf16), span, lambda t: not matched(t)).astype(f32)
            sums.append(total)
    fresh = []
    upper = plane // 2 == 1
    for g in range(2):
        low, high = sums[g], sums[2 + g]
        keep = jnp.where(upper, high, low)
        got = swap(jnp.where(upper, low, high).astype(bf16), 2 * span, matched)
        new = renew(where, keep, got, fast_weights, step_sizes, g, 2)
        for b in reversed(inner_bits[1:]):
            far = swap(new, 1 << b, matched)
            new = jnp.where(
                bit_of(b) == 1,
                jnp.concatenate([far, new], axis=1),
                jnp.concatenate([new, far], axis=1),
            )
        fresh.append(new)
    far = [swap(x, 2, matched) for x in fresh]
    near = [swap(x, 1, matched) for x in fresh] + [swap(x, 1, matched) for x in far]

    blocks = finish(where, queries, attended, fresh + far + near, heads)
    got = [swap(x, step * span) if step else x for step, x in enumerate(blocks)]
    return join(where, got, heads, width)


def solution(mesh):
    rows = P(("groups", "tokens"), None)
    return jax.shard_map(
        on_device,
        mesh=mesh,
        in_specs=(
            rows,
            rows,
            rows,
            P(("groups", "tokens")),
            P(),
            P(),
            rows,
            rows,
            rows,
            P(("groups", "tokens")),
        ),
        out_specs=rows,
        check_vma=False,
    )
```

time: 212 us -> 154 us (0.73)
  Pallas kernels: 0 us -> 33.1 us
  blocking collectives: 29.4 us -> 0 us
  starting transfers between devices: 66.3 us -> 42.4 us
  waiting for transfers between devices: 52.1 us -> 73 us
  local copies, waits for them, and re-layouts: 21.7 us -> 1.94 us
  matrix products: 19 us -> 0 us
  other arithmetic: 21.3 us -> 2.71 us
    pallas_call x0 -> x10, Pallas kernels: none -> 33.1 us  [call(): pl.pallas_call(body, name=name, grid_spec=pltpu.PrefetchScalarGridSpec(nu...]
    all_gather x1 -> x0, blocking collectives: 29.4 us -> none  [on_device(): views = lax.all_gather(target_views, AXIS, axis=0, tiled=True)]
    ppermute x44 -> x29, starting transfers between devices: 66.3 us -> 42.4 us  [swap(): return lax.ppermute(value, AXIS, pairs)]
    ppermute x44 -> x29, waiting for transfers between devices: 52.1 us -> 73 us  [swap(): return lax.ppermute(value, AXIS, pairs)]
    dot_general x19 -> x0, matrix products: 19 us -> none  [the longest x6 5.48 us: head_partials(): lax.dot_general(left, right, (((0,), (0,)), ((), ())), preferred_element_...]
    unnamed x52 -> x14, local copies, waits for them, and re-layouts: 12.3 us -> 1.62 us
    convert_element_type x4 -> x2, other arithmetic: 6.88 us -> 0.7 us  [on_device(): got = swap(jnp.where(upper, low, high).astype(bf16), 2 * span, matched)]
    another operation x6 -> x2, other arithmetic: 4.09 us -> 0.02 us  [on_device(): tag = jnp.stack([target_views // 256, target_views % 256]).astype(bf16)]
  transfers between devices with their start and end apart: 44 -> 29, of which waited for: 15 -> 12; matrix products, arithmetic and copies ran while one was open for 23% -> 1% of each run, Pallas kernels for 0% -> 12%
where the time goes in v2:
time: 154 us; the launch traced here: 153 us
  waiting for transfers between devices  73 us (47%)
  starting transfers between devices  42.4 us (28%)
  Pallas kernels  33.1 us (21%)
  other arithmetic  2.71 us (2%)
  local copies, waits for them, and re-layouts  1.94 us (1%)
    ppermute x29, waiting for transfers between devices, swap(): return lax.ppermute(value, AXIS, pairs)  73 us
    ppermute x29, starting transfers between devices, swap(): return lax.ppermute(value, AXIS, pairs)  42.4 us
    pallas_call x10, Pallas kernels, call(): pl.pallas_call(body, name=name, grid_spec=pltpu.PrefetchScalarGridSpec(nu...  33.1 us
  transfers between devices with their start and end apart: 29, of which 12 were waited for; matrix products, arithmetic and copies ran while one was open for 1% of the time, Pallas kernels for 12%

profile of v2, /device:TPU:0, one launch (start us, length us, event | category | flops | bytes accessed | tf_op | source)
XLA Modules:
  0.0 153.5 jit_solution(15377175910510827213)
XLA Ops:
  0.0 0.7 convert_element_type.47
  0.7 0.7 broadcast_multiply_fusion
  1.4 0.1 copy.13
  1.6 0.1 stack.55.where
  1.7 1.6 %copy-done = bf16[512,2048]{1,0:T(8,128)(2,1)S(1)} copy-done((bf16[512,2048]{1,0:T(8,128)(2,1)S(1)}, bf16[512,2048]{1,0:T(8,128)(2,1)}, u32[]{:S(2)}) %copy-start) | copy-done | bytes 2097176
  3.3 4.4 %pack_update.1 = bf16[2,512,1024]{2,1,0:T(8,128)(2,1)} custom-call(s32[9]{0:T(128)S(1)} %stack.55.where, bf16[512,2048]{1,0:T(8,128)(2,1)S(1)} %copy-done, bf16[512,2048]{1,0:T(8,128)(2,1)} %values.7, f32[512,4]{1,0:T(8,128)S(1)} %neg.3.rates), custom_call_target="tpu_custom_call" | custom-call | bytes 6299648 | tf_op jit(solution)/shard_map/pack_update/pallas_call | solution.py:39
  7.7 0.5 collective-permute-start.9
  8.2 0.1 collective-permute-start
  8.3 0.1 pad.4.clone
  8.4 3.5 %collective-permute-done = bf16[16,128]{1,0:T(8,128)(2,1)S(1)} collective-permute-done((bf16[16,128]{1,0:T(8,128)(2,1)S(1)}, bf16[16,128]{1,0:T(8,128)(2,1)S(1)}, u32[]{:S(2)}, u32[]{:S(2)}) %collective-permute-start) | collective-permute-done | bytes 4128 | tf_op jit(solution)/shard_map/ppermute | solution.py:23
  11.9 0.4 collective-permute-done.9.other
  12.3 6.7 %head_grad_1.1 = (bf16[3,128,512]{2,1,0:T(8,128)(2,1)S(1)}, bf16[3,128,512]{2,1,0:T(8,128)(2,1)S(1)}, f32[3,128,512]{2,1,0:T(8,128)S(1)}, f32[3,128,512]{2,1,0:T(8,128)S(1)}) custom-call(s32[9]{0:T(128)S(1)} %stack.55.where, bf16[512,2048]{1,0:T(8,128)(2,1)S(1)} %copy-done.1, bf16[512,2048]{1,0:T(8,128)(2,1)} %values.7, f32[512,4]{1,0:T(8,128)S(1)} %neg.3.rates, ...), custom_call_target="tpu_custom_call" | custom-call | flops 3221225472 | bytes 14950400 | tf_op jit(solution)/shard_map/head_grad_1/pallas_call | solution.py:39
  19.0 2.9 %collective-permute-start.10 = (bf16[3,128,512]{2,1,0:T(8,128)(2,1)S(1)}, bf16[3,128,512]{2,1,0:T(8,128)(2,1)S(1)}, u32[]{:S(2)}, u32[]{:S(2)}) collective-permute-start(bf16[3,128,512]{2,1,0:T(8,128)(2,1)S(1)} %get-tuple-element.34), channel_id=1, source_target_pairs={{0,2},{1,3},{2,0},{3,1},{4,6},{5,7},{6,4},{7,5},{8,10},{9,11},{10,... | collective-permute-start | bytes 1179656 | tf_op jit(solution)/shard_map/ppermute | solution.py:23
  22.0 0.1 fusion.7.tags
  22.1 0.7 pack_target.1
  22.7 1.6 %collective-permute-start.2 = (bf16[400,512]{1,0:T(8,128)(2,1)S(1)}, bf16[400,512]{1,0:T(8,128)(2,1)S(1)}, u32[]{:S(2)}, u32[]{:S(2)}) collective-permute-start(bf16[400,512]{1,0:T(8,128)(2,1)S(1)} %get-tuple-element.26), channel_id=1, source_target_pairs={{0,4},{1,5},{2,6},{3,7},{4,0},{5,1},{6,2},{7,3},{8,12},{9,13},{10,... | collective-permute-start | bytes 1228808 | tf_op jit(solution)/shard_map/ppermute | solution.py:23
  24.4 2.6 %collective-permute-start.4 = (bf16[400,512]{1,0:T(8,128)(2,1)S(1)}, bf16[400,512]{1,0:T(8,128)(2,1)S(1)}, u32[]{:S(2)}, u32[]{:S(2)}) collective-permute-start(bf16[400,512]{1,0:T(8,128)(2,1)S(1)} %get-tuple-element.27), channel_id=1, source_target_pairs={{0,8},{1,9},{2,10},{3,11},{4,12},{5,13},{6,14},{7,15},{8,0},{9,1},... | collective-permute-start | bytes 1228808 | tf_op jit(solution)/shard_map/ppermute | solution.py:23
  27.0 0.2 collective-permute-start.6
  27.2 0.3 collective-permute-start.15
  27.5 6.7 %head_grad_0.1 = (bf16[3,128,512]{2,1,0:T(8,128)(2,1)S(1)}, bf16[3,128,512]{2,1,0:T(8,128)(2,1)S(1)}, f32[3,128,512]{2,1,0:T(8,128)S(1)}, f32[3,128,512]{2,1,0:T(8,128)S(1)}) custom-call(s32[9]{0:T(128)S(1)} %stack.55.where, bf16[512,2048]{1,0:T(8,128)(2,1)S(1)} %copy-done.1, bf16[512,2048]{1,0:T(8,128)(2,1)} %values.7, f32[512,4]{1,0:T(8,128)S(1)} %neg.3.rates, ...), custom_call_target="tpu_custom_call" | custom-call | flops 3221225472 | bytes 14950400 | tf_op jit(solution)/shard_map/head_grad_0/pallas_call | solution.py:39
  34.3 1.8 %collective-permute-start.12 = (bf16[3,128,512]{2,1,0:T(8,128)(2,1)S(1)}, bf16[3,128,512]{2,1,0:T(8,128)(2,1)S(1)}, u32[]{:S(2)}, u32[]{:S(2)}) collective-permute-start(bf16[3,128,512]{2,1,0:T(8,128)(2,1)S(1)} %get-tuple-element.36), channel_id=1, source_target_pairs={{0,2},{1,3},{2,0},{3,1},{4,6},{5,7},{6,4},{7,5},{8,10},{9,11},{10,... | collective-permute-start | bytes 1179656 | tf_op jit(solution)/shard_map/ppermute | solution.py:23
  36.1 0.1 fusion
  36.2 5.9 %collective-permute-done.2.refs_2_ = bf16[400,512]{1,0:T(8,128)(2,1)S(1)} collective-permute-done((bf16[400,512]{1,0:T(8,128)(2,1)S(1)}, bf16[400,512]{1,0:T(8,128)(2,1)S(1)}, u32[]{:S(2)}, u32[]{:S(2)}) %collective-permute-start.2) | collective-permute-done | bytes 409632 | tf_op jit(solution)/shard_map/ppermute | solution.py:23
  42.1 0.4 collective-permute-start.1
  42.4 1.7 %collective-permute-start.17 = (bf16[3,128,512]{2,1,0:T(8,128)(2,1)S(1)}, bf16[3,128,512]{2,1,0:T(8,128)(2,1)S(1)}, u32[]{:S(2)}, u32[]{:S(2)}) collective-permute-start(bf16[3,128,512]{2,1,0:T(8,128)(2,1)S(1)} %get-tuple-element.40), channel_id=1, source_target_pairs={{0,2},{1,3},{2,0},{3,1},{4,6},{5,7},{6,4},{7,5},{8,10},{9,11},{10,... | collective-permute-start | bytes 1179656 | tf_op jit(solution)/shard_map/ppermute | solution.py:23
  44.1 0.1 fusion.2
  44.2 11.0 %collective-permute-done.4.refs_4_ = bf16[400,512]{1,0:T(8,128)(2,1)S(1)} collective-permute-done((bf16[400,512]{1,0:T(8,128)(2,1)S(1)}, bf16[400,512]{1,0:T(8,128)(2,1)S(1)}, u32[]{:S(2)}, u32[]{:S(2)}) %collective-permute-start.4) | collective-permute-done | bytes 409632 | tf_op jit(solution)/shard_map/ppermute | solution.py:23
  55.2 0.5 collective-permute-start.3
  55.7 1.5 collective-permute-start.5
  57.3 0.5 collective-permute-start.7
  57.8 0.1 fusion.1
  57.9 1.3 collective-permute-start.11
  59.2 6.7 %collective-permute-done.17 = bf16[3,128,512]{2,1,0:T(8,128)(2,1)S(1)} collective-permute-done((bf16[3,128,512]{2,1,0:T(8,128)(2,1)S(1)}, bf16[3,128,512]{2,1,0:T(8,128)(2,1)S(1)}, u32[]{:S(2)}, u32[]{:S(2)}) %collective-permute-start.17) | collective-permute-done | bytes 393248 | tf_op jit(solution)/shard_map/ppermute | solution.py:23
  65.9 1.3 collective-permute-start.13
  67.2 0.1 fusion.3
  67.4 7.4 %collective-permute-done.3.refs_3_ = bf16[400,512]{1,0:T(8,128)(2,1)S(1)} collective-permute-done((bf16[400,512]{1,0:T(8,128)(2,1)S(1)}, bf16[400,512]{1,0:T(8,128)(2,1)S(1)}, u32[]{:S(2)}, u32[]{:S(2)}) %collective-permute-start.3) | collective-permute-done | bytes 409632 | tf_op jit(solution)/shard_map/ppermute | solution.py:23
  74.7 1.3 collective-permute-start.16
  76.0 7.5 %collective-permute-done.5.refs_5_ = bf16[400,512]{1,0:T(8,128)(2,1)S(1)} collective-permute-done((bf16[400,512]{1,0:T(8,128)(2,1)S(1)}, bf16[400,512]{1,0:T(8,128)(2,1)S(1)}, u32[]{:S(2)}, u32[]{:S(2)}) %collective-permute-start.5) | collective-permute-done | bytes 409632 | tf_op jit(solution)/shard_map/ppermute | solution.py:23
  83.5 1.5 collective-permute-start.18
  85.0 6.8 %collective-permute-done.7.refs_7_ = bf16[400,512]{1,0:T(8,128)(2,1)S(1)} collective-permute-done((bf16[400,512]{1,0:T(8,128)(2,1)S(1)}, bf16[400,512]{1,0:T(8,128)(2,1)S(1)}, u32[]{:S(2)}, u32[]{:S(2)}) %collective-permute-start.7) | collective-permute-done | bytes 409632 | tf_op jit(solution)/shard_map/ppermute | solution.py:23
  91.8 5.6 %arrange.1 = (bf16[3,512,512]{2,1,0:T(8,128)(2,1)S(1)}, bf16[3,512,512]{2,1,0:T(8,128)(2,1)}) custom-call(s32[9]{0:T(128)S(1)} %stack.55.where, bf16[400,512]{1,0:T(8,128)(2,1)S(1)} %get-tuple-element.25.refs_0_, bf16[400,512]{1,0:T(8,128)(2,1)S(1)} %collective-permute-done.1.refs_1_, bf16[400,512]{1,0:T(8,128)(2,1)S(1)} %collective-permute-done.2.refs_2_, ...), custom_call_target="tpu_custom_call" | custom-call | flops 3221225472 | bytes 6422528 | tf_op jit(solution)/shard_map/arrange/pallas_call | solution.py:39
  97.4 0.3 select_convert_fusion.1
  97.7 0.0 copy-start.5
  97.8 4.7 %collective-permute-start.14 = (bf16[3,128,512]{2,1,0:T(8,128)(2,1)S(1)}, bf16[3,128,512]{2,1,0:T(8,128)(2,1)S(1)}, u32[]{:S(2)}, u32[]{:S(2)}) collective-permute-start(bf16[3,128,512]{2,1,0:T(8,128)(2,1)S(1)} %get-tuple-element.47), channel_id=1, source_target_pairs={{0,8},{2,10},{5,13},{7,15},{8,0},{10,2},{13,5},{15,7},{16,24},{18,... | collective-permute-start | bytes 1179656 | tf_op jit(solution)/shard_map/ppermute | solution.py:23
  102.5 0.3 select_convert_fusion
  102.9 2.0 %collective-permute-start.19 = (bf16[3,128,512]{2,1,0:T(8,128)(2,1)S(1)}, bf16[3,128,512]{2,1,0:T(8,128)(2,1)S(1)}, u32[]{:S(2)}, u32[]{:S(2)}) collective-permute-start(bf16[3,128,512]{2,1,0:T(8,128)(2,1)S(1)} %get-tuple-element.45), channel_id=1, source_target_pairs={{0,8},{2,10},{5,13},{7,15},{8,0},{10,2},{13,5},{15,7},{16,24},{18,... | collective-permute-start | bytes 1179656 | tf_op jit(solution)/shard_map/ppermute | solution.py:23
  104.9 11.9 %collective-permute-done.14.got = bf16[3,128,512]{2,1,0:T(8,128)(2,1)S(1)} collective-permute-done((bf16[3,128,512]{2,1,0:T(8,128)(2,1)S(1)}, bf16[3,128,512]{2,1,0:T(8,128)(2,1)S(1)}, u32[]{:S(2)}, u32[]{:S(2)}) %collective-permute-start.14) | collective-permute-done | bytes 393248 | tf_op jit(solution)/shard_map/ppermute | solution.py:23
  116.8 1.8 %renew.2.refs_0_ = bf16[3,128,512]{2,1,0:T(8,128)(2,1)S(1)} custom-call(s32[9]{0:T(128)S(1)} %stack.55.where, f32[3,128,512]{2,1,0:T(8,128)S(1)} %get-tuple-element.48.keep, bf16[3,128,512]{2,1,0:T(8,128)(2,1)S(1)} %collective-permute-done.14.got, bf16[4,3,512,512]{3,2,1,0:T(8,128)(2,1)} %old.3, f32[4]{0:T(128)S(1)} %copy-done.5), custom_call_target="tpu_custom_call" | custom-call | bytes 7864336 | tf_op jit(solution)/shard_map/renew/pallas_call | solution.py:39
  118.6 3.6 %collective-permute-start.20 = (bf16[3,128,512]{2,1,0:T(8,128)(2,1)S(1)}, bf16[3,128,512]{2,1,0:T(8,128)(2,1)S(1)}, u32[]{:S(2)}, u32[]{:S(2)}) collective-permute-start(bf16[3,128,512]{2,1,0:T(8,128)(2,1)S(1)} %renew.2.refs_0_), channel_id=1, source_target_pairs={{0,2},{2,0},{5,7},{7,5},{8,10},{10,8},{13,15},{15,13},{16,18},{18,... | collective-permute-start | bytes 1179656 | tf_op jit(solution)/shard_map/ppermute | solution.py:23
  122.2 1.8 %renew.3.refs_1_ = bf16[3,128,512]{2,1,0:T(8,128)(2,1)S(1)} custom-call(s32[9]{0:T(128)S(1)} %stack.55.where, f32[3,128,512]{2,1,0:T(8,128)S(1)} %get-tuple-element.46.keep, bf16[3,128,512]{2,1,0:T(8,128)(2,1)S(1)} %collective-permute-done.19.got, bf16[4,3,512,512]{3,2,1,0:T(8,128)(2,1)} %old.3, f32[4]{0:T(128)S(1)} %copy-done.5), custom_call_target="tpu_custom_call" | custom-call | bytes 7864336 | tf_op jit(solution)/shard_map/renew/pallas_call | solution.py:39
  124.0 2.4 %collective-permute-start.21 = (bf16[3,128,512]{2,1,0:T(8,128)(2,1)S(1)}, bf16[3,128,512]{2,1,0:T(8,128)(2,1)S(1)}, u32[]{:S(2)}, u32[]{:S(2)}) collective-permute-start(bf16[3,128,512]{2,1,0:T(8,128)(2,1)S(1)} %renew.3.refs_1_), channel_id=1, source_target_pairs={{0,2},{2,0},{5,7},{7,5},{8,10},{10,8},{13,15},{15,13},{16,18},{18,... | collective-permute-start | bytes 1179656 | tf_op jit(solution)/shard_map/ppermute | solution.py:23
  126.4 1.3 collective-permute-start.22
  127.7 1.3 collective-permute-start.23
  129.1 1.3 collective-permute-start.24
  130.4 3.3 %collective-permute-done.21.refs_3_ = bf16[3,128,512]{2,1,0:T(8,128)(2,1)S(1)} collective-permute-done((bf16[3,128,512]{2,1,0:T(8,128)(2,1)S(1)}, bf16[3,128,512]{2,1,0:T(8,128)(2,1)S(1)}, u32[]{:S(2)}, u32[]{:S(2)}) %collective-permute-start.21) | collective-permute-done | bytes 393248 | tf_op jit(solution)/shard_map/ppermute | solution.py:23
  133.7 1.3 collective-permute-start.25
  135.0 1.7 %attend.1 = (bf16[512,512]{1,0:T(8,128)(2,1)S(1)}, f32[512,512]{1,0:T(8,128)S(1)}) custom-call(s32[9]{0:T(128)S(1)} %stack.55.where, bf16[3,512,512]{2,1,0:T(8,128)(2,1)S(1)} %get-tuple-element.29.own, bf16[3,512,512]{2,1,0:T(8,128)(2,1)S(1)} %collective-permute-done.8.other), custom_call_target="tpu_custom_call" | custom-call | flops 134217728 | bytes 4718592 | tf_op jit(solution)/shard_map/attend/pallas_call | solution.py:39
  136.8 2.2 %finish.1 = (bf16[128,512]{1,0:T(8,128)(2,1)S(1)}, bf16[128,512]{1,0:T(8,128)(2,1)S(1)}, bf16[128,512]{1,0:T(8,128)(2,1)S(1)}, bf16[128,512]{1,0:T(8,128)(2,1)S(1)}) custom-call(s32[9]{0:T(128)S(1)} %stack.55.where, bf16[512,512]{1,0:T(8,128)(2,1)S(1)} %get-tuple-element.31.queries, f32[512,512]{1,0:T(8,128)S(1)} %get-tuple-element.32.attended, ...), custom_call_target="tpu_custom_call" | custom-call | flops 805306368 | bytes 5242880 | tf_op jit(solution)/shard_map/finish/pallas_call | solution.py:39
  139.0 0.1 collective-permute-start.26
  139.1 1.4 collective-permute-start.27
  140.6 2.9 %collective-permute-start.28 = (bf16[128,512]{1,0:T(8,128)(2,1)S(1)}, bf16[128,512]{1,0:T(8,128)(2,1)S(1)}, u32[]{:S(2)}, u32[]{:S(2)}) collective-permute-start(bf16[128,512]{1,0:T(8,128)(2,1)S(1)} %get-tuple-element.44), channel_id=1, source_target_pairs={{0,12},{1,13},{2,14},{3,15},{4,8},{5,9},{6,10},{7,11},{8,4},{9,5},... | collective-permute-start | bytes 393224 | tf_op jit(solution)/shard_map/ppermute | solution.py:23
  143.5 2.7 %collective-permute-done.26.refs_1_ = bf16[128,512]{1,0:T(8,128)(2,1)S(1)} collective-permute-done((bf16[128,512]{1,0:T(8,128)(2,1)S(1)}, bf16[128,512]{1,0:T(8,128)(2,1)S(1)}, u32[]{:S(2)}, u32[]{:S(2)}) %collective-permute-start.26) | collective-permute-done | bytes 131104 | tf_op jit(solution)/shard_map/ppermute | solution.py:23
  146.2 5.9 %collective-permute-done.27.refs_2_ = bf16[128,512]{1,0:T(8,128)(2,1)S(1)} collective-permute-done((bf16[128,512]{1,0:T(8,128)(2,1)S(1)}, bf16[128,512]{1,0:T(8,128)(2,1)S(1)}, u32[]{:S(2)}, u32[]{:S(2)}) %collective-permute-start.27) | collective-permute-done | bytes 131104 | tf_op jit(solution)/shard_map/ppermute | solution.py:23
  152.1 1.4 join.1
  (35 shorter events, 0.1 us)
Async XLA Ops:
  1.7 1.6 %copy-start = (bf16[512,2048]{1,0:T(8,128)(2,1)S(1)}, bf16[512,2048]{1,0:T(8,128)(2,1)}, u32[]{:S(2)}) copy-start(bf16[512,2048]{1,0:T(8,128)(2,1)} %keys.7) | copy-start | bytes 6291460
  3.3 4.9 %copy-start.6 = (s32[128]{0:T(128)S(1)}, s32[128]{0:T(128)}, u32[]{:S(2)}) copy-start(s32[128]{0:T(128)} %param.19) | copy-start | bytes 1540
  3.3 9.0 %copy-start.1 = (bf16[512,2048]{1,0:T(8,128)(2,1)S(1)}, bf16[512,2048]{1,0:T(8,128)(2,1)}, u32[]{:S(2)}) copy-start(bf16[512,2048]{1,0:T(8,128)(2,1)} %keys.7) | copy-start | bytes 6291460
  7.7 4.6 %collective-permute-start.9 = (bf16[2,512,1024]{2,1,0:T(8,128)(2,1)}, bf16[2,512,1024]{2,1,0:T(8,128)(2,1)}, u32[]{:S(2)}, u32[]{:S(2)}) collective-permute-start(bf16[2,512,1024]{2,1,0:T(8,128)(2,1)} %pack_update.1), channel_id=1, source_target_pairs={{0,1},{1,0},{2,3},{3,2},{4,5},{5,4},{6,7},{7,6},{8,9},{9,8},{10,11... | collective-permute-start | bytes 6291464 | tf_op jit(solution)/shard_map/ppermute | solution.py:23
  8.2 3.7 %collective-permute-start = (bf16[16,128]{1,0:T(8,128)(2,1)S(1)}, bf16[16,128]{1,0:T(8,128)(2,1)S(1)}, u32[]{:S(2)}, u32[]{:S(2)}) collective-permute-start(bf16[16,128]{1,0:T(8,128)(2,1)S(1)} %fusion.8), channel_id=1, source_target_pairs={{0,1},{1,0},{2,3},{3,2},{4,5},{5,4},{6,7},{7,6},{8,9},{9,8},{10,11... | collective-permute-start | bytes 12296 | tf_op jit(solution)/shard_map/ppermute | solution.py:23
  11.9 10.2 %copy-start.2 = (bf16[128,2048]{1,0:T(8,128)(2,1)S(1)}, bf16[128,2048]{1,0:T(8,128)(2,1)}, u32[]{:S(2)}) copy-start(bf16[128,2048]{1,0:T(8,128)(2,1)} %queries.1) | copy-start | bytes 1572868
  11.9 10.2 %copy-start.3 = (bf16[128,2048]{1,0:T(8,128)(2,1)S(1)}, bf16[128,2048]{1,0:T(8,128)(2,1)}, u32[]{:S(2)}) copy-start(bf16[128,2048]{1,0:T(8,128)(2,1)} %keys.4) | copy-start | bytes 1572868
  11.9 10.2 %copy-start.4 = (bf16[128,2048]{1,0:T(8,128)(2,1)S(1)}, bf16[128,2048]{1,0:T(8,128)(2,1)}, u32[]{:S(2)}) copy-start(bf16[128,2048]{1,0:T(8,128)(2,1)} %values.4) | copy-start | bytes 1572868
  19.0 15.2 %collective-permute-start.10 = (bf16[3,128,512]{2,1,0:T(8,128)(2,1)S(1)}, bf16[3,128,512]{2,1,0:T(8,128)(2,1)S(1)}, u32[]{:S(2)}, u32[]{:S(2)}) collective-permute-start(bf16[3,128,512]{2,1,0:T(8,128)(2,1)S(1)} %get-tuple-element.34), channel_id=1, source_target_pairs={{0,2},{1,3},{2,0},{3,1},{4,6},{5,7},{6,4},{7,5},{8,10},{9,11},{10,... | collective-permute-start | bytes 1179656 | tf_op jit(solution)/shard_map/ppermute | solution.py:23
  22.7 19.3 %collective-permute-start.2 = (bf16[400,512]{1,0:T(8,128)(2,1)S(1)}, bf16[400,512]{1,0:T(8,128)(2,1)S(1)}, u32[]{:S(2)}, u32[]{:S(2)}) collective-permute-start(bf16[400,512]{1,0:T(8,128)(2,1)S(1)} %get-tuple-element.26), channel_id=1, source_target_pairs={{0,4},{1,5},{2,6},{3,7},{4,0},{5,1},{6,2},{7,3},{8,12},{9,13},{10,... | collective-permute-start | bytes 1228808 | tf_op jit(solution)/shard_map/ppermute | solution.py:23
  24.4 30.8 %collective-permute-start.4 = (bf16[400,512]{1,0:T(8,128)(2,1)S(1)}, bf16[400,512]{1,0:T(8,128)(2,1)S(1)}, u32[]{:S(2)}, u32[]{:S(2)}) collective-permute-start(bf16[400,512]{1,0:T(8,128)(2,1)S(1)} %get-tuple-element.27), channel_id=1, source_target_pairs={{0,8},{1,9},{2,10},{3,11},{4,12},{5,13},{6,14},{7,15},{8,0},{9,1},... | collective-permute-start | bytes 1228808 | tf_op jit(solution)/shard_map/ppermute | solution.py:23
  27.0 28.8 %collective-permute-start.6 = (bf16[400,512]{1,0:T(8,128)(2,1)S(1)}, bf16[400,512]{1,0:T(8,128)(2,1)S(1)}, u32[]{:S(2)}, u32[]{:S(2)}) collective-permute-start(bf16[400,512]{1,0:T(8,128)(2,1)S(1)} %get-tuple-element.28), channel_id=1, source_target_pairs={{0,12},{1,13},{2,14},{3,15},{4,8},{5,9},{6,10},{7,11},{8,4},{9,5},... | collective-permute-start | bytes 1228808 | tf_op jit(solution)/shard_map/ppermute | solution.py:23
  27.2 15.2 %collective-permute-start.15 = (bf16[3,128,512]{2,1,0:T(8,128)(2,1)S(1)}, bf16[3,128,512]{2,1,0:T(8,128)(2,1)S(1)}, u32[]{:S(2)}, u32[]{:S(2)}) collective-permute-start(bf16[3,128,512]{2,1,0:T(8,128)(2,1)S(1)} %get-tuple-element.38), channel_id=1, source_target_pairs={{0,2},{1,3},{2,0},{3,1},{4,6},{5,7},{6,4},{7,5},{8,10},{9,11},{10,... | collective-permute-start | bytes 1179656 | tf_op jit(solution)/shard_map/ppermute | solution.py:23
  34.3 23.0 %collective-permute-start.12 = (bf16[3,128,512]{2,1,0:T(8,128)(2,1)S(1)}, bf16[3,128,512]{2,1,0:T(8,128)(2,1)S(1)}, u32[]{:S(2)}, u32[]{:S(2)}) collective-permute-start(bf16[3,128,512]{2,1,0:T(8,128)(2,1)S(1)} %get-tuple-element.36), channel_id=1, source_target_pairs={{0,2},{1,3},{2,0},{3,1},{4,6},{5,7},{6,4},{7,5},{8,10},{9,11},{10,... | collective-permute-start | bytes 1179656 | tf_op jit(solution)/shard_map/ppermute | solution.py:23
  42.1 15.8 %collective-permute-start.1 = (bf16[400,512]{1,0:T(8,128)(2,1)S(1)}, bf16[400,512]{1,0:T(8,128)(2,1)S(1)}, u32[]{:S(2)}, u32[]{:S(2)}) collective-permute-start(bf16[400,512]{1,0:T(8,128)(2,1)S(1)} %get-tuple-element.25.refs_0_), channel_id=1, source_target_pairs={{0,2},{1,3},{2,0},{3,1},{4,6},{5,7},{6,4},{7,5},{8,10},{9,11},{10,... | collective-permute-start | bytes 1228808 | tf_op jit(solution)/shard_map/ppermute | solution.py:23
  42.4 23.5 %collective-permute-start.17 = (bf16[3,128,512]{2,1,0:T(8,128)(2,1)S(1)}, bf16[3,128,512]{2,1,0:T(8,128)(2,1)S(1)}, u32[]{:S(2)}, u32[]{:S(2)}) collective-permute-start(bf16[3,128,512]{2,1,0:T(8,128)(2,1)S(1)} %get-tuple-element.40), channel_id=1, source_target_pairs={{0,2},{1,3},{2,0},{3,1},{4,6},{5,7},{6,4},{7,5},{8,10},{9,11},{10,... | collective-permute-start | bytes 1179656 | tf_op jit(solution)/shard_map/ppermute | solution.py:23
  55.2 19.5 %collective-permute-start.3 = (bf16[400,512]{1,0:T(8,128)(2,1)S(1)}, bf16[400,512]{1,0:T(8,128)(2,1)S(1)}, u32[]{:S(2)}, u32[]{:S(2)}) collective-permute-start(bf16[400,512]{1,0:T(8,128)(2,1)S(1)} %collective-permute-done.2.refs_2_), channel_id=1, source_target_pairs={{0,2},{1,3},{2,0},{3,1},{4,6},{5,7},{6,4},{7,5},{8,10},{9,11},{10,... | collective-permute-start | bytes 1228808 | tf_op jit(solution)/shard_map/ppermute | solution.py:23
  55.7 27.8 %collective-permute-start.5 = (bf16[400,512]{1,0:T(8,128)(2,1)S(1)}, bf16[400,512]{1,0:T(8,128)(2,1)S(1)}, u32[]{:S(2)}, u32[]{:S(2)}) collective-permute-start(bf16[400,512]{1,0:T(8,128)(2,1)S(1)} %collective-permute-done.4.refs_4_), channel_id=1, source_target_pairs={{0,2},{1,3},{2,0},{3,1},{4,6},{5,7},{6,4},{7,5},{8,10},{9,11},{10,... | collective-permute-start | bytes 1228808 | tf_op jit(solution)/shard_map/ppermute | solution.py:23
  57.3 34.5 %collective-permute-start.7 = (bf16[400,512]{1,0:T(8,128)(2,1)S(1)}, bf16[400,512]{1,0:T(8,128)(2,1)S(1)}, u32[]{:S(2)}, u32[]{:S(2)}) collective-permute-start(bf16[400,512]{1,0:T(8,128)(2,1)S(1)} %collective-permute-done.6.refs_6_), channel_id=1, source_target_pairs={{0,2},{1,3},{2,0},{3,1},{4,6},{5,7},{6,4},{7,5},{8,10},{9,11},{10,... | collective-permute-start | bytes 1228808 | tf_op jit(solution)/shard_map/ppermute | solution.py:23
  57.9 39.5 %collective-permute-start.11 = (bf16[3,128,512]{2,1,0:T(8,128)(2,1)S(1)}, bf16[3,128,512]{2,1,0:T(8,128)(2,1)S(1)}, u32[]{:S(2)}, u32[]{:S(2)}) collective-permute-start(bf16[3,128,512]{2,1,0:T(8,128)(2,1)S(1)} %fusion), channel_id=1, source_target_pairs={{1,5},{3,7},{4,0},{6,2},{9,13},{11,15},{12,8},{14,10},{17,21},{19,... | collective-permute-start | bytes 1179656 | tf_op jit(solution)/shard_map/ppermute | solution.py:23
  65.9 31.4 %collective-permute-start.13 = (bf16[3,128,512]{2,1,0:T(8,128)(2,1)S(1)}, bf16[3,128,512]{2,1,0:T(8,128)(2,1)S(1)}, u32[]{:S(2)}, u32[]{:S(2)}) collective-permute-start(bf16[3,128,512]{2,1,0:T(8,128)(2,1)S(1)} %fusion.1), channel_id=1, source_target_pairs={{1,5},{3,7},{4,0},{6,2},{9,13},{11,15},{12,8},{14,10},{17,21},{19,... | collective-permute-start | bytes 1179656 | tf_op jit(solution)/shard_map/ppermute | solution.py:23
  74.7 27.8 %collective-permute-start.16 = (bf16[3,128,512]{2,1,0:T(8,128)(2,1)S(1)}, bf16[3,128,512]{2,1,0:T(8,128)(2,1)S(1)}, u32[]{:S(2)}, u32[]{:S(2)}) collective-permute-start(bf16[3,128,512]{2,1,0:T(8,128)(2,1)S(1)} %fusion.2), channel_id=1, source_target_pairs={{1,5},{3,7},{4,0},{6,2},{9,13},{11,15},{12,8},{14,10},{17,21},{19,... | collective-permute-start | bytes 1179656 | tf_op jit(solution)/shard_map/ppermute | solution.py:23
  83.5 19.0 %collective-permute-start.18 = (bf16[3,128,512]{2,1,0:T(8,128)(2,1)S(1)}, bf16[3,128,512]{2,1,0:T(8,128)(2,1)S(1)}, u32[]{:S(2)}, u32[]{:S(2)}) collective-permute-start(bf16[3,128,512]{2,1,0:T(8,128)(2,1)S(1)} %fusion.3), channel_id=1, source_target_pairs={{1,5},{3,7},{4,0},{6,2},{9,13},{11,15},{12,8},{14,10},{17,21},{19,... | collective-permute-start | bytes 1179656 | tf_op jit(solution)/shard_map/ppermute | solution.py:23
  97.4 37.6 %collective-permute-start.8 = (bf16[3,512,512]{2,1,0:T(8,128)(2,1)}, bf16[3,512,512]{2,1,0:T(8,128)(2,1)S(1)}, u32[]{:S(2)}, u32[]{:S(2)}) collective-permute-start(bf16[3,512,512]{2,1,0:T(8,128)(2,1)} %get-tuple-element.30), channel_id=1, source_target_pairs={{0,1},{1,0},{2,3},{3,2},{4,5},{5,4},{6,7},{7,6},{8,9},{9,8},{10,11... | collective-permute-start | bytes 4718600 | tf_op jit(solution)/shard_map/ppermute | solution.py:23
  97.7 19.0 %copy-start.5 = (f32[4]{0:T(128)S(1)}, f32[4]{0:T(128)}, u32[]{:S(2)}) copy-start(f32[4]{0:T(128)} %steps.3) | copy-start | bytes 52
  97.8 19.0 %collective-permute-start.14 = (bf16[3,128,512]{2,1,0:T(8,128)(2,1)S(1)}, bf16[3,128,512]{2,1,0:T(8,128)(2,1)S(1)}, u32[]{:S(2)}, u32[]{:S(2)}) collective-permute-start(bf16[3,128,512]{2,1,0:T(8,128)(2,1)S(1)} %get-tuple-element.47), channel_id=1, source_target_pairs={{0,8},{2,10},{5,13},{7,15},{8,0},{10,2},{13,5},{15,7},{16,24},{18,... | collective-permute-start | bytes 1179656 | tf_op jit(solution)/shard_map/ppermute | solution.py:23
  102.9 19.4 %collective-permute-start.19 = (bf16[3,128,512]{2,1,0:T(8,128)(2,1)S(1)}, bf16[3,128,512]{2,1,0:T(8,128)(2,1)S(1)}, u32[]{:S(2)}, u32[]{:S(2)}) collective-permute-start(bf16[3,128,512]{2,1,0:T(8,128)(2,1)S(1)} %get-tuple-element.45), channel_id=1, source_target_pairs={{0,8},{2,10},{5,13},{7,15},{8,0},{10,2},{13,5},{15,7},{16,24},{18,... | collective-permute-start | bytes 1179656 | tf_op jit(solution)/shard_map/ppermute | solution.py:23
  118.6 10.5 %collective-permute-start.20 = (bf16[3,128,512]{2,1,0:T(8,128)(2,1)S(1)}, bf16[3,128,512]{2,1,0:T(8,128)(2,1)S(1)}, u32[]{:S(2)}, u32[]{:S(2)}) collective-permute-start(bf16[3,128,512]{2,1,0:T(8,128)(2,1)S(1)} %renew.2.refs_0_), channel_id=1, source_target_pairs={{0,2},{2,0},{5,7},{7,5},{8,10},{10,8},{13,15},{15,13},{16,18},{18,... | collective-permute-start | bytes 1179656 | tf_op jit(solution)/shard_map/ppermute | solution.py:23
  124.0 9.7 %collective-permute-start.21 = (bf16[3,128,512]{2,1,0:T(8,128)(2,1)S(1)}, bf16[3,128,512]{2,1,0:T(8,128)(2,1)S(1)}, u32[]{:S(2)}, u32[]{:S(2)}) collective-permute-start(bf16[3,128,512]{2,1,0:T(8,128)(2,1)S(1)} %renew.3.refs_1_), channel_id=1, source_target_pairs={{0,2},{2,0},{5,7},{7,5},{8,10},{10,8},{13,15},{15,13},{16,18},{18,... | collective-permute-start | bytes 1179656 | tf_op jit(solution)/shard_map/ppermute | solution.py:23
  126.4 10.3 %collective-permute-start.22 = (bf16[3,128,512]{2,1,0:T(8,128)(2,1)S(1)}, bf16[3,128,512]{2,1,0:T(8,128)(2,1)S(1)}, u32[]{:S(2)}, u32[]{:S(2)}) collective-permute-start(bf16[3,128,512]{2,1,0:T(8,128)(2,1)S(1)} %renew.2.refs_0_), channel_id=1, source_target_pairs={{0,1},{2,3},{5,4},{7,6},{8,9},{10,11},{13,12},{15,14},{16,17},{18,... | collective-permute-start | bytes 1179656 | tf_op jit(solution)/shard_map/ppermute | solution.py:23
  127.7 9.0 %collective-permute-start.23 = (bf16[3,128,512]{2,1,0:T(8,128)(2,1)S(1)}, bf16[3,128,512]{2,1,0:T(8,128)(2,1)S(1)}, u32[]{:S(2)}, u32[]{:S(2)}) collective-permute-start(bf16[3,128,512]{2,1,0:T(8,128)(2,1)S(1)} %renew.3.refs_1_), channel_id=1, source_target_pairs={{0,1},{2,3},{5,4},{7,6},{8,9},{10,11},{13,12},{15,14},{16,17},{18,... | collective-permute-start | bytes 1179656 | tf_op jit(solution)/shard_map/ppermute | solution.py:23
  129.1 7.7 %collective-permute-start.24 = (bf16[3,128,512]{2,1,0:T(8,128)(2,1)S(1)}, bf16[3,128,512]{2,1,0:T(8,128)(2,1)S(1)}, u32[]{:S(2)}, u32[]{:S(2)}) collective-permute-start(bf16[3,128,512]{2,1,0:T(8,128)(2,1)S(1)} %collective-permute-done.20.refs_2_), channel_id=1, source_target_pairs={{0,1},{2,3},{5,4},{7,6},{8,9},{10,11},{13,12},{15,14},{16,17},{18,... | collective-permute-start | bytes 1179656 | tf_op jit(solution)/shard_map/ppermute | solution.py:23
  133.7 3.1 %collective-permute-start.25 = (bf16[3,128,512]{2,1,0:T(8,128)(2,1)S(1)}, bf16[3,128,512]{2,1,0:T(8,128)(2,1)S(1)}, u32[]{:S(2)}, u32[]{:S(2)}) collective-permute-start(bf16[3,128,512]{2,1,0:T(8,128)(2,1)S(1)} %collective-permute-done.21.refs_3_), channel_id=1, source_target_pairs={{0,1},{2,3},{5,4},{7,6},{8,9},{10,11},{13,12},{15,14},{16,17},{18,... | collective-permute-start | bytes 1179656 | tf_op jit(solution)/shard_map/ppermute | solution.py:23
  139.0 7.1 %collective-permute-start.26 = (bf16[128,512]{1,0:T(8,128)(2,1)S(1)}, bf16[128,512]{1,0:T(8,128)(2,1)S(1)}, u32[]{:S(2)}, u32[]{:S(2)}) collective-permute-start(bf16[128,512]{1,0:T(8,128)(2,1)S(1)} %get-tuple-element.42), channel_id=1, source_target_pairs={{0,4},{1,5},{2,6},{3,7},{4,0},{5,1},{6,2},{7,3},{8,12},{9,13},{10,... | collective-permute-start | bytes 393224 | tf_op jit(solution)/shard_map/ppermute | solution.py:23
  139.1 13.0 %collective-permute-start.27 = (bf16[128,512]{1,0:T(8,128)(2,1)S(1)}, bf16[128,512]{1,0:T(8,128)(2,1)S(1)}, u32[]{:S(2)}, u32[]{:S(2)}) collective-permute-start(bf16[128,512]{1,0:T(8,128)(2,1)S(1)} %get-tuple-element.43), channel_id=1, source_target_pairs={{0,8},{1,9},{2,10},{3,11},{4,12},{5,13},{6,14},{7,15},{8,0},{9,1},... | collective-permute-start | bytes 393224 | tf_op jit(solution)/shard_map/ppermute | solution.py:23
  140.6 11.5 %collective-permute-start.28 = (bf16[128,512]{1,0:T(8,128)(2,1)S(1)}, bf16[128,512]{1,0:T(8,128)(2,1)S(1)}, u32[]{:S(2)}, u32[]{:S(2)}) collective-permute-start(bf16[128,512]{1,0:T(8,128)(2,1)S(1)} %get-tuple-element.44), channel_id=1, source_target_pairs={{0,12},{1,13},{2,14},{3,15},{4,8},{5,9},{6,10},{7,11},{8,4},{9,5},... | collective-permute-start | bytes 393224 | tf_op jit(solution)/shard_map/ppermute | solution.py:23

commit v3 on v2

v3 whole, which is shorter than its diff:
```python
import functools

import jax
import jax.numpy as jnp
from jax import lax
from jax.experimental import pallas as pl
from jax.experimental.pallas import tpu as pltpu
from jax.sharding import PartitionSpec as P

VIEW_ROWS = 128
AXIS = "tokens"
epsilon = 1e-05
f32 = jnp.float32
bf16 = jnp.bfloat16
i32 = jnp.int32
TAG_ROWS = 16
VMEM_LIMIT = 24 * 1024 * 1024


def swap(value, mask, senders=None):
    count = lax.axis_size(AXIS)
    pairs = [(t, t ^ mask) for t in range(count) if senders is None or senders(t)]
    return lax.ppermute(value, AXIS, pairs)


def after(value, *others):
    return lax.optimization_barrier((value, *others))[0]


def head_of(plane, head_count):
    half = head_count // 2
    return (plane % 2) * half + plane // 2


def whole(shape):
    return pl.BlockSpec(shape, lambda *_: (0,) * len(shape))


def call(body, name, scalars, inputs, specs, outs, grid=(1,), out_specs=None, scratch=()):
    return pl.pallas_call(
        body,
        name=name,
        grid_spec=pltpu.PrefetchScalarGridSpec(
            num_scalar_prefetch=1,
            grid=grid,
            in_specs=specs,
            out_specs=out_specs or [whole(o.shape) for o in outs],
            scratch_shapes=list(scratch),
        ),
        out_shape=list(outs),
        cost_estimate=pl.CostEstimate(flops=0, bytes_accessed=0, transcendentals=0),
        compiler_params=pltpu.CompilerParams(vmem_limit_bytes=VMEM_LIMIT),
    )(scalars, *inputs)


def rate_column(rates, mask, head):
    at = lax.broadcasted_iota(i32, rates.shape, 0) == head
    row = jnp.sum(jnp.where(at, rates, 0.0), axis=0, keepdims=True) * mask.astype(f32)
    return -jnp.transpose(jnp.broadcast_to(row, (8, row.shape[1])))[:, 0:1]


def pack_update_body(lane, half, where, rates, mask, keys, values, out, rows_s, tg_s, in_sem, out_sem):
    rows, width = rows_s.shape[1:]
    head = (1 - where[1]) * half + lane
    cols = pl.ds(pl.multiple_of(head * width, width), width)
    loads = []
    for i, source in ((1, values), (0, keys)):
        loads.append(pltpu.make_async_copy(source.at[:, cols], rows_s.at[i], in_sem.at[i]))
        loads[-1].start()
    rate = rate_column(rates[...], mask[...], head)
    loads[0].wait()
    tg_s[...] = (rate * rows_s[1].astype(f32)).astype(bf16)
    stores = [pltpu.make_async_copy(tg_s, out.at[1], out_sem.at[1])]
    stores[0].start()
    loads[1].wait()
    stores.append(pltpu.make_async_copy(rows_s.at[0], out.at[0], out_sem.at[0]))
    stores[1].start()
    for store in stores:
        store.wait()


def pack_update(where, rates, mask, keys, values, lane, half, width):
    rows = keys.shape[0]
    return call(
        functools.partial(pack_update_body, lane, half),
        "pack_update_%d" % lane,
        where,
        (rates, mask, keys, values),
        [whole(rates.shape), whole(mask.shape)] + [pl.BlockSpec(memory_space=pltpu.HBM)] * 2,
        [jax.ShapeDtypeStruct((2, rows, width), bf16)],
        out_specs=[pl.BlockSpec(memory_space=pl.ANY)],
        scratch=[
            pltpu.VMEM((2, rows, width), bf16),
            pltpu.VMEM((rows, width), bf16),
            pltpu.SemaphoreType.DMA((2,)),
            pltpu.SemaphoreType.DMA((2,)),
        ],
    )[0]


def pack_target_body(heads, width, where, queries, keys, values, views, *outs):
    rows = queries.shape[0]
    for step in range(heads):
        head = head_of(where[0] ^ step, heads)
        cols = pl.ds(pl.multiple_of(head * width, width), width)
        for i, source in enumerate((queries, keys, values)):
            outs[step][pl.ds(i * rows, rows), :] = source[:, cols]
        outs[step][pl.ds(3 * rows, TAG_ROWS), :] = jnp.zeros((TAG_ROWS, width), bf16)
        high, low = views[...] // 256, views[...] % 256
        row_at = lax.broadcasted_iota(i32, (TAG_ROWS, rows), 0)
        digits = jnp.where(row_at == 0, high, jnp.where(row_at == 1, low, 0))
        outs[step][pl.ds(3 * rows, TAG_ROWS), pl.ds(0, rows)] = digits.astype(f32).astype(bf16)


def pack_target(where, queries, keys, values, views, heads, width):
    rows = queries.shape[0]
    out = jax.ShapeDtypeStruct((3 * rows + TAG_ROWS, width), bf16)
    inputs = (queries, keys, values, views)
    return call(
        functools.partial(pack_target_body, heads, width),
        "pack_target",
        where,
        inputs,
        [whole(x.shape) for x in inputs],
        [out] * heads,
    )


def head_grad_body(
    lane, half, cut, where, rates, mask, keys, values, other, weights, *refs
):
    sends, keeps = refs[:2], refs[2:4]
    k_s, v_s, w_s, tg_s, hidden_s, gate_s, up_s, full, send_s, keep_s, in_sem, out_sem = refs[4:]
    rows, width = v_s.shape
    head = where[1] * half + lane
    cols = pl.ds(pl.multiple_of(head * width, width), width)
    upper, lower = pl.ds(0, rows), pl.ds(rows, rows)
    loads = [
        pltpu.make_async_copy(keys.at[:, cols], k_s.at[upper], in_sem.at[0]),
        pltpu.make_async_copy(weights.at[head, 0], w_s.at[0], in_sem.at[1]),
        pltpu.make_async_copy(weights.at[head, 1], w_s.at[1], in_sem.at[2]),
        pltpu.make_async_copy(values.at[:, cols], v_s, in_sem.at[3]),
        pltpu.make_async_copy(weights.at[head, 2], w_s.at[2], in_sem.at[4]),
        pltpu.make_async_copy(other.at[0], k_s.at[lower], in_sem.at[5]),
        pltpu.make_async_copy(other.at[1], tg_s.at[lower], in_sem.at[6]),
    ]
    for load in loads:
        load.start()
    rate = rate_column(rates[...], mask[...], head)
    chunk = 256
    for at in range(0, 2 * rows, chunk):
        span = pl.ds(at, chunk)
        if at == 0:
            loads[0].wait()
            loads[1].wait()
        if at == rows:
            loads[5].wait()
        k = k_s[span, :]
        pre_gate = jnp.dot(k, w_s[0], preferred_element_type=f32)
        if at == 0:
            loads[2].wait()
        pre_up = jnp.dot(k, w_s[1], preferred_element_type=f32)
        if at == 0:
            loads[3].wait()
            loads[4].wait()
        if at == rows:
            loads[6].wait()
        if at < rows:
            tg = (rate[at : at + chunk] * v_s[span, :].astype(f32)).astype(bf16)
            tg_s[span, :] = tg
        else:
            tg = tg_s[span, :]
        back = lax.dot_general(tg, w_s[2], (((1,), (1,)), ((), ())), preferred_element_type=f32)
        sigma = 0.5 * jnp.tanh(0.5 * pre_gate) + 0.5
        activated = pre_gate * sigma
        hidden_s[span, :] = (activated * pre_up).astype(bf16)
        gate_s[span, :] = (back * pre_up * (sigma + activated * (1.0 - sigma))).astype(bf16)
        up_s[span, :] = (back * activated).astype(bf16)
    quarter = width // 4
    bit = where[2]
    stores = []
    for i, left, right in ((2, hidden_s, tg_s), (0, k_s, gate_s), (1, k_s, up_s)):
        full[...] = lax.dot_general(
            left[...], right[...], (((0,), (0,)), ((), ())), preferred_element_type=f32
        )
        for g in range(2):
            for side in range(2):
                at = pl.ds((2 * side + g) * quarter, quarter)
                if cut:
                    rows_at = pl.ds(
                        pl.multiple_of(((bit + 1 - side) % 2) * 2 * quarter + g * quarter, quarter),
                        quarter,
                    )
                    if side == 0:
                        send_s[g, i] = full[rows_at, :].astype(bf16)
                    else:
                        keep_s[g, i] = full[rows_at, :]
                else:
                    half_at = pl.ds(side * quarter, quarter)
                    send_s[g, i, half_at] = full[at, :].astype(bf16)
                    keep_s[g, i, half_at] = full[at, :]
            stores += [
                (pltpu.make_async_copy(send_s.at[g, i], sends[g].at[i], out_sem.at[0, g, i]), 0),
                (pltpu.make_async_copy(keep_s.at[g, i], keeps[g].at[i], out_sem.at[1, g, i]), 1),
            ]
            for store, when in stores[-2:]:
                if cut:
                    store.start()
                else:
                    pl.when(where[8] == when)(store.start)
    for store, when in stores:
        if cut:
            store.wait()
        else:
            pl.when(where[8] == when)(store.wait)


def head_grad(where, rates, mask, keys, values, other, weights, lane, half, width, cut):
    rows = keys.shape[0]
    shape = (3, width // 4 if cut else width // 2, width)
    anywhere = pl.BlockSpec(memory_space=pl.ANY)
    in_hbm = pl.BlockSpec(memory_space=pltpu.HBM)
    both = pltpu.VMEM((2 * rows, width), bf16)
    outs = call(
        functools.partial(head_grad_body, lane, half, cut),
        "head_grad_%d" % lane,
        where,
        (rates, mask, keys, values, other, weights),
        [whole(rates.shape), whole(mask.shape), in_hbm, in_hbm, anywhere, in_hbm],
        [jax.ShapeDtypeStruct(shape, bf16)] * 2 + [jax.ShapeDtypeStruct(shape, f32)] * 2,
        out_specs=[anywhere] * 4,
        scratch=[
            both,
            pltpu.VMEM((rows, width), bf16),
            pltpu.VMEM((3, width, width), bf16),
            both,
            both,
            both,
            both,
            pltpu.VMEM((width, width), f32),
            pltpu.VMEM((2, *shape), bf16),
            pltpu.VMEM((2, *shape), f32),
            pltpu.SemaphoreType.DMA((7,)),
            pltpu.SemaphoreType.DMA((2, 2, 3)),
        ],
    )
    return outs[:2], outs[2:]


def arrange_body(span, where, *refs):
    pieces, out = refs[:-1], refs[-1]
    me, inner = where[3], where[4]
    rows = (pieces[0].shape[0] - TAG_ROWS) // 3
    count = len(pieces)
    heads = count // span
    tags = [p[pl.ds(3 * rows, TAG_ROWS), pl.ds(0, rows)].astype(f32) for p in pieces]
    ids = jnp.concatenate([t[0:1, :] * 256.0 + t[1:2, :] for t in tags], axis=0).astype(i32)
    square = (count, count)
    earlier = (
        (me ^ lax.broadcasted_iota(i32, square, 1)) < (me ^ lax.broadcasted_iota(i32, square, 0))
    ).astype(f32)
    before = (
        lax.broadcasted_iota(i32, (rows, rows), 0) < lax.broadcasted_iota(i32, (rows, rows), 1)
    ).astype(f32)
    place = jnp.full((count, rows), -1.0, f32)
    for j in range(heads):
        hit = (ids == j * span + inner).astype(f32)
        rank = jnp.dot(hit, before, preferred_element_type=f32) + jnp.sum(
            jnp.dot(earlier, hit, preferred_element_type=f32), axis=1, keepdims=True
        )
        place = jnp.where(hit > 0.0, rank + float(j * VIEW_ROWS), place)
    place = place.astype(i32)
    group = 4
    totals = [None] * 3
    for first in range(0, count, group):
        row_at = lax.broadcasted_iota(i32, (heads * VIEW_ROWS, rows), 0)
        pick = jnp.concatenate(
            [
                (row_at == place[n : n + 1, :]).astype(f32).astype(bf16)
                for n in range(first, first + group)
            ],
            axis=1,
        )
        for i in range(3):
            source = jnp.concatenate(
                [pieces[n][pl.ds(i * rows, rows), :] for n in range(first, first + group)],
                axis=0,
            )
            part = jnp.dot(pick, source, preferred_element_type=f32)
            totals[i] = part if totals[i] is None else totals[i] + part
    for i in range(3):
        out[i] = totals[i].astype(bf16)


def arrange(where, pieces, span, heads, width):
    return call(
        functools.partial(arrange_body, span),
        "arrange",
        where,
        tuple(pieces),
        [whole(x.shape) for x in pieces],
        [jax.ShapeDtypeStruct((3, heads * VIEW_ROWS, width), bf16)],
    )[0]


def attend_body(where, rows, attended):
    width = rows.shape[2]
    for v in range(rows.shape[1] // VIEW_ROWS):
        at = pl.ds(v * VIEW_ROWS, VIEW_ROWS)
        scores = lax.dot_general(
            rows[0, at, :], rows[1, at, :], (((1,), (1,)), ((), ())), preferred_element_type=f32
        ) * width ** (-0.5)
        top = jnp.max(scores, axis=1, keepdims=True)
        raised = jnp.exp(scores - top)
        probs = (raised / jnp.sum(raised, axis=1, keepdims=True)).astype(bf16)
        attended[at, :] = jnp.dot(probs, rows[2, at, :], preferred_element_type=f32)


def attend(where, rows):
    return call(
        attend_body,
        "attend",
        where,
        (rows,),
        [whole(rows.shape)],
        [jax.ShapeDtypeStruct(rows.shape[1:], f32)],
    )[0]


def renew_body(where, keep, got, old, steps, fresh):
    total = keep[...] + got[...].astype(f32)
    scale = lax.rsqrt(jnp.mean(total * total, axis=-1, keepdims=True) + epsilon)
    step = steps[where[5]]
    fresh[...] = (old[0].astype(f32) - step * (total * scale)).astype(bf16)


def renew(where, keep, got, weights, steps, group, groups):
    parts, rows, width = keep.shape
    return call(
        renew_body,
        "renew",
        where,
        (keep, got, weights, steps),
        [
            whole(keep.shape),
            whole(got.shape),
            pl.BlockSpec(
                (1, parts, rows, width), lambda i, w: (w[5], 0, w[6 + group], 0)
            ),
            pl.BlockSpec(memory_space=pltpu.SMEM),
        ],
        [jax.ShapeDtypeStruct(keep.shape, bf16)],
    )[0]


def finish_body(where, rows, attended, *refs):
    weights = refs[:8]
    outs, full = refs[8:-1], refs[-1]
    bit, is_owner = where[2], where[8]
    quarter = weights[0].shape[1]

    def place(blocks):
        for side in range(2):
            half = bit if side == 0 else 1 - bit
            for g in range(2):
                at = pl.ds(pl.multiple_of(half * 2 * quarter + g * quarter, quarter), quarter)
                for i in range(3):
                    full[i, at, :] = blocks[2 * side + g][i]

    @pl.when(is_owner == 1)
    def _():
        place(weights[:4])

    @pl.when(is_owner == 0)
    def _():
        place(weights[4:])

    for step, out in enumerate(outs):
        at = pl.ds(pl.multiple_of((where[0] ^ step) * VIEW_ROWS, VIEW_ROWS), VIEW_ROWS)
        q = rows[0, at, :]
        pre_gate = jnp.dot(q, full[0], preferred_element_type=f32)
        pre_up = jnp.dot(q, full[1], preferred_element_type=f32)
        hidden = (pre_gate * jax.nn.sigmoid(pre_gate) * pre_up).astype(bf16)
        fast = jnp.dot(hidden, full[2], preferred_element_type=f32)
        scale = lax.rsqrt(jnp.mean(fast * fast, axis=-1, keepdims=True) + epsilon)
        out[...] = (fast * scale + attended[at, :]).astype(bf16)


def finish(where, rows, attended, weights, heads):
    width = rows.shape[2]
    inputs = (rows, attended, *weights)
    return call(
        finish_body,
        "finish",
        where,
        inputs,
        [pl.BlockSpec((1, *rows.shape[1:]), lambda i, w: (0, 0, 0))]
        + [whole(x.shape) for x in inputs[1:]],
        [jax.ShapeDtypeStruct((VIEW_ROWS, width), bf16)] * heads,
        scratch=[pltpu.VMEM((3, width, width), bf16)],
    )


def join_body(heads, width, where, *refs):
    out = refs[-1]
    for step in range(heads):
        head = head_of(where[0] ^ step, heads)
        out[:, pl.ds(pl.multiple_of(head * width, width), width)] = refs[step][...]


def join(where, blocks, heads, width):
    rows = blocks[0].shape[0]
    return call(
        functools.partial(join_body, heads, width),
        "join",
        where,
        tuple(blocks),
        [whole(x.shape) for x in blocks],
        [jax.ShapeDtypeStruct((rows, heads * width), bf16)],
    )[0]


def on_device(
    update_keys,
    update_values,
    update_rates,
    update_mask,
    fast_weights,
    step_sizes,
    target_queries,
    target_keys,
    target_values,
    target_views,
):
    heads, _, width, _ = fast_weights.shape
    half = heads // 2
    count = lax.axis_size(AXIS)
    me = lax.axis_index(AXIS)
    span = count // heads
    plane, inner = me // span, me % span
    core = inner % 2
    inner_bits = list(range(1, span.bit_length() - 1))
    bit_of = lambda b: (me >> b) & 1
    matched = lambda t: (t // span) % 2 == t % 2

    share = width // 4 // 2 ** (len(inner_bits) - 1)
    first = [bit_of(1) * 2 + g for g in range(2)]
    for b in inner_bits[1:]:
        first = [2 * f + bit_of(b) for f in first]
    is_owner = (plane % 2 == core).astype(i32)
    where = jnp.stack(
        [plane, core, bit_of(1), me, inner, head_of(plane, heads), first[0], first[1], is_owner]
    ).astype(i32)

    rates, mask = update_rates.T, update_mask[None, :]

    turn = where

    others = []
    for j in range(half):
        packed = pack_update(turn, rates, mask, update_keys, update_values, j, half, width)
        turn = after(turn, packed)
        others.append(swap(packed, 1))
        if j == 0:
            sent = pack_target(
                turn, target_queries, target_keys, target_values, target_views[None, :], heads, width
            )
            turn = after(turn, sent[0])

    group = {0: sent[0]}
    came = {step: swap(sent[step], step * span) for step in (1, 2)}

    def spread(step, bits):
        for b in bits:
            for n, x in list(group.items()):
                if n // span == step:
                    group[n | (1 << b)] = swap(x, 1 << b)

    outer_bits = list(reversed(inner_bits))
    spread(0, outer_bits)

    sends, keeps = head_grad(
        turn, rates, mask, update_keys, update_values, others[0], fast_weights, 0, half, width, True
    )
    moved = [swap(x, 2) for x in sends]
    turn = after(turn, sends[0], came[1], *group.values())
    spread(0, [0])
    group[span] = came[1]
    whole_sends, whole_keeps = head_grad(
        turn, rates, mask, update_keys, update_values, others[1], fast_weights, 1, half, width, False
    )
    crossed = [swap(x, span, lambda t: not matched(t)) for x in whole_sends]
    turn = after(turn, whole_sends[0])

    def narrow(total, bits, senders=None):
        for b in bits:
            rows = total.shape[1] // 2
            send = lax.dynamic_slice_in_dim(total, (1 - bit_of(b)) * rows, rows, 1)
            keep = lax.dynamic_slice_in_dim(total, bit_of(b) * rows, rows, 1)
            total = keep + swap(send.astype(bf16), 1 << b, senders).astype(f32)
        return total

    low = []
    for g in range(2):
        total = after(keeps[g], turn) + moved[g].astype(f32)
        total = narrow(total, inner_bits[1:])
        low.append((total, swap(total.astype(bf16), span, lambda t: not matched(t))))
        turn = after(turn, total)
        if g == 0:
            turn = after(turn, came[2])
            group[2 * span] = came[2]
            came[3] = swap(after(sent[3], turn), 3 * span)
    group[span] = after(group[span], turn)
    spread(1, outer_bits)
    high = []
    for g in range(2):
        total = after(whole_keeps[g], turn) + crossed[g].astype(f32)
        turn = after(turn, total)
        high.append(narrow(total, inner_bits, matched))
    group[2 * span] = after(group[2 * span], turn)
    spread(2, outer_bits)
    turn = after(turn, *[x for n, x in group.items() if n // span == 0])

    fresh = []
    upper = plane // 2 == 1
    for g in range(2):
        mine_low = after(low[g][0], turn) + low[g][1].astype(f32)
        keep = jnp.where(upper, high[g], mine_low)
        got = swap(jnp.where(upper, mine_low, high[g]).astype(bf16), 2 * span, matched)
        turn = after(turn, keep)
        if g == 0:
            turn = after(turn, came[3])
            group[3 * span] = came[3]
            spread(3, outer_bits)
            spread(1, [0])
        new = renew(turn, keep, got, fast_weights, step_sizes, g, 2)
        turn = after(turn, new)
        for b in reversed(inner_bits[1:]):
            far = swap(new, 1 << b, matched)
            new = jnp.where(
                bit_of(b) == 1,
                jnp.concatenate([far, new], axis=1),
                jnp.concatenate([new, far], axis=1),
            )
        fresh.append(new)
    spread(2, [0])
    spread(3, [0])
    far = [swap(x, 2, matched) for x in fresh]
    near = [swap(x, 1, matched) for x in fresh] + [swap(x, 1, matched) for x in far]

    rows = arrange(turn, [group[n] for n in sorted(group)], span, heads, width)
    attended = attend(turn, rows)
    blocks = finish(where, rows, attended, fresh + far + near, heads)
    got = [swap(x, step * span) if step else x for step, x in enumerate(blocks)]
    return join(where, got, heads, width)


def solution(mesh):
    rows = P(("groups", "tokens"), None)
    return jax.shard_map(
        on_device,
        mesh=mesh,
        in_specs=(
            rows,
            rows,
            rows,
            P(("groups", "tokens")),
            P(),
            P(),
            rows,
            rows,
            rows,
            P(("groups", "tokens")),
        ),
        out_specs=rows,
        check_vma=False,
    )
```

time: 154 us -> 152 us (0.987)
  waiting for transfers between devices: 73 us -> 53.3 us
  local copies, waits for them, and re-layouts: 1.94 us -> 10.1 us
  other arithmetic: 2.71 us -> 9.44 us
  starting transfers between devices: 42.4 us -> 47.1 us
  Pallas kernels: 33.1 us -> 30.3 us
    ppermute x29 -> x36, waiting for transfers between devices: 73 us -> 53.3 us  [swap(): return lax.ppermute(value, AXIS, pairs)]
    unnamed x14 -> x54, local copies, waits for them, and re-layouts: 1.62 us -> 9.14 us
    ppermute x29 -> x36, starting transfers between devices: 42.4 us -> 47.1 us  [swap(): return lax.ppermute(value, AXIS, pairs)]
    convert_element_type x4 -> x2, other arithmetic: 0.51 us -> 4.37 us  [on_device(): total.astype(bf16)]
    add x0 -> x2, other arithmetic: none -> 3.44 us  [on_device(): total = after(whole_keeps[g], turn) + crossed[g].astype(f32)]
    pallas_call x10 -> x11, Pallas kernels: 33.1 us -> 30.3 us  [call(): pl.pallas_call(body, name=name, grid_spec=pltpu.PrefetchScalarGridSpec(nu...]
  transfers between devices with their start and end apart: 29 -> 36, of which waited for: 12 -> 12; matrix products, arithmetic and copies ran while one was open for 1% -> 7% of each run, Pallas kernels for 12% -> 17%
where the time goes in v3:
time: 152 us; the launch traced here: 151 us
  waiting for transfers between devices  53.3 us (35%)
  starting transfers between devices  47.1 us (31%)
  Pallas kernels  30.3 us (20%)
  local copies, waits for them, and re-layouts  10.1 us (7%)
  other arithmetic  9.44 us (6%)
    ppermute x36, waiting for transfers between devices, swap(): return lax.ppermute(value, AXIS, pairs)  53.3 us
    ppermute x36, starting transfers between devices, swap(): return lax.ppermute(value, AXIS, pairs)  47.1 us
    pallas_call x11, Pallas kernels, call(): pl.pallas_call(body, name=name, grid_spec=pltpu.PrefetchScalarGridSpec(nu...  30.3 us
    unnamed x54, local copies, waits for them, and re-layouts  9.14 us
    convert_element_type x2, other arithmetic, on_device(): total.astype(bf16)  4.37 us
    add x2, other arithmetic, on_device(): total = after(whole_keeps[g], turn) + crossed[g].astype(f32)  3.44 us
  transfers between devices with their start and end apart: 36, of which 12 were waited for; matrix products, arithmetic and copies ran while one was open for 7% of the time, Pallas kernels for 17%

profile of v3, /device:TPU:0, one launch (start us, length us, event | category | flops | bytes accessed | tf_op | source)
XLA Modules:
  0.0 150.8 jit_solution(9068185691478250286)
XLA Ops:
  0.1 1.6 %copy-done.1 = bf16[512,2048]{1,0:T(8,128)(2,1)S(1)} copy-done((bf16[512,2048]{1,0:T(8,128)(2,1)S(1)}, bf16[512,2048]{1,0:T(8,128)(2,1)}, u32[]{:S(2)}) %copy-start.1) | copy-done | bytes 2097176
  1.7 1.6 %copy-done.3 = bf16[512,2048]{1,0:T(8,128)(2,1)S(1)} copy-done((bf16[512,2048]{1,0:T(8,128)(2,1)S(1)}, bf16[512,2048]{1,0:T(8,128)(2,1)}, u32[]{:S(2)}) %copy-start.3) | copy-done | bytes 2097176
  3.3 0.7 copy-done.13
  4.0 0.7 copy-done.15
  4.7 1.1 pack_update_0.1
  5.8 0.5 collective-permute-start
  6.3 1.0 copy-done.10
  7.4 1.4 pack_target.1
  8.8 1.1 pack_update_1.1
  9.9 0.4 collective-permute-start.3
  10.4 2.7 %collective-permute-start.1 = (bf16[400,512]{1,0:T(8,128)(2,1)S(1)}, bf16[400,512]{1,0:T(8,128)(2,1)S(1)}, u32[]{:S(2)}, u32[]{:S(2)}) collective-permute-start(bf16[400,512]{1,0:T(8,128)(2,1)S(1)} %get-tuple-element.51), channel_id=1, source_target_pairs={{0,4},{1,5},{2,6},{3,7},{4,0},{5,1},{6,2},{7,3},{8,12},{9,13},{10,... | collective-permute-start | bytes 1228808 | tf_op jit(solution)/shard_map/ppermute | solution.py:23
  13.1 1.5 %collective-permute-start.2 = (bf16[400,512]{1,0:T(8,128)(2,1)S(1)}, bf16[400,512]{1,0:T(8,128)(2,1)S(1)}, u32[]{:S(2)}, u32[]{:S(2)}) collective-permute-start(bf16[400,512]{1,0:T(8,128)(2,1)S(1)} %get-tuple-element.47.refs_0_), channel_id=1, source_target_pairs={{0,2},{1,3},{2,0},{3,1},{4,6},{5,7},{6,4},{7,5},{8,10},{9,11},{10,... | collective-permute-start | bytes 1228808 | tf_op jit(solution)/shard_map/ppermute | solution.py:23
  14.6 7.0 %head_grad_0.1 = (bf16[3,128,512]{2,1,0:T(8,128)(2,1)}, bf16[3,128,512]{2,1,0:T(8,128)(2,1)}, f32[3,128,512]{2,1,0:T(8,128)S(1)}, f32[3,128,512]{2,1,0:T(8,128)S(1)}) custom-call(s32[9]{0:T(128)S(1)} %stack.43.where, f32[4,512]{1,0:T(4,128)S(1)} %bitcast.16, s32[1,512]{1,0:T(1,128)S(1)} %bitcast.20, bf16[512,2048]{1,0:T(8,128)(2,1)S(1)} %copy-done.2, ...), custom_call_target="tpu_custom_call" | custom-call | tf_op jit(solution)/shard_map/head_grad_0/pallas_call | solution.py:40
  21.6 0.6 collective-permute-start.4
  22.2 0.9 collective-permute-done.1.refs_4_
  23.1 1.7 %collective-permute-done.2.refs_2_ = bf16[400,512]{1,0:T(8,128)(2,1)S(1)} collective-permute-done((bf16[400,512]{1,0:T(8,128)(2,1)S(1)}, bf16[400,512]{1,0:T(8,128)(2,1)S(1)}, u32[]{:S(2)}, u32[]{:S(2)}) %collective-permute-start.2) | collective-permute-done | bytes 409632 | tf_op jit(solution)/shard_map/ppermute | solution.py:23
  24.8 6.4 %head_grad_1.1 = (bf16[3,256,512]{2,1,0:T(8,128)(2,1)}, bf16[3,256,512]{2,1,0:T(8,128)(2,1)}, f32[3,256,512]{2,1,0:T(8,128)S(1)}, f32[3,256,512]{2,1,0:T(8,128)S(1)}) custom-call(s32[9]{0:T(128)S(1)} %stack.43.where, f32[4,512]{1,0:T(4,128)S(1)} %bitcast.17, s32[1,512]{1,0:T(1,128)S(1)} %bitcast.21, bf16[512,2048]{1,0:T(8,128)(2,1)S(1)} %copy-done.2, ...), custom_call_target="tpu_custom_call" | custom-call | tf_op jit(solution)/shard_map/head_grad_1/pallas_call | solution.py:40
  31.2 1.2 copy-done.5
  32.4 1.1 copy-done.6
  33.5 1.3 collective-permute-start.7
  34.8 2.7 %collective-permute-start.5 = (bf16[400,512]{1,0:T(8,128)(2,1)}, bf16[400,512]{1,0:T(8,128)(2,1)S(1)}, u32[]{:S(2)}, u32[]{:S(2)}) collective-permute-start(bf16[400,512]{1,0:T(8,128)(2,1)} %get-tuple-element.58), channel_id=1, source_target_pairs={{0,8},{1,9},{2,10},{3,11},{4,12},{5,13},{6,14},{7,15},{8,0},{9,1},... | collective-permute-start | bytes 1228808 | tf_op jit(solution)/shard_map/ppermute | solution.py:23
  37.5 2.2 %collective-permute-start.6 = (bf16[3,128,512]{2,1,0:T(8,128)(2,1)}, bf16[3,128,512]{2,1,0:T(8,128)(2,1)}, u32[]{:S(2)}, u32[]{:S(2)}) collective-permute-start(bf16[3,128,512]{2,1,0:T(8,128)(2,1)} %get-tuple-element.62), channel_id=1, source_target_pairs={{0,2},{1,3},{2,0},{3,1},{4,6},{5,7},{6,4},{7,5},{8,10},{9,11},{10,... | collective-permute-start | bytes 1179656 | tf_op jit(solution)/shard_map/ppermute | solution.py:23
  39.7 0.5 collective-permute-start.10
  40.2 2.2 %fusion.3 = (bf16[3,128,512]{2,1,0:T(8,128)(2,1)}, f32[3,128,512]{2,1,0:T(8,128)}) fusion(f32[3,128,512]{2,1,0:T(8,128)S(1)} %get-tuple-element.56, bf16[3,128,512]{2,1,0:T(8,128)(2,1)} %collective-permute-done.4), kind=kLoop, calls=%fused_computation.15 | loop fusion | flops 589824 | bytes 2359296 | tf_op jit(solution)/shard_map/convert_element_type | solution.py:507
  42.4 13.0 %collective-permute-done.5.refs_8_ = bf16[400,512]{1,0:T(8,128)(2,1)S(1)} collective-permute-done((bf16[400,512]{1,0:T(8,128)(2,1)}, bf16[400,512]{1,0:T(8,128)(2,1)S(1)}, u32[]{:S(2)}, u32[]{:S(2)}) %collective-permute-start.5) | collective-permute-done | bytes 409632 | tf_op jit(solution)/shard_map/ppermute | solution.py:23
  55.4 1.3 collective-permute-start.8
  56.7 2.2 %fusion.2 = (bf16[3,128,512]{2,1,0:T(8,128)(2,1)}, f32[3,128,512]{2,1,0:T(8,128)}) fusion(f32[3,128,512]{2,1,0:T(8,128)S(1)} %get-tuple-element.61, bf16[3,128,512]{2,1,0:T(8,128)(2,1)} %collective-permute-done.6), kind=kLoop, calls=%fused_computation.14 | loop fusion | flops 589824 | bytes 2359296 | tf_op jit(solution)/shard_map/convert_element_type | solution.py:507
  58.9 1.3 collective-permute-start.12
  60.2 1.6 %convert_add_fusion.1 = f32[3,256,512]{2,1,0:T(8,128)S(1)} fusion(f32[3,256,512]{2,1,0:T(8,128)S(1)} %copy-done.7, bf16[3,256,512]{2,1,0:T(8,128)(2,1)} %collective-permute-done.7), kind=kLoop, calls=%fused_computation.1 | loop fusion | flops 786432 | bytes 3932160 | tf_op jit(solution)/shard_map/add | solution.py:517
  61.8 1.1 copy-done.20
  62.9 0.8 dynamic-slice_convert_fusion.1
  63.8 3.4 %collective-permute-start.11 = (bf16[3,128,512]{2,1,0:T(8,128)(2,1)}, bf16[3,128,512]{2,1,0:T(8,128)(2,1)}, u32[]{:S(2)}, u32[]{:S(2)}) collective-permute-start(bf16[3,128,512]{2,1,0:T(8,128)(2,1)} %dynamic-slice_convert_fusion.1), channel_id=1, source_target_pairs={{0,2},{2,0},{5,7},{7,5},{8,10},{10,8},{13,15},{15,13},{16,18},{18,... | collective-permute-start | bytes 1179656 | tf_op jit(solution)/shard_map/ppermute | solution.py:23
  67.2 2.4 %collective-permute-done.8 = bf16[3,256,512]{2,1,0:T(8,128)(2,1)} collective-permute-done((bf16[3,256,512]{2,1,0:T(8,128)(2,1)}, bf16[3,256,512]{2,1,0:T(8,128)(2,1)}, u32[]{:S(2)}, u32[]{:S(2)}) %collective-permute-start.8) | collective-permute-done | bytes 786464 | tf_op jit(solution)/shard_map/ppermute | solution.py:23
  69.6 1.9 %convert_add_fusion = f32[3,256,512]{2,1,0:T(8,128)S(1)} fusion(f32[3,256,512]{2,1,0:T(8,128)} %copy-done.5, bf16[3,256,512]{2,1,0:T(8,128)(2,1)} %collective-permute-done.8), kind=kLoop, calls=%fused_computation | loop fusion | flops 786432 | bytes 3932160 | tf_op jit(solution)/shard_map/add | solution.py:517
  71.5 1.4 collective-permute-start.16
  73.0 3.2 %collective-permute-done.12 = bf16[3,128,512]{2,1,0:T(8,128)(2,1)} collective-permute-done((bf16[3,128,512]{2,1,0:T(8,128)(2,1)}, bf16[3,128,512]{2,1,0:T(8,128)(2,1)}, u32[]{:S(2)}, u32[]{:S(2)}) %collective-permute-start.12) | collective-permute-done | bytes 393248 | tf_op jit(solution)/shard_map/ppermute | solution.py:23
  76.1 1.4 select_convert_fusion.1
  77.5 1.9 %collective-permute-start.14 = (bf16[3,128,512]{2,1,0:T(8,128)(2,1)S(1)}, bf16[3,128,512]{2,1,0:T(8,128)(2,1)S(1)}, u32[]{:S(2)}, u32[]{:S(2)}) collective-permute-start(bf16[3,128,512]{2,1,0:T(8,128)(2,1)S(1)} %get-tuple-element.93), channel_id=1, source_target_pairs={{0,8},{2,10},{5,13},{7,15},{8,0},{10,2},{13,5},{15,7},{16,24},{18,... | collective-permute-start | bytes 1179656 | tf_op jit(solution)/shard_map/ppermute | solution.py:23
  79.5 3.8 %collective-permute-start.15 = (bf16[3,128,512]{2,1,0:T(8,128)(2,1)S(1)}, bf16[3,128,512]{2,1,0:T(8,128)(2,1)S(1)}, u32[]{:S(2)}, u32[]{:S(2)}) collective-permute-start(bf16[3,128,512]{2,1,0:T(8,128)(2,1)S(1)} %dynamic-slice_convert_fusion), channel_id=1, source_target_pairs={{0,2},{2,0},{5,7},{7,5},{8,10},{10,8},{13,15},{15,13},{16,18},{18,... | collective-permute-start | bytes 1179656 | tf_op jit(solution)/shard_map/ppermute | solution.py:23
  83.3 0.4 collective-permute-start.19
  83.7 0.7 collective-permute-done.13.refs_12_
  84.4 12.0 %collective-permute-done.14.got = bf16[3,128,512]{2,1,0:T(8,128)(2,1)S(1)} collective-permute-done((bf16[3,128,512]{2,1,0:T(8,128)(2,1)S(1)}, bf16[3,128,512]{2,1,0:T(8,128)(2,1)S(1)}, u32[]{:S(2)}, u32[]{:S(2)}) %collective-permute-start.14) | collective-permute-done | bytes 393248 | tf_op jit(solution)/shard_map/ppermute | solution.py:23
  96.3 1.4 collective-permute-start.22
  97.8 1.3 renew.2.refs_0_
  99.4 1.9 %collective-permute-start.17 = (bf16[3,128,512]{2,1,0:T(8,128)(2,1)S(1)}, bf16[3,128,512]{2,1,0:T(8,128)(2,1)S(1)}, u32[]{:S(2)}, u32[]{:S(2)}) collective-permute-start(bf16[3,128,512]{2,1,0:T(8,128)(2,1)S(1)} %get-tuple-element.91), channel_id=1, source_target_pairs={{0,8},{2,10},{5,13},{7,15},{8,0},{10,2},{13,5},{15,7},{16,24},{18,... | collective-permute-start | bytes 1179656 | tf_op jit(solution)/shard_map/ppermute | solution.py:23
  101.4 0.5 collective-permute-start.20
  101.9 0.6 collective-permute-start.25
  102.5 1.8 %collective-permute-done.22.refs_10_ = bf16[400,512]{1,0:T(8,128)(2,1)S(1)} collective-permute-done((bf16[400,512]{1,0:T(8,128)(2,1)S(1)}, bf16[400,512]{1,0:T(8,128)(2,1)S(1)}, u32[]{:S(2)}, u32[]{:S(2)}) %collective-permute-start.22) | collective-permute-done | bytes 409632 | tf_op jit(solution)/shard_map/ppermute | solution.py:23
  104.3 7.0 %collective-permute-done.17.got = bf16[3,128,512]{2,1,0:T(8,128)(2,1)S(1)} collective-permute-done((bf16[3,128,512]{2,1,0:T(8,128)(2,1)S(1)}, bf16[3,128,512]{2,1,0:T(8,128)(2,1)S(1)}, u32[]{:S(2)}, u32[]{:S(2)}) %collective-permute-start.17) | collective-permute-done | bytes 393248 | tf_op jit(solution)/shard_map/ppermute | solution.py:23
  111.3 1.3 renew.3.refs_1_
  112.7 2.5 %collective-permute-start.27 = (bf16[3,128,512]{2,1,0:T(8,128)(2,1)S(1)}, bf16[3,128,512]{2,1,0:T(8,128)(2,1)S(1)}, u32[]{:S(2)}, u32[]{:S(2)}) collective-permute-start(bf16[3,128,512]{2,1,0:T(8,128)(2,1)S(1)} %renew.2.refs_0_), channel_id=1, source_target_pairs={{0,2},{2,0},{5,7},{7,5},{8,10},{10,8},{13,15},{15,13},{16,18},{18,... | collective-permute-start | bytes 1179656 | tf_op jit(solution)/shard_map/ppermute | solution.py:23
  115.2 3.4 %collective-permute-start.28 = (bf16[3,128,512]{2,1,0:T(8,128)(2,1)S(1)}, bf16[3,128,512]{2,1,0:T(8,128)(2,1)S(1)}, u32[]{:S(2)}, u32[]{:S(2)}) collective-permute-start(bf16[3,128,512]{2,1,0:T(8,128)(2,1)S(1)} %renew.3.refs_1_), channel_id=1, source_target_pairs={{0,2},{2,0},{5,7},{7,5},{8,10},{10,8},{13,15},{15,13},{16,18},{18,... | collective-permute-start | bytes 1179656 | tf_op jit(solution)/shard_map/ppermute | solution.py:23
  118.6 2.4 %collective-permute-start.29 = (bf16[3,128,512]{2,1,0:T(8,128)(2,1)S(1)}, bf16[3,128,512]{2,1,0:T(8,128)(2,1)S(1)}, u32[]{:S(2)}, u32[]{:S(2)}) collective-permute-start(bf16[3,128,512]{2,1,0:T(8,128)(2,1)S(1)} %renew.2.refs_0_), channel_id=1, source_target_pairs={{0,1},{2,3},{5,4},{7,6},{8,9},{10,11},{13,12},{15,14},{16,17},{18,... | collective-permute-start | bytes 1179656 | tf_op jit(solution)/shard_map/ppermute | solution.py:23
  121.1 1.3 collective-permute-start.30
  122.4 1.3 collective-permute-start.31
  123.7 2.8 %collective-permute-done.28.refs_3_ = bf16[3,128,512]{2,1,0:T(8,128)(2,1)S(1)} collective-permute-done((bf16[3,128,512]{2,1,0:T(8,128)(2,1)S(1)}, bf16[3,128,512]{2,1,0:T(8,128)(2,1)S(1)}, u32[]{:S(2)}, u32[]{:S(2)}) %collective-permute-start.28) | collective-permute-done | bytes 393248 | tf_op jit(solution)/shard_map/ppermute | solution.py:23
  126.5 1.3 collective-permute-start.32
  127.9 5.3 %arrange.1.rows = bf16[3,512,512]{2,1,0:T(8,128)(2,1)S(1)} custom-call(s32[9]{0:T(128)S(1)} %stack.43.where, bf16[400,512]{1,0:T(8,128)(2,1)S(1)} %get-tuple-element.47.refs_0_, bf16[400,512]{1,0:T(8,128)(2,1)} %collective-permute-done.9.refs_1_, bf16[400,512]{1,0:T(8,128)(2,1)S(1)} %collective-permute-done.2.refs_2_, ...), custom_call_target="tpu_custom_call" | custom-call | tf_op jit(solution)/shard_map/arrange/pallas_call | solution.py:40
  133.2 1.7 %attend.1.attended = f32[512,512]{1,0:T(8,128)S(1)} custom-call(s32[9]{0:T(128)S(1)} %stack.43.where, bf16[3,512,512]{2,1,0:T(8,128)(2,1)S(1)} %arrange.1.rows), custom_call_target="tpu_custom_call" | custom-call | tf_op jit(solution)/shard_map/attend/pallas_call | solution.py:40
  134.9 2.2 %finish.1 = (bf16[128,512]{1,0:T(8,128)(2,1)S(1)}, bf16[128,512]{1,0:T(8,128)(2,1)S(1)}, bf16[128,512]{1,0:T(8,128)(2,1)S(1)}, bf16[128,512]{1,0:T(8,128)(2,1)S(1)}) custom-call(s32[9]{0:T(128)S(1)} %stack.43.where, bf16[3,512,512]{2,1,0:T(8,128)(2,1)S(1)} %arrange.1.rows, f32[512,512]{1,0:T(8,128)S(1)} %attend.1.attended, ...), custom_call_target="tpu_custom_call" | custom-call | tf_op jit(solution)/shard_map/finish/pallas_call | solution.py:40
  137.2 4.3 %collective-permute-start.35 = (bf16[128,512]{1,0:T(8,128)(2,1)S(1)}, bf16[128,512]{1,0:T(8,128)(2,1)S(1)}, u32[]{:S(2)}, u32[]{:S(2)}) collective-permute-start(bf16[128,512]{1,0:T(8,128)(2,1)S(1)} %get-tuple-element.86), channel_id=1, source_target_pairs={{0,12},{1,13},{2,14},{3,15},{4,8},{5,9},{6,10},{7,11},{8,4},{9,5},... | collective-permute-start | bytes 393224 | tf_op jit(solution)/shard_map/ppermute | solution.py:23
  141.5 1.1 collective-permute-done.33.refs_1_
  142.6 6.8 %collective-permute-done.34.refs_2_ = bf16[128,512]{1,0:T(8,128)(2,1)S(1)} collective-permute-done((bf16[128,512]{1,0:T(8,128)(2,1)S(1)}, bf16[128,512]{1,0:T(8,128)(2,1)S(1)}, u32[]{:S(2)}, u32[]{:S(2)}) %collective-permute-start.34) | collective-permute-done | bytes 131104 | tf_op jit(solution)/shard_map/ppermute | solution.py:23
  149.4 1.4 join.1
  (83 shorter events, 0.9 us)
Async XLA Ops:
  0.1 1.6 %copy-start.1 = (bf16[512,2048]{1,0:T(8,128)(2,1)S(1)}, bf16[512,2048]{1,0:T(8,128)(2,1)}, u32[]{:S(2)}) copy-start(bf16[512,2048]{1,0:T(8,128)(2,1)} %keys.9) | copy-start | bytes 6291460
  1.7 1.6 %copy-start.3 = (bf16[512,2048]{1,0:T(8,128)(2,1)S(1)}, bf16[512,2048]{1,0:T(8,128)(2,1)}, u32[]{:S(2)}) copy-start(bf16[512,2048]{1,0:T(8,128)(2,1)} %values.9) | copy-start | bytes 6291460
  3.3 0.7 copy-start.13
  4.0 0.7 copy-start.15
  4.7 1.7 %copy-start.8 = (bf16[128,2048]{1,0:T(8,128)(2,1)S(1)}, bf16[128,2048]{1,0:T(8,128)(2,1)}, u32[]{:S(2)}) copy-start(bf16[128,2048]{1,0:T(8,128)(2,1)} %queries.1) | copy-start | bytes 1572868
  4.7 1.7 %copy-start.9 = (bf16[128,2048]{1,0:T(8,128)(2,1)S(1)}, bf16[128,2048]{1,0:T(8,128)(2,1)}, u32[]{:S(2)}) copy-start(bf16[128,2048]{1,0:T(8,128)(2,1)} %keys.6) | copy-start | bytes 1572868
  4.7 1.7 %copy-start.18 = (s32[128]{0:T(128)S(1)}, s32[128]{0:T(128)}, u32[]{:S(2)}) copy-start(s32[128]{0:T(128)} %param.19) | copy-start | bytes 1540
  4.7 4.2 %copy-start.2 = (bf16[512,2048]{1,0:T(8,128)(2,1)S(1)}, bf16[512,2048]{1,0:T(8,128)(2,1)}, u32[]{:S(2)}) copy-start(bf16[512,2048]{1,0:T(8,128)(2,1)} %keys.9) | copy-start | bytes 6291460
  4.7 4.2 %copy-start.4 = (bf16[512,2048]{1,0:T(8,128)(2,1)S(1)}, bf16[512,2048]{1,0:T(8,128)(2,1)}, u32[]{:S(2)}) copy-start(bf16[512,2048]{1,0:T(8,128)(2,1)} %values.9) | copy-start | bytes 6291460
  4.7 4.1 %copy-start.14 = (f32[512,4]{0,1:T(4,128)S(1)}, f32[512,4]{0,1:T(4,128)}, u32[]{:S(2)}) copy-start(f32[512,4]{0,1:T(4,128)} %param.12) | copy-start | bytes 24580
  4.7 4.1 %copy-start.16 = (s32[512]{0:T(512)S(1)}, s32[512]{0:T(512)}, u32[]{:S(2)}) copy-start(s32[512]{0:T(512)} %param.13) | copy-start | bytes 6148
  5.8 8.8 %collective-permute-start = (bf16[2,512,512]{2,1,0:T(8,128)(2,1)S(1)}, bf16[2,512,512]{2,1,0:T(8,128)(2,1)S(1)}, u32[]{:S(2)}, u32[]{:S(2)}) collective-permute-start(bf16[2,512,512]{2,1,0:T(8,128)(2,1)S(1)} %pack_update_0.1), channel_id=1, source_target_pairs={{0,1},{1,0},{2,3},{3,2},{4,5},{5,4},{6,7},{7,6},{8,9},{9,8},{10,11... | collective-permute-start | bytes 3145736 | tf_op jit(solution)/shard_map/ppermute | solution.py:23
  6.3 1.0 copy-start.10
  7.4 7.3 %copy-start = (bf16[4,3,512,512]{3,2,1,0:T(8,128)(2,1)S(1)}, bf16[4,3,512,512]{3,2,1,0:T(8,128)(2,1)}, u32[]{:S(2)}) copy-start(bf16[4,3,512,512]{3,2,1,0:T(8,128)(2,1)} %old.3) | copy-start | bytes 18874372
  8.8 12.8 %copy-start.19 = (bf16[400,512]{1,0:T(8,128)(2,1)}, bf16[400,512]{1,0:T(8,128)(2,1)S(1)}, u32[]{:S(2)}) copy-start(bf16[400,512]{1,0:T(8,128)(2,1)S(1)} %get-tuple-element.75) | copy-start | bytes 1228804
  9.9 14.8 %collective-permute-start.3 = (bf16[2,512,512]{2,1,0:T(8,128)(2,1)S(1)}, bf16[2,512,512]{2,1,0:T(8,128)(2,1)S(1)}, u32[]{:S(2)}, u32[]{:S(2)}) collective-permute-start(bf16[2,512,512]{2,1,0:T(8,128)(2,1)S(1)} %pack_update_1.1), channel_id=1, source_target_pairs={{0,1},{1,0},{2,3},{3,2},{4,5},{5,4},{6,7},{7,6},{8,9},{9,8},{10,11... | collective-permute-start | bytes 3145736 | tf_op jit(solution)/shard_map/ppermute | solution.py:23
  10.4 12.7 %collective-permute-start.1 = (bf16[400,512]{1,0:T(8,128)(2,1)S(1)}, bf16[400,512]{1,0:T(8,128)(2,1)S(1)}, u32[]{:S(2)}, u32[]{:S(2)}) collective-permute-start(bf16[400,512]{1,0:T(8,128)(2,1)S(1)} %get-tuple-element.51), channel_id=1, source_target_pairs={{0,4},{1,5},{2,6},{3,7},{4,0},{5,1},{6,2},{7,3},{8,12},{9,13},{10,... | collective-permute-start | bytes 1228808 | tf_op jit(solution)/shard_map/ppermute | solution.py:23
  13.1 11.6 %collective-permute-start.2 = (bf16[400,512]{1,0:T(8,128)(2,1)S(1)}, bf16[400,512]{1,0:T(8,128)(2,1)S(1)}, u32[]{:S(2)}, u32[]{:S(2)}) collective-permute-start(bf16[400,512]{1,0:T(8,128)(2,1)S(1)} %get-tuple-element.47.refs_0_), channel_id=1, source_target_pairs={{0,2},{1,3},{2,0},{3,1},{4,6},{5,7},{6,4},{7,5},{8,10},{9,11},{10,... | collective-permute-start | bytes 1228808 | tf_op jit(solution)/shard_map/ppermute | solution.py:23
  21.6 18.1 %collective-permute-start.4 = (bf16[3,128,512]{2,1,0:T(8,128)(2,1)}, bf16[3,128,512]{2,1,0:T(8,128)(2,1)}, u32[]{:S(2)}, u32[]{:S(2)}) collective-permute-start(bf16[3,128,512]{2,1,0:T(8,128)(2,1)} %get-tuple-element.50), channel_id=1, source_target_pairs={{0,2},{1,3},{2,0},{3,1},{4,6},{5,7},{6,4},{7,5},{8,10},{9,11},{10,... | collective-permute-start | bytes 1179656 | tf_op jit(solution)/shard_map/ppermute | solution.py:23
  31.2 1.2 copy-start.5
  32.4 1.1 copy-start.6
  33.5 26.6 %collective-permute-start.7 = (bf16[3,256,512]{2,1,0:T(8,128)(2,1)}, bf16[3,256,512]{2,1,0:T(8,128)(2,1)}, u32[]{:S(2)}, u32[]{:S(2)}) collective-permute-start(bf16[3,256,512]{2,1,0:T(8,128)(2,1)} %get-tuple-element.53), channel_id=1, source_target_pairs={{1,5},{3,7},{4,0},{6,2},{9,13},{11,15},{12,8},{14,10},{17,21},{19,... | collective-permute-start | bytes 2359304 | tf_op jit(solution)/shard_map/ppermute | solution.py:23
  34.8 20.6 %collective-permute-start.5 = (bf16[400,512]{1,0:T(8,128)(2,1)}, bf16[400,512]{1,0:T(8,128)(2,1)S(1)}, u32[]{:S(2)}, u32[]{:S(2)}) collective-permute-start(bf16[400,512]{1,0:T(8,128)(2,1)} %get-tuple-element.58), channel_id=1, source_target_pairs={{0,8},{1,9},{2,10},{3,11},{4,12},{5,13},{6,14},{7,15},{8,0},{9,1},... | collective-permute-start | bytes 1228808 | tf_op jit(solution)/shard_map/ppermute | solution.py:23
  37.5 19.2 %collective-permute-start.6 = (bf16[3,128,512]{2,1,0:T(8,128)(2,1)}, bf16[3,128,512]{2,1,0:T(8,128)(2,1)}, u32[]{:S(2)}, u32[]{:S(2)}) collective-permute-start(bf16[3,128,512]{2,1,0:T(8,128)(2,1)} %get-tuple-element.62), channel_id=1, source_target_pairs={{0,2},{1,3},{2,0},{3,1},{4,6},{5,7},{6,4},{7,5},{8,10},{9,11},{10,... | collective-permute-start | bytes 1179656 | tf_op jit(solution)/shard_map/ppermute | solution.py:23
  39.7 31.8 %collective-permute-start.9 = (bf16[400,512]{1,0:T(8,128)(2,1)S(1)}, bf16[400,512]{1,0:T(8,128)(2,1)}, u32[]{:S(2)}, u32[]{:S(2)}) collective-permute-start(bf16[400,512]{1,0:T(8,128)(2,1)S(1)} %get-tuple-element.47.refs_0_), channel_id=1, source_target_pairs={{0,1},{1,0},{2,3},{3,2},{4,5},{5,4},{6,7},{7,6},{8,9},{9,8},{10,11... | collective-permute-start | bytes 1228808 | tf_op jit(solution)/shard_map/ppermute | solution.py:23
  39.7 33.3 %collective-permute-start.10 = (bf16[400,512]{1,0:T(8,128)(2,1)S(1)}, bf16[400,512]{1,0:T(8,128)(2,1)}, u32[]{:S(2)}, u32[]{:S(2)}) collective-permute-start(bf16[400,512]{1,0:T(8,128)(2,1)S(1)} %collective-permute-done.2.refs_2_), channel_id=1, source_target_pairs={{0,1},{1,0},{2,3},{3,2},{4,5},{5,4},{6,7},{7,6},{8,9},{9,8},{10,11... | collective-permute-start | bytes 1228808 | tf_op jit(solution)/shard_map/ppermute | solution.py:23
  42.4 17.8 %copy-start.7 = (f32[3,256,512]{2,1,0:T(8,128)S(1)}, f32[3,256,512]{2,1,0:T(8,128)}, u32[]{:S(2)}) copy-start(f32[3,256,512]{2,1,0:T(8,128)} %copy-done.6) | copy-start | bytes 4718596
  55.4 4.8 %copy-start.11 = (bf16[400,512]{1,0:T(8,128)(2,1)}, bf16[400,512]{1,0:T(8,128)(2,1)S(1)}, u32[]{:S(2)}) copy-start(bf16[400,512]{1,0:T(8,128)(2,1)S(1)} %collective-permute-done.5.refs_8_) | copy-start | bytes 1228804
  55.4 14.2 %collective-permute-start.8 = (bf16[3,256,512]{2,1,0:T(8,128)(2,1)}, bf16[3,256,512]{2,1,0:T(8,128)(2,1)}, u32[]{:S(2)}, u32[]{:S(2)}) collective-permute-start(bf16[3,256,512]{2,1,0:T(8,128)(2,1)} %get-tuple-element.69), channel_id=1, source_target_pairs={{1,5},{3,7},{4,0},{6,2},{9,13},{11,15},{12,8},{14,10},{17,21},{19,... | collective-permute-start | bytes 2359304 | tf_op jit(solution)/shard_map/ppermute | solution.py:23
  58.9 17.2 %collective-permute-start.12 = (bf16[3,128,512]{2,1,0:T(8,128)(2,1)}, bf16[3,128,512]{2,1,0:T(8,128)(2,1)}, u32[]{:S(2)}, u32[]{:S(2)}) collective-permute-start(bf16[3,128,512]{2,1,0:T(8,128)(2,1)} %get-tuple-element.89), channel_id=1, source_target_pairs={{1,5},{3,7},{4,0},{6,2},{9,13},{11,15},{12,8},{14,10},{17,21},{19,... | collective-permute-start | bytes 1179656 | tf_op jit(solution)/shard_map/ppermute | solution.py:23
  60.2 37.6 %slice-start = ((s8[6291456]{0:T(1024)(128)(4,1)}), s8[2097152]{0:T(1024)(128)(4,1)S(1)}, s32[]{:S(2)}) async-start(s8[6291456]{0:T(1024)(128)(4,1)} %bitcast.12), calls=%async_computation | async-start | bytes 4194304
  61.8 1.1 copy-start.20
  63.8 12.4 %collective-permute-start.11 = (bf16[3,128,512]{2,1,0:T(8,128)(2,1)}, bf16[3,128,512]{2,1,0:T(8,128)(2,1)}, u32[]{:S(2)}, u32[]{:S(2)}) collective-permute-start(bf16[3,128,512]{2,1,0:T(8,128)(2,1)} %dynamic-slice_convert_fusion.1), channel_id=1, source_target_pairs={{0,2},{2,0},{5,7},{7,5},{8,10},{10,8},{13,15},{15,13},{16,18},{18,... | collective-permute-start | bytes 1179656 | tf_op jit(solution)/shard_map/ppermute | solution.py:23
  67.2 4.3 %copy-start.24 = (bf16[3,128,512]{2,1,0:T(8,128)(2,1)S(1)}, bf16[3,128,512]{2,1,0:T(8,128)(2,1)}, u32[]{:S(2)}) copy-start(bf16[3,128,512]{2,1,0:T(8,128)(2,1)} %get-tuple-element.87) | copy-start | bytes 1179652
  67.2 8.9 %copy-start.21 = (f32[3,256,512]{2,1,0:T(8,128)S(1)}, f32[3,256,512]{2,1,0:T(8,128)}, u32[]{:S(2)}) copy-start(f32[3,256,512]{2,1,0:T(8,128)} %copy-done.20) | copy-start | bytes 4718596
  67.2 8.9 %copy-start.23 = (f32[3,128,512]{2,1,0:T(8,128)S(1)}, f32[3,128,512]{2,1,0:T(8,128)}, u32[]{:S(2)}) copy-start(f32[3,128,512]{2,1,0:T(8,128)} %get-tuple-element.72) | copy-start | bytes 2359300
  67.2 30.6 %slice-start.1 = ((s8[6291456]{0:T(1024)(128)(4,1)}), s8[4194304]{0:T(1024)(128)(4,1)S(1)}, s32[]{:S(2)}) async-start(s8[6291456]{0:T(1024)(128)(4,1)} %bitcast.12), calls=%async_computation.1 | async-start | bytes 8388608
  69.6 14.8 %collective-permute-start.13 = (bf16[400,512]{1,0:T(8,128)(2,1)}, bf16[400,512]{1,0:T(8,128)(2,1)S(1)}, u32[]{:S(2)}, u32[]{:S(2)}) collective-permute-start(bf16[400,512]{1,0:T(8,128)(2,1)} %copy-done.19), channel_id=1, source_target_pairs={{0,12},{1,13},{2,14},{3,15},{4,8},{5,9},{6,10},{7,11},{8,4},{9,5},... | collective-permute-start | bytes 1228808 | tf_op jit(solution)/shard_map/ppermute | solution.py:23
  71.5 24.8 %copy-start.12 = (bf16[400,512]{1,0:T(8,128)(2,1)S(1)}, bf16[400,512]{1,0:T(8,128)(2,1)}, u32[]{:S(2)}) copy-start(bf16[400,512]{1,0:T(8,128)(2,1)} %copy-done.11) | copy-start | bytes 1228804
  71.5 26.3 %copy-start.17 = (f32[4]{0:T(128)S(1)}, f32[4]{0:T(128)}, u32[]{:S(2)}) copy-start(f32[4]{0:T(128)} %steps.3) | copy-start | bytes 52
  71.5 27.6 %collective-permute-start.16 = (bf16[3,128,512]{2,1,0:T(8,128)(2,1)S(1)}, bf16[3,128,512]{2,1,0:T(8,128)(2,1)S(1)}, u32[]{:S(2)}, u32[]{:S(2)}) collective-permute-start(bf16[3,128,512]{2,1,0:T(8,128)(2,1)S(1)} %copy-done.24), channel_id=1, source_target_pairs={{1,5},{3,7},{4,0},{6,2},{9,13},{11,15},{12,8},{14,10},{17,21},{19,... | collective-permute-start | bytes 1179656 | tf_op jit(solution)/shard_map/ppermute | solution.py:23
  77.5 18.8 %collective-permute-start.14 = (bf16[3,128,512]{2,1,0:T(8,128)(2,1)S(1)}, bf16[3,128,512]{2,1,0:T(8,128)(2,1)S(1)}, u32[]{:S(2)}, u32[]{:S(2)}) collective-permute-start(bf16[3,128,512]{2,1,0:T(8,128)(2,1)S(1)} %get-tuple-element.93), channel_id=1, source_target_pairs={{0,8},{2,10},{5,13},{7,15},{8,0},{10,2},{13,5},{15,7},{16,24},{18,... | collective-permute-start | bytes 1179656 | tf_op jit(solution)/shard_map/ppermute | solution.py:23
  79.5 19.6 %collective-permute-start.15 = (bf16[3,128,512]{2,1,0:T(8,128)(2,1)S(1)}, bf16[3,128,512]{2,1,0:T(8,128)(2,1)S(1)}, u32[]{:S(2)}, u32[]{:S(2)}) collective-permute-start(bf16[3,128,512]{2,1,0:T(8,128)(2,1)S(1)} %dynamic-slice_convert_fusion), channel_id=1, source_target_pairs={{0,2},{2,0},{5,7},{7,5},{8,10},{10,8},{13,15},{15,13},{16,18},{18,... | collective-permute-start | bytes 1179656 | tf_op jit(solution)/shard_map/ppermute | solution.py:23
  83.3 18.1 %collective-permute-start.19 = (bf16[400,512]{1,0:T(8,128)(2,1)S(1)}, bf16[400,512]{1,0:T(8,128)(2,1)S(1)}, u32[]{:S(2)}, u32[]{:S(2)}) collective-permute-start(bf16[400,512]{1,0:T(8,128)(2,1)S(1)} %collective-permute-done.1.refs_4_), channel_id=1, source_target_pairs={{0,2},{1,3},{2,0},{3,1},{4,6},{5,7},{6,4},{7,5},{8,10},{9,11},{10,... | collective-permute-start | bytes 1228808 | tf_op jit(solution)/shard_map/ppermute | solution.py:23
  83.7 15.4 %copy-start.22 = (f32[3,128,512]{2,1,0:T(8,128)S(1)}, f32[3,128,512]{2,1,0:T(8,128)}, u32[]{:S(2)}) copy-start(f32[3,128,512]{2,1,0:T(8,128)} %get-tuple-element.78) | copy-start | bytes 2359300
  84.4 17.6 %collective-permute-start.18 = (bf16[400,512]{1,0:T(8,128)(2,1)S(1)}, bf16[400,512]{1,0:T(8,128)(2,1)S(1)}, u32[]{:S(2)}, u32[]{:S(2)}) collective-permute-start(bf16[400,512]{1,0:T(8,128)(2,1)S(1)} %collective-permute-done.1.refs_4_), channel_id=1, source_target_pairs={{0,1},{1,0},{2,3},{3,2},{4,5},{5,4},{6,7},{7,6},{8,9},{9,8},{10,11... | collective-permute-start | bytes 1228808 | tf_op jit(solution)/shard_map/ppermute | solution.py:23
  96.3 8.0 %collective-permute-start.22 = (bf16[400,512]{1,0:T(8,128)(2,1)S(1)}, bf16[400,512]{1,0:T(8,128)(2,1)S(1)}, u32[]{:S(2)}, u32[]{:S(2)}) collective-permute-start(bf16[400,512]{1,0:T(8,128)(2,1)S(1)} %copy-done.12), channel_id=1, source_target_pairs={{0,2},{1,3},{2,0},{3,1},{4,6},{5,7},{6,4},{7,5},{8,10},{9,11},{10,... | collective-permute-start | bytes 1228808 | tf_op jit(solution)/shard_map/ppermute | solution.py:23
  99.4 11.9 %collective-permute-start.17 = (bf16[3,128,512]{2,1,0:T(8,128)(2,1)S(1)}, bf16[3,128,512]{2,1,0:T(8,128)(2,1)S(1)}, u32[]{:S(2)}, u32[]{:S(2)}) collective-permute-start(bf16[3,128,512]{2,1,0:T(8,128)(2,1)S(1)} %get-tuple-element.91), channel_id=1, source_target_pairs={{0,8},{2,10},{5,13},{7,15},{8,0},{10,2},{13,5},{15,7},{16,24},{18,... | collective-permute-start | bytes 1179656 | tf_op jit(solution)/shard_map/ppermute | solution.py:23
  101.3 11.3 %collective-permute-start.21 = (bf16[400,512]{1,0:T(8,128)(2,1)S(1)}, bf16[400,512]{1,0:T(8,128)(2,1)S(1)}, u32[]{:S(2)}, u32[]{:S(2)}) collective-permute-start(bf16[400,512]{1,0:T(8,128)(2,1)S(1)} %copy-done.12), channel_id=1, source_target_pairs={{0,1},{1,0},{2,3},{3,2},{4,5},{5,4},{6,7},{7,6},{8,9},{9,8},{10,11... | collective-permute-start | bytes 1228808 | tf_op jit(solution)/shard_map/ppermute | solution.py:23
  101.4 13.7 %collective-permute-start.20 = (bf16[400,512]{1,0:T(8,128)(2,1)S(1)}, bf16[400,512]{1,0:T(8,128)(2,1)S(1)}, u32[]{:S(2)}, u32[]{:S(2)}) collective-permute-start(bf16[400,512]{1,0:T(8,128)(2,1)S(1)} %collective-permute-done.19.refs_6_), channel_id=1, source_target_pairs={{0,1},{1,0},{2,3},{3,2},{4,5},{5,4},{6,7},{7,6},{8,9},{9,8},{10,11... | collective-permute-start | bytes 1228808 | tf_op jit(solution)/shard_map/ppermute | solution.py:23
  101.9 16.6 %collective-permute-start.25 = (bf16[400,512]{1,0:T(8,128)(2,1)S(1)}, bf16[400,512]{1,0:T(8,128)(2,1)S(1)}, u32[]{:S(2)}, u32[]{:S(2)}) collective-permute-start(bf16[400,512]{1,0:T(8,128)(2,1)S(1)} %collective-permute-done.13.refs_12_), channel_id=1, source_target_pairs={{0,2},{1,3},{2,0},{3,1},{4,6},{5,7},{6,4},{7,5},{8,10},{9,11},{10,... | collective-permute-start | bytes 1228808 | tf_op jit(solution)/shard_map/ppermute | solution.py:23
  104.3 14.3 %collective-permute-start.24 = (bf16[400,512]{1,0:T(8,128)(2,1)S(1)}, bf16[400,512]{1,0:T(8,128)(2,1)S(1)}, u32[]{:S(2)}, u32[]{:S(2)}) collective-permute-start(bf16[400,512]{1,0:T(8,128)(2,1)S(1)} %collective-permute-done.13.refs_12_), channel_id=1, source_target_pairs={{0,1},{1,0},{2,3},{3,2},{4,5},{5,4},{6,7},{7,6},{8,9},{9,8},{10,11... | collective-permute-start | bytes 1228808 | tf_op jit(solution)/shard_map/ppermute | solution.py:23
  111.3 9.7 %collective-permute-start.23 = (bf16[400,512]{1,0:T(8,128)(2,1)S(1)}, bf16[400,512]{1,0:T(8,128)(2,1)S(1)}, u32[]{:S(2)}, u32[]{:S(2)}) collective-permute-start(bf16[400,512]{1,0:T(8,128)(2,1)S(1)} %collective-permute-done.22.refs_10_), channel_id=1, source_target_pairs={{0,1},{1,0},{2,3},{3,2},{4,5},{5,4},{6,7},{7,6},{8,9},{9,8},{10,11... | collective-permute-start | bytes 1228808 | tf_op jit(solution)/shard_map/ppermute | solution.py:23
  112.7 9.7 %collective-permute-start.27 = (bf16[3,128,512]{2,1,0:T(8,128)(2,1)S(1)}, bf16[3,128,512]{2,1,0:T(8,128)(2,1)S(1)}, u32[]{:S(2)}, u32[]{:S(2)}) collective-permute-start(bf16[3,128,512]{2,1,0:T(8,128)(2,1)S(1)} %renew.2.refs_0_), channel_id=1, source_target_pairs={{0,2},{2,0},{5,7},{7,5},{8,10},{10,8},{13,15},{15,13},{16,18},{18,... | collective-permute-start | bytes 1179656 | tf_op jit(solution)/shard_map/ppermute | solution.py:23
  115.2 11.4 %collective-permute-start.28 = (bf16[3,128,512]{2,1,0:T(8,128)(2,1)S(1)}, bf16[3,128,512]{2,1,0:T(8,128)(2,1)S(1)}, u32[]{:S(2)}, u32[]{:S(2)}) collective-permute-start(bf16[3,128,512]{2,1,0:T(8,128)(2,1)S(1)} %renew.3.refs_1_), channel_id=1, source_target_pairs={{0,2},{2,0},{5,7},{7,5},{8,10},{10,8},{13,15},{15,13},{16,18},{18,... | collective-permute-start | bytes 1179656 | tf_op jit(solution)/shard_map/ppermute | solution.py:23
  118.5 9.3 %collective-permute-start.26 = (bf16[400,512]{1,0:T(8,128)(2,1)S(1)}, bf16[400,512]{1,0:T(8,128)(2,1)S(1)}, u32[]{:S(2)}, u32[]{:S(2)}) collective-permute-start(bf16[400,512]{1,0:T(8,128)(2,1)S(1)} %collective-permute-done.25.refs_14_), channel_id=1, source_target_pairs={{0,1},{1,0},{2,3},{3,2},{4,5},{5,4},{6,7},{7,6},{8,9},{9,8},{10,11... | collective-permute-start | bytes 1228808 | tf_op jit(solution)/shard_map/ppermute | solution.py:23
  118.6 16.2 %collective-permute-start.29 = (bf16[3,128,512]{2,1,0:T(8,128)(2,1)S(1)}, bf16[3,128,512]{2,1,0:T(8,128)(2,1)S(1)}, u32[]{:S(2)}, u32[]{:S(2)}) collective-permute-start(bf16[3,128,512]{2,1,0:T(8,128)(2,1)S(1)} %renew.2.refs_0_), channel_id=1, source_target_pairs={{0,1},{2,3},{5,4},{7,6},{8,9},{10,11},{13,12},{15,14},{16,17},{18,... | collective-permute-start | bytes 1179656 | tf_op jit(solution)/shard_map/ppermute | solution.py:23
  121.1 13.8 %collective-permute-start.30 = (bf16[3,128,512]{2,1,0:T(8,128)(2,1)S(1)}, bf16[3,128,512]{2,1,0:T(8,128)(2,1)S(1)}, u32[]{:S(2)}, u32[]{:S(2)}) collective-permute-start(bf16[3,128,512]{2,1,0:T(8,128)(2,1)S(1)} %renew.3.refs_1_), channel_id=1, source_target_pairs={{0,1},{2,3},{5,4},{7,6},{8,9},{10,11},{13,12},{15,14},{16,17},{18,... | collective-permute-start | bytes 1179656 | tf_op jit(solution)/shard_map/ppermute | solution.py:23
  122.4 12.5 %collective-permute-start.31 = (bf16[3,128,512]{2,1,0:T(8,128)(2,1)S(1)}, bf16[3,128,512]{2,1,0:T(8,128)(2,1)S(1)}, u32[]{:S(2)}, u32[]{:S(2)}) collective-permute-start(bf16[3,128,512]{2,1,0:T(8,128)(2,1)S(1)} %collective-permute-done.27.refs_2_), channel_id=1, source_target_pairs={{0,1},{2,3},{5,4},{7,6},{8,9},{10,11},{13,12},{15,14},{16,17},{18,... | collective-permute-start | bytes 1179656 | tf_op jit(solution)/shard_map/ppermute | solution.py:23
  126.5 8.3 %collective-permute-start.32 = (bf16[3,128,512]{2,1,0:T(8,128)(2,1)S(1)}, bf16[3,128,512]{2,1,0:T(8,128)(2,1)S(1)}, u32[]{:S(2)}, u32[]{:S(2)}) collective-permute-start(bf16[3,128,512]{2,1,0:T(8,128)(2,1)S(1)} %collective-permute-done.28.refs_3_), channel_id=1, source_target_pairs={{0,1},{2,3},{5,4},{7,6},{8,9},{10,11},{13,12},{15,14},{16,17},{18,... | collective-permute-start | bytes 1179656 | tf_op jit(solution)/shard_map/ppermute | solution.py:23
  137.1 5.5 %collective-permute-start.33 = (bf16[128,512]{1,0:T(8,128)(2,1)S(1)}, bf16[128,512]{1,0:T(8,128)(2,1)S(1)}, u32[]{:S(2)}, u32[]{:S(2)}) collective-permute-start(bf16[128,512]{1,0:T(8,128)(2,1)S(1)} %get-tuple-element.84), channel_id=1, source_target_pairs={{0,4},{1,5},{2,6},{3,7},{4,0},{5,1},{6,2},{7,3},{8,12},{9,13},{10,... | collective-permute-start | bytes 393224 | tf_op jit(solution)/shard_map/ppermute | solution.py:23
  137.2 12.3 %collective-permute-start.34 = (bf16[128,512]{1,0:T(8,128)(2,1)S(1)}, bf16[128,512]{1,0:T(8,128)(2,1)S(1)}, u32[]{:S(2)}, u32[]{:S(2)}) collective-permute-start(bf16[128,512]{1,0:T(8,128)(2,1)S(1)} %get-tuple-element.85), channel_id=1, source_target_pairs={{0,8},{1,9},{2,10},{3,11},{4,12},{5,13},{6,14},{7,15},{8,0},{9,1},... | collective-permute-start | bytes 393224 | tf_op jit(solution)/shard_map/ppermute | solution.py:23
  137.2 12.2 %collective-permute-start.35 = (bf16[128,512]{1,0:T(8,128)(2,1)S(1)}, bf16[128,512]{1,0:T(8,128)(2,1)S(1)}, u32[]{:S(2)}, u32[]{:S(2)}) collective-permute-start(bf16[128,512]{1,0:T(8,128)(2,1)S(1)} %get-tuple-element.86), channel_id=1, source_target_pairs={{0,12},{1,13},{2,14},{3,15},{4,8},{5,9},{6,10},{7,11},{8,4},{9,5},... | collective-permute-start | bytes 393224 | tf_op jit(solution)/shard_map/ppermute | solution.py:23

commit v4 on v3

--- a/solution.py
+++ b/solution.py
@@ -14,7 +14,7 @@
 bf16 = jnp.bfloat16
 i32 = jnp.int32
 TAG_ROWS = 16
-VMEM_LIMIT = 24 * 1024 * 1024
+MIB = 1024 * 1024
 
 
 def swap(value, mask, senders=None):
@@ -36,7 +36,7 @@
     return pl.BlockSpec(shape, lambda *_: (0,) * len(shape))
 
 
-def call(body, name, scalars, inputs, specs, outs, grid=(1,), out_specs=None, scratch=()):
+def call(body, name, scalars, inputs, specs, outs, grid=(1,), out_specs=None, scratch=(), vmem=8):
     return pl.pallas_call(
         body,
         name=name,
@@ -49,7 +49,7 @@
         ),
         out_shape=list(outs),
         cost_estimate=pl.CostEstimate(flops=0, bytes_accessed=0, transcendentals=0),
-        compiler_params=pltpu.CompilerParams(vmem_limit_bytes=VMEM_LIMIT),
+        compiler_params=pltpu.CompilerParams(vmem_limit_bytes=vmem * MIB),
     )(scalars, *inputs)
 
 
@@ -59,75 +59,88 @@
     return -jnp.transpose(jnp.broadcast_to(row, (8, row.shape[1])))[:, 0:1]
 
 
-def pack_update_body(lane, half, where, rates, mask, keys, values, out, rows_s, tg_s, in_sem, out_sem):
-    rows, width = rows_s.shape[1:]
-    head = (1 - where[1]) * half + lane
-    cols = pl.ds(pl.multiple_of(head * width, width), width)
+def pack_body(heads, where, rates, mask, views, keys, values, *refs):
+    half = heads // 2
+    target, refs = refs[:3], refs[3:]
+    packed, sent = refs[:half], refs[half : half + heads]
+    value_s, pack_s, sent_s, in_sem, target_sem, out_sem = refs[half + heads :]
+    rows, width = value_s.shape[1:]
+    count = target[0].shape[0]
+
+    def columns(head):
+        return pl.ds(pl.multiple_of(head * width, width), width)
+
     loads = []
-    for i, source in ((1, values), (0, keys)):
-        loads.append(pltpu.make_async_copy(source.at[:, cols], rows_s.at[i], in_sem.at[i]))
-        loads[-1].start()
-    rate = rate_column(rates[...], mask[...], head)
-    loads[0].wait()
-    tg_s[...] = (rate * rows_s[1].astype(f32)).astype(bf16)
-    stores = [pltpu.make_async_copy(tg_s, out.at[1], out_sem.at[1])]
-    stores[0].start()
-    loads[1].wait()
-    stores.append(pltpu.make_async_copy(rows_s.at[0], out.at[0], out_sem.at[0]))
-    stores[1].start()
+    for j in range(half):
+        head = (1 - where[1]) * half + j
+        for i, to in ((1, value_s.at[j]), (0, pack_s.at[j, 0])):
+            source = (keys, values)[i]
+            loads.append(pltpu.make_async_copy(source.at[:, columns(head)], to, in_sem.at[j, i]))
+            loads[-1].start()
+    rows_in = []
+    for step in range(heads):
+        head = head_of(where[0] ^ step, heads)
+        for i in range(3):
+            to = sent_s.at[step, pl.ds(i * count, count)]
+            rows_in.append(
+                pltpu.make_async_copy(
+                    target[i].at[:, columns(head)], to, target_sem.at[step, i]
+                )
+            )
+            rows_in[-1].start()
+    row_at = lax.broadcasted_iota(i32, (TAG_ROWS, count), 0)
+    digits = jnp.where(
+        row_at == 0, views[...] // 256, jnp.where(row_at == 1, views[...] % 256, 0)
+    )
+    for step in range(heads):
+        sent_s[step, pl.ds(3 * count, TAG_ROWS), :] = jnp.zeros((TAG_ROWS, width), bf16)
+        sent_s[step, pl.ds(3 * count, TAG_ROWS), pl.ds(0, count)] = digits.astype(f32).astype(bf16)
+    stores = []
+    for j in range(half):
+        rate = rate_column(rates[...], mask[...], (1 - where[1]) * half + j)
+        loads[2 * j].wait()
+        pack_s[j, 1] = (rate * value_s[j].astype(f32)).astype(bf16)
+        loads[2 * j + 1].wait()
+        stores.append(pltpu.make_async_copy(pack_s.at[j], packed[j], out_sem.at[j]))
+        stores[-1].start()
+    for step in range(heads):
+        for i in range(3):
+            rows_in[3 * step + i].wait()
+        stores.append(pltpu.make_async_copy(sent_s.at[step], sent[step], out_sem.at[half + step]))
+        stores[-1].start()
     for store in stores:
         store.wait()
 
 
-def pack_update(where, rates, mask, keys, values, lane, half, width):
-    rows = keys.shape[0]
-    return call(
-        functools.partial(pack_update_body, lane, half),
-        "pack_update_%d" % lane,
-        where,
-        (rates, mask, keys, values),
-        [whole(rates.shape), whole(mask.shape)] + [pl.BlockSpec(memory_space=pltpu.HBM)] * 2,
-        [jax.ShapeDtypeStruct((2, rows, width), bf16)],
-        out_specs=[pl.BlockSpec(memory_space=pl.ANY)],
+def pack(where, rates, mask, views, keys, values, target, heads, width):
+    half, rows, count = heads // 2, keys.shape[0], views.shape[1]
+    small = (rates, mask, views)
+    anywhere = pl.BlockSpec(memory_space=pl.ANY)
+    piece = (3 * count + TAG_ROWS, width)
+    outs = call(
+        functools.partial(pack_body, heads),
+        "pack",
+        where,
+        (*small, keys, values, *target),
+        [whole(x.shape) for x in small] + [anywhere] * 5,
+        [jax.ShapeDtypeStruct((2, rows, width), bf16)] * half
+        + [jax.ShapeDtypeStruct(piece, bf16)] * heads,
+        out_specs=[anywhere] * (half + heads),
         scratch=[
-            pltpu.VMEM((2, rows, width), bf16),
-            pltpu.VMEM((rows, width), bf16),
-            pltpu.SemaphoreType.DMA((2,)),
-            pltpu.SemaphoreType.DMA((2,)),
+            pltpu.VMEM((half, rows, width), bf16),
+            pltpu.VMEM((half, 2, rows, width), bf16),
+            pltpu.VMEM((heads, *piece), bf16),
+            pltpu.SemaphoreType.DMA((half, 2)),
+            pltpu.SemaphoreType.DMA((heads, 3)),
+            pltpu.SemaphoreType.DMA((half + heads,)),
         ],
-    )[0]
-
-
-def pack_target_body(heads, width, where, queries, keys, values, views, *outs):
-    rows = queries.shape[0]
-    for step in range(heads):
-        head = head_of(where[0] ^ step, heads)
-        cols = pl.ds(pl.multiple_of(head * width, width), width)
-        for i, source in enumerate((queries, keys, values)):
-            outs[step][pl.ds(i * rows, rows), :] = source[:, cols]
-        outs[step][pl.ds(3 * rows, TAG_ROWS), :] = jnp.zeros((TAG_ROWS, width), bf16)
-        high, low = views[...] // 256, views[...] % 256
-        row_at = lax.broadcasted_iota(i32, (TAG_ROWS, rows), 0)
-        digits = jnp.where(row_at == 0, high, jnp.where(row_at == 1, low, 0))
-        outs[step][pl.ds(3 * rows, TAG_ROWS), pl.ds(0, rows)] = digits.astype(f32).astype(bf16)
-
-
-def pack_target(where, queries, keys, values, views, heads, width):
-    rows = queries.shape[0]
-    out = jax.ShapeDtypeStruct((3 * rows + TAG_ROWS, width), bf16)
-    inputs = (queries, keys, values, views)
-    return call(
-        functools.partial(pack_target_body, heads, width),
-        "pack_target",
-        where,
-        inputs,
-        [whole(x.shape) for x in inputs],
-        [out] * heads,
-    )
+        vmem=62,
+    )
+    return outs[:half], outs[half:]
 
 
 def head_grad_body(
-    lane, half, cut, where, rates, mask, keys, values, other, weights, *refs
+    lane, half, where, rates, mask, keys, values, other, weights, *refs
 ):
     sends, keeps = refs[:2], refs[2:4]
     k_s, v_s, w_s, tg_s, hidden_s, gate_s, up_s, full, send_s, keep_s, in_sem, out_sem = refs[4:]
@@ -184,45 +197,28 @@
             left[...], right[...], (((0,), (0,)), ((), ())), preferred_element_type=f32
         )
         for g in range(2):
-            for side in range(2):
-                at = pl.ds((2 * side + g) * quarter, quarter)
-                if cut:
-                    rows_at = pl.ds(
-                        pl.multiple_of(((bit + 1 - side) % 2) * 2 * quarter + g * quarter, quarter),
-                        quarter,
-                    )
-                    if side == 0:
-                        send_s[g, i] = full[rows_at, :].astype(bf16)
-                    else:
-                        keep_s[g, i] = full[rows_at, :]
-                else:
-                    half_at = pl.ds(side * quarter, quarter)
-                    send_s[g, i, half_at] = full[at, :].astype(bf16)
-                    keep_s[g, i, half_at] = full[at, :]
+            kept = pl.ds(pl.multiple_of(bit * 2 * quarter + g * quarter, quarter), quarter)
+            sent = pl.ds(pl.multiple_of((1 - bit) * 2 * quarter + g * quarter, quarter), quarter)
+            send_s[g, i] = full[sent, :].astype(bf16)
+            keep_s[g, i] = full[kept, :]
             stores += [
-                (pltpu.make_async_copy(send_s.at[g, i], sends[g].at[i], out_sem.at[0, g, i]), 0),
-                (pltpu.make_async_copy(keep_s.at[g, i], keeps[g].at[i], out_sem.at[1, g, i]), 1),
+                pltpu.make_async_copy(send_s.at[g, i], sends[g].at[i], out_sem.at[0, g, i]),
+                pltpu.make_async_copy(keep_s.at[g, i], keeps[g].at[i], out_sem.at[1, g, i]),
             ]
-            for store, when in stores[-2:]:
-                if cut:
-                    store.start()
-                else:
-                    pl.when(where[8] == when)(store.start)
-    for store, when in stores:
-        if cut:
-            store.wait()
-        else:
-            pl.when(where[8] == when)(store.wait)
-
-
-def head_grad(where, rates, mask, keys, values, other, weights, lane, half, width, cut):
+            stores[-2].start()
+            stores[-1].start()
+    for store in stores:
+        store.wait()
+
+
+def head_grad(where, rates, mask, keys, values, other, weights, lane, half, width):
     rows = keys.shape[0]
-    shape = (3, width // 4 if cut else width // 2, width)
+    shape = (3, width // 4, width)
     anywhere = pl.BlockSpec(memory_space=pl.ANY)
     in_hbm = pl.BlockSpec(memory_space=pltpu.HBM)
     both = pltpu.VMEM((2 * rows, width), bf16)
     outs = call(
-        functools.partial(head_grad_body, lane, half, cut),
+        functools.partial(head_grad_body, lane, half),
         "head_grad_%d" % lane,
         where,
         (rates, mask, keys, values, other, weights),
@@ -243,12 +239,16 @@
             pltpu.SemaphoreType.DMA((7,)),
             pltpu.SemaphoreType.DMA((2, 2, 3)),
         ],
+        vmem=62,
     )
     return outs[:2], outs[2:]
 
 
-def arrange_body(span, where, *refs):
-    pieces, out = refs[:-1], refs[-1]
+def arrange_body(slots, span, where, *refs):
+    out = refs[-1]
+    pieces = []
+    for n, at in slots:
+        pieces.append(refs[n] if at is None else refs[n].at[at])
     me, inner = where[3], where[4]
     rows = (pieces[0].shape[0] - TAG_ROWS) // 3
     count = len(pieces)
@@ -292,14 +292,15 @@
         out[i] = totals[i].astype(bf16)
 
 
-def arrange(where, pieces, span, heads, width):
+def arrange(where, pieces, slots, span, heads, width):
     return call(
-        functools.partial(arrange_body, span),
+        functools.partial(arrange_body, slots, span),
         "arrange",
         where,
         tuple(pieces),
         [whole(x.shape) for x in pieces],
         [jax.ShapeDtypeStruct((3, heads * VIEW_ROWS, width), bf16)],
+        vmem=20,
     )[0]
 
 
@@ -331,24 +332,16 @@
     total = keep[...] + got[...].astype(f32)
     scale = lax.rsqrt(jnp.mean(total * total, axis=-1, keepdims=True) + epsilon)
     step = steps[where[5]]
-    fresh[...] = (old[0].astype(f32) - step * (total * scale)).astype(bf16)
-
-
-def renew(where, keep, got, weights, steps, group, groups):
-    parts, rows, width = keep.shape
+    fresh[...] = (old[...].astype(f32) - step * (total * scale)).astype(bf16)
+
+
+def renew(where, keep, got, old, steps):
     return call(
         renew_body,
         "renew",
         where,
-        (keep, got, weights, steps),
-        [
-            whole(keep.shape),
-            whole(got.shape),
-            pl.BlockSpec(
-                (1, parts, rows, width), lambda i, w: (w[5], 0, w[6 + group], 0)
-            ),
-            pl.BlockSpec(memory_space=pltpu.SMEM),
-        ],
+        (keep, got, old, steps),
+        [whole(keep.shape)] * 3 + [pl.BlockSpec(memory_space=pltpu.SMEM)],
         [jax.ShapeDtypeStruct(keep.shape, bf16)],
     )[0]
 
@@ -398,6 +391,7 @@
         + [whole(x.shape) for x in inputs[1:]],
         [jax.ShapeDtypeStruct((VIEW_ROWS, width), bf16)] * heads,
         scratch=[pltpu.VMEM((3, width, width), bf16)],
+        vmem=12,
     )
 
 
@@ -456,100 +450,116 @@
 
     turn = where
 
-    others = []
-    for j in range(half):
-        packed = pack_update(turn, rates, mask, update_keys, update_values, j, half, width)
-        turn = after(turn, packed)
-        others.append(swap(packed, 1))
-        if j == 0:
-            sent = pack_target(
-                turn, target_queries, target_keys, target_values, target_views[None, :], heads, width
-            )
-            turn = after(turn, sent[0])
-
-    group = {0: sent[0]}
-    came = {step: swap(sent[step], step * span) for step in (1, 2)}
-
-    def spread(step, bits):
+    others, sent = pack(
+        turn,
+        rates,
+        mask,
+        target_views[None, :],
+        update_keys,
+        update_values,
+        (target_queries, target_keys, target_values),
+        heads,
+        width,
+    )
+    turn = after(turn, sent[0])
+    others = [swap(x, 1) for x in others]
+
+    outer_bits = list(reversed(inner_bits))
+
+    def spread(parts, bits):
         for b in bits:
-            for n, x in list(group.items()):
-                if n // span == step:
-                    group[n | (1 << b)] = swap(x, 1 << b)
-
-    outer_bits = list(reversed(inner_bits))
-    spread(0, outer_bits)
+            parts.update({n | (1 << b): swap(x, 1 << b) for n, x in list(parts.items())})
+
+    early = {0: sent[0]}
+    spread(early, outer_bits)
+    came = [swap(sent[step], step * span) for step in (1, 2)]
 
     sends, keeps = head_grad(
-        turn, rates, mask, update_keys, update_values, others[0], fast_weights, 0, half, width, True
-    )
-    moved = [swap(x, 2) for x in sends]
-    turn = after(turn, sends[0], came[1], *group.values())
-    spread(0, [0])
-    group[span] = came[1]
-    whole_sends, whole_keeps = head_grad(
-        turn, rates, mask, update_keys, update_values, others[1], fast_weights, 1, half, width, False
-    )
-    crossed = [swap(x, span, lambda t: not matched(t)) for x in whole_sends]
-    turn = after(turn, whole_sends[0])
-
-    def narrow(total, bits, senders=None):
-        for b in bits:
-            rows = total.shape[1] // 2
-            send = lax.dynamic_slice_in_dim(total, (1 - bit_of(b)) * rows, rows, 1)
-            keep = lax.dynamic_slice_in_dim(total, bit_of(b) * rows, rows, 1)
-            total = keep + swap(send.astype(bf16), 1 << b, senders).astype(f32)
-        return total
-
-    low = []
+        turn, rates, mask, update_keys, update_values, others[0], fast_weights, 0, half, width
+    )
+    moved = [swap(sends[0], 2)]
+    turn = after(turn, sends[0], *early.values())
+    spread(early, [0])
+    more_sends, more_keeps = head_grad(
+        turn, rates, mask, update_keys, update_values, others[1], fast_weights, 1, half, width
+    )
+    turn = after(turn, more_sends[0], *came)
+    keeps = [*keeps, *more_keeps]
+    moved.append(swap(after(sends[1], more_sends[0]), 2))
+    moved.append(swap(after(more_sends[0], turn), 2))
+    came.append(swap(after(sent[3], turn), 3 * span))
+
+    def cut(pair, b, side):
+        rows = pair[0].shape[1] // 2
+        return sum(
+            lax.dynamic_slice_in_dim(x, side * rows, rows, 1).astype(f32) for x in pair
+        )
+
+    sums = []
+
+    def settle(n):
+        keep, got = keeps[n], after(moved[n], turn)
+        for b in inner_bits[1:]:
+            send = cut((keep, got), b, 1 - bit_of(b)).astype(bf16)
+            keep, got = cut((keep, got), b, bit_of(b)), swap(send, 1 << b)
+        total = keep + got.astype(f32)
+        send = total.astype(bf16)
+        sums.append((total, swap(send, span, lambda t: not matched(t))))
+        return after(turn, send)
+
+    turn = settle(0)
+    turn = settle(1)
+    moved.append(swap(after(more_sends[1], turn), 2))
+    turn = after(turn, came[2], sums[0][1])
+    turn = settle(2)
+    turn = after(turn, sums[1][1])
+    turn = settle(3)
+    late = {0: jnp.stack([after(x, turn) for x in came])}
+    spread(late, outer_bits)
+
+    olds = [
+        lax.dynamic_slice(
+            fast_weights, (where[5], 0, where[6 + g] * share, 0), (1, 3, share, width)
+        )[0]
+        for g in range(2)
+    ]
+    upper = plane // 2 == 1
+    held = []
     for g in range(2):
-        total = after(keeps[g], turn) + moved[g].astype(f32)
-        total = narrow(total, inner_bits[1:])
-        low.append((total, swap(total.astype(bf16), span, lambda t: not matched(t))))
-        turn = after(turn, total)
-        if g == 0:
-            turn = after(turn, came[2])
-            group[2 * span] = came[2]
-            came[3] = swap(after(sent[3], turn), 3 * span)
-    group[span] = after(group[span], turn)
-    spread(1, outer_bits)
-    high = []
-    for g in range(2):
-        total = after(whole_keeps[g], turn) + crossed[g].astype(f32)
-        turn = after(turn, total)
-        high.append(narrow(total, inner_bits, matched))
-    group[2 * span] = after(group[2 * span], turn)
-    spread(2, outer_bits)
-    turn = after(turn, *[x for n, x in group.items() if n // span == 0])
-
-    fresh = []
-    upper = plane // 2 == 1
-    for g in range(2):
-        mine_low = after(low[g][0], turn) + low[g][1].astype(f32)
-        keep = jnp.where(upper, high[g], mine_low)
-        got = swap(jnp.where(upper, mine_low, high[g]).astype(bf16), 2 * span, matched)
-        turn = after(turn, keep)
-        if g == 0:
-            turn = after(turn, came[3])
-            group[3 * span] = came[3]
-            spread(3, outer_bits)
-            spread(1, [0])
-        new = renew(turn, keep, got, fast_weights, step_sizes, g, 2)
+        low, high = (after(sums[n][0], turn) + sums[n][1].astype(f32) for n in (g, 2 + g))
+        keep = jnp.where(upper, high, low)
+        send = jnp.where(upper, low, high).astype(bf16)
+        held.append((keep, swap(send, 2 * span, matched)))
+        turn = after(turn, send)
+    turn = after(turn, *early.values())
+    fresh, far = [], []
+    for g, (keep, got) in enumerate(held):
+        new = renew(turn, keep, got, olds[g], step_sizes)
         turn = after(turn, new)
         for b in reversed(inner_bits[1:]):
-            far = swap(new, 1 << b, matched)
+            other = swap(new, 1 << b, matched)
             new = jnp.where(
                 bit_of(b) == 1,
-                jnp.concatenate([far, new], axis=1),
-                jnp.concatenate([new, far], axis=1),
+                jnp.concatenate([other, new], axis=1),
+                jnp.concatenate([new, other], axis=1),
             )
         fresh.append(new)
-    spread(2, [0])
-    spread(3, [0])
-    far = [swap(x, 2, matched) for x in fresh]
-    near = [swap(x, 1, matched) for x in fresh] + [swap(x, 1, matched) for x in far]
-
-    rows = arrange(turn, [group[n] for n in sorted(group)], span, heads, width)
+        far.append(swap(new, 2, matched))
+    late = {n: x if n == 0 else after(x, turn) for n, x in late.items()}
+    spread(late, [0])
+
+    pieces, slots = [], {}
+    for e in sorted(early):
+        slots[e] = (len(pieces), None)
+        pieces.append(early[e])
+        for step in range(1, heads):
+            slots[step * span + e] = (len(pieces), step - 1)
+        pieces.append(late[e])
+    slots = [slots[n] for n in range(count)]
+    rows = arrange(turn, pieces, slots, span, heads, width)
     attended = attend(turn, rows)
+    far = [after(x, attended) for x in far]
+    near = [swap(x, 1, matched) for x in fresh + far]
     blocks = finish(where, rows, attended, fresh + far + near, heads)
     got = [swap(x, step * span) if step else x for step, x in enumerate(blocks)]
     return join(where, got, heads, width)

time: 152 us -> 130 us (0.86)
  waiting for transfers between devices: 53.3 us -> 35.2 us
  local copies, waits for them, and re-layouts: 10.1 us -> 2.96 us
  Pallas kernels: 30.3 us -> 36.3 us
  starting transfers between devices: 47.1 us -> 44.2 us
    ppermute x36 -> x30, waiting for transfers between devices: 53.3 us -> 35.2 us  [swap(): return lax.ppermute(value, AXIS, pairs)]
    unnamed x54 -> x28, local copies, waits for them, and re-layouts: 9.14 us -> 1.1 us
    pallas_call x11 -> x9, Pallas kernels: 30.3 us -> 36.3 us  [call(): pl.pallas_call(body, name=name, grid_spec=pltpu.PrefetchScalarGridSpec(nu...]
    select_n x0 -> x2, other arithmetic: none -> 4.53 us  [on_device(): keep = jnp.where(upper, high, low)]
    add x2 -> x0, other arithmetic: 3.44 us -> none  [on_device(): total = after(whole_keeps[g], turn) + crossed[g].astype(f32)]
    ppermute x36 -> x30, starting transfers between devices: 47.1 us -> 44.2 us  [swap(): return lax.ppermute(value, AXIS, pairs)]
    convert_element_type x4, other arithmetic: 6 us -> 4.45 us  [settle(): send = total.astype(bf16)]
  transfers between devices with their start and end apart: 36 -> 30, of which waited for: 12 -> 11; matrix products, arithmetic and copies ran while one was open for 7% -> 9% of each run, Pallas kernels for 17% -> 21%
where the time goes in v4:
time: 130 us; the launch traced here: 129 us
  starting transfers between devices  44.2 us (34%)
  Pallas kernels  36.3 us (28%)
  waiting for transfers between devices  35.2 us (27%)
  other arithmetic  10.3 us (8%)
  local copies, waits for them, and re-layouts  2.96 us (2%)
    ppermute x30, starting transfers between devices, swap(): return lax.ppermute(value, AXIS, pairs)  44.2 us
    pallas_call x9, Pallas kernels, call(): pl.pallas_call(body, name=name, grid_spec=pltpu.PrefetchScalarGridSpec(nu...  36.3 us
    ppermute x30, waiting for transfers between devices, swap(): return lax.ppermute(value, AXIS, pairs)  35.2 us
    select_n x2, other arithmetic, on_device(): keep = jnp.where(upper, high, low)  4.53 us
    convert_element_type x4, other arithmetic, settle(): send = total.astype(bf16)  4.45 us
  transfers between devices with their start and end apart: 30, of which 11 were waited for; matrix products, arithmetic and copies ran while one was open for 9% of the time, Pallas kernels for 21%

profile of v4, /device:TPU:0, one launch (start us, length us, event | category | flops | bytes accessed | tf_op | source)
XLA Modules:
  0.0 129.3 jit_solution(1813121825862367287)
XLA Ops:
  0.0 0.7 stack.55.where
  0.7 5.2 %pack.1 = (bf16[2,512,512]{2,1,0:T(8,128)(2,1)}, bf16[2,512,512]{2,1,0:T(8,128)(2,1)}, bf16[400,512]{1,0:T(8,128)(2,1)}, bf16[400,512]{1,0:T(8,128)(2,1)}, bf16[...) custom-call(s32[9]{0:T(128)} %stack.55.where, f32[4,512]{1,0:T(4,128)} %bitcast.20, s32[1,512]{1,0:T(1,128)} %bitcast.23, ...), custom_call_target="tpu_custom_call" | custom-call | tf_op jit(solution)/shard_map/pack/pallas_call | solution.py:40
  5.9 0.5 collective-permute-start
  6.4 0.1 collective-permute-start.2
  6.5 2.9 %collective-permute-start.1 = (bf16[400,512]{1,0:T(8,128)(2,1)}, bf16[400,512]{1,0:T(8,128)(2,1)}, u32[]{:S(2)}, u32[]{:S(2)}) collective-permute-start(bf16[400,512]{1,0:T(8,128)(2,1)} %get-tuple-element.55.refs_0_), channel_id=1, source_target_pairs={{0,2},{1,3},{2,0},{3,1},{4,6},{5,7},{6,4},{7,5},{8,10},{9,11},{10,... | collective-permute-start | bytes 1228808 | tf_op jit(solution)/shard_map/ppermute | solution.py:23
  9.4 1.6 %collective-permute-start.3 = (bf16[400,512]{1,0:T(8,128)(2,1)}, bf16[400,512]{1,0:T(8,128)(2,1)}, u32[]{:S(2)}, u32[]{:S(2)}) collective-permute-start(bf16[400,512]{1,0:T(8,128)(2,1)} %get-tuple-element.62), channel_id=1, source_target_pairs={{0,4},{1,5},{2,6},{3,7},{4,0},{5,1},{6,2},{7,3},{8,12},{9,13},{10,... | collective-permute-start | bytes 1228808 | tf_op jit(solution)/shard_map/ppermute | solution.py:23
  11.0 2.6 %collective-permute-start.4 = (bf16[400,512]{1,0:T(8,128)(2,1)}, bf16[400,512]{1,0:T(8,128)(2,1)}, u32[]{:S(2)}, u32[]{:S(2)}) collective-permute-start(bf16[400,512]{1,0:T(8,128)(2,1)} %get-tuple-element.63), channel_id=1, source_target_pairs={{0,8},{1,9},{2,10},{3,11},{4,12},{5,13},{6,14},{7,15},{8,0},{9,1},... | collective-permute-start | bytes 1228808 | tf_op jit(solution)/shard_map/ppermute | solution.py:23
  13.6 8.2 %head_grad_0.1 = (bf16[3,128,512]{2,1,0:T(8,128)(2,1)}, bf16[3,128,512]{2,1,0:T(8,128)(2,1)}, f32[3,128,512]{2,1,0:T(8,128)}, f32[3,128,512]{2,1,0:T(8,128)}) custom-call(s32[9]{0:T(128)} %stack.55.where, f32[4,512]{1,0:T(4,128)} %bitcast.21, s32[1,512]{1,0:T(1,128)} %bitcast.24, bf16[512,2048]{1,0:T(8,128)(2,1)} %keys.5, bf16[512,2048]{1,0:T(8,128)(2,1)} %values.5, ...), custom_call_target="tpu_custom_call" | custom-call | tf_op jit(solution)/shard_map/head_grad_0/pallas_call | solution.py:40
  21.8 0.6 collective-permute-start.5
  22.4 0.0 collective-permute-done.1.refs_4_
  22.4 0.0 collective-permute-done.2.other
  22.4 1.0 copy-done.5
  23.5 8.2 %head_grad_1.1 = (bf16[3,128,512]{2,1,0:T(8,128)(2,1)}, bf16[3,128,512]{2,1,0:T(8,128)(2,1)}, f32[3,128,512]{2,1,0:T(8,128)}, f32[3,128,512]{2,1,0:T(8,128)}) custom-call(s32[9]{0:T(128)} %stack.55.where, f32[4,512]{1,0:T(4,128)} %bitcast.22, s32[1,512]{1,0:T(1,128)} %bitcast.25, bf16[512,2048]{1,0:T(8,128)(2,1)} %keys.5, bf16[512,2048]{1,0:T(8,128)(2,1)} %values.5, ...), custom_call_target="tpu_custom_call" | custom-call | tf_op jit(solution)/shard_map/head_grad_1/pallas_call | solution.py:40
  31.7 1.6 %collective-permute-start.6 = (bf16[3,128,512]{2,1,0:T(8,128)(2,1)}, bf16[3,128,512]{2,1,0:T(8,128)(2,1)S(1)}, u32[]{:S(2)}, u32[]{:S(2)}) collective-permute-start(bf16[3,128,512]{2,1,0:T(8,128)(2,1)} %get-tuple-element.70), channel_id=1, source_target_pairs={{0,2},{1,3},{2,0},{3,1},{4,6},{5,7},{6,4},{7,5},{8,10},{9,11},{10,... | collective-permute-start | bytes 1179656 | tf_op jit(solution)/shard_map/ppermute | solution.py:23
  33.3 0.0 collective-permute-done.3
  33.3 1.1 collective-permute-start.7
  34.4 1.5 %collective-permute-start.9 = (bf16[3,128,512]{2,1,0:T(8,128)(2,1)}, bf16[3,128,512]{2,1,0:T(8,128)(2,1)S(1)}, u32[]{:S(2)}, u32[]{:S(2)}) collective-permute-start(bf16[3,128,512]{2,1,0:T(8,128)(2,1)} %get-tuple-element.77), channel_id=1, source_target_pairs={{0,2},{1,3},{2,0},{3,1},{4,6},{5,7},{6,4},{7,5},{8,10},{9,11},{10,... | collective-permute-start | bytes 1179656 | tf_op jit(solution)/shard_map/ppermute | solution.py:23
  35.9 1.1 fusion.5
  37.1 1.4 %collective-permute-start.8 = (bf16[3,128,512]{2,1,0:T(8,128)(2,1)S(1)}, bf16[3,128,512]{2,1,0:T(8,128)(2,1)S(1)}, u32[]{:S(2)}, u32[]{:S(2)}) collective-permute-start(bf16[3,128,512]{2,1,0:T(8,128)(2,1)S(1)} %get-tuple-element.111), channel_id=1, source_target_pairs={{1,5},{3,7},{4,0},{6,2},{9,13},{11,15},{12,8},{14,10},{17,21},{19,... | collective-permute-start | bytes 1179656 | tf_op jit(solution)/shard_map/ppermute | solution.py:23
  38.5 5.5 %collective-permute-done.6 = bf16[3,128,512]{2,1,0:T(8,128)(2,1)S(1)} collective-permute-done((bf16[3,128,512]{2,1,0:T(8,128)(2,1)}, bf16[3,128,512]{2,1,0:T(8,128)(2,1)S(1)}, u32[]{:S(2)}, u32[]{:S(2)}) %collective-permute-start.6) | collective-permute-done | bytes 393248 | tf_op jit(solution)/shard_map/ppermute | solution.py:23
  44.0 1.0 fusion.4
  45.1 1.4 %collective-permute-start.10 = (bf16[3,128,512]{2,1,0:T(8,128)(2,1)S(1)}, bf16[3,128,512]{2,1,0:T(8,128)(2,1)S(1)}, u32[]{:S(2)}, u32[]{:S(2)}) collective-permute-start(bf16[3,128,512]{2,1,0:T(8,128)(2,1)S(1)} %get-tuple-element.109), channel_id=1, source_target_pairs={{1,5},{3,7},{4,0},{6,2},{9,13},{11,15},{12,8},{14,10},{17,21},{19,... | collective-permute-start | bytes 1179656 | tf_op jit(solution)/shard_map/ppermute | solution.py:23
  46.5 1.6 %collective-permute-start.11 = (bf16[3,128,512]{2,1,0:T(8,128)(2,1)S(1)}, bf16[3,128,512]{2,1,0:T(8,128)(2,1)S(1)}, u32[]{:S(2)}, u32[]{:S(2)}) collective-permute-start(bf16[3,128,512]{2,1,0:T(8,128)(2,1)S(1)} %copy-done.13), channel_id=1, source_target_pairs={{0,2},{1,3},{2,0},{3,1},{4,6},{5,7},{6,4},{7,5},{8,10},{9,11},{10,... | collective-permute-start | bytes 1179656 | tf_op jit(solution)/shard_map/ppermute | solution.py:23
  48.1 1.6 %collective-permute-done.8 = bf16[3,128,512]{2,1,0:T(8,128)(2,1)S(1)} collective-permute-done((bf16[3,128,512]{2,1,0:T(8,128)(2,1)S(1)}, bf16[3,128,512]{2,1,0:T(8,128)(2,1)S(1)}, u32[]{:S(2)}, u32[]{:S(2)}) %collective-permute-start.8) | collective-permute-done | bytes 393248 | tf_op jit(solution)/shard_map/ppermute | solution.py:23
  49.7 2.8 %collective-permute-done.9 = bf16[3,128,512]{2,1,0:T(8,128)(2,1)S(1)} collective-permute-done((bf16[3,128,512]{2,1,0:T(8,128)(2,1)}, bf16[3,128,512]{2,1,0:T(8,128)(2,1)S(1)}, u32[]{:S(2)}, u32[]{:S(2)}) %collective-permute-start.9) | collective-permute-done | bytes 393248 | tf_op jit(solution)/shard_map/ppermute | solution.py:23
  52.5 1.1 fusion.3
  53.5 1.3 collective-permute-start.12
  54.8 0.1 collective-permute-done.10
  54.9 3.9 %collective-permute-done.11 = bf16[3,128,512]{2,1,0:T(8,128)(2,1)S(1)} collective-permute-done((bf16[3,128,512]{2,1,0:T(8,128)(2,1)S(1)}, bf16[3,128,512]{2,1,0:T(8,128)(2,1)S(1)}, u32[]{:S(2)}, u32[]{:S(2)}) %collective-permute-start.11) | collective-permute-done | bytes 393248 | tf_op jit(solution)/shard_map/ppermute | solution.py:23
  58.8 1.2 fusion.2
  60.0 1.3 %pad_maximum_fusion.refs_1_ = bf16[3,400,512]{2,1,0:T(8,128)(2,1)S(1)} fusion(bf16[1,400,512]{2,1,0:T(8,128)(2,1)S(1)} %bitcast.19, bf16[1,400,512]{2,1,0:T(8,128)(2,1)} %bitcast.15, bf16[1,400,512]{2,1,0:T(8,128)(2,1)} %bitcast.14), kind=kLoop, calls=%fused_computation | loop fusion | flops 1228800 | bytes 2457600 | tf_op jit(solution)/shard_map/stack | solution.py:517
  61.4 1.6 %collective-permute-start.19 = (bf16[3,400,512]{2,1,0:T(8,128)(2,1)S(1)}, bf16[3,400,512]{2,1,0:T(8,128)(2,1)}, u32[]{:S(2)}, u32[]{:S(2)}) collective-permute-start(bf16[3,400,512]{2,1,0:T(8,128)(2,1)S(1)} %pad_maximum_fusion.refs_1_), channel_id=1, source_target_pairs={{0,2},{1,3},{2,0},{3,1},{4,6},{5,7},{6,4},{7,5},{8,10},{9,11},{10,... | collective-permute-start | bytes 3686408 | tf_op jit(solution)/shard_map/ppermute | solution.py:23
  63.0 1.3 collective-permute-start.13
  64.2 0.1 collective-permute-start.14
  64.3 0.5 collective-permute-start.15
  64.8 2.5 %fusion = (f32[3,128,512]{2,1,0:T(8,128)S(1)}, bf16[3,128,512]{2,1,0:T(8,128)(2,1)}) fusion(f32[3,128,512]{2,1,0:T(8,128)S(1)} %get-tuple-element.86, bf16[3,128,512]{2,1,0:T(8,128)(2,1)} %copy-done.12, f32[3,128,512]{2,1,0:T(8,128)} %get-tuple-element.87, bf16[3,128,512]{2,1,0:T(8,128)(2,1)} %collective-permute-done.12, pred[]{:T(512)S(6)} %eq.12), kind=kLoop, calls=%fused_computation.11 | loop fusion | flops 1376256 | bytes 3538945 | tf_op jit(solution)/shard_map/jit(_where)/select_n | solution.py:530
  67.4 3.7 %collective-permute-start.16 = (bf16[3,128,512]{2,1,0:T(8,128)(2,1)}, bf16[3,128,512]{2,1,0:T(8,128)(2,1)}, u32[]{:S(2)}, u32[]{:S(2)}) collective-permute-start(bf16[3,128,512]{2,1,0:T(8,128)(2,1)} %get-tuple-element.118), channel_id=1, source_target_pairs={{0,8},{2,10},{5,13},{7,15},{8,0},{10,2},{13,5},{15,7},{16,24},{18,... | collective-permute-start | bytes 1179656 | tf_op jit(solution)/shard_map/ppermute | solution.py:23
  71.0 1.9 %collective-permute-done.13 = bf16[3,128,512]{2,1,0:T(8,128)(2,1)} collective-permute-done((bf16[3,128,512]{2,1,0:T(8,128)(2,1)}, bf16[3,128,512]{2,1,0:T(8,128)(2,1)}, u32[]{:S(2)}, u32[]{:S(2)}) %collective-permute-start.13) | collective-permute-done | bytes 393248 | tf_op jit(solution)/shard_map/ppermute | solution.py:23
  72.9 2.0 %fusion.1 = (f32[3,128,512]{2,1,0:T(8,128)S(1)}, bf16[3,128,512]{2,1,0:T(8,128)(2,1)}) fusion(f32[3,128,512]{2,1,0:T(8,128)S(1)} %copy-done.3, bf16[3,128,512]{2,1,0:T(8,128)(2,1)S(1)} %copy-done.11, f32[3,128,512]{2,1,0:T(8,128)S(1)} %copy-done.4, bf16[3,128,512]{2,1,0:T(8,128)(2,1)} %collective-permute-done.13, pred[]{:T(512)S(6)} %eq.12), kind=kLoop, calls=%fused_computation.12 | loop fusion | flops 1376256 | bytes 3538945 | tf_op jit(solution)/shard_map/jit(_where)/select_n | solution.py:530
  75.0 3.2 %collective-permute-start.17 = (bf16[3,128,512]{2,1,0:T(8,128)(2,1)}, bf16[3,128,512]{2,1,0:T(8,128)(2,1)}, u32[]{:S(2)}, u32[]{:S(2)}) collective-permute-start(bf16[3,128,512]{2,1,0:T(8,128)(2,1)} %get-tuple-element.116), channel_id=1, source_target_pairs={{0,8},{2,10},{5,13},{7,15},{8,0},{10,2},{13,5},{15,7},{16,24},{18,... | collective-permute-start | bytes 1179656 | tf_op jit(solution)/shard_map/ppermute | solution.py:23
  78.2 1.2 dynamic-slice_bitcast_fusion
  79.4 0.1 collective-permute-start.18
  79.5 7.2 %collective-permute-done.16.got = bf16[3,128,512]{2,1,0:T(8,128)(2,1)} collective-permute-done((bf16[3,128,512]{2,1,0:T(8,128)(2,1)}, bf16[3,128,512]{2,1,0:T(8,128)(2,1)}, u32[]{:S(2)}, u32[]{:S(2)}) %collective-permute-start.16) | collective-permute-done | bytes 393248 | tf_op jit(solution)/shard_map/ppermute | solution.py:23
  86.7 1.8 %renew.2.refs_0_ = bf16[3,128,512]{2,1,0:T(8,128)(2,1)S(1)} custom-call(s32[9]{0:T(128)S(1)} %copy-done.1, f32[3,128,512]{2,1,0:T(8,128)S(1)} %get-tuple-element.117.keep, bf16[3,128,512]{2,1,0:T(8,128)(2,1)} %collective-permute-done.16.got, bf16[3,128,512]{2,1,0:T(8,128)(2,1)S(1)} %get-tuple-element.114.old, f32[4]{0:T(128)S(1)} %copy-done.2), custom_call_target="tpu_custom_call" | custom-call | tf_op jit(solution)/shard_map/renew/pallas_call | solution.py:40
  88.5 2.4 %collective-permute-done.17.got = bf16[3,128,512]{2,1,0:T(8,128)(2,1)} collective-permute-done((bf16[3,128,512]{2,1,0:T(8,128)(2,1)}, bf16[3,128,512]{2,1,0:T(8,128)(2,1)}, u32[]{:S(2)}, u32[]{:S(2)}) %collective-permute-start.17) | collective-permute-done | bytes 393248 | tf_op jit(solution)/shard_map/ppermute | solution.py:23
  90.9 1.8 %renew.3.refs_1_ = bf16[3,128,512]{2,1,0:T(8,128)(2,1)S(1)} custom-call(s32[9]{0:T(128)S(1)} %copy-done.1, f32[3,128,512]{2,1,0:T(8,128)S(1)} %get-tuple-element.115.keep, bf16[3,128,512]{2,1,0:T(8,128)(2,1)} %collective-permute-done.17.got, bf16[3,128,512]{2,1,0:T(8,128)(2,1)S(1)} %get-tuple-element.113.old, f32[4]{0:T(128)S(1)} %copy-done.2), custom_call_target="tpu_custom_call" | custom-call | tf_op jit(solution)/shard_map/renew/pallas_call | solution.py:40
  92.7 0.1 collective-permute-start.20
  92.8 2.4 %collective-permute-start.21 = (bf16[3,128,512]{2,1,0:T(8,128)(2,1)S(1)}, bf16[3,128,512]{2,1,0:T(8,128)(2,1)S(1)}, u32[]{:S(2)}, u32[]{:S(2)}) collective-permute-start(bf16[3,128,512]{2,1,0:T(8,128)(2,1)S(1)} %renew.2.refs_0_), channel_id=1, source_target_pairs={{0,2},{2,0},{5,7},{7,5},{8,10},{10,8},{13,15},{15,13},{16,18},{18,... | collective-permute-start | bytes 1179656 | tf_op jit(solution)/shard_map/ppermute | solution.py:23
  95.2 3.4 %collective-permute-start.22 = (bf16[3,128,512]{2,1,0:T(8,128)(2,1)S(1)}, bf16[3,128,512]{2,1,0:T(8,128)(2,1)S(1)}, u32[]{:S(2)}, u32[]{:S(2)}) collective-permute-start(bf16[3,128,512]{2,1,0:T(8,128)(2,1)S(1)} %renew.3.refs_1_), channel_id=1, source_target_pairs={{0,2},{2,0},{5,7},{7,5},{8,10},{10,8},{13,15},{15,13},{16,18},{18,... | collective-permute-start | bytes 1179656 | tf_op jit(solution)/shard_map/ppermute | solution.py:23
  98.6 1.3 %collective-permute-start.23 = (bf16[3,128,512]{2,1,0:T(8,128)(2,1)S(1)}, bf16[3,128,512]{2,1,0:T(8,128)(2,1)S(1)}, u32[]{:S(2)}, u32[]{:S(2)}) collective-permute-start(bf16[3,128,512]{2,1,0:T(8,128)(2,1)S(1)} %renew.2.refs_0_), channel_id=1, source_target_pairs={{0,1},{2,3},{5,4},{7,6},{8,9},{10,11},{13,12},{15,14},{16,17},{18,... | collective-permute-start | bytes 1179656 | tf_op jit(solution)/shard_map/ppermute | solution.py:23
  99.9 1.3 %collective-permute-start.24 = (bf16[3,128,512]{2,1,0:T(8,128)(2,1)S(1)}, bf16[3,128,512]{2,1,0:T(8,128)(2,1)S(1)}, u32[]{:S(2)}, u32[]{:S(2)}) collective-permute-start(bf16[3,128,512]{2,1,0:T(8,128)(2,1)S(1)} %renew.3.refs_1_), channel_id=1, source_target_pairs={{0,1},{2,3},{5,4},{7,6},{8,9},{10,11},{13,12},{15,14},{16,17},{18,... | collective-permute-start | bytes 1179656 | tf_op jit(solution)/shard_map/ppermute | solution.py:23
  101.3 5.8 %arrange.1.rows = bf16[3,512,512]{2,1,0:T(8,128)(2,1)S(1)} custom-call(s32[9]{0:T(128)S(1)} %copy-done.1, bf16[400,512]{1,0:T(8,128)(2,1)S(1)} %copy-done, bf16[3,400,512]{2,1,0:T(8,128)(2,1)S(1)} %pad_maximum_fusion.refs_1_, bf16[400,512]{1,0:T(8,128)(2,1)} %collective-permute-done.14.refs_2_, bf16[3,400,512]{2,1,0:T(8,128)(2,1)S(1)} %collective-permute-done.18.refs_3_, ...), custom_call_target="tpu_custom_call" | custom-call | tf_op jit(solution)/shard_map/arrange/pallas_call | solution.py:40
  107.1 1.7 %attend.1.attended = f32[512,512]{1,0:T(8,128)S(1)} custom-call(s32[9]{0:T(128)S(1)} %copy-done.1, bf16[3,512,512]{2,1,0:T(8,128)(2,1)S(1)} %arrange.1.rows), custom_call_target="tpu_custom_call" | custom-call | tf_op jit(solution)/shard_map/attend/pallas_call | solution.py:40
  108.8 0.0 collective-permute-done.22.refs_3_
  108.8 1.3 %collective-permute-start.25 = (bf16[3,128,512]{2,1,0:T(8,128)(2,1)S(1)}, bf16[3,128,512]{2,1,0:T(8,128)(2,1)S(1)}, u32[]{:S(2)}, u32[]{:S(2)}) collective-permute-start(bf16[3,128,512]{2,1,0:T(8,128)(2,1)S(1)} %collective-permute-done.21.refs_2_), channel_id=1, source_target_pairs={{0,1},{2,3},{5,4},{7,6},{8,9},{10,11},{13,12},{15,14},{16,17},{18,... | collective-permute-start | bytes 1179656 | tf_op jit(solution)/shard_map/ppermute | solution.py:23
  110.1 1.3 %collective-permute-start.26 = (bf16[3,128,512]{2,1,0:T(8,128)(2,1)S(1)}, bf16[3,128,512]{2,1,0:T(8,128)(2,1)S(1)}, u32[]{:S(2)}, u32[]{:S(2)}) collective-permute-start(bf16[3,128,512]{2,1,0:T(8,128)(2,1)S(1)} %collective-permute-done.22.refs_3_), channel_id=1, source_target_pairs={{0,1},{2,3},{5,4},{7,6},{8,9},{10,11},{13,12},{15,14},{16,17},{18,... | collective-permute-start | bytes 1179656 | tf_op jit(solution)/shard_map/ppermute | solution.py:23
  111.5 1.3 collective-permute-done.26.refs_7_
  112.7 2.2 %finish.1 = (bf16[128,512]{1,0:T(8,128)(2,1)S(1)}, bf16[128,512]{1,0:T(8,128)(2,1)S(1)}, bf16[128,512]{1,0:T(8,128)(2,1)S(1)}, bf16[128,512]{1,0:T(8,128)(2,1)S(1)}) custom-call(s32[9]{0:T(128)S(1)} %copy-done.1, bf16[3,512,512]{2,1,0:T(8,128)(2,1)S(1)} %arrange.1.rows, f32[512,512]{1,0:T(8,128)S(1)} %attend.1.attended, ...), custom_call_target="tpu_custom_call" | custom-call | tf_op jit(solution)/shard_map/finish/pallas_call | solution.py:40
  114.9 0.1 collective-permute-start.27
  115.0 2.3 %collective-permute-start.28 = (bf16[128,512]{1,0:T(8,128)(2,1)S(1)}, bf16[128,512]{1,0:T(8,128)(2,1)S(1)}, u32[]{:S(2)}, u32[]{:S(2)}) collective-permute-start(bf16[128,512]{1,0:T(8,128)(2,1)S(1)} %get-tuple-element.103), channel_id=1, source_target_pairs={{0,8},{1,9},{2,10},{3,11},{4,12},{5,13},{6,14},{7,15},{8,0},{9,1},... | collective-permute-start | bytes 393224 | tf_op jit(solution)/shard_map/ppermute | solution.py:23
  117.3 2.0 %collective-permute-start.29 = (bf16[128,512]{1,0:T(8,128)(2,1)S(1)}, bf16[128,512]{1,0:T(8,128)(2,1)S(1)}, u32[]{:S(2)}, u32[]{:S(2)}) collective-permute-start(bf16[128,512]{1,0:T(8,128)(2,1)S(1)} %get-tuple-element.104), channel_id=1, source_target_pairs={{0,12},{1,13},{2,14},{3,15},{4,8},{5,9},{6,10},{7,11},{8,4},{9,5},... | collective-permute-start | bytes 393224 | tf_op jit(solution)/shard_map/ppermute | solution.py:23
  119.4 3.1 %collective-permute-done.27.refs_1_ = bf16[128,512]{1,0:T(8,128)(2,1)S(1)} collective-permute-done((bf16[128,512]{1,0:T(8,128)(2,1)S(1)}, bf16[128,512]{1,0:T(8,128)(2,1)S(1)}, u32[]{:S(2)}, u32[]{:S(2)}) %collective-permute-start.27) | collective-permute-done | bytes 131104 | tf_op jit(solution)/shard_map/ppermute | solution.py:23
  122.5 5.5 %collective-permute-done.28.refs_2_ = bf16[128,512]{1,0:T(8,128)(2,1)S(1)} collective-permute-done((bf16[128,512]{1,0:T(8,128)(2,1)S(1)}, bf16[128,512]{1,0:T(8,128)(2,1)S(1)}, u32[]{:S(2)}, u32[]{:S(2)}) %collective-permute-start.28) | collective-permute-done | bytes 131104 | tf_op jit(solution)/shard_map/ppermute | solution.py:23
  128.0 1.4 %join.1 = bf16[128,2048]{1,0:T(8,128)(2,1)} custom-call(s32[9]{0:T(128)S(1)} %copy-done.1, bf16[128,512]{1,0:T(8,128)(2,1)S(1)} %get-tuple-element.101.refs_0_, bf16[128,512]{1,0:T(8,128)(2,1)S(1)} %collective-permute-done.27.refs_1_, bf16[128,512]{1,0:T(8,128)(2,1)S(1)} %collective-permute-done.28.refs_2_, bf16[128,512]{1,0:T(8,128)(2,1)S(1)} %collective-permute-done.29.refs_3_), custom_call_target="tpu_custom_call" | custom-call | tf_op jit(solution)/shard_map/join/pallas_call | solution.py:40
  (42 shorter events, 0.1 us)
Async XLA Ops:
  5.9 7.7 %collective-permute-start = (bf16[2,512,512]{2,1,0:T(8,128)(2,1)}, bf16[2,512,512]{2,1,0:T(8,128)(2,1)}, u32[]{:S(2)}, u32[]{:S(2)}) collective-permute-start(bf16[2,512,512]{2,1,0:T(8,128)(2,1)} %get-tuple-element.57), channel_id=1, source_target_pairs={{0,1},{1,0},{2,3},{3,2},{4,5},{5,4},{6,7},{7,6},{8,9},{9,8},{10,11... | collective-permute-start | bytes 3145736 | tf_op jit(solution)/shard_map/ppermute | solution.py:23
  6.4 16.0 %collective-permute-start.2 = (bf16[2,512,512]{2,1,0:T(8,128)(2,1)}, bf16[2,512,512]{2,1,0:T(8,128)(2,1)S(1)}, u32[]{:S(2)}, u32[]{:S(2)}) collective-permute-start(bf16[2,512,512]{2,1,0:T(8,128)(2,1)} %get-tuple-element.60), channel_id=1, source_target_pairs={{0,1},{1,0},{2,3},{3,2},{4,5},{5,4},{6,7},{7,6},{8,9},{9,8},{10,11... | collective-permute-start | bytes 3145736 | tf_op jit(solution)/shard_map/ppermute | solution.py:23
  6.5 15.9 %collective-permute-start.1 = (bf16[400,512]{1,0:T(8,128)(2,1)}, bf16[400,512]{1,0:T(8,128)(2,1)}, u32[]{:S(2)}, u32[]{:S(2)}) collective-permute-start(bf16[400,512]{1,0:T(8,128)(2,1)} %get-tuple-element.55.refs_0_), channel_id=1, source_target_pairs={{0,2},{1,3},{2,0},{3,1},{4,6},{5,7},{6,4},{7,5},{8,10},{9,11},{10,... | collective-permute-start | bytes 1228808 | tf_op jit(solution)/shard_map/ppermute | solution.py:23
  9.4 23.9 %collective-permute-start.3 = (bf16[400,512]{1,0:T(8,128)(2,1)}, bf16[400,512]{1,0:T(8,128)(2,1)}, u32[]{:S(2)}, u32[]{:S(2)}) collective-permute-start(bf16[400,512]{1,0:T(8,128)(2,1)} %get-tuple-element.62), channel_id=1, source_target_pairs={{0,4},{1,5},{2,6},{3,7},{4,0},{5,1},{6,2},{7,3},{8,12},{9,13},{10,... | collective-permute-start | bytes 1228808 | tf_op jit(solution)/shard_map/ppermute | solution.py:23
  11.0 22.3 %collective-permute-start.4 = (bf16[400,512]{1,0:T(8,128)(2,1)}, bf16[400,512]{1,0:T(8,128)(2,1)}, u32[]{:S(2)}, u32[]{:S(2)}) collective-permute-start(bf16[400,512]{1,0:T(8,128)(2,1)} %get-tuple-element.63), channel_id=1, source_target_pairs={{0,8},{1,9},{2,10},{3,11},{4,12},{5,13},{6,14},{7,15},{8,0},{9,1},... | collective-permute-start | bytes 1228808 | tf_op jit(solution)/shard_map/ppermute | solution.py:23
  21.8 14.1 %copy-start.9 = (f32[3,128,512]{2,1,0:T(8,128)S(1)}, f32[3,128,512]{2,1,0:T(8,128)}, u32[]{:S(2)}) copy-start(f32[3,128,512]{2,1,0:T(8,128)} %get-tuple-element.65) | copy-start | bytes 2359300
  21.8 14.1 %collective-permute-start.5 = (bf16[3,128,512]{2,1,0:T(8,128)(2,1)}, bf16[3,128,512]{2,1,0:T(8,128)(2,1)}, u32[]{:S(2)}, u32[]{:S(2)}) collective-permute-start(bf16[3,128,512]{2,1,0:T(8,128)(2,1)} %get-tuple-element.58), channel_id=1, source_target_pairs={{0,2},{1,3},{2,0},{3,1},{4,6},{5,7},{6,4},{7,5},{8,10},{9,11},{10,... | collective-permute-start | bytes 1179656 | tf_op jit(solution)/shard_map/ppermute | solution.py:23
  22.4 1.0 copy-start.5
  31.7 12.3 %copy-start.8 = (f32[3,128,512]{2,1,0:T(8,128)S(1)}, f32[3,128,512]{2,1,0:T(8,128)}, u32[]{:S(2)}) copy-start(f32[3,128,512]{2,1,0:T(8,128)} %get-tuple-element.68) | copy-start | bytes 2359300
  31.7 12.3 %collective-permute-start.6 = (bf16[3,128,512]{2,1,0:T(8,128)(2,1)}, bf16[3,128,512]{2,1,0:T(8,128)(2,1)S(1)}, u32[]{:S(2)}, u32[]{:S(2)}) collective-permute-start(bf16[3,128,512]{2,1,0:T(8,128)(2,1)} %get-tuple-element.70), channel_id=1, source_target_pairs={{0,2},{1,3},{2,0},{3,1},{4,6},{5,7},{6,4},{7,5},{8,10},{9,11},{10,... | collective-permute-start | bytes 1179656 | tf_op jit(solution)/shard_map/ppermute | solution.py:23
  33.3 14.8 %collective-permute-start.7 = (bf16[400,512]{1,0:T(8,128)(2,1)}, bf16[400,512]{1,0:T(8,128)(2,1)S(1)}, u32[]{:S(2)}, u32[]{:S(2)}) collective-permute-start(bf16[400,512]{1,0:T(8,128)(2,1)} %get-tuple-element.74), channel_id=1, source_target_pairs={{0,12},{1,13},{2,14},{3,15},{4,8},{5,9},{6,10},{7,11},{8,4},{9,5},... | collective-permute-start | bytes 1228808 | tf_op jit(solution)/shard_map/ppermute | solution.py:23
  34.4 18.1 %collective-permute-start.9 = (bf16[3,128,512]{2,1,0:T(8,128)(2,1)}, bf16[3,128,512]{2,1,0:T(8,128)(2,1)S(1)}, u32[]{:S(2)}, u32[]{:S(2)}) collective-permute-start(bf16[3,128,512]{2,1,0:T(8,128)(2,1)} %get-tuple-element.77), channel_id=1, source_target_pairs={{0,2},{1,3},{2,0},{3,1},{4,6},{5,7},{6,4},{7,5},{8,10},{9,11},{10,... | collective-permute-start | bytes 1179656 | tf_op jit(solution)/shard_map/ppermute | solution.py:23
  37.1 9.4 %copy-start.13 = (bf16[3,128,512]{2,1,0:T(8,128)(2,1)S(1)}, bf16[3,128,512]{2,1,0:T(8,128)(2,1)}, u32[]{:S(2)}) copy-start(bf16[3,128,512]{2,1,0:T(8,128)(2,1)} %get-tuple-element.83) | copy-start | bytes 1179652
  37.1 15.4 %copy-start.7 = (f32[3,128,512]{2,1,0:T(8,128)S(1)}, f32[3,128,512]{2,1,0:T(8,128)}, u32[]{:S(2)}) copy-start(f32[3,128,512]{2,1,0:T(8,128)} %get-tuple-element.76) | copy-start | bytes 2359300
  37.1 12.6 %collective-permute-start.8 = (bf16[3,128,512]{2,1,0:T(8,128)(2,1)S(1)}, bf16[3,128,512]{2,1,0:T(8,128)(2,1)S(1)}, u32[]{:S(2)}, u32[]{:S(2)}) collective-permute-start(bf16[3,128,512]{2,1,0:T(8,128)(2,1)S(1)} %get-tuple-element.111), channel_id=1, source_target_pairs={{1,5},{3,7},{4,0},{6,2},{9,13},{11,15},{12,8},{14,10},{17,21},{19,... | collective-permute-start | bytes 1179656 | tf_op jit(solution)/shard_map/ppermute | solution.py:23
  45.1 13.7 %copy-start.6 = (f32[3,128,512]{2,1,0:T(8,128)S(1)}, f32[3,128,512]{2,1,0:T(8,128)}, u32[]{:S(2)}) copy-start(f32[3,128,512]{2,1,0:T(8,128)} %get-tuple-element.81) | copy-start | bytes 2359300
  45.1 9.8 %collective-permute-start.10 = (bf16[3,128,512]{2,1,0:T(8,128)(2,1)S(1)}, bf16[3,128,512]{2,1,0:T(8,128)(2,1)S(1)}, u32[]{:S(2)}, u32[]{:S(2)}) collective-permute-start(bf16[3,128,512]{2,1,0:T(8,128)(2,1)S(1)} %get-tuple-element.109), channel_id=1, source_target_pairs={{1,5},{3,7},{4,0},{6,2},{9,13},{11,15},{12,8},{14,10},{17,21},{19,... | collective-permute-start | bytes 1179656 | tf_op jit(solution)/shard_map/ppermute | solution.py:23
  46.5 12.3 %collective-permute-start.11 = (bf16[3,128,512]{2,1,0:T(8,128)(2,1)S(1)}, bf16[3,128,512]{2,1,0:T(8,128)(2,1)S(1)}, u32[]{:S(2)}, u32[]{:S(2)}) collective-permute-start(bf16[3,128,512]{2,1,0:T(8,128)(2,1)S(1)} %copy-done.13), channel_id=1, source_target_pairs={{0,2},{1,3},{2,0},{3,1},{4,6},{5,7},{6,4},{7,5},{8,10},{9,11},{10,... | collective-permute-start | bytes 1179656 | tf_op jit(solution)/shard_map/ppermute | solution.py:23
  49.7 13.3 %copy-start.12 = (bf16[3,128,512]{2,1,0:T(8,128)(2,1)}, bf16[3,128,512]{2,1,0:T(8,128)(2,1)S(1)}, u32[]{:S(2)}) copy-start(bf16[3,128,512]{2,1,0:T(8,128)(2,1)S(1)} %collective-permute-done.8) | copy-start | bytes 1179652
  53.5 11.3 %collective-permute-start.12 = (bf16[3,128,512]{2,1,0:T(8,128)(2,1)S(1)}, bf16[3,128,512]{2,1,0:T(8,128)(2,1)}, u32[]{:S(2)}, u32[]{:S(2)}) collective-permute-start(bf16[3,128,512]{2,1,0:T(8,128)(2,1)S(1)} %get-tuple-element.107), channel_id=1, source_target_pairs={{1,5},{3,7},{4,0},{6,2},{9,13},{11,15},{12,8},{14,10},{17,21},{19,... | collective-permute-start | bytes 1179656 | tf_op jit(solution)/shard_map/ppermute | solution.py:23
  54.9 6.5 %copy-start.10 = (bf16[3,128,512]{2,1,0:T(8,128)(2,1)}, bf16[3,128,512]{2,1,0:T(8,128)(2,1)S(1)}, u32[]{:S(2)}) copy-start(bf16[3,128,512]{2,1,0:T(8,128)(2,1)S(1)} %collective-permute-done.10) | copy-start | bytes 1179652
  60.0 4.2 %copy-start = (bf16[400,512]{1,0:T(8,128)(2,1)S(1)}, bf16[400,512]{1,0:T(8,128)(2,1)}, u32[]{:S(2)}) copy-start(bf16[400,512]{1,0:T(8,128)(2,1)} %get-tuple-element.55.refs_0_) | copy-start | bytes 1228804
  61.4 31.3 %collective-permute-start.19 = (bf16[3,400,512]{2,1,0:T(8,128)(2,1)S(1)}, bf16[3,400,512]{2,1,0:T(8,128)(2,1)}, u32[]{:S(2)}, u32[]{:S(2)}) collective-permute-start(bf16[3,400,512]{2,1,0:T(8,128)(2,1)S(1)} %pad_maximum_fusion.refs_1_), channel_id=1, source_target_pairs={{0,2},{1,3},{2,0},{3,1},{4,6},{5,7},{6,4},{7,5},{8,10},{9,11},{10,... | collective-permute-start | bytes 3686408 | tf_op jit(solution)/shard_map/ppermute | solution.py:23
  63.0 10.0 %collective-permute-start.13 = (bf16[3,128,512]{2,1,0:T(8,128)(2,1)}, bf16[3,128,512]{2,1,0:T(8,128)(2,1)}, u32[]{:S(2)}, u32[]{:S(2)}) collective-permute-start(bf16[3,128,512]{2,1,0:T(8,128)(2,1)} %get-tuple-element.105), channel_id=1, source_target_pairs={{1,5},{3,7},{4,0},{6,2},{9,13},{11,15},{12,8},{14,10},{17,21},{19,... | collective-permute-start | bytes 1179656 | tf_op jit(solution)/shard_map/ppermute | solution.py:23
  64.2 15.1 %collective-permute-start.14 = (bf16[400,512]{1,0:T(8,128)(2,1)S(1)}, bf16[400,512]{1,0:T(8,128)(2,1)}, u32[]{:S(2)}, u32[]{:S(2)}) collective-permute-start(bf16[400,512]{1,0:T(8,128)(2,1)S(1)} %copy-done), channel_id=1, source_target_pairs={{0,1},{1,0},{2,3},{3,2},{4,5},{5,4},{6,7},{7,6},{8,9},{9,8},{10,11... | collective-permute-start | bytes 1228808 | tf_op jit(solution)/shard_map/ppermute | solution.py:23
  64.3 15.1 %collective-permute-start.15 = (bf16[400,512]{1,0:T(8,128)(2,1)}, bf16[400,512]{1,0:T(8,128)(2,1)}, u32[]{:S(2)}, u32[]{:S(2)}) collective-permute-start(bf16[400,512]{1,0:T(8,128)(2,1)} %collective-permute-done.1.refs_4_), channel_id=1, source_target_pairs={{0,1},{1,0},{2,3},{3,2},{4,5},{5,4},{6,7},{7,6},{8,9},{9,8},{10,11... | collective-permute-start | bytes 1228808 | tf_op jit(solution)/shard_map/ppermute | solution.py:23
  64.8 8.1 %copy-start.3 = (f32[3,128,512]{2,1,0:T(8,128)S(1)}, f32[3,128,512]{2,1,0:T(8,128)}, u32[]{:S(2)}) copy-start(f32[3,128,512]{2,1,0:T(8,128)} %get-tuple-element.89) | copy-start | bytes 2359300
  64.8 8.1 %copy-start.4 = (f32[3,128,512]{2,1,0:T(8,128)S(1)}, f32[3,128,512]{2,1,0:T(8,128)}, u32[]{:S(2)}) copy-start(f32[3,128,512]{2,1,0:T(8,128)} %get-tuple-element.90) | copy-start | bytes 2359300
  64.8 8.1 %copy-start.11 = (bf16[3,128,512]{2,1,0:T(8,128)(2,1)S(1)}, bf16[3,128,512]{2,1,0:T(8,128)(2,1)}, u32[]{:S(2)}) copy-start(bf16[3,128,512]{2,1,0:T(8,128)(2,1)} %copy-done.10) | copy-start | bytes 1179652
  67.4 19.3 %collective-permute-start.16 = (bf16[3,128,512]{2,1,0:T(8,128)(2,1)}, bf16[3,128,512]{2,1,0:T(8,128)(2,1)}, u32[]{:S(2)}, u32[]{:S(2)}) collective-permute-start(bf16[3,128,512]{2,1,0:T(8,128)(2,1)} %get-tuple-element.118), channel_id=1, source_target_pairs={{0,8},{2,10},{5,13},{7,15},{8,0},{10,2},{13,5},{15,7},{16,24},{18,... | collective-permute-start | bytes 1179656 | tf_op jit(solution)/shard_map/ppermute | solution.py:23
  75.0 11.7 %copy-start.1 = (s32[9]{0:T(128)S(1)}, s32[9]{0:T(128)}, u32[]{:S(2)}) copy-start(s32[9]{0:T(128)} %stack.55.where) | copy-start | bytes 112
  75.0 11.7 %copy-start.2 = (f32[4]{0:T(128)S(1)}, f32[4]{0:T(128)}, u32[]{:S(2)}) copy-start(f32[4]{0:T(128)} %steps.3) | copy-start | bytes 52
  75.0 15.9 %collective-permute-start.17 = (bf16[3,128,512]{2,1,0:T(8,128)(2,1)}, bf16[3,128,512]{2,1,0:T(8,128)(2,1)}, u32[]{:S(2)}, u32[]{:S(2)}) collective-permute-start(bf16[3,128,512]{2,1,0:T(8,128)(2,1)} %get-tuple-element.116), channel_id=1, source_target_pairs={{0,8},{2,10},{5,13},{7,15},{8,0},{10,2},{13,5},{15,7},{16,24},{18,... | collective-permute-start | bytes 1179656 | tf_op jit(solution)/shard_map/ppermute | solution.py:23
  79.4 20.5 %collective-permute-start.18 = (bf16[3,400,512]{2,1,0:T(8,128)(2,1)S(1)}, bf16[3,400,512]{2,1,0:T(8,128)(2,1)S(1)}, u32[]{:S(2)}, u32[]{:S(2)}) collective-permute-start(bf16[3,400,512]{2,1,0:T(8,128)(2,1)S(1)} %pad_maximum_fusion.refs_1_), channel_id=1, source_target_pairs={{0,1},{1,0},{2,3},{3,2},{4,5},{5,4},{6,7},{7,6},{8,9},{9,8},{10,11... | collective-permute-start | bytes 3686408 | tf_op jit(solution)/shard_map/ppermute | solution.py:23
  92.7 8.6 %collective-permute-start.20 = (bf16[3,400,512]{2,1,0:T(8,128)(2,1)}, bf16[3,400,512]{2,1,0:T(8,128)(2,1)S(1)}, u32[]{:S(2)}, u32[]{:S(2)}) collective-permute-start(bf16[3,400,512]{2,1,0:T(8,128)(2,1)} %collective-permute-done.19.refs_5_), channel_id=1, source_target_pairs={{0,1},{1,0},{2,3},{3,2},{4,5},{5,4},{6,7},{7,6},{8,9},{9,8},{10,11... | collective-permute-start | bytes 3686408 | tf_op jit(solution)/shard_map/ppermute | solution.py:23
  92.8 16.0 %collective-permute-start.21 = (bf16[3,128,512]{2,1,0:T(8,128)(2,1)S(1)}, bf16[3,128,512]{2,1,0:T(8,128)(2,1)S(1)}, u32[]{:S(2)}, u32[]{:S(2)}) collective-permute-start(bf16[3,128,512]{2,1,0:T(8,128)(2,1)S(1)} %renew.2.refs_0_), channel_id=1, source_target_pairs={{0,2},{2,0},{5,7},{7,5},{8,10},{10,8},{13,15},{15,13},{16,18},{18,... | collective-permute-start | bytes 1179656 | tf_op jit(solution)/shard_map/ppermute | solution.py:23
  95.2 13.6 %collective-permute-start.22 = (bf16[3,128,512]{2,1,0:T(8,128)(2,1)S(1)}, bf16[3,128,512]{2,1,0:T(8,128)(2,1)S(1)}, u32[]{:S(2)}, u32[]{:S(2)}) collective-permute-start(bf16[3,128,512]{2,1,0:T(8,128)(2,1)S(1)} %renew.3.refs_1_), channel_id=1, source_target_pairs={{0,2},{2,0},{5,7},{7,5},{8,10},{10,8},{13,15},{15,13},{16,18},{18,... | collective-permute-start | bytes 1179656 | tf_op jit(solution)/shard_map/ppermute | solution.py:23
  98.6 12.8 %collective-permute-start.23 = (bf16[3,128,512]{2,1,0:T(8,128)(2,1)S(1)}, bf16[3,128,512]{2,1,0:T(8,128)(2,1)S(1)}, u32[]{:S(2)}, u32[]{:S(2)}) collective-permute-start(bf16[3,128,512]{2,1,0:T(8,128)(2,1)S(1)} %renew.2.refs_0_), channel_id=1, source_target_pairs={{0,1},{2,3},{5,4},{7,6},{8,9},{10,11},{13,12},{15,14},{16,17},{18,... | collective-permute-start | bytes 1179656 | tf_op jit(solution)/shard_map/ppermute | solution.py:23
  99.9 11.5 %collective-permute-start.24 = (bf16[3,128,512]{2,1,0:T(8,128)(2,1)S(1)}, bf16[3,128,512]{2,1,0:T(8,128)(2,1)S(1)}, u32[]{:S(2)}, u32[]{:S(2)}) collective-permute-start(bf16[3,128,512]{2,1,0:T(8,128)(2,1)S(1)} %renew.3.refs_1_), channel_id=1, source_target_pairs={{0,1},{2,3},{5,4},{7,6},{8,9},{10,11},{13,12},{15,14},{16,17},{18,... | collective-permute-start | bytes 1179656 | tf_op jit(solution)/shard_map/ppermute | solution.py:23
  108.8 2.7 %collective-permute-start.25 = (bf16[3,128,512]{2,1,0:T(8,128)(2,1)S(1)}, bf16[3,128,512]{2,1,0:T(8,128)(2,1)S(1)}, u32[]{:S(2)}, u32[]{:S(2)}) collective-permute-start(bf16[3,128,512]{2,1,0:T(8,128)(2,1)S(1)} %collective-permute-done.21.refs_2_), channel_id=1, source_target_pairs={{0,1},{2,3},{5,4},{7,6},{8,9},{10,11},{13,12},{15,14},{16,17},{18,... | collective-permute-start | bytes 1179656 | tf_op jit(solution)/shard_map/ppermute | solution.py:23
  110.1 2.6 %collective-permute-start.26 = (bf16[3,128,512]{2,1,0:T(8,128)(2,1)S(1)}, bf16[3,128,512]{2,1,0:T(8,128)(2,1)S(1)}, u32[]{:S(2)}, u32[]{:S(2)}) collective-permute-start(bf16[3,128,512]{2,1,0:T(8,128)(2,1)S(1)} %collective-permute-done.22.refs_3_), channel_id=1, source_target_pairs={{0,1},{2,3},{5,4},{7,6},{8,9},{10,11},{13,12},{15,14},{16,17},{18,... | collective-permute-start | bytes 1179656 | tf_op jit(solution)/shard_map/ppermute | solution.py:23
  114.9 7.5 %collective-permute-start.27 = (bf16[128,512]{1,0:T(8,128)(2,1)S(1)}, bf16[128,512]{1,0:T(8,128)(2,1)S(1)}, u32[]{:S(2)}, u32[]{:S(2)}) collective-permute-start(bf16[128,512]{1,0:T(8,128)(2,1)S(1)} %get-tuple-element.102), channel_id=1, source_target_pairs={{0,4},{1,5},{2,6},{3,7},{4,0},{5,1},{6,2},{7,3},{8,12},{9,13},{10,... | collective-permute-start | bytes 393224 | tf_op jit(solution)/shard_map/ppermute | solution.py:23
  115.0 13.0 %collective-permute-start.28 = (bf16[128,512]{1,0:T(8,128)(2,1)S(1)}, bf16[128,512]{1,0:T(8,128)(2,1)S(1)}, u32[]{:S(2)}, u32[]{:S(2)}) collective-permute-start(bf16[128,512]{1,0:T(8,128)(2,1)S(1)} %get-tuple-element.103), channel_id=1, source_target_pairs={{0,8},{1,9},{2,10},{3,11},{4,12},{5,13},{6,14},{7,15},{8,0},{9,1},... | collective-permute-start | bytes 393224 | tf_op jit(solution)/shard_map/ppermute | solution.py:23
  117.3 10.6 %collective-permute-start.29 = (bf16[128,512]{1,0:T(8,128)(2,1)S(1)}, bf16[128,512]{1,0:T(8,128)(2,1)S(1)}, u32[]{:S(2)}, u32[]{:S(2)}) collective-permute-start(bf16[128,512]{1,0:T(8,128)(2,1)S(1)} %get-tuple-element.104), channel_id=1, source_target_pairs={{0,12},{1,13},{2,14},{3,15},{4,8},{5,9},{6,10},{7,11},{8,4},{9,5},... | collective-permute-start | bytes 393224 | tf_op jit(solution)/shard_map/ppermute | solution.py:23

commit v5 on v4

--- a/solution.py
+++ b/solution.py
@@ -33,24 +33,46 @@
 
 
 def whole(shape):
-    return pl.BlockSpec(shape, lambda *_: (0,) * len(shape))
-
-
-def call(body, name, scalars, inputs, specs, outs, grid=(1,), out_specs=None, scratch=(), vmem=8):
+    return pl.BlockSpec(shape, lambda i: (0,) * len(shape))
+
+
+def position(span, heads):
+    me = lax.axis_index(AXIS)
+    plane, inner = me // span, me % span
+    core = me % 2
+    return (
+        plane,
+        core,
+        (me // 2) % 2,
+        me,
+        inner,
+        head_of(plane, heads),
+        (plane % 2 == core).astype(i32),
+    )
+
+
+def call(body, name, inputs, specs, outs, out_specs=None, scratch=(), vmem=8, flops=0):
     return pl.pallas_call(
         body,
         name=name,
-        grid_spec=pltpu.PrefetchScalarGridSpec(
-            num_scalar_prefetch=1,
-            grid=grid,
-            in_specs=specs,
-            out_specs=out_specs or [whole(o.shape) for o in outs],
-            scratch_shapes=list(scratch),
-        ),
+        grid=(1,),
+        in_specs=specs,
+        out_specs=out_specs or [whole(o.shape) for o in outs],
+        scratch_shapes=list(scratch),
         out_shape=list(outs),
-        cost_estimate=pl.CostEstimate(flops=0, bytes_accessed=0, transcendentals=0),
+        cost_estimate=pl.CostEstimate(flops=flops, bytes_accessed=0, transcendentals=0),
         compiler_params=pltpu.CompilerParams(vmem_limit_bytes=vmem * MIB),
-    )(scalars, *inputs)
+    )(*inputs)
+
+
+def fetch_small(sources, buffers, sem):
+    copies = [
+        pltpu.make_async_copy(source, to, sem.at[n])
+        for n, (source, to) in enumerate(zip(sources, buffers))
+    ]
+    for copy in copies:
+        copy.start()
+    return copies
 
 
 def rate_column(rates, mask, head):
@@ -59,17 +81,21 @@
     return -jnp.transpose(jnp.broadcast_to(row, (8, row.shape[1])))[:, 0:1]
 
 
-def pack_body(heads, where, rates, mask, views, keys, values, *refs):
+def pack_body(span, heads, rates, mask, views, keys, values, *refs):
     half = heads // 2
     target, refs = refs[:3], refs[3:]
     packed, sent = refs[:half], refs[half : half + heads]
-    value_s, pack_s, sent_s, in_sem, target_sem, out_sem = refs[half + heads :]
+    rates_s, mask_s, views_s, value_s, pack_s, sent_s, in_sem, target_sem, out_sem = refs[
+        half + heads :
+    ]
+    where = position(span, heads)
     rows, width = value_s.shape[1:]
     count = target[0].shape[0]
 
     def columns(head):
         return pl.ds(pl.multiple_of(head * width, width), width)
 
+    small = fetch_small((rates, mask, views), (rates_s, mask_s, views_s), in_sem.at[half])
     loads = []
     for j in range(half):
         head = (1 - where[1]) * half + j
@@ -88,16 +114,17 @@
                 )
             )
             rows_in[-1].start()
+    for copy in small:
+        copy.wait()
     row_at = lax.broadcasted_iota(i32, (TAG_ROWS, count), 0)
-    digits = jnp.where(
-        row_at == 0, views[...] // 256, jnp.where(row_at == 1, views[...] % 256, 0)
-    )
+    ids = views_s[...]
+    digits = jnp.where(row_at == 0, ids // 256, jnp.where(row_at == 1, ids % 256, 0))
     for step in range(heads):
         sent_s[step, pl.ds(3 * count, TAG_ROWS), :] = jnp.zeros((TAG_ROWS, width), bf16)
         sent_s[step, pl.ds(3 * count, TAG_ROWS), pl.ds(0, count)] = digits.astype(f32).astype(bf16)
     stores = []
     for j in range(half):
-        rate = rate_column(rates[...], mask[...], (1 - where[1]) * half + j)
+        rate = rate_column(rates_s[...], mask_s[...], (1 - where[1]) * half + j)
         loads[2 * j].wait()
         pack_s[j, 1] = (rate * value_s[j].astype(f32)).astype(bf16)
         loads[2 * j + 1].wait()
@@ -112,25 +139,25 @@
         store.wait()
 
 
-def pack(where, rates, mask, views, keys, values, target, heads, width):
+def pack(rates, mask, views, keys, values, target, span, heads, width):
     half, rows, count = heads // 2, keys.shape[0], views.shape[1]
     small = (rates, mask, views)
     anywhere = pl.BlockSpec(memory_space=pl.ANY)
     piece = (3 * count + TAG_ROWS, width)
     outs = call(
-        functools.partial(pack_body, heads),
+        functools.partial(pack_body, span, heads),
         "pack",
-        where,
         (*small, keys, values, *target),
-        [whole(x.shape) for x in small] + [anywhere] * 5,
+        [anywhere] * 8,
         [jax.ShapeDtypeStruct((2, rows, width), bf16)] * half
         + [jax.ShapeDtypeStruct(piece, bf16)] * heads,
         out_specs=[anywhere] * (half + heads),
         scratch=[
+            *[pltpu.VMEM(x.shape, x.dtype) for x in small],
             pltpu.VMEM((half, rows, width), bf16),
             pltpu.VMEM((half, 2, rows, width), bf16),
             pltpu.VMEM((heads, *piece), bf16),
-            pltpu.SemaphoreType.DMA((half, 2)),
+            pltpu.SemaphoreType.DMA((half + 1, 3)),
             pltpu.SemaphoreType.DMA((heads, 3)),
             pltpu.SemaphoreType.DMA((half + heads,)),
         ],
@@ -139,13 +166,15 @@
     return outs[:half], outs[half:]
 
 
-def head_grad_body(
-    lane, half, where, rates, mask, keys, values, other, weights, *refs
-):
-    sends, keeps = refs[:2], refs[2:4]
-    k_s, v_s, w_s, tg_s, hidden_s, gate_s, up_s, full, send_s, keep_s, in_sem, out_sem = refs[4:]
+def head_grad_body(span, heads, lane, rates, mask, keys, values, other, weights, *refs):
+    rates_s, mask_s, k_s, v_s, w_s, tg_s, hidden_s, gate_s, up_s, full, send_s, keep_s = refs[-14:-2]
+    in_sem, out_sem = refs[-2:]
+    outs = refs[:-14]
+    arrays = len(outs) // 2
+    sends, keeps = outs[:arrays], outs[arrays:]
     rows, width = v_s.shape
-    head = where[1] * half + lane
+    where = position(span, heads)
+    head = where[1] * (heads // 2) + lane
     cols = pl.ds(pl.multiple_of(head * width, width), width)
     upper, lower = pl.ds(0, rows), pl.ds(rows, rows)
     loads = [
@@ -159,7 +188,10 @@
     ]
     for load in loads:
         load.start()
-    rate = rate_column(rates[...], mask[...], head)
+    small = fetch_small((rates, mask), (rates_s, mask_s), in_sem.at[pl.ds(7, 2)])
+    for copy in small:
+        copy.wait()
+    rate = rate_column(rates_s[...], mask_s[...], head)
     chunk = 256
     for at in range(0, 2 * rows, chunk):
         span = pl.ds(at, chunk)
@@ -202,8 +234,12 @@
             send_s[g, i] = full[sent, :].astype(bf16)
             keep_s[g, i] = full[kept, :]
             stores += [
-                pltpu.make_async_copy(send_s.at[g, i], sends[g].at[i], out_sem.at[0, g, i]),
-                pltpu.make_async_copy(keep_s.at[g, i], keeps[g].at[i], out_sem.at[1, g, i]),
+                pltpu.make_async_copy(
+                    send_s.at[g, i], sends[g % arrays].at[g // arrays, i], out_sem.at[0, g, i]
+                ),
+                pltpu.make_async_copy(
+                    keep_s.at[g, i], keeps[g % arrays].at[g // arrays, i], out_sem.at[1, g, i]
+                ),
             ]
             stores[-2].start()
             stores[-1].start()
@@ -211,21 +247,23 @@
         store.wait()
 
 
-def head_grad(where, rates, mask, keys, values, other, weights, lane, half, width):
+def head_grad(rates, mask, keys, values, other, weights, span, heads, lane, width, arrays):
     rows = keys.shape[0]
     shape = (3, width // 4, width)
+    out = (2 // arrays, *shape)
     anywhere = pl.BlockSpec(memory_space=pl.ANY)
     in_hbm = pl.BlockSpec(memory_space=pltpu.HBM)
     both = pltpu.VMEM((2 * rows, width), bf16)
     outs = call(
-        functools.partial(head_grad_body, lane, half),
+        functools.partial(head_grad_body, span, heads, lane),
         "head_grad_%d" % lane,
-        where,
         (rates, mask, keys, values, other, weights),
-        [whole(rates.shape), whole(mask.shape), in_hbm, in_hbm, anywhere, in_hbm],
-        [jax.ShapeDtypeStruct(shape, bf16)] * 2 + [jax.ShapeDtypeStruct(shape, f32)] * 2,
-        out_specs=[anywhere] * 4,
+        [anywhere, anywhere, in_hbm, in_hbm, anywhere, in_hbm],
+        [jax.ShapeDtypeStruct(out, bf16)] * arrays + [jax.ShapeDtypeStruct(out, f32)] * arrays,
+        out_specs=[anywhere] * 2 * arrays,
         scratch=[
+            pltpu.VMEM(rates.shape, f32),
+            pltpu.VMEM(mask.shape, i32),
             both,
             pltpu.VMEM((rows, width), bf16),
             pltpu.VMEM((3, width, width), bf16),
@@ -236,20 +274,21 @@
             pltpu.VMEM((width, width), f32),
             pltpu.VMEM((2, *shape), bf16),
             pltpu.VMEM((2, *shape), f32),
-            pltpu.SemaphoreType.DMA((7,)),
+            pltpu.SemaphoreType.DMA((9,)),
             pltpu.SemaphoreType.DMA((2, 2, 3)),
         ],
         vmem=62,
     )
-    return outs[:2], outs[2:]
-
-
-def arrange_body(slots, span, where, *refs):
+    return outs[:arrays], outs[arrays:]
+
+
+def arrange_body(slots, span, *refs):
     out = refs[-1]
     pieces = []
     for n, at in slots:
         pieces.append(refs[n] if at is None else refs[n].at[at])
-    me, inner = where[3], where[4]
+    me = lax.axis_index(AXIS)
+    inner = me % span
     rows = (pieces[0].shape[0] - TAG_ROWS) // 3
     count = len(pieces)
     heads = count // span
@@ -292,11 +331,10 @@
         out[i] = totals[i].astype(bf16)
 
 
-def arrange(where, pieces, slots, span, heads, width):
+def arrange(pieces, slots, span, heads, width):
     return call(
         functools.partial(arrange_body, slots, span),
         "arrange",
-        where,
         tuple(pieces),
         [whole(x.shape) for x in pieces],
         [jax.ShapeDtypeStruct((3, heads * VIEW_ROWS, width), bf16)],
@@ -304,7 +342,7 @@
     )[0]
 
 
-def attend_body(where, rows, attended):
+def attend_body(rows, attended):
     width = rows.shape[2]
     for v in range(rows.shape[1] // VIEW_ROWS):
         at = pl.ds(v * VIEW_ROWS, VIEW_ROWS)
@@ -317,58 +355,126 @@
         attended[at, :] = jnp.dot(probs, rows[2, at, :], preferred_element_type=f32)
 
 
-def attend(where, rows):
+def attend(rows):
     return call(
         attend_body,
         "attend",
-        where,
         (rows,),
         [whole(rows.shape)],
         [jax.ShapeDtypeStruct(rows.shape[1:], f32)],
     )[0]
 
 
-def renew_body(where, keep, got, old, steps, fresh):
+def add_body(keep, got, total, send):
+    total[...] = keep[...] + got[...].astype(f32)
+    send[...] = total[...].astype(bf16)
+
+
+def add(keep, got):
+    return call(
+        add_body,
+        "add",
+        (keep, got),
+        [whole(keep.shape)] * 2,
+        [jax.ShapeDtypeStruct(keep.shape, t) for t in (f32, bf16)],
+        flops=9000000000,
+    )
+
+
+def hand_over_body(span, *refs):
+    upper = lax.axis_index(AXIS) // span // 2 == 1
+    sources, sends, keeps, total_s, got_s, sem = refs[:4], refs[4], refs[5], *refs[6:]
+
+    def fetch(first, second):
+        copies = []
+        for n, pair in enumerate((first, second)):
+            for i, (source, to) in enumerate(zip(pair, (total_s, got_s))):
+                copies.append(pltpu.make_async_copy(source, to.at[n], sem.at[n, i]))
+                copies[-1].start()
+        for copy in copies:
+            copy.wait()
+
+    @pl.when(upper)
+    def _():
+        fetch(sources[:2], sources[2:])
+
+    @pl.when(jnp.logical_not(upper))
+    def _():
+        fetch(sources[2:], sources[:2])
+
+    sends[...] = (total_s[0] + got_s[0].astype(f32)).astype(bf16)
+    keeps[...] = total_s[1] + got_s[1].astype(f32)
+
+
+def hand_over(low, high, span):
+    shape = low[0].shape
+    sources = (*low, *high)
+    return call(
+        functools.partial(hand_over_body, span),
+        "hand_over",
+        sources,
+        [pl.BlockSpec(memory_space=pl.ANY)] * 4,
+        [jax.ShapeDtypeStruct(shape, bf16), jax.ShapeDtypeStruct(shape, f32)],
+        scratch=[
+            pltpu.VMEM((2, *shape), f32),
+            pltpu.VMEM((2, *shape), bf16),
+            pltpu.SemaphoreType.DMA((2, 2)),
+        ],
+    )
+
+
+def renew_body(span, heads, keep, got, old, steps, *refs):
+    *earlier, fresh = refs
+    step = jnp.where(
+        lax.broadcasted_iota(i32, steps.shape, 1) == position(span, heads)[5], steps[...], 0.0
+    )
+    step = jnp.sum(step, axis=1, keepdims=True)
     total = keep[...] + got[...].astype(f32)
     scale = lax.rsqrt(jnp.mean(total * total, axis=-1, keepdims=True) + epsilon)
-    step = steps[where[5]]
-    fresh[...] = (old[...].astype(f32) - step * (total * scale)).astype(bf16)
-
-
-def renew(where, keep, got, old, steps):
+    new = (old[...].astype(f32) - step * (total * scale)).astype(bf16)
+    if earlier:
+        fresh[pl.ds(0, 1)] = earlier[0][...]
+        fresh[pl.ds(1, 1)] = new
+    else:
+        fresh[...] = new
+
+
+def renew(keep, got, old, steps, span, heads, *earlier):
+    shape = (keep.shape[0] + len(earlier), *keep.shape[1:])
+    inputs = (keep, got, old, steps, *earlier)
     return call(
-        renew_body,
-        "renew",
-        where,
-        (keep, got, old, steps),
-        [whole(keep.shape)] * 3 + [pl.BlockSpec(memory_space=pltpu.SMEM)],
-        [jax.ShapeDtypeStruct(keep.shape, bf16)],
+        functools.partial(renew_body, span, heads),
+        "renew_%d" % len(earlier),
+        inputs,
+        [whole(x.shape) for x in inputs],
+        [jax.ShapeDtypeStruct(shape, bf16)],
     )[0]
 
 
-def finish_body(where, rows, attended, *refs):
-    weights = refs[:8]
-    outs, full = refs[8:-1], refs[-1]
-    bit, is_owner = where[2], where[8]
-    quarter = weights[0].shape[1]
+def finish_body(span, heads, steps, rows, attended, *refs):
+    weights = refs[:4]
+    outs, full = refs[4:-1], refs[-1]
+    where = position(span, heads)
+    bit, is_owner = where[2], where[6]
+    quarter = weights[0].shape[2]
 
     def place(blocks):
-        for side in range(2):
+        for side, block in enumerate(blocks):
             half = bit if side == 0 else 1 - bit
             for g in range(2):
                 at = pl.ds(pl.multiple_of(half * 2 * quarter + g * quarter, quarter), quarter)
                 for i in range(3):
-                    full[i, at, :] = blocks[2 * side + g][i]
+                    full[i, at, :] = block[g, i]
 
     @pl.when(is_owner == 1)
     def _():
-        place(weights[:4])
+        place(weights[:2])
 
     @pl.when(is_owner == 0)
     def _():
-        place(weights[4:])
-
-    for step, out in enumerate(outs):
+        place(weights[2:])
+
+    for step, out in zip(steps, outs):
         at = pl.ds(pl.multiple_of((where[0] ^ step) * VIEW_ROWS, VIEW_ROWS), VIEW_ROWS)
         q = rows[0, at, :]
         pre_gate = jnp.dot(q, full[0], preferred_element_type=f32)
@@ -379,35 +485,34 @@
         out[...] = (fast * scale + attended[at, :]).astype(bf16)
 
 
-def finish(where, rows, attended, weights, heads):
+def finish(rows, attended, weights, span, heads, steps):
     width = rows.shape[2]
     inputs = (rows, attended, *weights)
     return call(
-        finish_body,
-        "finish",
-        where,
+        functools.partial(finish_body, span, heads, steps),
+        "finish_%d" % steps[0],
         inputs,
-        [pl.BlockSpec((1, *rows.shape[1:]), lambda i, w: (0, 0, 0))]
+        [pl.BlockSpec((1, *rows.shape[1:]), lambda i: (0, 0, 0))]
         + [whole(x.shape) for x in inputs[1:]],
-        [jax.ShapeDtypeStruct((VIEW_ROWS, width), bf16)] * heads,
+        [jax.ShapeDtypeStruct((VIEW_ROWS, width), bf16)] * len(steps),
         scratch=[pltpu.VMEM((3, width, width), bf16)],
         vmem=12,
     )
 
 
-def join_body(heads, width, where, *refs):
+def join_body(span, heads, width, *refs):
     out = refs[-1]
+    plane = lax.axis_index(AXIS) // span
     for step in range(heads):
-        head = head_of(where[0] ^ step, heads)
+        head = head_of(plane ^ step, heads)
         out[:, pl.ds(pl.multiple_of(head * width, width), width)] = refs[step][...]
 
 
-def join(where, blocks, heads, width):
+def join(blocks, span, heads, width):
     rows = blocks[0].shape[0]
     return call(
-        functools.partial(join_body, heads, width),
+        functools.partial(join_body, span, heads, width),
         "join",
-        where,
         tuple(blocks),
         [whole(x.shape) for x in blocks],
         [jax.ShapeDtypeStruct((rows, heads * width), bf16)],
@@ -441,27 +546,22 @@
     first = [bit_of(1) * 2 + g for g in range(2)]
     for b in inner_bits[1:]:
         first = [2 * f + bit_of(b) for f in first]
-    is_owner = (plane % 2 == core).astype(i32)
-    where = jnp.stack(
-        [plane, core, bit_of(1), me, inner, head_of(plane, heads), first[0], first[1], is_owner]
-    ).astype(i32)
 
     rates, mask = update_rates.T, update_mask[None, :]
-
-    turn = where
+    steps = step_sizes[None, :]
 
     others, sent = pack(
-        turn,
         rates,
         mask,
         target_views[None, :],
         update_keys,
         update_values,
         (target_queries, target_keys, target_values),
+        span,
         heads,
         width,
     )
-    turn = after(turn, sent[0])
+    turn = [sent[0]]
     others = [swap(x, 1) for x in others]
 
     outer_bits = list(reversed(inner_bits))
@@ -474,78 +574,80 @@
     spread(early, outer_bits)
     came = [swap(sent[step], step * span) for step in (1, 2)]
 
+    grad_inputs = (mask, update_keys, update_values)
     sends, keeps = head_grad(
-        turn, rates, mask, update_keys, update_values, others[0], fast_weights, 0, half, width
-    )
-    moved = [swap(sends[0], 2)]
-    turn = after(turn, sends[0], *early.values())
+        after(rates, *turn), *grad_inputs, others[0], fast_weights, span, heads, 0, width, 2
+    )
+    turn = [sends[0], *early.values()]
     spread(early, [0])
     more_sends, more_keeps = head_grad(
-        turn, rates, mask, update_keys, update_values, others[1], fast_weights, 1, half, width
-    )
-    turn = after(turn, more_sends[0], *came)
+        after(rates, *turn), *grad_inputs, others[1], fast_weights, span, heads, 1, width, 2
+    )
+    turn = [more_sends[0], *came]
     keeps = [*keeps, *more_keeps]
-    moved.append(swap(after(sends[1], more_sends[0]), 2))
-    moved.append(swap(after(more_sends[0], turn), 2))
-    came.append(swap(after(sent[3], turn), 3 * span))
+    moved = [
+        swap(sends[0], 2),
+        swap(after(sends[1], more_sends[0]), 2),
+        swap(after(more_sends[0], *turn[1:]), 2),
+    ]
+    came.append(swap(after(sent[3], *turn), 3 * span))
 
     def cut(pair, b, side):
-        rows = pair[0].shape[1] // 2
+        rows = pair[0].shape[2] // 2
         return sum(
-            lax.dynamic_slice_in_dim(x, side * rows, rows, 1).astype(f32) for x in pair
+            lax.dynamic_slice_in_dim(x, side * rows, rows, 2).astype(f32) for x in pair
         )
 
     sums = []
 
     def settle(n):
-        keep, got = keeps[n], after(moved[n], turn)
+        keep, got = keeps[n], after(moved[n], *turn)
         for b in inner_bits[1:]:
             send = cut((keep, got), b, 1 - bit_of(b)).astype(bf16)
             keep, got = cut((keep, got), b, bit_of(b)), swap(send, 1 << b)
-        total = keep + got.astype(f32)
-        send = total.astype(bf16)
-        sums.append((total, swap(send, span, lambda t: not matched(t))))
-        return after(turn, send)
+        total, send = add(keep, got)
+        sums.append((total, send))
+        if n >= 2:
+            both = swap(
+                jnp.concatenate([sums[n - 2][1], send]), span, lambda t: not matched(t)
+            )
+            sums[n - 2], sums[n] = (sums[n - 2][0], both[:1]), (total, both[1:])
+        return [send]
 
     turn = settle(0)
     turn = settle(1)
-    moved.append(swap(after(more_sends[1], turn), 2))
-    turn = after(turn, came[2], sums[0][1])
+    moved.append(swap(after(more_sends[1], *turn), 2))
+    turn += [came[2]]
     turn = settle(2)
-    turn = after(turn, sums[1][1])
     turn = settle(3)
-    late = {0: jnp.stack([after(x, turn) for x in came])}
+    late = {0: jnp.stack([after(x, *turn) for x in came])}
     spread(late, outer_bits)
 
     olds = [
         lax.dynamic_slice(
-            fast_weights, (where[5], 0, where[6 + g] * share, 0), (1, 3, share, width)
-        )[0]
+            fast_weights, (head_of(plane, heads), 0, first[g] * share, 0), (1, 3, share, width)
+        )
         for g in range(2)
     ]
-    upper = plane // 2 == 1
     held = []
     for g in range(2):
-        low, high = (after(sums[n][0], turn) + sums[n][1].astype(f32) for n in (g, 2 + g))
-        keep = jnp.where(upper, high, low)
-        send = jnp.where(upper, low, high).astype(bf16)
+        low = (after(sums[g][0], *turn), sums[g][1])
+        send, keep = hand_over(low, sums[2 + g], span)
         held.append((keep, swap(send, 2 * span, matched)))
-        turn = after(turn, send)
-    turn = after(turn, *early.values())
-    fresh, far = [], []
-    for g, (keep, got) in enumerate(held):
-        new = renew(turn, keep, got, olds[g], step_sizes)
-        turn = after(turn, new)
-        for b in reversed(inner_bits[1:]):
-            other = swap(new, 1 << b, matched)
-            new = jnp.where(
-                bit_of(b) == 1,
-                jnp.concatenate([other, new], axis=1),
-                jnp.concatenate([new, other], axis=1),
-            )
-        fresh.append(new)
-        far.append(swap(new, 2, matched))
-    late = {n: x if n == 0 else after(x, turn) for n, x in late.items()}
+        turn = [send]
+    turn += early.values()
+    fresh = renew(after(held[0][0], *turn), held[0][1], olds[0], steps, span, heads)
+    fresh = renew(*held[1], olds[1], steps, span, heads, fresh)
+    turn = [fresh]
+    for b in reversed(inner_bits[1:]):
+        other = swap(fresh, 1 << b, matched)
+        fresh = jnp.where(
+            bit_of(b) == 1,
+            jnp.concatenate([other, fresh], axis=2),
+            jnp.concatenate([fresh, other], axis=2),
+        )
+    far = swap(fresh, 2, matched)
+    late = {n: x if n == 0 else after(x, *turn) for n, x in late.items()}
     spread(late, [0])
 
     pieces, slots = [], {}
@@ -556,13 +658,18 @@
             slots[step * span + e] = (len(pieces), step - 1)
         pieces.append(late[e])
     slots = [slots[n] for n in range(count)]
-    rows = arrange(turn, pieces, slots, span, heads, width)
-    attended = attend(turn, rows)
-    far = [after(x, attended) for x in far]
-    near = [swap(x, 1, matched) for x in fresh + far]
-    blocks = finish(where, rows, attended, fresh + far + near, heads)
-    got = [swap(x, step * span) if step else x for step, x in enumerate(blocks)]
-    return join(where, got, heads, width)
+    rows = arrange([after(pieces[0], *turn), *pieces[1:]], slots, span, heads, width)
+    attended = attend(rows)
+    far = after(far, attended)
+    weights = [fresh, far, swap(fresh, 1, matched), swap(far, 1, matched)]
+    split = heads // 2
+    far_blocks = finish(rows, attended, weights, span, heads, tuple(range(split, heads)))
+    got = [swap(x, (split + n) * span) for n, x in enumerate(far_blocks)]
+    near_blocks = finish(
+        after(rows, far_blocks[0]), attended, weights, span, heads, tuple(range(split))
+    )
+    got = [swap(x, step * span) if step else x for step, x in enumerate(near_blocks)] + got
+    return join(got, span, heads, width)
 
 
 def solution(mesh):

time: 130 us -> 122 us (0.938)
  other arithmetic: 10.3 us -> 1.29 us
  waiting for transfers between devices: 35.2 us -> 40.8 us
  starting transfers between devices: 44.2 us -> 40.7 us
  Pallas kernels: 36.3 us -> 34.3 us
    ppermute x30 -> x25, waiting for transfers between devices: 35.2 us -> 40.8 us  [swap(): return lax.ppermute(value, AXIS, pairs)]
    select_n x2 -> x0, other arithmetic: 4.53 us -> none  [on_device(): keep = jnp.where(upper, high, low)]
    convert_element_type x4 -> x0, other arithmetic: 4.45 us -> none  [settle(): send = total.astype(bf16)]
    ppermute x30 -> x25, starting transfers between devices: 44.2 us -> 40.7 us  [swap(): return lax.ppermute(value, AXIS, pairs)]
    pallas_call x9 -> x16, Pallas kernels: 36.3 us -> 34.3 us  [call(): pl.pallas_call(body, name=name, grid=(1,), in_specs=specs, out_specs=out_...]
    unnamed x28 -> x20, local copies, waits for them, and re-layouts: 1.1 us -> 2.74 us
  transfers between devices with their start and end apart: 30 -> 25, of which waited for: 11 -> 9; matrix products, arithmetic and copies ran while one was open for 9% -> 2% of each run, Pallas kernels for 21% -> 24%
where the time goes in v5:
time: 122 us
  waiting for transfers between devices  40.8 us (33%)
  starting transfers between devices  40.7 us (33%)
  Pallas kernels  34.3 us (28%)
  local copies, waits for them, and re-layouts  4.06 us (3%)
  other arithmetic  1.29 us (1%)
    ppermute x25, waiting for transfers between devices, swap(): return lax.ppermute(value, AXIS, pairs)  40.8 us
    ppermute x25, starting transfers between devices, swap(): return lax.ppermute(value, AXIS, pairs)  40.7 us
    pallas_call x16, Pallas kernels, call(): pl.pallas_call(body, name=name, grid=(1,), in_specs=specs, out_specs=out_...  34.3 us
    unnamed x20, local copies, waits for them, and re-layouts  2.74 us
  transfers between devices with their start and end apart: 25, of which 9 were waited for; matrix products, arithmetic and copies ran while one was open for 2% of the time, Pallas kernels for 24%

profile of v5, /device:TPU:0, one launch (start us, length us, event | category | flops | bytes accessed | tf_op | source)
XLA Modules:
  0.0 121.5 jit_solution(12872261957235385217)
XLA Ops:
  0.0 3.8 %pack.1 = (bf16[2,512,512]{2,1,0:T(8,128)(2,1)}, bf16[2,512,512]{2,1,0:T(8,128)(2,1)}, bf16[400,512]{1,0:T(8,128)(2,1)}, bf16[400,512]{1,0:T(8,128)(2,1)}, bf16[...) custom-call(f32[4,512]{1,0:T(4,128)} %bitcast.11, s32[1,512]{1,0:T(1,128)} %bitcast.14, s32[1,128]{1,0:T(1,128)} %bitcast.17, ...), custom_call_target="tpu_custom_call" | custom-call | tf_op jit(solution)/shard_map/pack/pallas_call | solution.py:55
  3.9 0.5 collective-permute-start
  4.4 0.1 collective-permute-start.2
  4.5 2.9 %collective-permute-start.1 = (bf16[400,512]{1,0:T(8,128)(2,1)}, bf16[400,512]{1,0:T(8,128)(2,1)}, u32[]{:S(2)}, u32[]{:S(2)}) collective-permute-start(bf16[400,512]{1,0:T(8,128)(2,1)} %get-tuple-element.94.refs_0_), channel_id=1, source_target_pairs={{0,2},{1,3},{2,0},{3,1},{4,6},{5,7},{6,4},{7,5},{8,10},{9,11},{10,... | collective-permute-start | bytes 1228808 | tf_op jit(solution)/shard_map/ppermute | solution.py:23
  7.4 1.6 %collective-permute-start.5 = (bf16[400,512]{1,0:T(8,128)(2,1)}, bf16[400,512]{1,0:T(8,128)(2,1)S(1)}, u32[]{:S(2)}, u32[]{:S(2)}) collective-permute-start(bf16[400,512]{1,0:T(8,128)(2,1)} %get-tuple-element.66), channel_id=1, source_target_pairs={{0,4},{1,5},{2,6},{3,7},{4,0},{5,1},{6,2},{7,3},{8,12},{9,13},{10,... | collective-permute-start | bytes 1228808 | tf_op jit(solution)/shard_map/ppermute | solution.py:23
  9.0 2.6 %collective-permute-start.6 = (bf16[400,512]{1,0:T(8,128)(2,1)}, bf16[400,512]{1,0:T(8,128)(2,1)}, u32[]{:S(2)}, u32[]{:S(2)}) collective-permute-start(bf16[400,512]{1,0:T(8,128)(2,1)} %get-tuple-element.67), channel_id=1, source_target_pairs={{0,8},{1,9},{2,10},{3,11},{4,12},{5,13},{6,14},{7,15},{8,0},{9,1},... | collective-permute-start | bytes 1228808 | tf_op jit(solution)/shard_map/ppermute | solution.py:23
  11.6 1.0 copy-done.7
  12.5 7.8 %head_grad_0.1 = (bf16[1,3,128,512]{3,2,1,0:T(8,128)(2,1)}, bf16[1,3,128,512]{3,2,1,0:T(8,128)(2,1)}, f32[1,3,128,512]{3,2,1,0:T(8,128)}, f32[1,3,128,512]{3,2,1,0:T(8,128)}) custom-call(f32[4,512]{1,0:T(4,128)} %bitcast.12, s32[1,512]{1,0:T(1,128)} %bitcast.15, bf16[512,2048]{1,0:T(8,128)(2,1)} %keys.5, bf16[512,2048]{1,0:T(8,128)(2,1)} %values.5, ...), custom_call_target="tpu_custom_call" | custom-call | tf_op jit(solution)/shard_map/head_grad_0/pallas_call | solution.py:55
  20.4 0.6 collective-permute-start.4
  20.9 0.0 collective-permute-done.1.refs_4_
  20.9 7.8 %head_grad_1.1 = (bf16[1,3,128,512]{3,2,1,0:T(8,128)(2,1)}, bf16[1,3,128,512]{3,2,1,0:T(8,128)(2,1)}, f32[1,3,128,512]{3,2,1,0:T(8,128)}, f32[1,3,128,512]{3,2,1,0:T(8,128)}) custom-call(f32[4,512]{1,0:T(4,128)} %bitcast.13, s32[1,512]{1,0:T(1,128)} %bitcast.16, bf16[512,2048]{1,0:T(8,128)(2,1)} %keys.5, bf16[512,2048]{1,0:T(8,128)(2,1)} %values.5, ...), custom_call_target="tpu_custom_call" | custom-call | tf_op jit(solution)/shard_map/head_grad_1/pallas_call | solution.py:55
  28.7 1.6 %collective-permute-start.3 = (bf16[1,3,128,512]{3,2,1,0:T(8,128)(2,1)S(1)}, bf16[1,3,128,512]{3,2,1,0:T(8,128)(2,1)S(1)}, u32[]{:S(2)}, u32[]{:S(2)}) collective-permute-start(bf16[1,3,128,512]{3,2,1,0:T(8,128)(2,1)S(1)} %copy-done.9), channel_id=1, source_target_pairs={{0,2},{1,3},{2,0},{3,1},{4,6},{5,7},{6,4},{7,5},{8,10},{9,11},{10,... | collective-permute-start | bytes 1179656 | tf_op jit(solution)/shard_map/ppermute | solution.py:23
  30.3 0.0 collective-permute-done.6
  30.3 0.5 collective-permute-start.8
  30.8 2.1 %collective-permute-start.9 = (bf16[400,512]{1,0:T(8,128)(2,1)}, bf16[400,512]{1,0:T(8,128)(2,1)S(1)}, u32[]{:S(2)}, u32[]{:S(2)}) collective-permute-start(bf16[400,512]{1,0:T(8,128)(2,1)} %get-tuple-element.80), channel_id=1, source_target_pairs={{0,12},{1,13},{2,14},{3,15},{4,8},{5,9},{6,10},{7,11},{8,4},{9,5},... | collective-permute-start | bytes 1228808 | tf_op jit(solution)/shard_map/ppermute | solution.py:23
  32.9 0.1 add.34
  33.0 7.8 %collective-permute-done.3.got = bf16[1,3,128,512]{3,2,1,0:T(8,128)(2,1)S(1)} collective-permute-done((bf16[1,3,128,512]{3,2,1,0:T(8,128)(2,1)S(1)}, bf16[1,3,128,512]{3,2,1,0:T(8,128)(2,1)S(1)}, u32[]{:S(2)}, u32[]{:S(2)}) %collective-permute-start.3) | collective-permute-done | bytes 393248 | tf_op jit(solution)/shard_map/ppermute | solution.py:23
  40.9 0.1 add.35
  41.0 0.8 copy-done.8
  41.8 1.5 %collective-permute-start.7 = (bf16[1,3,128,512]{3,2,1,0:T(8,128)(2,1)S(1)}, bf16[1,3,128,512]{3,2,1,0:T(8,128)(2,1)S(1)}, u32[]{:S(2)}, u32[]{:S(2)}) collective-permute-start(bf16[1,3,128,512]{3,2,1,0:T(8,128)(2,1)S(1)} %copy-done.8), channel_id=1, source_target_pairs={{0,2},{1,3},{2,0},{3,1},{4,6},{5,7},{6,4},{7,5},{8,10},{9,11},{10,... | collective-permute-start | bytes 1179656 | tf_op jit(solution)/shard_map/ppermute | solution.py:23
  43.4 5.9 %collective-permute-done.8.got = bf16[1,3,128,512]{3,2,1,0:T(8,128)(2,1)S(1)} collective-permute-done((bf16[1,3,128,512]{3,2,1,0:T(8,128)(2,1)}, bf16[1,3,128,512]{3,2,1,0:T(8,128)(2,1)S(1)}, u32[]{:S(2)}, u32[]{:S(2)}) %collective-permute-start.8) | collective-permute-done | bytes 393248 | tf_op jit(solution)/shard_map/ppermute | solution.py:23
  49.3 0.1 add.36
  49.4 0.1 pad_maximum_fusion.1
  49.5 1.4 %collective-permute-start.10 = (bf16[2,3,128,512]{3,2,1,0:T(8,128)(2,1)S(1)}, bf16[2,3,128,512]{3,2,1,0:T(8,128)(2,1)S(1)}, u32[]{:S(2)}, u32[]{:S(2)}) collective-permute-start(bf16[2,3,128,512]{3,2,1,0:T(8,128)(2,1)S(1)} %pad_maximum_fusion.1), channel_id=1, source_target_pairs={{1,5},{3,7},{4,0},{6,2},{9,13},{11,15},{12,8},{14,10},{17,21},{19,... | collective-permute-start | bytes 2359304 | tf_op jit(solution)/shard_map/ppermute | solution.py:23
  51.0 5.2 %collective-permute-done.7.got = bf16[1,3,128,512]{3,2,1,0:T(8,128)(2,1)S(1)} collective-permute-done((bf16[1,3,128,512]{3,2,1,0:T(8,128)(2,1)S(1)}, bf16[1,3,128,512]{3,2,1,0:T(8,128)(2,1)S(1)}, u32[]{:S(2)}, u32[]{:S(2)}) %collective-permute-start.7) | collective-permute-done | bytes 393248 | tf_op jit(solution)/shard_map/ppermute | solution.py:23
  56.2 0.1 add.37
  56.3 0.1 pad_maximum_fusion.2
  56.4 1.3 %collective-permute-start.11 = (bf16[2,3,128,512]{3,2,1,0:T(8,128)(2,1)S(1)}, bf16[2,3,128,512]{3,2,1,0:T(8,128)(2,1)S(1)}, u32[]{:S(2)}, u32[]{:S(2)}) collective-permute-start(bf16[2,3,128,512]{3,2,1,0:T(8,128)(2,1)S(1)} %pad_maximum_fusion.2), channel_id=1, source_target_pairs={{1,5},{3,7},{4,0},{6,2},{9,13},{11,15},{12,8},{14,10},{17,21},{19,... | collective-permute-start | bytes 2359304 | tf_op jit(solution)/shard_map/ppermute | solution.py:23
  57.7 1.1 pad_maximum_fusion.refs_1_
  58.9 1.0 collective-permute-start.17
  59.9 0.0 collective-permute-start.13
  59.9 0.5 collective-permute-start.14
  60.4 3.2 %collective-permute-done.10 = bf16[2,3,128,512]{3,2,1,0:T(8,128)(2,1)S(1)} collective-permute-done((bf16[2,3,128,512]{3,2,1,0:T(8,128)(2,1)S(1)}, bf16[2,3,128,512]{3,2,1,0:T(8,128)(2,1)S(1)}, u32[]{:S(2)}, u32[]{:S(2)}) %collective-permute-start.10) | collective-permute-done | bytes 786464 | tf_op jit(solution)/shard_map/ppermute | solution.py:23
  63.5 0.1 fusion.1
  63.6 1.4 %hand_over.2 = (bf16[1,3,128,512]{3,2,1,0:T(8,128)(2,1)}, f32[1,3,128,512]{3,2,1,0:T(8,128)S(1)}) custom-call(f32[1,3,128,512]{3,2,1,0:T(8,128)S(1)} %get-tuple-element.85.refs_0_, bf16[1,3,128,512]{3,2,1,0:T(8,128)(2,1)S(1)} %get-tuple-element.110.refs_1_, f32[1,3,128,512]{3,2,1,0:T(8,128)S(1)} %get-tuple-element.86.refs_2_, ...), custom_call_target="tpu_custom_call" | custom-call | tf_op jit(solution)/shard_map/hand_over/pallas_call | solution.py:55
  65.0 4.1 %collective-permute-start.15 = (bf16[1,3,128,512]{3,2,1,0:T(8,128)(2,1)}, bf16[1,3,128,512]{3,2,1,0:T(8,128)(2,1)}, u32[]{:S(2)}, u32[]{:S(2)}) collective-permute-start(bf16[1,3,128,512]{3,2,1,0:T(8,128)(2,1)} %get-tuple-element.87), channel_id=1, source_target_pairs={{0,8},{2,10},{5,13},{7,15},{8,0},{10,2},{13,5},{15,7},{16,24},{18,... | collective-permute-start | bytes 1179656 | tf_op jit(solution)/shard_map/ppermute | solution.py:23
  69.0 3.4 %collective-permute-done.11 = bf16[2,3,128,512]{3,2,1,0:T(8,128)(2,1)S(1)} collective-permute-done((bf16[2,3,128,512]{3,2,1,0:T(8,128)(2,1)S(1)}, bf16[2,3,128,512]{3,2,1,0:T(8,128)(2,1)S(1)}, u32[]{:S(2)}, u32[]{:S(2)}) %collective-permute-start.11) | collective-permute-done | bytes 786464 | tf_op jit(solution)/shard_map/ppermute | solution.py:23
  72.4 0.1 fusion
  72.5 1.4 %hand_over.3 = (bf16[1,3,128,512]{3,2,1,0:T(8,128)(2,1)}, f32[1,3,128,512]{3,2,1,0:T(8,128)S(1)}) custom-call(f32[1,3,128,512]{3,2,1,0:T(8,128)S(1)} %get-tuple-element.88.refs_0_, bf16[1,3,128,512]{3,2,1,0:T(8,128)(2,1)S(1)} %get-tuple-element.108.refs_1_, f32[1,3,128,512]{3,2,1,0:T(8,128)S(1)} %get-tuple-element.89.refs_2_, ...), custom_call_target="tpu_custom_call" | custom-call | tf_op jit(solution)/shard_map/hand_over/pallas_call | solution.py:55
  73.9 0.9 copy-done
  74.8 7.9 %collective-permute-start.12 = (bf16[1,3,128,512]{3,2,1,0:T(8,128)(2,1)}, bf16[1,3,128,512]{3,2,1,0:T(8,128)(2,1)}, u32[]{:S(2)}, u32[]{:S(2)}) collective-permute-start(bf16[1,3,128,512]{3,2,1,0:T(8,128)(2,1)} %get-tuple-element.91), channel_id=1, source_target_pairs={{0,8},{2,10},{5,13},{7,15},{8,0},{10,2},{13,5},{15,7},{16,24},{18,... | collective-permute-start | bytes 1179656 | tf_op jit(solution)/shard_map/ppermute | solution.py:23
  82.7 1.2 constant_dynamic-slice_fusion
  84.0 0.1 collective-permute-start.16
  84.0 0.0 collective-permute-done.14.refs_6_
  84.1 1.3 %renew_0.1.refs_0_ = bf16[1,3,128,512]{3,2,1,0:T(8,128)(2,1)S(1)} custom-call(f32[1,3,128,512]{3,2,1,0:T(8,128)S(1)} %get-tuple-element.93.keep, bf16[1,3,128,512]{3,2,1,0:T(8,128)(2,1)} %collective-permute-done.15.got, bf16[1,3,128,512]{3,2,1,0:T(8,128)(2,1)S(1)} %get-tuple-element.105.old, f32[1,4]{1,0:T(1,128)S(1)} %bitcast.7), custom_call_target="tpu_custom_call" | custom-call | tf_op jit(solution)/shard_map/renew_0/pallas_call | solution.py:55
  85.4 3.1 %collective-permute-done.12.got = bf16[1,3,128,512]{3,2,1,0:T(8,128)(2,1)} collective-permute-done((bf16[1,3,128,512]{3,2,1,0:T(8,128)(2,1)}, bf16[1,3,128,512]{3,2,1,0:T(8,128)(2,1)}, u32[]{:S(2)}, u32[]{:S(2)}) %collective-permute-start.12) | collective-permute-done | bytes 393248 | tf_op jit(solution)/shard_map/ppermute | solution.py:23
  88.6 1.3 %renew_1.1.refs_0_ = bf16[2,3,128,512]{3,2,1,0:T(8,128)(2,1)S(1)} custom-call(f32[1,3,128,512]{3,2,1,0:T(8,128)S(1)} %copy-done.1, bf16[1,3,128,512]{3,2,1,0:T(8,128)(2,1)} %collective-permute-done.12.got, bf16[1,3,128,512]{3,2,1,0:T(8,128)(2,1)S(1)} %get-tuple-element.106.old, f32[1,4]{1,0:T(1,128)S(1)} %bitcast.8, bf16[1,3,128,512]{3,2,1,0:T(8,128)(2,1)S(1)} %renew_0.1.refs_0_), custom_call_target="tpu_custom_call" | custom-call | tf_op jit(solution)/shard_map/renew_1/pallas_call | solution.py:55
  89.9 0.0 collective-permute-done.17.refs_5_
  89.9 0.1 collective-permute-start.18
  90.0 3.1 %collective-permute-start.19 = (bf16[2,3,128,512]{3,2,1,0:T(8,128)(2,1)S(1)}, bf16[2,3,128,512]{3,2,1,0:T(8,128)(2,1)S(1)}, u32[]{:S(2)}, u32[]{:S(2)}) collective-permute-start(bf16[2,3,128,512]{3,2,1,0:T(8,128)(2,1)S(1)} %renew_1.1.refs_0_), channel_id=1, source_target_pairs={{0,2},{2,0},{5,7},{7,5},{8,10},{10,8},{13,15},{15,13},{16,18},{18,... | collective-permute-start | bytes 2359304 | tf_op jit(solution)/shard_map/ppermute | solution.py:23
  93.1 1.3 %collective-permute-start.20 = (bf16[2,3,128,512]{3,2,1,0:T(8,128)(2,1)S(1)}, bf16[2,3,128,512]{3,2,1,0:T(8,128)(2,1)S(1)}, u32[]{:S(2)}, u32[]{:S(2)}) collective-permute-start(bf16[2,3,128,512]{3,2,1,0:T(8,128)(2,1)S(1)} %renew_1.1.refs_0_), channel_id=1, source_target_pairs={{0,1},{2,3},{5,4},{7,6},{8,9},{10,11},{13,12},{15,14},{16,17},{18,... | collective-permute-start | bytes 2359304 | tf_op jit(solution)/shard_map/ppermute | solution.py:23
  94.5 0.0 collective-permute-done.18.refs_7_
  94.5 5.0 %arrange.1.rows = bf16[3,512,512]{2,1,0:T(8,128)(2,1)S(1)} custom-call(bf16[400,512]{1,0:T(8,128)(2,1)} %get-tuple-element.94.refs_0_, bf16[3,400,512]{2,1,0:T(8,128)(2,1)S(1)} %pad_maximum_fusion.refs_1_, bf16[400,512]{1,0:T(8,128)(2,1)} %collective-permute-done.13.refs_2_, bf16[3,400,512]{2,1,0:T(8,128)(2,1)S(1)} %collective-permute-done.16.refs_3_, ...), custom_call_target="tpu_custom_call" | custom-call | tf_op jit(solution)/shard_map/arrange/pallas_call | solution.py:55
  99.5 1.2 attend.1.attended
  100.6 3.2 %collective-permute-done.19.refs_1_ = bf16[2,3,128,512]{3,2,1,0:T(8,128)(2,1)S(1)} collective-permute-done((bf16[2,3,128,512]{3,2,1,0:T(8,128)(2,1)S(1)}, bf16[2,3,128,512]{3,2,1,0:T(8,128)(2,1)S(1)}, u32[]{:S(2)}, u32[]{:S(2)}) %collective-permute-start.19) | collective-permute-done | bytes 786464 | tf_op jit(solution)/shard_map/ppermute | solution.py:23
  103.8 1.3 %collective-permute-start.21 = (bf16[2,3,128,512]{3,2,1,0:T(8,128)(2,1)S(1)}, bf16[2,3,128,512]{3,2,1,0:T(8,128)(2,1)S(1)}, u32[]{:S(2)}, u32[]{:S(2)}) collective-permute-start(bf16[2,3,128,512]{3,2,1,0:T(8,128)(2,1)S(1)} %collective-permute-done.19.refs_1_), channel_id=1, source_target_pairs={{0,1},{2,3},{5,4},{7,6},{8,9},{10,11},{13,12},{15,14},{16,17},{18,... | collective-permute-start | bytes 2359304 | tf_op jit(solution)/shard_map/ppermute | solution.py:23
  105.2 1.8 %collective-permute-done.21.refs_3_ = bf16[2,3,128,512]{3,2,1,0:T(8,128)(2,1)S(1)} collective-permute-done((bf16[2,3,128,512]{3,2,1,0:T(8,128)(2,1)S(1)}, bf16[2,3,128,512]{3,2,1,0:T(8,128)(2,1)S(1)}, u32[]{:S(2)}, u32[]{:S(2)}) %collective-permute-start.21) | collective-permute-done | bytes 786464 | tf_op jit(solution)/shard_map/ppermute | solution.py:23
  107.0 1.0 finish_2.1
  108.0 3.0 %collective-permute-start.23 = (bf16[128,512]{1,0:T(8,128)(2,1)S(1)}, bf16[128,512]{1,0:T(8,128)(2,1)S(1)}, u32[]{:S(2)}, u32[]{:S(2)}) collective-permute-start(bf16[128,512]{1,0:T(8,128)(2,1)S(1)} %get-tuple-element.100), channel_id=1, source_target_pairs={{0,8},{1,9},{2,10},{3,11},{4,12},{5,13},{6,14},{7,15},{8,0},{9,1},... | collective-permute-start | bytes 393224 | tf_op jit(solution)/shard_map/ppermute | solution.py:23
  111.0 1.0 finish_0.1
  112.0 0.1 collective-permute-start.22
  112.1 1.5 %collective-permute-start.24 = (bf16[128,512]{1,0:T(8,128)(2,1)S(1)}, bf16[128,512]{1,0:T(8,128)(2,1)S(1)}, u32[]{:S(2)}, u32[]{:S(2)}) collective-permute-start(bf16[128,512]{1,0:T(8,128)(2,1)S(1)} %get-tuple-element.104), channel_id=1, source_target_pairs={{0,12},{1,13},{2,14},{3,15},{4,8},{5,9},{6,10},{7,11},{8,4},{9,5},... | collective-permute-start | bytes 393224 | tf_op jit(solution)/shard_map/ppermute | solution.py:23
  113.6 7.1 %collective-permute-done.22.refs_1_ = bf16[128,512]{1,0:T(8,128)(2,1)S(1)} collective-permute-done((bf16[128,512]{1,0:T(8,128)(2,1)S(1)}, bf16[128,512]{1,0:T(8,128)(2,1)S(1)}, u32[]{:S(2)}, u32[]{:S(2)}) %collective-permute-start.22) | collective-permute-done | bytes 131104 | tf_op jit(solution)/shard_map/ppermute | solution.py:23
  120.7 0.9 join.1
  (28 shorter events, 0.1 us)
Async XLA Ops:
  3.9 7.7 %collective-permute-start = (bf16[2,512,512]{2,1,0:T(8,128)(2,1)}, bf16[2,512,512]{2,1,0:T(8,128)(2,1)S(1)}, u32[]{:S(2)}, u32[]{:S(2)}) collective-permute-start(bf16[2,512,512]{2,1,0:T(8,128)(2,1)} %get-tuple-element.57), channel_id=1, source_target_pairs={{0,1},{1,0},{2,3},{3,2},{4,5},{5,4},{6,7},{7,6},{8,9},{9,8},{10,11... | collective-permute-start | bytes 3145736 | tf_op jit(solution)/shard_map/ppermute | solution.py:23
  4.4 16.6 %collective-permute-start.2 = (bf16[2,512,512]{2,1,0:T(8,128)(2,1)}, bf16[2,512,512]{2,1,0:T(8,128)(2,1)}, u32[]{:S(2)}, u32[]{:S(2)}) collective-permute-start(bf16[2,512,512]{2,1,0:T(8,128)(2,1)} %get-tuple-element.62), channel_id=1, source_target_pairs={{0,1},{1,0},{2,3},{3,2},{4,5},{5,4},{6,7},{7,6},{8,9},{9,8},{10,11... | collective-permute-start | bytes 3145736 | tf_op jit(solution)/shard_map/ppermute | solution.py:23
  4.5 16.5 %collective-permute-start.1 = (bf16[400,512]{1,0:T(8,128)(2,1)}, bf16[400,512]{1,0:T(8,128)(2,1)}, u32[]{:S(2)}, u32[]{:S(2)}) collective-permute-start(bf16[400,512]{1,0:T(8,128)(2,1)} %get-tuple-element.94.refs_0_), channel_id=1, source_target_pairs={{0,2},{1,3},{2,0},{3,1},{4,6},{5,7},{6,4},{7,5},{8,10},{9,11},{10,... | collective-permute-start | bytes 1228808 | tf_op jit(solution)/shard_map/ppermute | solution.py:23
  7.4 22.9 %collective-permute-start.5 = (bf16[400,512]{1,0:T(8,128)(2,1)}, bf16[400,512]{1,0:T(8,128)(2,1)S(1)}, u32[]{:S(2)}, u32[]{:S(2)}) collective-permute-start(bf16[400,512]{1,0:T(8,128)(2,1)} %get-tuple-element.66), channel_id=1, source_target_pairs={{0,4},{1,5},{2,6},{3,7},{4,0},{5,1},{6,2},{7,3},{8,12},{9,13},{10,... | collective-permute-start | bytes 1228808 | tf_op jit(solution)/shard_map/ppermute | solution.py:23
  9.0 21.3 %collective-permute-start.6 = (bf16[400,512]{1,0:T(8,128)(2,1)}, bf16[400,512]{1,0:T(8,128)(2,1)}, u32[]{:S(2)}, u32[]{:S(2)}) collective-permute-start(bf16[400,512]{1,0:T(8,128)(2,1)} %get-tuple-element.67), channel_id=1, source_target_pairs={{0,8},{1,9},{2,10},{3,11},{4,12},{5,13},{6,14},{7,15},{8,0},{9,1},... | collective-permute-start | bytes 1228808 | tf_op jit(solution)/shard_map/ppermute | solution.py:23
  11.6 1.0 copy-start.7
  20.3 8.4 %copy-start.9 = (bf16[1,3,128,512]{3,2,1,0:T(8,128)(2,1)S(1)}, bf16[1,3,128,512]{3,2,1,0:T(8,128)(2,1)}, u32[]{:S(2)}) copy-start(bf16[1,3,128,512]{3,2,1,0:T(8,128)(2,1)} %get-tuple-element.64) | copy-start | bytes 1179652
  20.4 12.5 %copy-start.6 = (f32[1,3,128,512]{3,2,1,0:T(8,128)S(1)}, f32[1,3,128,512]{3,2,1,0:T(8,128)}, u32[]{:S(2)}) copy-start(f32[1,3,128,512]{3,2,1,0:T(8,128)} %get-tuple-element.65.keep) | copy-start | bytes 2359300
  20.4 12.5 %collective-permute-start.4 = (bf16[1,3,128,512]{3,2,1,0:T(8,128)(2,1)}, bf16[1,3,128,512]{3,2,1,0:T(8,128)(2,1)S(1)}, u32[]{:S(2)}, u32[]{:S(2)}) collective-permute-start(bf16[1,3,128,512]{3,2,1,0:T(8,128)(2,1)} %get-tuple-element.60), channel_id=1, source_target_pairs={{0,2},{1,3},{2,0},{3,1},{4,6},{5,7},{6,4},{7,5},{8,10},{9,11},{10,... | collective-permute-start | bytes 1179656 | tf_op jit(solution)/shard_map/ppermute | solution.py:23
  28.7 12.1 %collective-permute-start.3 = (bf16[1,3,128,512]{3,2,1,0:T(8,128)(2,1)S(1)}, bf16[1,3,128,512]{3,2,1,0:T(8,128)(2,1)S(1)}, u32[]{:S(2)}, u32[]{:S(2)}) collective-permute-start(bf16[1,3,128,512]{3,2,1,0:T(8,128)(2,1)S(1)} %copy-done.9), channel_id=1, source_target_pairs={{0,2},{1,3},{2,0},{3,1},{4,6},{5,7},{6,4},{7,5},{8,10},{9,11},{10,... | collective-permute-start | bytes 1179656 | tf_op jit(solution)/shard_map/ppermute | solution.py:23
  30.3 19.0 %collective-permute-start.8 = (bf16[1,3,128,512]{3,2,1,0:T(8,128)(2,1)}, bf16[1,3,128,512]{3,2,1,0:T(8,128)(2,1)S(1)}, u32[]{:S(2)}, u32[]{:S(2)}) collective-permute-start(bf16[1,3,128,512]{3,2,1,0:T(8,128)(2,1)} %get-tuple-element.78), channel_id=1, source_target_pairs={{0,2},{1,3},{2,0},{3,1},{4,6},{5,7},{6,4},{7,5},{8,10},{9,11},{10,... | collective-permute-start | bytes 1179656 | tf_op jit(solution)/shard_map/ppermute | solution.py:23
  30.8 18.4 %collective-permute-start.9 = (bf16[400,512]{1,0:T(8,128)(2,1)}, bf16[400,512]{1,0:T(8,128)(2,1)S(1)}, u32[]{:S(2)}, u32[]{:S(2)}) collective-permute-start(bf16[400,512]{1,0:T(8,128)(2,1)} %get-tuple-element.80), channel_id=1, source_target_pairs={{0,12},{1,13},{2,14},{3,15},{4,8},{5,9},{6,10},{7,11},{8,4},{9,5},... | collective-permute-start | bytes 1228808 | tf_op jit(solution)/shard_map/ppermute | solution.py:23
  32.9 8.0 %copy-start.5 = (f32[1,3,128,512]{3,2,1,0:T(8,128)S(1)}, f32[1,3,128,512]{3,2,1,0:T(8,128)}, u32[]{:S(2)}) copy-start(f32[1,3,128,512]{3,2,1,0:T(8,128)} %get-tuple-element.58.keep) | copy-start | bytes 2359300
  40.8 1.0 copy-start.8
  40.9 8.4 %copy-start.4 = (f32[1,3,128,512]{3,2,1,0:T(8,128)S(1)}, f32[1,3,128,512]{3,2,1,0:T(8,128)}, u32[]{:S(2)}) copy-start(f32[1,3,128,512]{3,2,1,0:T(8,128)} %get-tuple-element.77.keep) | copy-start | bytes 2359300
  41.8 14.3 %collective-permute-start.7 = (bf16[1,3,128,512]{3,2,1,0:T(8,128)(2,1)S(1)}, bf16[1,3,128,512]{3,2,1,0:T(8,128)(2,1)S(1)}, u32[]{:S(2)}, u32[]{:S(2)}) collective-permute-start(bf16[1,3,128,512]{3,2,1,0:T(8,128)(2,1)S(1)} %copy-done.8), channel_id=1, source_target_pairs={{0,2},{1,3},{2,0},{3,1},{4,6},{5,7},{6,4},{7,5},{8,10},{9,11},{10,... | collective-permute-start | bytes 1179656 | tf_op jit(solution)/shard_map/ppermute | solution.py:23
  49.4 6.7 %copy-start.3 = (f32[1,3,128,512]{3,2,1,0:T(8,128)S(1)}, f32[1,3,128,512]{3,2,1,0:T(8,128)}, u32[]{:S(2)}) copy-start(f32[1,3,128,512]{3,2,1,0:T(8,128)} %get-tuple-element.73.keep) | copy-start | bytes 2359300
  49.5 14.0 %collective-permute-start.10 = (bf16[2,3,128,512]{3,2,1,0:T(8,128)(2,1)S(1)}, bf16[2,3,128,512]{3,2,1,0:T(8,128)(2,1)S(1)}, u32[]{:S(2)}, u32[]{:S(2)}) collective-permute-start(bf16[2,3,128,512]{3,2,1,0:T(8,128)(2,1)S(1)} %pad_maximum_fusion.1), channel_id=1, source_target_pairs={{1,5},{3,7},{4,0},{6,2},{9,13},{11,15},{12,8},{14,10},{17,21},{19,... | collective-permute-start | bytes 2359304 | tf_op jit(solution)/shard_map/ppermute | solution.py:23
  56.4 16.0 %collective-permute-start.11 = (bf16[2,3,128,512]{3,2,1,0:T(8,128)(2,1)S(1)}, bf16[2,3,128,512]{3,2,1,0:T(8,128)(2,1)S(1)}, u32[]{:S(2)}, u32[]{:S(2)}) collective-permute-start(bf16[2,3,128,512]{3,2,1,0:T(8,128)(2,1)S(1)} %pad_maximum_fusion.2), channel_id=1, source_target_pairs={{1,5},{3,7},{4,0},{6,2},{9,13},{11,15},{12,8},{14,10},{17,21},{19,... | collective-permute-start | bytes 2359304 | tf_op jit(solution)/shard_map/ppermute | solution.py:23
  58.9 31.0 %collective-permute-start.17 = (bf16[3,400,512]{2,1,0:T(8,128)(2,1)S(1)}, bf16[3,400,512]{2,1,0:T(8,128)(2,1)S(1)}, u32[]{:S(2)}, u32[]{:S(2)}) collective-permute-start(bf16[3,400,512]{2,1,0:T(8,128)(2,1)S(1)} %pad_maximum_fusion.refs_1_), channel_id=1, source_target_pairs={{0,2},{1,3},{2,0},{3,1},{4,6},{5,7},{6,4},{7,5},{8,10},{9,11},{10,... | collective-permute-start | bytes 3686408 | tf_op jit(solution)/shard_map/ppermute | solution.py:23
  59.9 24.1 %collective-permute-start.13 = (bf16[400,512]{1,0:T(8,128)(2,1)}, bf16[400,512]{1,0:T(8,128)(2,1)}, u32[]{:S(2)}, u32[]{:S(2)}) collective-permute-start(bf16[400,512]{1,0:T(8,128)(2,1)} %get-tuple-element.94.refs_0_), channel_id=1, source_target_pairs={{0,1},{1,0},{2,3},{3,2},{4,5},{5,4},{6,7},{7,6},{8,9},{9,8},{10,11... | collective-permute-start | bytes 1228808 | tf_op jit(solution)/shard_map/ppermute | solution.py:23
  59.9 24.2 %collective-permute-start.14 = (bf16[400,512]{1,0:T(8,128)(2,1)}, bf16[400,512]{1,0:T(8,128)(2,1)}, u32[]{:S(2)}, u32[]{:S(2)}) collective-permute-start(bf16[400,512]{1,0:T(8,128)(2,1)} %collective-permute-done.1.refs_4_), channel_id=1, source_target_pairs={{0,1},{1,0},{2,3},{3,2},{4,5},{5,4},{6,7},{7,6},{8,9},{9,8},{10,11... | collective-permute-start | bytes 1228808 | tf_op jit(solution)/shard_map/ppermute | solution.py:23
  65.0 19.1 %collective-permute-start.15 = (bf16[1,3,128,512]{3,2,1,0:T(8,128)(2,1)}, bf16[1,3,128,512]{3,2,1,0:T(8,128)(2,1)}, u32[]{:S(2)}, u32[]{:S(2)}) collective-permute-start(bf16[1,3,128,512]{3,2,1,0:T(8,128)(2,1)} %get-tuple-element.87), channel_id=1, source_target_pairs={{0,8},{2,10},{5,13},{7,15},{8,0},{10,2},{13,5},{15,7},{16,24},{18,... | collective-permute-start | bytes 1179656 | tf_op jit(solution)/shard_map/ppermute | solution.py:23
  73.9 0.9 copy-start
  74.8 9.3 %copy-start.2 = (f32[4]{0:T(128)S(1)}, f32[4]{0:T(128)}, u32[]{:S(2)}) copy-start(f32[4]{0:T(128)} %param.15) | copy-start | bytes 52
  74.8 13.8 %collective-permute-start.12 = (bf16[1,3,128,512]{3,2,1,0:T(8,128)(2,1)}, bf16[1,3,128,512]{3,2,1,0:T(8,128)(2,1)}, u32[]{:S(2)}, u32[]{:S(2)}) collective-permute-start(bf16[1,3,128,512]{3,2,1,0:T(8,128)(2,1)} %get-tuple-element.91), channel_id=1, source_target_pairs={{0,8},{2,10},{5,13},{7,15},{8,0},{10,2},{13,5},{15,7},{16,24},{18,... | collective-permute-start | bytes 1179656 | tf_op jit(solution)/shard_map/ppermute | solution.py:23
  83.9 4.6 %copy-start.1 = (f32[1,3,128,512]{3,2,1,0:T(8,128)S(1)}, f32[1,3,128,512]{3,2,1,0:T(8,128)}, u32[]{:S(2)}) copy-start(f32[1,3,128,512]{3,2,1,0:T(8,128)} %copy-done) | copy-start | bytes 2359300
  84.0 10.5 %collective-permute-start.16 = (bf16[3,400,512]{2,1,0:T(8,128)(2,1)S(1)}, bf16[3,400,512]{2,1,0:T(8,128)(2,1)S(1)}, u32[]{:S(2)}, u32[]{:S(2)}) collective-permute-start(bf16[3,400,512]{2,1,0:T(8,128)(2,1)S(1)} %pad_maximum_fusion.refs_1_), channel_id=1, source_target_pairs={{0,1},{1,0},{2,3},{3,2},{4,5},{5,4},{6,7},{7,6},{8,9},{9,8},{10,11... | collective-permute-start | bytes 3686408 | tf_op jit(solution)/shard_map/ppermute | solution.py:23
  89.9 4.6 %collective-permute-start.18 = (bf16[3,400,512]{2,1,0:T(8,128)(2,1)S(1)}, bf16[3,400,512]{2,1,0:T(8,128)(2,1)S(1)}, u32[]{:S(2)}, u32[]{:S(2)}) collective-permute-start(bf16[3,400,512]{2,1,0:T(8,128)(2,1)S(1)} %collective-permute-done.17.refs_5_), channel_id=1, source_target_pairs={{0,1},{1,0},{2,3},{3,2},{4,5},{5,4},{6,7},{7,6},{8,9},{9,8},{10,11... | collective-permute-start | bytes 3686408 | tf_op jit(solution)/shard_map/ppermute | solution.py:23
  90.0 13.9 %collective-permute-start.19 = (bf16[2,3,128,512]{3,2,1,0:T(8,128)(2,1)S(1)}, bf16[2,3,128,512]{3,2,1,0:T(8,128)(2,1)S(1)}, u32[]{:S(2)}, u32[]{:S(2)}) collective-permute-start(bf16[2,3,128,512]{3,2,1,0:T(8,128)(2,1)S(1)} %renew_1.1.refs_0_), channel_id=1, source_target_pairs={{0,2},{2,0},{5,7},{7,5},{8,10},{10,8},{13,15},{15,13},{16,18},{18,... | collective-permute-start | bytes 2359304 | tf_op jit(solution)/shard_map/ppermute | solution.py:23
  93.1 12.1 %collective-permute-start.20 = (bf16[2,3,128,512]{3,2,1,0:T(8,128)(2,1)S(1)}, bf16[2,3,128,512]{3,2,1,0:T(8,128)(2,1)S(1)}, u32[]{:S(2)}, u32[]{:S(2)}) collective-permute-start(bf16[2,3,128,512]{3,2,1,0:T(8,128)(2,1)S(1)} %renew_1.1.refs_0_), channel_id=1, source_target_pairs={{0,1},{2,3},{5,4},{7,6},{8,9},{10,11},{13,12},{15,14},{16,17},{18,... | collective-permute-start | bytes 2359304 | tf_op jit(solution)/shard_map/ppermute | solution.py:23
  103.8 3.2 %collective-permute-start.21 = (bf16[2,3,128,512]{3,2,1,0:T(8,128)(2,1)S(1)}, bf16[2,3,128,512]{3,2,1,0:T(8,128)(2,1)S(1)}, u32[]{:S(2)}, u32[]{:S(2)}) collective-permute-start(bf16[2,3,128,512]{3,2,1,0:T(8,128)(2,1)S(1)} %collective-permute-done.19.refs_1_), channel_id=1, source_target_pairs={{0,1},{2,3},{5,4},{7,6},{8,9},{10,11},{13,12},{15,14},{16,17},{18,... | collective-permute-start | bytes 2359304 | tf_op jit(solution)/shard_map/ppermute | solution.py:23
  108.0 12.6 %collective-permute-start.23 = (bf16[128,512]{1,0:T(8,128)(2,1)S(1)}, bf16[128,512]{1,0:T(8,128)(2,1)S(1)}, u32[]{:S(2)}, u32[]{:S(2)}) collective-permute-start(bf16[128,512]{1,0:T(8,128)(2,1)S(1)} %get-tuple-element.100), channel_id=1, source_target_pairs={{0,8},{1,9},{2,10},{3,11},{4,12},{5,13},{6,14},{7,15},{8,0},{9,1},... | collective-permute-start | bytes 393224 | tf_op jit(solution)/shard_map/ppermute | solution.py:23
  112.0 8.6 %collective-permute-start.22 = (bf16[128,512]{1,0:T(8,128)(2,1)S(1)}, bf16[128,512]{1,0:T(8,128)(2,1)S(1)}, u32[]{:S(2)}, u32[]{:S(2)}) collective-permute-start(bf16[128,512]{1,0:T(8,128)(2,1)S(1)} %get-tuple-element.103), channel_id=1, source_target_pairs={{0,4},{1,5},{2,6},{3,7},{4,0},{5,1},{6,2},{7,3},{8,12},{9,13},{10,... | collective-permute-start | bytes 393224 | tf_op jit(solution)/shard_map/ppermute | solution.py:23
  112.1 8.6 %collective-permute-start.24 = (bf16[128,512]{1,0:T(8,128)(2,1)S(1)}, bf16[128,512]{1,0:T(8,128)(2,1)S(1)}, u32[]{:S(2)}, u32[]{:S(2)}) collective-permute-start(bf16[128,512]{1,0:T(8,128)(2,1)S(1)} %get-tuple-element.104), channel_id=1, source_target_pairs={{0,12},{1,13},{2,14},{3,15},{4,8},{5,9},{6,10},{7,11},{8,4},{9,5},... | collective-permute-start | bytes 393224 | tf_op jit(solution)/shard_map/ppermute | solution.py:23

commit v6 on v5

--- a/solution.py
+++ b/solution.py
@@ -186,11 +186,13 @@
         pltpu.make_async_copy(other.at[0], k_s.at[lower], in_sem.at[5]),
         pltpu.make_async_copy(other.at[1], tg_s.at[lower], in_sem.at[6]),
     ]
-    for load in loads:
+    small = fetch_small((rates, mask), (rates_s, mask_s), in_sem.at[pl.ds(7, 2)])
+    for load in loads[:2]:
         load.start()
-    small = fetch_small((rates, mask), (rates_s, mask_s), in_sem.at[pl.ds(7, 2)])
     for copy in small:
         copy.wait()
+    for load in loads[2:]:
+        load.start()
     rate = rate_column(rates_s[...], mask_s[...], head)
     chunk = 256
     for at in range(0, 2 * rows, chunk):
@@ -377,7 +379,7 @@
         (keep, got),
         [whole(keep.shape)] * 2,
         [jax.ShapeDtypeStruct(keep.shape, t) for t in (f32, bf16)],
-        flops=9000000000,
+        flops=2000000000,
     )
 
 
@@ -420,6 +422,7 @@
             pltpu.VMEM((2, *shape), bf16),
             pltpu.SemaphoreType.DMA((2, 2)),
         ],
+        flops=4000000000,
     )
 
 
@@ -606,19 +609,15 @@
             send = cut((keep, got), b, 1 - bit_of(b)).astype(bf16)
             keep, got = cut((keep, got), b, bit_of(b)), swap(send, 1 << b)
         total, send = add(keep, got)
-        sums.append((total, send))
-        if n >= 2:
-            both = swap(
-                jnp.concatenate([sums[n - 2][1], send]), span, lambda t: not matched(t)
-            )
-            sums[n - 2], sums[n] = (sums[n - 2][0], both[:1]), (total, both[1:])
+        sums.append((total, swap(send, span, lambda t: not matched(t))))
         return [send]
 
     turn = settle(0)
     turn = settle(1)
     moved.append(swap(after(more_sends[1], *turn), 2))
-    turn += [came[2]]
+    turn += [came[2], sums[0][1]]
     turn = settle(2)
+    turn += [sums[1][1]]
     turn = settle(3)
     late = {0: jnp.stack([after(x, *turn) for x in came])}
     spread(late, outer_bits)

time: 122 us -> 117 us (0.959)
  waiting for transfers between devices: 40.8 us -> 38.8 us
    ppermute x25 -> x27, waiting for transfers between devices: 40.8 us -> 38.8 us  [swap(): return lax.ppermute(value, AXIS, pairs)]
    ppermute x25 -> x27, starting transfers between devices: 40.7 us -> 39.9 us  [swap(): return lax.ppermute(value, AXIS, pairs)]
    unnamed x20 -> x18, local copies, waits for them, and re-layouts: 2.74 us -> 2.73 us
  transfers between devices with their start and end apart: 25 -> 27, of which waited for: 9 -> 10; matrix products, arithmetic and copies ran while one was open for 2% -> 1% of each run, Pallas kernels for 24% -> 24%
where the time goes in v6:
time: 117 us; the launch traced here: 116 us
  starting transfers between devices  39.9 us (34%)
  waiting for transfers between devices  38.8 us (33%)
  Pallas kernels  33.4 us (29%)
  local copies, waits for them, and re-layouts  3.93 us (3%)
    ppermute x27, starting transfers between devices, swap(): return lax.ppermute(value, AXIS, pairs)  39.9 us
    ppermute x27, waiting for transfers between devices, swap(): return lax.ppermute(value, AXIS, pairs)  38.8 us
    pallas_call x16, Pallas kernels, call(): pl.pallas_call(body, name=name, grid=(1,), in_specs=specs, out_specs=out_...  33.4 us
    unnamed x18, local copies, waits for them, and re-layouts  2.73 us
  transfers between devices with their start and end apart: 27, of which 10 were waited for; matrix products, arithmetic and copies ran while one was open for 1% of the time, Pallas kernels for 24%

profile of v6, /device:TPU:0, one launch (start us, length us, event | category | flops | bytes accessed | tf_op | source)
XLA Modules:
  0.0 116.4 jit_solution(2384789514052076477)
XLA Ops:
  0.0 3.9 %pack.1 = (bf16[2,512,512]{2,1,0:T(8,128)(2,1)}, bf16[2,512,512]{2,1,0:T(8,128)(2,1)}, bf16[400,512]{1,0:T(8,128)(2,1)}, bf16[400,512]{1,0:T(8,128)(2,1)}, bf16[...) custom-call(f32[4,512]{1,0:T(4,128)} %bitcast.12, s32[1,512]{1,0:T(1,128)} %bitcast.15, s32[1,128]{1,0:T(1,128)} %bitcast.18, ...), custom_call_target="tpu_custom_call" | custom-call | tf_op jit(solution)/shard_map/pack/pallas_call | solution.py:55
  3.9 0.5 collective-permute-start
  4.4 0.1 collective-permute-start.2
  4.5 2.9 %collective-permute-start.1 = (bf16[400,512]{1,0:T(8,128)(2,1)}, bf16[400,512]{1,0:T(8,128)(2,1)}, u32[]{:S(2)}, u32[]{:S(2)}) collective-permute-start(bf16[400,512]{1,0:T(8,128)(2,1)} %get-tuple-element.94.refs_0_), channel_id=1, source_target_pairs={{0,2},{1,3},{2,0},{3,1},{4,6},{5,7},{6,4},{7,5},{8,10},{9,11},{10,... | collective-permute-start | bytes 1228808 | tf_op jit(solution)/shard_map/ppermute | solution.py:23
  7.4 1.6 %collective-permute-start.5 = (bf16[400,512]{1,0:T(8,128)(2,1)}, bf16[400,512]{1,0:T(8,128)(2,1)S(1)}, u32[]{:S(2)}, u32[]{:S(2)}) collective-permute-start(bf16[400,512]{1,0:T(8,128)(2,1)} %get-tuple-element.66), channel_id=1, source_target_pairs={{0,4},{1,5},{2,6},{3,7},{4,0},{5,1},{6,2},{7,3},{8,12},{9,13},{10,... | collective-permute-start | bytes 1228808 | tf_op jit(solution)/shard_map/ppermute | solution.py:23
  9.0 2.6 %collective-permute-start.6 = (bf16[400,512]{1,0:T(8,128)(2,1)}, bf16[400,512]{1,0:T(8,128)(2,1)S(1)}, u32[]{:S(2)}, u32[]{:S(2)}) collective-permute-start(bf16[400,512]{1,0:T(8,128)(2,1)} %get-tuple-element.67), channel_id=1, source_target_pairs={{0,8},{1,9},{2,10},{3,11},{4,12},{5,13},{6,14},{7,15},{8,0},{9,1},... | collective-permute-start | bytes 1228808 | tf_op jit(solution)/shard_map/ppermute | solution.py:23
  11.6 1.0 copy-done.7
  12.5 7.3 %head_grad_0.1 = (bf16[1,3,128,512]{3,2,1,0:T(8,128)(2,1)}, bf16[1,3,128,512]{3,2,1,0:T(8,128)(2,1)}, f32[1,3,128,512]{3,2,1,0:T(8,128)}, f32[1,3,128,512]{3,2,1,0:T(8,128)}) custom-call(f32[4,512]{1,0:T(4,128)} %bitcast.13, s32[1,512]{1,0:T(1,128)} %bitcast.16, bf16[512,2048]{1,0:T(8,128)(2,1)} %keys.5, bf16[512,2048]{1,0:T(8,128)(2,1)} %values.5, ...), custom_call_target="tpu_custom_call" | custom-call | tf_op jit(solution)/shard_map/head_grad_0/pallas_call | solution.py:55
  19.9 0.6 collective-permute-start.4
  20.5 0.0 collective-permute-done.1.refs_4_
  20.5 0.0 collective-permute-done.2.other
  20.5 7.4 %head_grad_1.1 = (bf16[1,3,128,512]{3,2,1,0:T(8,128)(2,1)}, bf16[1,3,128,512]{3,2,1,0:T(8,128)(2,1)}, f32[1,3,128,512]{3,2,1,0:T(8,128)}, f32[1,3,128,512]{3,2,1,0:T(8,128)}) custom-call(f32[4,512]{1,0:T(4,128)} %bitcast.14, s32[1,512]{1,0:T(1,128)} %bitcast.17, bf16[512,2048]{1,0:T(8,128)(2,1)} %keys.5, bf16[512,2048]{1,0:T(8,128)(2,1)} %values.5, ...), custom_call_target="tpu_custom_call" | custom-call | tf_op jit(solution)/shard_map/head_grad_1/pallas_call | solution.py:55
  27.9 1.6 %collective-permute-start.3 = (bf16[1,3,128,512]{3,2,1,0:T(8,128)(2,1)}, bf16[1,3,128,512]{3,2,1,0:T(8,128)(2,1)S(1)}, u32[]{:S(2)}, u32[]{:S(2)}) collective-permute-start(bf16[1,3,128,512]{3,2,1,0:T(8,128)(2,1)} %get-tuple-element.64), channel_id=1, source_target_pairs={{0,2},{1,3},{2,0},{3,1},{4,6},{5,7},{6,4},{7,5},{8,10},{9,11},{10,... | collective-permute-start | bytes 1179656 | tf_op jit(solution)/shard_map/ppermute | solution.py:23
  29.4 0.0 collective-permute-done.5
  29.4 0.4 collective-permute-done.6
  29.8 0.5 collective-permute-start.8
  30.3 2.5 %collective-permute-start.9 = (bf16[400,512]{1,0:T(8,128)(2,1)}, bf16[400,512]{1,0:T(8,128)(2,1)S(1)}, u32[]{:S(2)}, u32[]{:S(2)}) collective-permute-start(bf16[400,512]{1,0:T(8,128)(2,1)} %get-tuple-element.80), channel_id=1, source_target_pairs={{0,12},{1,13},{2,14},{3,15},{4,8},{5,9},{6,10},{7,11},{8,4},{9,5},... | collective-permute-start | bytes 1228808 | tf_op jit(solution)/shard_map/ppermute | solution.py:23
  32.8 0.1 add.34
  32.9 1.4 %collective-permute-start.10 = (bf16[1,3,128,512]{3,2,1,0:T(8,128)(2,1)S(1)}, bf16[1,3,128,512]{3,2,1,0:T(8,128)(2,1)S(1)}, u32[]{:S(2)}, u32[]{:S(2)}) collective-permute-start(bf16[1,3,128,512]{3,2,1,0:T(8,128)(2,1)S(1)} %get-tuple-element.69), channel_id=1, source_target_pairs={{1,5},{3,7},{4,0},{6,2},{9,13},{11,15},{12,8},{14,10},{17,21},{19,... | collective-permute-start | bytes 1179656 | tf_op jit(solution)/shard_map/ppermute | solution.py:23
  34.4 5.8 %collective-permute-done.3.got = bf16[1,3,128,512]{3,2,1,0:T(8,128)(2,1)S(1)} collective-permute-done((bf16[1,3,128,512]{3,2,1,0:T(8,128)(2,1)}, bf16[1,3,128,512]{3,2,1,0:T(8,128)(2,1)S(1)}, u32[]{:S(2)}, u32[]{:S(2)}) %collective-permute-start.3) | collective-permute-done | bytes 393248 | tf_op jit(solution)/shard_map/ppermute | solution.py:23
  40.2 0.1 add.35
  40.3 0.8 copy-done.8
  41.2 1.5 %collective-permute-start.7 = (bf16[1,3,128,512]{3,2,1,0:T(8,128)(2,1)S(1)}, bf16[1,3,128,512]{3,2,1,0:T(8,128)(2,1)S(1)}, u32[]{:S(2)}, u32[]{:S(2)}) collective-permute-start(bf16[1,3,128,512]{3,2,1,0:T(8,128)(2,1)S(1)} %copy-done.8), channel_id=1, source_target_pairs={{0,2},{1,3},{2,0},{3,1},{4,6},{5,7},{6,4},{7,5},{8,10},{9,11},{10,... | collective-permute-start | bytes 1179656 | tf_op jit(solution)/shard_map/ppermute | solution.py:23
  42.7 1.3 %collective-permute-start.11 = (bf16[1,3,128,512]{3,2,1,0:T(8,128)(2,1)S(1)}, bf16[1,3,128,512]{3,2,1,0:T(8,128)(2,1)S(1)}, u32[]{:S(2)}, u32[]{:S(2)}) collective-permute-start(bf16[1,3,128,512]{3,2,1,0:T(8,128)(2,1)S(1)} %get-tuple-element.75), channel_id=1, source_target_pairs={{1,5},{3,7},{4,0},{6,2},{9,13},{11,15},{12,8},{14,10},{17,21},{19,... | collective-permute-start | bytes 1179656 | tf_op jit(solution)/shard_map/ppermute | solution.py:23
  44.0 4.6 %collective-permute-done.8.got = bf16[1,3,128,512]{3,2,1,0:T(8,128)(2,1)S(1)} collective-permute-done((bf16[1,3,128,512]{3,2,1,0:T(8,128)(2,1)}, bf16[1,3,128,512]{3,2,1,0:T(8,128)(2,1)S(1)}, u32[]{:S(2)}, u32[]{:S(2)}) %collective-permute-start.8) | collective-permute-done | bytes 393248 | tf_op jit(solution)/shard_map/ppermute | solution.py:23
  48.6 0.0 collective-permute-done.9
  48.6 0.0 collective-permute-done.10.refs_1_
  48.6 0.2 add.36
  48.8 1.4 %collective-permute-start.12 = (bf16[1,3,128,512]{3,2,1,0:T(8,128)(2,1)S(1)}, bf16[1,3,128,512]{3,2,1,0:T(8,128)(2,1)S(1)}, u32[]{:S(2)}, u32[]{:S(2)}) collective-permute-start(bf16[1,3,128,512]{3,2,1,0:T(8,128)(2,1)S(1)} %get-tuple-element.82), channel_id=1, source_target_pairs={{1,5},{3,7},{4,0},{6,2},{9,13},{11,15},{12,8},{14,10},{17,21},{19,... | collective-permute-start | bytes 1179656 | tf_op jit(solution)/shard_map/ppermute | solution.py:23
  50.2 5.5 %collective-permute-done.7.got = bf16[1,3,128,512]{3,2,1,0:T(8,128)(2,1)S(1)} collective-permute-done((bf16[1,3,128,512]{3,2,1,0:T(8,128)(2,1)S(1)}, bf16[1,3,128,512]{3,2,1,0:T(8,128)(2,1)S(1)}, u32[]{:S(2)}, u32[]{:S(2)}) %collective-permute-start.7) | collective-permute-done | bytes 393248 | tf_op jit(solution)/shard_map/ppermute | solution.py:23
  55.7 0.0 collective-permute-done.11.refs_1_
  55.7 0.1 add.37
  55.9 0.1 pad_maximum_fusion.refs_1_
  56.0 0.8 collective-permute-start.19
  56.8 1.3 %collective-permute-start.13 = (bf16[1,3,128,512]{3,2,1,0:T(8,128)(2,1)S(1)}, bf16[1,3,128,512]{3,2,1,0:T(8,128)(2,1)S(1)}, u32[]{:S(2)}, u32[]{:S(2)}) collective-permute-start(bf16[1,3,128,512]{3,2,1,0:T(8,128)(2,1)S(1)} %get-tuple-element.84), channel_id=1, source_target_pairs={{1,5},{3,7},{4,0},{6,2},{9,13},{11,15},{12,8},{14,10},{17,21},{19,... | collective-permute-start | bytes 1179656 | tf_op jit(solution)/shard_map/ppermute | solution.py:23
  58.1 0.1 collective-permute-start.15
  58.2 0.5 collective-permute-start.16
  58.7 1.3 %hand_over.2 = (bf16[1,3,128,512]{3,2,1,0:T(8,128)(2,1)}, f32[1,3,128,512]{3,2,1,0:T(8,128)S(1)}) custom-call(f32[1,3,128,512]{3,2,1,0:T(8,128)S(1)} %get-tuple-element.85.refs_0_, bf16[1,3,128,512]{3,2,1,0:T(8,128)(2,1)S(1)} %collective-permute-done.10.refs_1_, f32[1,3,128,512]{3,2,1,0:T(8,128)S(1)} %get-tuple-element.86.refs_2_, ...), custom_call_target="tpu_custom_call" | custom-call | flops 4000000000 | tf_op jit(solution)/shard_map/hand_over/pallas_call | solution.py:55
  60.0 4.2 %collective-permute-start.17 = (bf16[1,3,128,512]{3,2,1,0:T(8,128)(2,1)}, bf16[1,3,128,512]{3,2,1,0:T(8,128)(2,1)}, u32[]{:S(2)}, u32[]{:S(2)}) collective-permute-start(bf16[1,3,128,512]{3,2,1,0:T(8,128)(2,1)} %get-tuple-element.87), channel_id=1, source_target_pairs={{0,8},{2,10},{5,13},{7,15},{8,0},{10,2},{13,5},{15,7},{16,24},{18,... | collective-permute-start | bytes 1179656 | tf_op jit(solution)/shard_map/ppermute | solution.py:23
  64.2 2.3 %collective-permute-done.13.refs_3_ = bf16[1,3,128,512]{3,2,1,0:T(8,128)(2,1)S(1)} collective-permute-done((bf16[1,3,128,512]{3,2,1,0:T(8,128)(2,1)S(1)}, bf16[1,3,128,512]{3,2,1,0:T(8,128)(2,1)S(1)}, u32[]{:S(2)}, u32[]{:S(2)}) %collective-permute-start.13) | collective-permute-done | bytes 393248 | tf_op jit(solution)/shard_map/ppermute | solution.py:23
  66.5 1.3 %hand_over.3 = (bf16[1,3,128,512]{3,2,1,0:T(8,128)(2,1)}, f32[1,3,128,512]{3,2,1,0:T(8,128)S(1)}) custom-call(f32[1,3,128,512]{3,2,1,0:T(8,128)S(1)} %get-tuple-element.88.refs_0_, bf16[1,3,128,512]{3,2,1,0:T(8,128)(2,1)S(1)} %collective-permute-done.11.refs_1_, f32[1,3,128,512]{3,2,1,0:T(8,128)S(1)} %get-tuple-element.89.refs_2_, ...), custom_call_target="tpu_custom_call" | custom-call | flops 4000000000 | tf_op jit(solution)/shard_map/hand_over/pallas_call | solution.py:55
  67.8 0.9 copy-done
  68.7 3.9 %collective-permute-start.14 = (bf16[1,3,128,512]{3,2,1,0:T(8,128)(2,1)}, bf16[1,3,128,512]{3,2,1,0:T(8,128)(2,1)}, u32[]{:S(2)}, u32[]{:S(2)}) collective-permute-start(bf16[1,3,128,512]{3,2,1,0:T(8,128)(2,1)} %get-tuple-element.91), channel_id=1, source_target_pairs={{0,8},{2,10},{5,13},{7,15},{8,0},{10,2},{13,5},{15,7},{16,24},{18,... | collective-permute-start | bytes 1179656 | tf_op jit(solution)/shard_map/ppermute | solution.py:23
  72.6 1.2 %constant_dynamic-slice_fusion = (bf16[1,3,128,512]{3,2,1,0:T(8,128)(2,1)S(1)}, bf16[1,3,128,512]{3,2,1,0:T(8,128)(2,1)S(1)}) fusion(bf16[4,3,512,512]{3,2,1,0:T(8,128)(2,1)} %weights.3, s32[]{:T(128)S(6)} %select_n.30, s32[]{:T(128)S(6)} %select_n.32, s32[]{:T(128)S(6)} %select_n.31), kind=kLoop, calls=%fused_computation.1 | loop fusion | bytes 1572876 | tf_op jit(solution)/shard_map/dynamic_slice | solution.py:626
  73.9 0.1 collective-permute-start.18
  74.0 5.4 %collective-permute-done.17.got = bf16[1,3,128,512]{3,2,1,0:T(8,128)(2,1)} collective-permute-done((bf16[1,3,128,512]{3,2,1,0:T(8,128)(2,1)}, bf16[1,3,128,512]{3,2,1,0:T(8,128)(2,1)}, u32[]{:S(2)}, u32[]{:S(2)}) %collective-permute-start.17) | collective-permute-done | bytes 393248 | tf_op jit(solution)/shard_map/ppermute | solution.py:23
  79.4 1.3 %renew_0.1.refs_0_ = bf16[1,3,128,512]{3,2,1,0:T(8,128)(2,1)S(1)} custom-call(f32[1,3,128,512]{3,2,1,0:T(8,128)S(1)} %get-tuple-element.93.keep, bf16[1,3,128,512]{3,2,1,0:T(8,128)(2,1)} %collective-permute-done.17.got, bf16[1,3,128,512]{3,2,1,0:T(8,128)(2,1)S(1)} %get-tuple-element.105.old, f32[1,4]{1,0:T(1,128)S(1)} %bitcast.7), custom_call_target="tpu_custom_call" | custom-call | tf_op jit(solution)/shard_map/renew_0/pallas_call | solution.py:55
  80.6 2.9 %collective-permute-done.14.got = bf16[1,3,128,512]{3,2,1,0:T(8,128)(2,1)} collective-permute-done((bf16[1,3,128,512]{3,2,1,0:T(8,128)(2,1)}, bf16[1,3,128,512]{3,2,1,0:T(8,128)(2,1)}, u32[]{:S(2)}, u32[]{:S(2)}) %collective-permute-start.14) | collective-permute-done | bytes 393248 | tf_op jit(solution)/shard_map/ppermute | solution.py:23
  83.6 1.3 %renew_1.1.refs_0_ = bf16[2,3,128,512]{3,2,1,0:T(8,128)(2,1)S(1)} custom-call(f32[1,3,128,512]{3,2,1,0:T(8,128)S(1)} %copy-done.1, bf16[1,3,128,512]{3,2,1,0:T(8,128)(2,1)} %collective-permute-done.14.got, bf16[1,3,128,512]{3,2,1,0:T(8,128)(2,1)S(1)} %get-tuple-element.106.old, f32[1,4]{1,0:T(1,128)S(1)} %bitcast.8, bf16[1,3,128,512]{3,2,1,0:T(8,128)(2,1)S(1)} %renew_0.1.refs_0_), custom_call_target="tpu_custom_call" | custom-call | tf_op jit(solution)/shard_map/renew_1/pallas_call | solution.py:55
  84.9 0.1 collective-permute-start.20
  85.0 3.3 %collective-permute-start.21 = (bf16[2,3,128,512]{3,2,1,0:T(8,128)(2,1)S(1)}, bf16[2,3,128,512]{3,2,1,0:T(8,128)(2,1)S(1)}, u32[]{:S(2)}, u32[]{:S(2)}) collective-permute-start(bf16[2,3,128,512]{3,2,1,0:T(8,128)(2,1)S(1)} %renew_1.1.refs_0_), channel_id=1, source_target_pairs={{0,2},{2,0},{5,7},{7,5},{8,10},{10,8},{13,15},{15,13},{16,18},{18,... | collective-permute-start | bytes 2359304 | tf_op jit(solution)/shard_map/ppermute | solution.py:23
  88.3 1.3 %collective-permute-start.22 = (bf16[2,3,128,512]{3,2,1,0:T(8,128)(2,1)S(1)}, bf16[2,3,128,512]{3,2,1,0:T(8,128)(2,1)S(1)}, u32[]{:S(2)}, u32[]{:S(2)}) collective-permute-start(bf16[2,3,128,512]{3,2,1,0:T(8,128)(2,1)S(1)} %renew_1.1.refs_0_), channel_id=1, source_target_pairs={{0,1},{2,3},{5,4},{7,6},{8,9},{10,11},{13,12},{15,14},{16,17},{18,... | collective-permute-start | bytes 2359304 | tf_op jit(solution)/shard_map/ppermute | solution.py:23
  89.7 5.0 %arrange.1.rows = bf16[3,512,512]{2,1,0:T(8,128)(2,1)S(1)} custom-call(bf16[400,512]{1,0:T(8,128)(2,1)} %get-tuple-element.94.refs_0_, bf16[3,400,512]{2,1,0:T(8,128)(2,1)S(1)} %pad_maximum_fusion.refs_1_, bf16[400,512]{1,0:T(8,128)(2,1)} %collective-permute-done.15.refs_2_, bf16[3,400,512]{2,1,0:T(8,128)(2,1)S(1)} %collective-permute-done.18.refs_3_, ...), custom_call_target="tpu_custom_call" | custom-call | tf_op jit(solution)/shard_map/arrange/pallas_call | solution.py:55
  94.7 1.2 attend.1.attended
  95.8 3.0 %collective-permute-done.21.refs_1_ = bf16[2,3,128,512]{3,2,1,0:T(8,128)(2,1)S(1)} collective-permute-done((bf16[2,3,128,512]{3,2,1,0:T(8,128)(2,1)S(1)}, bf16[2,3,128,512]{3,2,1,0:T(8,128)(2,1)S(1)}, u32[]{:S(2)}, u32[]{:S(2)}) %collective-permute-start.21) | collective-permute-done | bytes 786464 | tf_op jit(solution)/shard_map/ppermute | solution.py:23
  98.8 1.3 %collective-permute-start.23 = (bf16[2,3,128,512]{3,2,1,0:T(8,128)(2,1)S(1)}, bf16[2,3,128,512]{3,2,1,0:T(8,128)(2,1)S(1)}, u32[]{:S(2)}, u32[]{:S(2)}) collective-permute-start(bf16[2,3,128,512]{3,2,1,0:T(8,128)(2,1)S(1)} %collective-permute-done.21.refs_1_), channel_id=1, source_target_pairs={{0,1},{2,3},{5,4},{7,6},{8,9},{10,11},{13,12},{15,14},{16,17},{18,... | collective-permute-start | bytes 2359304 | tf_op jit(solution)/shard_map/ppermute | solution.py:23
  100.2 1.8 %collective-permute-done.23.refs_3_ = bf16[2,3,128,512]{3,2,1,0:T(8,128)(2,1)S(1)} collective-permute-done((bf16[2,3,128,512]{3,2,1,0:T(8,128)(2,1)S(1)}, bf16[2,3,128,512]{3,2,1,0:T(8,128)(2,1)S(1)}, u32[]{:S(2)}, u32[]{:S(2)}) %collective-permute-start.23) | collective-permute-done | bytes 786464 | tf_op jit(solution)/shard_map/ppermute | solution.py:23
  102.0 1.0 finish_2.1
  103.0 0.2 collective-permute-start.25
  103.3 1.0 finish_0.1
  104.3 1.8 %collective-permute-start.24 = (bf16[128,512]{1,0:T(8,128)(2,1)S(1)}, bf16[128,512]{1,0:T(8,128)(2,1)S(1)}, u32[]{:S(2)}, u32[]{:S(2)}) collective-permute-start(bf16[128,512]{1,0:T(8,128)(2,1)S(1)} %get-tuple-element.103), channel_id=1, source_target_pairs={{0,4},{1,5},{2,6},{3,7},{4,0},{5,1},{6,2},{7,3},{8,12},{9,13},{10,... | collective-permute-start | bytes 393224 | tf_op jit(solution)/shard_map/ppermute | solution.py:23
  106.1 2.5 %collective-permute-start.26 = (bf16[128,512]{1,0:T(8,128)(2,1)S(1)}, bf16[128,512]{1,0:T(8,128)(2,1)S(1)}, u32[]{:S(2)}, u32[]{:S(2)}) collective-permute-start(bf16[128,512]{1,0:T(8,128)(2,1)S(1)} %get-tuple-element.104), channel_id=1, source_target_pairs={{0,12},{1,13},{2,14},{3,15},{4,8},{5,9},{6,10},{7,11},{8,4},{9,5},... | collective-permute-start | bytes 393224 | tf_op jit(solution)/shard_map/ppermute | solution.py:23
  108.6 7.0 %collective-permute-done.24.refs_1_ = bf16[128,512]{1,0:T(8,128)(2,1)S(1)} collective-permute-done((bf16[128,512]{1,0:T(8,128)(2,1)S(1)}, bf16[128,512]{1,0:T(8,128)(2,1)S(1)}, u32[]{:S(2)}, u32[]{:S(2)}) %collective-permute-start.24) | collective-permute-done | bytes 131104 | tf_op jit(solution)/shard_map/ppermute | solution.py:23
  115.6 0.9 join.1
  (26 shorter events, 0.1 us)
Async XLA Ops:
  3.9 7.7 %collective-permute-start = (bf16[2,512,512]{2,1,0:T(8,128)(2,1)}, bf16[2,512,512]{2,1,0:T(8,128)(2,1)S(1)}, u32[]{:S(2)}, u32[]{:S(2)}) collective-permute-start(bf16[2,512,512]{2,1,0:T(8,128)(2,1)} %get-tuple-element.57), channel_id=1, source_target_pairs={{0,1},{1,0},{2,3},{3,2},{4,5},{5,4},{6,7},{7,6},{8,9},{9,8},{10,11... | collective-permute-start | bytes 3145736 | tf_op jit(solution)/shard_map/ppermute | solution.py:23
  4.4 16.1 %collective-permute-start.2 = (bf16[2,512,512]{2,1,0:T(8,128)(2,1)}, bf16[2,512,512]{2,1,0:T(8,128)(2,1)}, u32[]{:S(2)}, u32[]{:S(2)}) collective-permute-start(bf16[2,512,512]{2,1,0:T(8,128)(2,1)} %get-tuple-element.62), channel_id=1, source_target_pairs={{0,1},{1,0},{2,3},{3,2},{4,5},{5,4},{6,7},{7,6},{8,9},{9,8},{10,11... | collective-permute-start | bytes 3145736 | tf_op jit(solution)/shard_map/ppermute | solution.py:23
  4.5 16.0 %collective-permute-start.1 = (bf16[400,512]{1,0:T(8,128)(2,1)}, bf16[400,512]{1,0:T(8,128)(2,1)}, u32[]{:S(2)}, u32[]{:S(2)}) collective-permute-start(bf16[400,512]{1,0:T(8,128)(2,1)} %get-tuple-element.94.refs_0_), channel_id=1, source_target_pairs={{0,2},{1,3},{2,0},{3,1},{4,6},{5,7},{6,4},{7,5},{8,10},{9,11},{10,... | collective-permute-start | bytes 1228808 | tf_op jit(solution)/shard_map/ppermute | solution.py:23
  7.4 22.0 %collective-permute-start.5 = (bf16[400,512]{1,0:T(8,128)(2,1)}, bf16[400,512]{1,0:T(8,128)(2,1)S(1)}, u32[]{:S(2)}, u32[]{:S(2)}) collective-permute-start(bf16[400,512]{1,0:T(8,128)(2,1)} %get-tuple-element.66), channel_id=1, source_target_pairs={{0,4},{1,5},{2,6},{3,7},{4,0},{5,1},{6,2},{7,3},{8,12},{9,13},{10,... | collective-permute-start | bytes 1228808 | tf_op jit(solution)/shard_map/ppermute | solution.py:23
  9.0 20.8 %collective-permute-start.6 = (bf16[400,512]{1,0:T(8,128)(2,1)}, bf16[400,512]{1,0:T(8,128)(2,1)S(1)}, u32[]{:S(2)}, u32[]{:S(2)}) collective-permute-start(bf16[400,512]{1,0:T(8,128)(2,1)} %get-tuple-element.67), channel_id=1, source_target_pairs={{0,8},{1,9},{2,10},{3,11},{4,12},{5,13},{6,14},{7,15},{8,0},{9,1},... | collective-permute-start | bytes 1228808 | tf_op jit(solution)/shard_map/ppermute | solution.py:23
  11.6 1.0 copy-start.7
  19.9 12.9 %copy-start.6 = (f32[1,3,128,512]{3,2,1,0:T(8,128)S(1)}, f32[1,3,128,512]{3,2,1,0:T(8,128)}, u32[]{:S(2)}) copy-start(f32[1,3,128,512]{3,2,1,0:T(8,128)} %get-tuple-element.65.keep) | copy-start | bytes 2359300
  19.9 12.9 %collective-permute-start.4 = (bf16[1,3,128,512]{3,2,1,0:T(8,128)(2,1)}, bf16[1,3,128,512]{3,2,1,0:T(8,128)(2,1)S(1)}, u32[]{:S(2)}, u32[]{:S(2)}) collective-permute-start(bf16[1,3,128,512]{3,2,1,0:T(8,128)(2,1)} %get-tuple-element.60), channel_id=1, source_target_pairs={{0,2},{1,3},{2,0},{3,1},{4,6},{5,7},{6,4},{7,5},{8,10},{9,11},{10,... | collective-permute-start | bytes 1179656 | tf_op jit(solution)/shard_map/ppermute | solution.py:23
  27.9 12.3 %collective-permute-start.3 = (bf16[1,3,128,512]{3,2,1,0:T(8,128)(2,1)}, bf16[1,3,128,512]{3,2,1,0:T(8,128)(2,1)S(1)}, u32[]{:S(2)}, u32[]{:S(2)}) collective-permute-start(bf16[1,3,128,512]{3,2,1,0:T(8,128)(2,1)} %get-tuple-element.64), channel_id=1, source_target_pairs={{0,2},{1,3},{2,0},{3,1},{4,6},{5,7},{6,4},{7,5},{8,10},{9,11},{10,... | collective-permute-start | bytes 1179656 | tf_op jit(solution)/shard_map/ppermute | solution.py:23
  29.8 18.8 %collective-permute-start.8 = (bf16[1,3,128,512]{3,2,1,0:T(8,128)(2,1)}, bf16[1,3,128,512]{3,2,1,0:T(8,128)(2,1)S(1)}, u32[]{:S(2)}, u32[]{:S(2)}) collective-permute-start(bf16[1,3,128,512]{3,2,1,0:T(8,128)(2,1)} %get-tuple-element.78), channel_id=1, source_target_pairs={{0,2},{1,3},{2,0},{3,1},{4,6},{5,7},{6,4},{7,5},{8,10},{9,11},{10,... | collective-permute-start | bytes 1179656 | tf_op jit(solution)/shard_map/ppermute | solution.py:23
  30.3 18.3 %collective-permute-start.9 = (bf16[400,512]{1,0:T(8,128)(2,1)}, bf16[400,512]{1,0:T(8,128)(2,1)S(1)}, u32[]{:S(2)}, u32[]{:S(2)}) collective-permute-start(bf16[400,512]{1,0:T(8,128)(2,1)} %get-tuple-element.80), channel_id=1, source_target_pairs={{0,12},{1,13},{2,14},{3,15},{4,8},{5,9},{6,10},{7,11},{8,4},{9,5},... | collective-permute-start | bytes 1228808 | tf_op jit(solution)/shard_map/ppermute | solution.py:23
  32.8 7.4 %copy-start.5 = (f32[1,3,128,512]{3,2,1,0:T(8,128)S(1)}, f32[1,3,128,512]{3,2,1,0:T(8,128)}, u32[]{:S(2)}) copy-start(f32[1,3,128,512]{3,2,1,0:T(8,128)} %get-tuple-element.58.keep) | copy-start | bytes 2359300
  32.9 15.7 %collective-permute-start.10 = (bf16[1,3,128,512]{3,2,1,0:T(8,128)(2,1)S(1)}, bf16[1,3,128,512]{3,2,1,0:T(8,128)(2,1)S(1)}, u32[]{:S(2)}, u32[]{:S(2)}) collective-permute-start(bf16[1,3,128,512]{3,2,1,0:T(8,128)(2,1)S(1)} %get-tuple-element.69), channel_id=1, source_target_pairs={{1,5},{3,7},{4,0},{6,2},{9,13},{11,15},{12,8},{14,10},{17,21},{19,... | collective-permute-start | bytes 1179656 | tf_op jit(solution)/shard_map/ppermute | solution.py:23
  40.2 1.0 copy-start.8
  40.2 8.4 %copy-start.4 = (f32[1,3,128,512]{3,2,1,0:T(8,128)S(1)}, f32[1,3,128,512]{3,2,1,0:T(8,128)}, u32[]{:S(2)}) copy-start(f32[1,3,128,512]{3,2,1,0:T(8,128)} %get-tuple-element.77.keep) | copy-start | bytes 2359300
  41.2 14.5 %collective-permute-start.7 = (bf16[1,3,128,512]{3,2,1,0:T(8,128)(2,1)S(1)}, bf16[1,3,128,512]{3,2,1,0:T(8,128)(2,1)S(1)}, u32[]{:S(2)}, u32[]{:S(2)}) collective-permute-start(bf16[1,3,128,512]{3,2,1,0:T(8,128)(2,1)S(1)} %copy-done.8), channel_id=1, source_target_pairs={{0,2},{1,3},{2,0},{3,1},{4,6},{5,7},{6,4},{7,5},{8,10},{9,11},{10,... | collective-permute-start | bytes 1179656 | tf_op jit(solution)/shard_map/ppermute | solution.py:23
  42.7 13.0 %collective-permute-start.11 = (bf16[1,3,128,512]{3,2,1,0:T(8,128)(2,1)S(1)}, bf16[1,3,128,512]{3,2,1,0:T(8,128)(2,1)S(1)}, u32[]{:S(2)}, u32[]{:S(2)}) collective-permute-start(bf16[1,3,128,512]{3,2,1,0:T(8,128)(2,1)S(1)} %get-tuple-element.75), channel_id=1, source_target_pairs={{1,5},{3,7},{4,0},{6,2},{9,13},{11,15},{12,8},{14,10},{17,21},{19,... | collective-permute-start | bytes 1179656 | tf_op jit(solution)/shard_map/ppermute | solution.py:23
  48.6 7.1 %copy-start.3 = (f32[1,3,128,512]{3,2,1,0:T(8,128)S(1)}, f32[1,3,128,512]{3,2,1,0:T(8,128)}, u32[]{:S(2)}) copy-start(f32[1,3,128,512]{3,2,1,0:T(8,128)} %get-tuple-element.73.keep) | copy-start | bytes 2359300
  48.8 9.9 %collective-permute-start.12 = (bf16[1,3,128,512]{3,2,1,0:T(8,128)(2,1)S(1)}, bf16[1,3,128,512]{3,2,1,0:T(8,128)(2,1)S(1)}, u32[]{:S(2)}, u32[]{:S(2)}) collective-permute-start(bf16[1,3,128,512]{3,2,1,0:T(8,128)(2,1)S(1)} %get-tuple-element.82), channel_id=1, source_target_pairs={{1,5},{3,7},{4,0},{6,2},{9,13},{11,15},{12,8},{14,10},{17,21},{19,... | collective-permute-start | bytes 1179656 | tf_op jit(solution)/shard_map/ppermute | solution.py:23
  56.0 28.9 %collective-permute-start.19 = (bf16[3,400,512]{2,1,0:T(8,128)(2,1)S(1)}, bf16[3,400,512]{2,1,0:T(8,128)(2,1)S(1)}, u32[]{:S(2)}, u32[]{:S(2)}) collective-permute-start(bf16[3,400,512]{2,1,0:T(8,128)(2,1)S(1)} %pad_maximum_fusion.refs_1_), channel_id=1, source_target_pairs={{0,2},{1,3},{2,0},{3,1},{4,6},{5,7},{6,4},{7,5},{8,10},{9,11},{10,... | collective-permute-start | bytes 3686408 | tf_op jit(solution)/shard_map/ppermute | solution.py:23
  56.8 9.7 %collective-permute-start.13 = (bf16[1,3,128,512]{3,2,1,0:T(8,128)(2,1)S(1)}, bf16[1,3,128,512]{3,2,1,0:T(8,128)(2,1)S(1)}, u32[]{:S(2)}, u32[]{:S(2)}) collective-permute-start(bf16[1,3,128,512]{3,2,1,0:T(8,128)(2,1)S(1)} %get-tuple-element.84), channel_id=1, source_target_pairs={{1,5},{3,7},{4,0},{6,2},{9,13},{11,15},{12,8},{14,10},{17,21},{19,... | collective-permute-start | bytes 1179656 | tf_op jit(solution)/shard_map/ppermute | solution.py:23
  58.1 15.7 %collective-permute-start.15 = (bf16[400,512]{1,0:T(8,128)(2,1)}, bf16[400,512]{1,0:T(8,128)(2,1)}, u32[]{:S(2)}, u32[]{:S(2)}) collective-permute-start(bf16[400,512]{1,0:T(8,128)(2,1)} %get-tuple-element.94.refs_0_), channel_id=1, source_target_pairs={{0,1},{1,0},{2,3},{3,2},{4,5},{5,4},{6,7},{7,6},{8,9},{9,8},{10,11... | collective-permute-start | bytes 1228808 | tf_op jit(solution)/shard_map/ppermute | solution.py:23
  58.2 15.8 %collective-permute-start.16 = (bf16[400,512]{1,0:T(8,128)(2,1)}, bf16[400,512]{1,0:T(8,128)(2,1)}, u32[]{:S(2)}, u32[]{:S(2)}) collective-permute-start(bf16[400,512]{1,0:T(8,128)(2,1)} %collective-permute-done.1.refs_4_), channel_id=1, source_target_pairs={{0,1},{1,0},{2,3},{3,2},{4,5},{5,4},{6,7},{7,6},{8,9},{9,8},{10,11... | collective-permute-start | bytes 1228808 | tf_op jit(solution)/shard_map/ppermute | solution.py:23
  60.0 19.3 %collective-permute-start.17 = (bf16[1,3,128,512]{3,2,1,0:T(8,128)(2,1)}, bf16[1,3,128,512]{3,2,1,0:T(8,128)(2,1)}, u32[]{:S(2)}, u32[]{:S(2)}) collective-permute-start(bf16[1,3,128,512]{3,2,1,0:T(8,128)(2,1)} %get-tuple-element.87), channel_id=1, source_target_pairs={{0,8},{2,10},{5,13},{7,15},{8,0},{10,2},{13,5},{15,7},{16,24},{18,... | collective-permute-start | bytes 1179656 | tf_op jit(solution)/shard_map/ppermute | solution.py:23
  67.8 0.9 copy-start
  68.7 10.6 %copy-start.2 = (f32[4]{0:T(128)S(1)}, f32[4]{0:T(128)}, u32[]{:S(2)}) copy-start(f32[4]{0:T(128)} %param.15) | copy-start | bytes 52
  68.7 14.8 %collective-permute-start.14 = (bf16[1,3,128,512]{3,2,1,0:T(8,128)(2,1)}, bf16[1,3,128,512]{3,2,1,0:T(8,128)(2,1)}, u32[]{:S(2)}, u32[]{:S(2)}) collective-permute-start(bf16[1,3,128,512]{3,2,1,0:T(8,128)(2,1)} %get-tuple-element.91), channel_id=1, source_target_pairs={{0,8},{2,10},{5,13},{7,15},{8,0},{10,2},{13,5},{15,7},{16,24},{18,... | collective-permute-start | bytes 1179656 | tf_op jit(solution)/shard_map/ppermute | solution.py:23
  73.8 9.7 %copy-start.1 = (f32[1,3,128,512]{3,2,1,0:T(8,128)S(1)}, f32[1,3,128,512]{3,2,1,0:T(8,128)}, u32[]{:S(2)}) copy-start(f32[1,3,128,512]{3,2,1,0:T(8,128)} %copy-done) | copy-start | bytes 2359300
  73.9 15.8 %collective-permute-start.18 = (bf16[3,400,512]{2,1,0:T(8,128)(2,1)S(1)}, bf16[3,400,512]{2,1,0:T(8,128)(2,1)S(1)}, u32[]{:S(2)}, u32[]{:S(2)}) collective-permute-start(bf16[3,400,512]{2,1,0:T(8,128)(2,1)S(1)} %pad_maximum_fusion.refs_1_), channel_id=1, source_target_pairs={{0,1},{1,0},{2,3},{3,2},{4,5},{5,4},{6,7},{7,6},{8,9},{9,8},{10,11... | collective-permute-start | bytes 3686408 | tf_op jit(solution)/shard_map/ppermute | solution.py:23
  84.9 4.8 %collective-permute-start.20 = (bf16[3,400,512]{2,1,0:T(8,128)(2,1)S(1)}, bf16[3,400,512]{2,1,0:T(8,128)(2,1)S(1)}, u32[]{:S(2)}, u32[]{:S(2)}) collective-permute-start(bf16[3,400,512]{2,1,0:T(8,128)(2,1)S(1)} %collective-permute-done.19.refs_5_), channel_id=1, source_target_pairs={{0,1},{1,0},{2,3},{3,2},{4,5},{5,4},{6,7},{7,6},{8,9},{9,8},{10,11... | collective-permute-start | bytes 3686408 | tf_op jit(solution)/shard_map/ppermute | solution.py:23
  85.0 13.9 %collective-permute-start.21 = (bf16[2,3,128,512]{3,2,1,0:T(8,128)(2,1)S(1)}, bf16[2,3,128,512]{3,2,1,0:T(8,128)(2,1)S(1)}, u32[]{:S(2)}, u32[]{:S(2)}) collective-permute-start(bf16[2,3,128,512]{3,2,1,0:T(8,128)(2,1)S(1)} %renew_1.1.refs_0_), channel_id=1, source_target_pairs={{0,2},{2,0},{5,7},{7,5},{8,10},{10,8},{13,15},{15,13},{16,18},{18,... | collective-permute-start | bytes 2359304 | tf_op jit(solution)/shard_map/ppermute | solution.py:23
  88.3 11.9 %collective-permute-start.22 = (bf16[2,3,128,512]{3,2,1,0:T(8,128)(2,1)S(1)}, bf16[2,3,128,512]{3,2,1,0:T(8,128)(2,1)S(1)}, u32[]{:S(2)}, u32[]{:S(2)}) collective-permute-start(bf16[2,3,128,512]{3,2,1,0:T(8,128)(2,1)S(1)} %renew_1.1.refs_0_), channel_id=1, source_target_pairs={{0,1},{2,3},{5,4},{7,6},{8,9},{10,11},{13,12},{15,14},{16,17},{18,... | collective-permute-start | bytes 2359304 | tf_op jit(solution)/shard_map/ppermute | solution.py:23
  98.8 3.2 %collective-permute-start.23 = (bf16[2,3,128,512]{3,2,1,0:T(8,128)(2,1)S(1)}, bf16[2,3,128,512]{3,2,1,0:T(8,128)(2,1)S(1)}, u32[]{:S(2)}, u32[]{:S(2)}) collective-permute-start(bf16[2,3,128,512]{3,2,1,0:T(8,128)(2,1)S(1)} %collective-permute-done.21.refs_1_), channel_id=1, source_target_pairs={{0,1},{2,3},{5,4},{7,6},{8,9},{10,11},{13,12},{15,14},{16,17},{18,... | collective-permute-start | bytes 2359304 | tf_op jit(solution)/shard_map/ppermute | solution.py:23
  103.0 12.6 %collective-permute-start.25 = (bf16[128,512]{1,0:T(8,128)(2,1)S(1)}, bf16[128,512]{1,0:T(8,128)(2,1)S(1)}, u32[]{:S(2)}, u32[]{:S(2)}) collective-permute-start(bf16[128,512]{1,0:T(8,128)(2,1)S(1)} %get-tuple-element.100), channel_id=1, source_target_pairs={{0,8},{1,9},{2,10},{3,11},{4,12},{5,13},{6,14},{7,15},{8,0},{9,1},... | collective-permute-start | bytes 393224 | tf_op jit(solution)/shard_map/ppermute | solution.py:23
  104.3 11.3 %collective-permute-start.24 = (bf16[128,512]{1,0:T(8,128)(2,1)S(1)}, bf16[128,512]{1,0:T(8,128)(2,1)S(1)}, u32[]{:S(2)}, u32[]{:S(2)}) collective-permute-start(bf16[128,512]{1,0:T(8,128)(2,1)S(1)} %get-tuple-element.103), channel_id=1, source_target_pairs={{0,4},{1,5},{2,6},{3,7},{4,0},{5,1},{6,2},{7,3},{8,12},{9,13},{10,... | collective-permute-start | bytes 393224 | tf_op jit(solution)/shard_map/ppermute | solution.py:23
  106.1 9.5 %collective-permute-start.26 = (bf16[128,512]{1,0:T(8,128)(2,1)S(1)}, bf16[128,512]{1,0:T(8,128)(2,1)S(1)}, u32[]{:S(2)}, u32[]{:S(2)}) collective-permute-start(bf16[128,512]{1,0:T(8,128)(2,1)S(1)} %get-tuple-element.104), channel_id=1, source_target_pairs={{0,12},{1,13},{2,14},{3,15},{4,8},{5,9},{6,10},{7,11},{8,4},{9,5},... | collective-permute-start | bytes 393224 | tf_op jit(solution)/shard_map/ppermute | solution.py:23

commit v7 on v6

--- a/solution.py
+++ b/solution.py
@@ -383,47 +383,46 @@
     )
 
 
-def hand_over_body(span, *refs):
+def pick_body(span, kept, *refs):
+    sources, out, total_s, got_s, sem = refs[:4], *refs[4:]
     upper = lax.axis_index(AXIS) // span // 2 == 1
-    sources, sends, keeps, total_s, got_s, sem = refs[:4], refs[4], refs[5], *refs[6:]
-
-    def fetch(first, second):
-        copies = []
-        for n, pair in enumerate((first, second)):
-            for i, (source, to) in enumerate(zip(pair, (total_s, got_s))):
-                copies.append(pltpu.make_async_copy(source, to.at[n], sem.at[n, i]))
-                copies[-1].start()
+
+    def fetch(pair):
+        copies = [
+            pltpu.make_async_copy(source, to, sem.at[n])
+            for n, (source, to) in enumerate(zip(pair, (total_s, got_s)))
+        ]
+        for copy in copies:
+            copy.start()
         for copy in copies:
             copy.wait()
 
     @pl.when(upper)
     def _():
-        fetch(sources[:2], sources[2:])
+        fetch(sources[2:] if kept else sources[:2])
 
     @pl.when(jnp.logical_not(upper))
     def _():
-        fetch(sources[2:], sources[:2])
-
-    sends[...] = (total_s[0] + got_s[0].astype(f32)).astype(bf16)
-    keeps[...] = total_s[1] + got_s[1].astype(f32)
-
-
-def hand_over(low, high, span):
+        fetch(sources[:2] if kept else sources[2:])
+
+    out[...] = (total_s[...] + got_s[...].astype(f32)).astype(out.dtype)
+
+
+def pick(low, high, span, kept):
     shape = low[0].shape
-    sources = (*low, *high)
     return call(
-        functools.partial(hand_over_body, span),
-        "hand_over",
-        sources,
+        functools.partial(pick_body, span, kept),
+        "keep" if kept else "hand_over",
+        (*low, *high),
         [pl.BlockSpec(memory_space=pl.ANY)] * 4,
-        [jax.ShapeDtypeStruct(shape, bf16), jax.ShapeDtypeStruct(shape, f32)],
+        [jax.ShapeDtypeStruct(shape, f32 if kept else bf16)],
         scratch=[
-            pltpu.VMEM((2, *shape), f32),
-            pltpu.VMEM((2, *shape), bf16),
-            pltpu.SemaphoreType.DMA((2, 2)),
+            pltpu.VMEM(shape, f32),
+            pltpu.VMEM(shape, bf16),
+            pltpu.SemaphoreType.DMA((2,)),
         ],
-        flops=4000000000,
-    )
+        flops=0 if kept else 4000000000,
+    )[0]
 
 
 def renew_body(span, heads, keep, got, old, steps, *refs):
@@ -631,9 +630,13 @@
     held = []
     for g in range(2):
         low = (after(sums[g][0], *turn), sums[g][1])
-        send, keep = hand_over(low, sums[2 + g], span)
-        held.append((keep, swap(send, 2 * span, matched)))
+        send = pick(low, sums[2 + g], span, False)
+        held.append(swap(send, 2 * span, matched))
         turn = [send]
+    held = [
+        (pick((after(sums[g][0], *turn), sums[g][1]), sums[2 + g], span, True), got)
+        for g, got in enumerate(held)
+    ]
     turn += early.values()
     fresh = renew(after(held[0][0], *turn), held[0][1], olds[0], steps, span, heads)
     fresh = renew(*held[1], olds[1], steps, span, heads, fresh)

time: 117 us -> 117 us (level)
  waiting for transfers between devices: 38.8 us -> 36.1 us
  local copies, waits for them, and re-layouts: 3.93 us -> 6.36 us
    ppermute x27, waiting for transfers between devices: 38.8 us -> 36.1 us  [swap(): return lax.ppermute(value, AXIS, pairs)]
    unnamed x18 -> x42, local copies, waits for them, and re-layouts: 2.73 us -> 5.05 us
    pallas_call x16 -> x18, Pallas kernels: 33.4 us -> 33.8 us  [call(): pl.pallas_call(body, name=name, grid=(1,), in_specs=specs, out_specs=out_...]
where the time goes in v7:
time: 117 us; the launch traced here: 116 us
  starting transfers between devices  39.5 us (34%)
  waiting for transfers between devices  36.1 us (31%)
  Pallas kernels  33.8 us (29%)
  local copies, waits for them, and re-layouts  6.36 us (5%)
    ppermute x27, starting transfers between devices, swap(): return lax.ppermute(value, AXIS, pairs)  39.5 us
    ppermute x27, waiting for transfers between devices, swap(): return lax.ppermute(value, AXIS, pairs)  36.1 us
    pallas_call x18, Pallas kernels, call(): pl.pallas_call(body, name=name, grid=(1,), in_specs=specs, out_specs=out_...  33.8 us
    unnamed x42, local copies, waits for them, and re-layouts  5.05 us
  transfers between devices with their start and end apart: 27, of which 10 were waited for; matrix products, arithmetic and copies ran while one was open for 1% of the time, Pallas kernels for 24%

profile of v7, /device:TPU:0, one launch (start us, length us, event | category | flops | bytes accessed | tf_op | source)
XLA Modules:
  0.0 116.3 jit_solution(930468286780831862)
XLA Ops:
  0.0 3.8 %pack.1 = (bf16[2,512,512]{2,1,0:T(8,128)(2,1)}, bf16[2,512,512]{2,1,0:T(8,128)(2,1)}, bf16[400,512]{1,0:T(8,128)(2,1)}, bf16[400,512]{1,0:T(8,128)(2,1)}, bf16[...) custom-call(f32[4,512]{1,0:T(4,128)} %bitcast.12, s32[1,512]{1,0:T(1,128)} %bitcast.15, s32[1,128]{1,0:T(1,128)} %bitcast.18, ...), custom_call_target="tpu_custom_call" | custom-call | tf_op jit(solution)/shard_map/pack/pallas_call | solution.py:55
  3.9 0.5 collective-permute-start
  4.4 0.1 collective-permute-start.2
  4.5 2.9 %collective-permute-start.1 = (bf16[400,512]{1,0:T(8,128)(2,1)}, bf16[400,512]{1,0:T(8,128)(2,1)}, u32[]{:S(2)}, u32[]{:S(2)}) collective-permute-start(bf16[400,512]{1,0:T(8,128)(2,1)} %get-tuple-element.90.refs_0_), channel_id=1, source_target_pairs={{0,2},{1,3},{2,0},{3,1},{4,6},{5,7},{6,4},{7,5},{8,10},{9,11},{10,... | collective-permute-start | bytes 1228808 | tf_op jit(solution)/shard_map/ppermute | solution.py:23
  7.4 1.6 %collective-permute-start.5 = (bf16[400,512]{1,0:T(8,128)(2,1)}, bf16[400,512]{1,0:T(8,128)(2,1)S(1)}, u32[]{:S(2)}, u32[]{:S(2)}) collective-permute-start(bf16[400,512]{1,0:T(8,128)(2,1)} %get-tuple-element.64), channel_id=1, source_target_pairs={{0,4},{1,5},{2,6},{3,7},{4,0},{5,1},{6,2},{7,3},{8,12},{9,13},{10,... | collective-permute-start | bytes 1228808 | tf_op jit(solution)/shard_map/ppermute | solution.py:23
  9.0 2.6 %collective-permute-start.6 = (bf16[400,512]{1,0:T(8,128)(2,1)}, bf16[400,512]{1,0:T(8,128)(2,1)S(1)}, u32[]{:S(2)}, u32[]{:S(2)}) collective-permute-start(bf16[400,512]{1,0:T(8,128)(2,1)} %get-tuple-element.65), channel_id=1, source_target_pairs={{0,8},{1,9},{2,10},{3,11},{4,12},{5,13},{6,14},{7,15},{8,0},{9,1},... | collective-permute-start | bytes 1228808 | tf_op jit(solution)/shard_map/ppermute | solution.py:23
  11.6 1.0 copy-done.19
  12.6 7.3 %head_grad_0.1 = (bf16[1,3,128,512]{3,2,1,0:T(8,128)(2,1)}, bf16[1,3,128,512]{3,2,1,0:T(8,128)(2,1)}, f32[1,3,128,512]{3,2,1,0:T(8,128)}, f32[1,3,128,512]{3,2,1,0:T(8,128)}) custom-call(f32[4,512]{1,0:T(4,128)} %bitcast.13, s32[1,512]{1,0:T(1,128)} %bitcast.16, bf16[512,2048]{1,0:T(8,128)(2,1)} %keys.5, bf16[512,2048]{1,0:T(8,128)(2,1)} %values.5, ...), custom_call_target="tpu_custom_call" | custom-call | tf_op jit(solution)/shard_map/head_grad_0/pallas_call | solution.py:55
  19.9 0.6 collective-permute-start.4
  20.5 7.4 %head_grad_1.1 = (bf16[1,3,128,512]{3,2,1,0:T(8,128)(2,1)}, bf16[1,3,128,512]{3,2,1,0:T(8,128)(2,1)}, f32[1,3,128,512]{3,2,1,0:T(8,128)}, f32[1,3,128,512]{3,2,1,0:T(8,128)}) custom-call(f32[4,512]{1,0:T(4,128)} %bitcast.14, s32[1,512]{1,0:T(1,128)} %bitcast.17, bf16[512,2048]{1,0:T(8,128)(2,1)} %keys.5, bf16[512,2048]{1,0:T(8,128)(2,1)} %values.5, ...), custom_call_target="tpu_custom_call" | custom-call | tf_op jit(solution)/shard_map/head_grad_1/pallas_call | solution.py:55
  27.9 1.6 %collective-permute-start.3 = (bf16[1,3,128,512]{3,2,1,0:T(8,128)(2,1)}, bf16[1,3,128,512]{3,2,1,0:T(8,128)(2,1)S(1)}, u32[]{:S(2)}, u32[]{:S(2)}) collective-permute-start(bf16[1,3,128,512]{3,2,1,0:T(8,128)(2,1)} %get-tuple-element.62), channel_id=1, source_target_pairs={{0,2},{1,3},{2,0},{3,1},{4,6},{5,7},{6,4},{7,5},{8,10},{9,11},{10,... | collective-permute-start | bytes 1179656 | tf_op jit(solution)/shard_map/ppermute | solution.py:23
  29.5 0.3 collective-permute-done.6
  29.8 0.5 collective-permute-start.8
  30.3 2.5 %collective-permute-start.9 = (bf16[400,512]{1,0:T(8,128)(2,1)}, bf16[400,512]{1,0:T(8,128)(2,1)S(1)}, u32[]{:S(2)}, u32[]{:S(2)}) collective-permute-start(bf16[400,512]{1,0:T(8,128)(2,1)} %get-tuple-element.78), channel_id=1, source_target_pairs={{0,12},{1,13},{2,14},{3,15},{4,8},{5,9},{6,10},{7,11},{8,4},{9,5},... | collective-permute-start | bytes 1228808 | tf_op jit(solution)/shard_map/ppermute | solution.py:23
  32.8 0.1 add.34
  32.9 1.4 %collective-permute-start.10 = (bf16[1,3,128,512]{3,2,1,0:T(8,128)(2,1)S(1)}, bf16[1,3,128,512]{3,2,1,0:T(8,128)(2,1)S(1)}, u32[]{:S(2)}, u32[]{:S(2)}) collective-permute-start(bf16[1,3,128,512]{3,2,1,0:T(8,128)(2,1)S(1)} %get-tuple-element.67), channel_id=1, source_target_pairs={{1,5},{3,7},{4,0},{6,2},{9,13},{11,15},{12,8},{14,10},{17,21},{19,... | collective-permute-start | bytes 1179656 | tf_op jit(solution)/shard_map/ppermute | solution.py:23
  34.4 5.8 %collective-permute-done.3.got = bf16[1,3,128,512]{3,2,1,0:T(8,128)(2,1)S(1)} collective-permute-done((bf16[1,3,128,512]{3,2,1,0:T(8,128)(2,1)}, bf16[1,3,128,512]{3,2,1,0:T(8,128)(2,1)S(1)}, u32[]{:S(2)}, u32[]{:S(2)}) %collective-permute-start.3) | collective-permute-done | bytes 393248 | tf_op jit(solution)/shard_map/ppermute | solution.py:23
  40.2 0.1 add.35
  40.4 0.8 copy-done.20
  41.2 1.5 %collective-permute-start.7 = (bf16[1,3,128,512]{3,2,1,0:T(8,128)(2,1)S(1)}, bf16[1,3,128,512]{3,2,1,0:T(8,128)(2,1)S(1)}, u32[]{:S(2)}, u32[]{:S(2)}) collective-permute-start(bf16[1,3,128,512]{3,2,1,0:T(8,128)(2,1)S(1)} %copy-done.20), channel_id=1, source_target_pairs={{0,2},{1,3},{2,0},{3,1},{4,6},{5,7},{6,4},{7,5},{8,10},{9,11},{10,... | collective-permute-start | bytes 1179656 | tf_op jit(solution)/shard_map/ppermute | solution.py:23
  42.7 1.3 %collective-permute-start.11 = (bf16[1,3,128,512]{3,2,1,0:T(8,128)(2,1)S(1)}, bf16[1,3,128,512]{3,2,1,0:T(8,128)(2,1)S(1)}, u32[]{:S(2)}, u32[]{:S(2)}) collective-permute-start(bf16[1,3,128,512]{3,2,1,0:T(8,128)(2,1)S(1)} %get-tuple-element.73), channel_id=1, source_target_pairs={{1,5},{3,7},{4,0},{6,2},{9,13},{11,15},{12,8},{14,10},{17,21},{19,... | collective-permute-start | bytes 1179656 | tf_op jit(solution)/shard_map/ppermute | solution.py:23
  44.0 4.6 %collective-permute-done.8.got = bf16[1,3,128,512]{3,2,1,0:T(8,128)(2,1)S(1)} collective-permute-done((bf16[1,3,128,512]{3,2,1,0:T(8,128)(2,1)}, bf16[1,3,128,512]{3,2,1,0:T(8,128)(2,1)S(1)}, u32[]{:S(2)}, u32[]{:S(2)}) %collective-permute-start.8) | collective-permute-done | bytes 393248 | tf_op jit(solution)/shard_map/ppermute | solution.py:23
  48.7 0.2 add.36
  48.8 1.4 %collective-permute-start.12 = (bf16[1,3,128,512]{3,2,1,0:T(8,128)(2,1)S(1)}, bf16[1,3,128,512]{3,2,1,0:T(8,128)(2,1)S(1)}, u32[]{:S(2)}, u32[]{:S(2)}) collective-permute-start(bf16[1,3,128,512]{3,2,1,0:T(8,128)(2,1)S(1)} %get-tuple-element.80), channel_id=1, source_target_pairs={{1,5},{3,7},{4,0},{6,2},{9,13},{11,15},{12,8},{14,10},{17,21},{19,... | collective-permute-start | bytes 1179656 | tf_op jit(solution)/shard_map/ppermute | solution.py:23
  50.3 5.5 %collective-permute-done.7.got = bf16[1,3,128,512]{3,2,1,0:T(8,128)(2,1)S(1)} collective-permute-done((bf16[1,3,128,512]{3,2,1,0:T(8,128)(2,1)S(1)}, bf16[1,3,128,512]{3,2,1,0:T(8,128)(2,1)S(1)}, u32[]{:S(2)}, u32[]{:S(2)}) %collective-permute-start.7) | collective-permute-done | bytes 393248 | tf_op jit(solution)/shard_map/ppermute | solution.py:23
  55.7 0.1 add.37
  55.9 0.1 pad_maximum_fusion.refs_1_
  56.0 0.8 collective-permute-start.19
  56.9 1.3 %collective-permute-start.13 = (bf16[1,3,128,512]{3,2,1,0:T(8,128)(2,1)S(1)}, bf16[1,3,128,512]{3,2,1,0:T(8,128)(2,1)S(1)}, u32[]{:S(2)}, u32[]{:S(2)}) collective-permute-start(bf16[1,3,128,512]{3,2,1,0:T(8,128)(2,1)S(1)} %get-tuple-element.82), channel_id=1, source_target_pairs={{1,5},{3,7},{4,0},{6,2},{9,13},{11,15},{12,8},{14,10},{17,21},{19,... | collective-permute-start | bytes 1179656 | tf_op jit(solution)/shard_map/ppermute | solution.py:23
  58.2 0.1 collective-permute-start.15
  58.3 0.5 collective-permute-start.16
  58.8 1.1 hand_over.2
  59.9 4.2 %collective-permute-start.17 = (bf16[1,3,128,512]{3,2,1,0:T(8,128)(2,1)}, bf16[1,3,128,512]{3,2,1,0:T(8,128)(2,1)}, u32[]{:S(2)}, u32[]{:S(2)}) collective-permute-start(bf16[1,3,128,512]{3,2,1,0:T(8,128)(2,1)} %hand_over.2), channel_id=1, source_target_pairs={{0,8},{2,10},{5,13},{7,15},{8,0},{10,2},{13,5},{15,7},{16,24},{18,... | collective-permute-start | bytes 1179656 | tf_op jit(solution)/shard_map/ppermute | solution.py:23
  64.1 2.5 %collective-permute-done.13.refs_3_ = bf16[1,3,128,512]{3,2,1,0:T(8,128)(2,1)S(1)} collective-permute-done((bf16[1,3,128,512]{3,2,1,0:T(8,128)(2,1)S(1)}, bf16[1,3,128,512]{3,2,1,0:T(8,128)(2,1)S(1)}, u32[]{:S(2)}, u32[]{:S(2)}) %collective-permute-start.13) | collective-permute-done | bytes 393248 | tf_op jit(solution)/shard_map/ppermute | solution.py:23
  66.6 1.1 hand_over.3
  67.7 3.5 %collective-permute-start.14 = (bf16[1,3,128,512]{3,2,1,0:T(8,128)(2,1)}, bf16[1,3,128,512]{3,2,1,0:T(8,128)(2,1)}, u32[]{:S(2)}, u32[]{:S(2)}) collective-permute-start(bf16[1,3,128,512]{3,2,1,0:T(8,128)(2,1)} %hand_over.3), channel_id=1, source_target_pairs={{0,8},{2,10},{5,13},{7,15},{8,0},{10,2},{13,5},{15,7},{16,24},{18,... | collective-permute-start | bytes 1179656 | tf_op jit(solution)/shard_map/ppermute | solution.py:23
  71.3 1.3 %constant_dynamic-slice_fusion = (bf16[1,3,128,512]{3,2,1,0:T(8,128)(2,1)S(1)}, bf16[1,3,128,512]{3,2,1,0:T(8,128)(2,1)S(1)}) fusion(bf16[4,3,512,512]{3,2,1,0:T(8,128)(2,1)} %weights.3, s32[]{:T(128)S(6)} %select_n.30, s32[]{:T(128)S(6)} %select_n.32, s32[]{:T(128)S(6)} %select_n.31), kind=kLoop, calls=%fused_computation.1 | loop fusion | bytes 1572876 | tf_op jit(solution)/shard_map/dynamic_slice | solution.py:625
  72.6 0.2 copy-done.3
  72.9 1.0 copy-done.7
  73.9 1.0 copy-done.11
  74.9 0.3 keep.3
  75.2 0.1 collective-permute-start.18
  75.3 0.7 copy-done.5
  76.0 0.1 copy-done.9
  76.1 0.1 copy-done.13
  76.2 0.5 keep.2
  76.7 2.5 %collective-permute-done.17.got = bf16[1,3,128,512]{3,2,1,0:T(8,128)(2,1)} collective-permute-done((bf16[1,3,128,512]{3,2,1,0:T(8,128)(2,1)}, bf16[1,3,128,512]{3,2,1,0:T(8,128)(2,1)}, u32[]{:S(2)}, u32[]{:S(2)}) %collective-permute-start.17) | collective-permute-done | bytes 393248 | tf_op jit(solution)/shard_map/ppermute | solution.py:23
  79.2 1.3 %renew_0.1.refs_0_ = bf16[1,3,128,512]{3,2,1,0:T(8,128)(2,1)S(1)} custom-call(f32[1,3,128,512]{3,2,1,0:T(8,128)S(1)} %keep.3, bf16[1,3,128,512]{3,2,1,0:T(8,128)(2,1)} %collective-permute-done.17.got, bf16[1,3,128,512]{3,2,1,0:T(8,128)(2,1)S(1)} %get-tuple-element.101.old, f32[1,4]{1,0:T(1,128)S(1)} %bitcast.7), custom_call_target="tpu_custom_call" | custom-call | tf_op jit(solution)/shard_map/renew_0/pallas_call | solution.py:55
  80.5 2.9 %collective-permute-done.14.got = bf16[1,3,128,512]{3,2,1,0:T(8,128)(2,1)} collective-permute-done((bf16[1,3,128,512]{3,2,1,0:T(8,128)(2,1)}, bf16[1,3,128,512]{3,2,1,0:T(8,128)(2,1)}, u32[]{:S(2)}, u32[]{:S(2)}) %collective-permute-start.14) | collective-permute-done | bytes 393248 | tf_op jit(solution)/shard_map/ppermute | solution.py:23
  83.4 1.3 %renew_1.1.refs_0_ = bf16[2,3,128,512]{3,2,1,0:T(8,128)(2,1)S(1)} custom-call(f32[1,3,128,512]{3,2,1,0:T(8,128)S(1)} %keep.2, bf16[1,3,128,512]{3,2,1,0:T(8,128)(2,1)} %collective-permute-done.14.got, bf16[1,3,128,512]{3,2,1,0:T(8,128)(2,1)S(1)} %get-tuple-element.102.old, f32[1,4]{1,0:T(1,128)S(1)} %bitcast.8, bf16[1,3,128,512]{3,2,1,0:T(8,128)(2,1)S(1)} %renew_0.1.refs_0_), custom_call_target="tpu_custom_call" | custom-call | tf_op jit(solution)/shard_map/renew_1/pallas_call | solution.py:55
  84.8 3.3 %collective-permute-start.21 = (bf16[2,3,128,512]{3,2,1,0:T(8,128)(2,1)S(1)}, bf16[2,3,128,512]{3,2,1,0:T(8,128)(2,1)S(1)}, u32[]{:S(2)}, u32[]{:S(2)}) collective-permute-start(bf16[2,3,128,512]{3,2,1,0:T(8,128)(2,1)S(1)} %renew_1.1.refs_0_), channel_id=1, source_target_pairs={{0,2},{2,0},{5,7},{7,5},{8,10},{10,8},{13,15},{15,13},{16,18},{18,... | collective-permute-start | bytes 2359304 | tf_op jit(solution)/shard_map/ppermute | solution.py:23
  88.1 1.3 %collective-permute-start.22 = (bf16[2,3,128,512]{3,2,1,0:T(8,128)(2,1)S(1)}, bf16[2,3,128,512]{3,2,1,0:T(8,128)(2,1)S(1)}, u32[]{:S(2)}, u32[]{:S(2)}) collective-permute-start(bf16[2,3,128,512]{3,2,1,0:T(8,128)(2,1)S(1)} %renew_1.1.refs_0_), channel_id=1, source_target_pairs={{0,1},{2,3},{5,4},{7,6},{8,9},{10,11},{13,12},{15,14},{16,17},{18,... | collective-permute-start | bytes 2359304 | tf_op jit(solution)/shard_map/ppermute | solution.py:23
  89.5 5.0 %arrange.1.rows = bf16[3,512,512]{2,1,0:T(8,128)(2,1)S(1)} custom-call(bf16[400,512]{1,0:T(8,128)(2,1)} %get-tuple-element.90.refs_0_, bf16[3,400,512]{2,1,0:T(8,128)(2,1)S(1)} %pad_maximum_fusion.refs_1_, bf16[400,512]{1,0:T(8,128)(2,1)} %collective-permute-done.15.refs_2_, bf16[3,400,512]{2,1,0:T(8,128)(2,1)S(1)} %collective-permute-done.18.refs_3_, ...), custom_call_target="tpu_custom_call" | custom-call | tf_op jit(solution)/shard_map/arrange/pallas_call | solution.py:55
  94.5 1.2 attend.1.attended
  95.6 3.1 %collective-permute-done.21.refs_1_ = bf16[2,3,128,512]{3,2,1,0:T(8,128)(2,1)S(1)} collective-permute-done((bf16[2,3,128,512]{3,2,1,0:T(8,128)(2,1)S(1)}, bf16[2,3,128,512]{3,2,1,0:T(8,128)(2,1)S(1)}, u32[]{:S(2)}, u32[]{:S(2)}) %collective-permute-start.21) | collective-permute-done | bytes 786464 | tf_op jit(solution)/shard_map/ppermute | solution.py:23
  98.7 1.3 %collective-permute-start.23 = (bf16[2,3,128,512]{3,2,1,0:T(8,128)(2,1)S(1)}, bf16[2,3,128,512]{3,2,1,0:T(8,128)(2,1)S(1)}, u32[]{:S(2)}, u32[]{:S(2)}) collective-permute-start(bf16[2,3,128,512]{3,2,1,0:T(8,128)(2,1)S(1)} %collective-permute-done.21.refs_1_), channel_id=1, source_target_pairs={{0,1},{2,3},{5,4},{7,6},{8,9},{10,11},{13,12},{15,14},{16,17},{18,... | collective-permute-start | bytes 2359304 | tf_op jit(solution)/shard_map/ppermute | solution.py:23
  100.1 1.8 %collective-permute-done.23.refs_3_ = bf16[2,3,128,512]{3,2,1,0:T(8,128)(2,1)S(1)} collective-permute-done((bf16[2,3,128,512]{3,2,1,0:T(8,128)(2,1)S(1)}, bf16[2,3,128,512]{3,2,1,0:T(8,128)(2,1)S(1)}, u32[]{:S(2)}, u32[]{:S(2)}) %collective-permute-start.23) | collective-permute-done | bytes 786464 | tf_op jit(solution)/shard_map/ppermute | solution.py:23
  101.9 1.0 finish_2.1
  102.9 0.4 collective-permute-start.25
  103.3 1.0 finish_0.1
  104.3 1.6 %collective-permute-start.24 = (bf16[128,512]{1,0:T(8,128)(2,1)S(1)}, bf16[128,512]{1,0:T(8,128)(2,1)S(1)}, u32[]{:S(2)}, u32[]{:S(2)}) collective-permute-start(bf16[128,512]{1,0:T(8,128)(2,1)S(1)} %get-tuple-element.99), channel_id=1, source_target_pairs={{0,4},{1,5},{2,6},{3,7},{4,0},{5,1},{6,2},{7,3},{8,12},{9,13},{10,... | collective-permute-start | bytes 393224 | tf_op jit(solution)/shard_map/ppermute | solution.py:23
  105.9 2.5 %collective-permute-start.26 = (bf16[128,512]{1,0:T(8,128)(2,1)S(1)}, bf16[128,512]{1,0:T(8,128)(2,1)S(1)}, u32[]{:S(2)}, u32[]{:S(2)}) collective-permute-start(bf16[128,512]{1,0:T(8,128)(2,1)S(1)} %get-tuple-element.100), channel_id=1, source_target_pairs={{0,12},{1,13},{2,14},{3,15},{4,8},{5,9},{6,10},{7,11},{8,4},{9,5},... | collective-permute-start | bytes 393224 | tf_op jit(solution)/shard_map/ppermute | solution.py:23
  108.5 7.0 %collective-permute-done.24.refs_1_ = bf16[128,512]{1,0:T(8,128)(2,1)S(1)} collective-permute-done((bf16[128,512]{1,0:T(8,128)(2,1)S(1)}, bf16[128,512]{1,0:T(8,128)(2,1)S(1)}, u32[]{:S(2)}, u32[]{:S(2)}) %collective-permute-start.24) | collective-permute-done | bytes 131104 | tf_op jit(solution)/shard_map/ppermute | solution.py:23
  115.5 0.9 join.1
  (52 shorter events, 0.2 us)
Async XLA Ops:
  3.9 7.7 %collective-permute-start = (bf16[2,512,512]{2,1,0:T(8,128)(2,1)}, bf16[2,512,512]{2,1,0:T(8,128)(2,1)S(1)}, u32[]{:S(2)}, u32[]{:S(2)}) collective-permute-start(bf16[2,512,512]{2,1,0:T(8,128)(2,1)} %get-tuple-element.55), channel_id=1, source_target_pairs={{0,1},{1,0},{2,3},{3,2},{4,5},{5,4},{6,7},{7,6},{8,9},{9,8},{10,11... | collective-permute-start | bytes 3145736 | tf_op jit(solution)/shard_map/ppermute | solution.py:23
  4.4 16.1 %collective-permute-start.2 = (bf16[2,512,512]{2,1,0:T(8,128)(2,1)}, bf16[2,512,512]{2,1,0:T(8,128)(2,1)}, u32[]{:S(2)}, u32[]{:S(2)}) collective-permute-start(bf16[2,512,512]{2,1,0:T(8,128)(2,1)} %get-tuple-element.60), channel_id=1, source_target_pairs={{0,1},{1,0},{2,3},{3,2},{4,5},{5,4},{6,7},{7,6},{8,9},{9,8},{10,11... | collective-permute-start | bytes 3145736 | tf_op jit(solution)/shard_map/ppermute | solution.py:23
  4.5 16.0 %collective-permute-start.1 = (bf16[400,512]{1,0:T(8,128)(2,1)}, bf16[400,512]{1,0:T(8,128)(2,1)}, u32[]{:S(2)}, u32[]{:S(2)}) collective-permute-start(bf16[400,512]{1,0:T(8,128)(2,1)} %get-tuple-element.90.refs_0_), channel_id=1, source_target_pairs={{0,2},{1,3},{2,0},{3,1},{4,6},{5,7},{6,4},{7,5},{8,10},{9,11},{10,... | collective-permute-start | bytes 1228808 | tf_op jit(solution)/shard_map/ppermute | solution.py:23
  7.4 22.1 %collective-permute-start.5 = (bf16[400,512]{1,0:T(8,128)(2,1)}, bf16[400,512]{1,0:T(8,128)(2,1)S(1)}, u32[]{:S(2)}, u32[]{:S(2)}) collective-permute-start(bf16[400,512]{1,0:T(8,128)(2,1)} %get-tuple-element.64), channel_id=1, source_target_pairs={{0,4},{1,5},{2,6},{3,7},{4,0},{5,1},{6,2},{7,3},{8,12},{9,13},{10,... | collective-permute-start | bytes 1228808 | tf_op jit(solution)/shard_map/ppermute | solution.py:23
  9.0 20.8 %collective-permute-start.6 = (bf16[400,512]{1,0:T(8,128)(2,1)}, bf16[400,512]{1,0:T(8,128)(2,1)S(1)}, u32[]{:S(2)}, u32[]{:S(2)}) collective-permute-start(bf16[400,512]{1,0:T(8,128)(2,1)} %get-tuple-element.65), channel_id=1, source_target_pairs={{0,8},{1,9},{2,10},{3,11},{4,12},{5,13},{6,14},{7,15},{8,0},{9,1},... | collective-permute-start | bytes 1228808 | tf_op jit(solution)/shard_map/ppermute | solution.py:23
  11.6 1.0 copy-start.19
  19.9 12.9 %copy-start.18 = (f32[1,3,128,512]{3,2,1,0:T(8,128)S(1)}, f32[1,3,128,512]{3,2,1,0:T(8,128)}, u32[]{:S(2)}) copy-start(f32[1,3,128,512]{3,2,1,0:T(8,128)} %get-tuple-element.63.keep) | copy-start | bytes 2359300
  19.9 12.9 %collective-permute-start.4 = (bf16[1,3,128,512]{3,2,1,0:T(8,128)(2,1)}, bf16[1,3,128,512]{3,2,1,0:T(8,128)(2,1)S(1)}, u32[]{:S(2)}, u32[]{:S(2)}) collective-permute-start(bf16[1,3,128,512]{3,2,1,0:T(8,128)(2,1)} %get-tuple-element.58), channel_id=1, source_target_pairs={{0,2},{1,3},{2,0},{3,1},{4,6},{5,7},{6,4},{7,5},{8,10},{9,11},{10,... | collective-permute-start | bytes 1179656 | tf_op jit(solution)/shard_map/ppermute | solution.py:23
  27.9 12.3 %collective-permute-start.3 = (bf16[1,3,128,512]{3,2,1,0:T(8,128)(2,1)}, bf16[1,3,128,512]{3,2,1,0:T(8,128)(2,1)S(1)}, u32[]{:S(2)}, u32[]{:S(2)}) collective-permute-start(bf16[1,3,128,512]{3,2,1,0:T(8,128)(2,1)} %get-tuple-element.62), channel_id=1, source_target_pairs={{0,2},{1,3},{2,0},{3,1},{4,6},{5,7},{6,4},{7,5},{8,10},{9,11},{10,... | collective-permute-start | bytes 1179656 | tf_op jit(solution)/shard_map/ppermute | solution.py:23
  29.8 18.8 %collective-permute-start.8 = (bf16[1,3,128,512]{3,2,1,0:T(8,128)(2,1)}, bf16[1,3,128,512]{3,2,1,0:T(8,128)(2,1)S(1)}, u32[]{:S(2)}, u32[]{:S(2)}) collective-permute-start(bf16[1,3,128,512]{3,2,1,0:T(8,128)(2,1)} %get-tuple-element.76), channel_id=1, source_target_pairs={{0,2},{1,3},{2,0},{3,1},{4,6},{5,7},{6,4},{7,5},{8,10},{9,11},{10,... | collective-permute-start | bytes 1179656 | tf_op jit(solution)/shard_map/ppermute | solution.py:23
  30.3 18.3 %collective-permute-start.9 = (bf16[400,512]{1,0:T(8,128)(2,1)}, bf16[400,512]{1,0:T(8,128)(2,1)S(1)}, u32[]{:S(2)}, u32[]{:S(2)}) collective-permute-start(bf16[400,512]{1,0:T(8,128)(2,1)} %get-tuple-element.78), channel_id=1, source_target_pairs={{0,12},{1,13},{2,14},{3,15},{4,8},{5,9},{6,10},{7,11},{8,4},{9,5},... | collective-permute-start | bytes 1228808 | tf_op jit(solution)/shard_map/ppermute | solution.py:23
  32.8 7.4 %copy-start.17 = (f32[1,3,128,512]{3,2,1,0:T(8,128)S(1)}, f32[1,3,128,512]{3,2,1,0:T(8,128)}, u32[]{:S(2)}) copy-start(f32[1,3,128,512]{3,2,1,0:T(8,128)} %get-tuple-element.56.keep) | copy-start | bytes 2359300
  32.9 25.8 %copy-start = (f32[1,3,128,512]{3,2,1,0:T(8,128)}, f32[1,3,128,512]{3,2,1,0:T(8,128)S(1)}, u32[]{:S(2)}) copy-start(f32[1,3,128,512]{3,2,1,0:T(8,128)S(1)} %get-tuple-element.88.refs_0_) | copy-start | bytes 2359300
  32.9 15.7 %collective-permute-start.10 = (bf16[1,3,128,512]{3,2,1,0:T(8,128)(2,1)S(1)}, bf16[1,3,128,512]{3,2,1,0:T(8,128)(2,1)S(1)}, u32[]{:S(2)}, u32[]{:S(2)}) collective-permute-start(bf16[1,3,128,512]{3,2,1,0:T(8,128)(2,1)S(1)} %get-tuple-element.67), channel_id=1, source_target_pairs={{1,5},{3,7},{4,0},{6,2},{9,13},{11,15},{12,8},{14,10},{17,21},{19,... | collective-permute-start | bytes 1179656 | tf_op jit(solution)/shard_map/ppermute | solution.py:23
  40.2 1.0 copy-start.20
  40.2 8.4 %copy-start.16 = (f32[1,3,128,512]{3,2,1,0:T(8,128)S(1)}, f32[1,3,128,512]{3,2,1,0:T(8,128)}, u32[]{:S(2)}) copy-start(f32[1,3,128,512]{3,2,1,0:T(8,128)} %get-tuple-element.75.keep) | copy-start | bytes 2359300
  41.2 14.5 %collective-permute-start.7 = (bf16[1,3,128,512]{3,2,1,0:T(8,128)(2,1)S(1)}, bf16[1,3,128,512]{3,2,1,0:T(8,128)(2,1)S(1)}, u32[]{:S(2)}, u32[]{:S(2)}) collective-permute-start(bf16[1,3,128,512]{3,2,1,0:T(8,128)(2,1)S(1)} %copy-done.20), channel_id=1, source_target_pairs={{0,2},{1,3},{2,0},{3,1},{4,6},{5,7},{6,4},{7,5},{8,10},{9,11},{10,... | collective-permute-start | bytes 1179656 | tf_op jit(solution)/shard_map/ppermute | solution.py:23
  42.7 13.0 %collective-permute-start.11 = (bf16[1,3,128,512]{3,2,1,0:T(8,128)(2,1)S(1)}, bf16[1,3,128,512]{3,2,1,0:T(8,128)(2,1)S(1)}, u32[]{:S(2)}, u32[]{:S(2)}) collective-permute-start(bf16[1,3,128,512]{3,2,1,0:T(8,128)(2,1)S(1)} %get-tuple-element.73), channel_id=1, source_target_pairs={{1,5},{3,7},{4,0},{6,2},{9,13},{11,15},{12,8},{14,10},{17,21},{19,... | collective-permute-start | bytes 1179656 | tf_op jit(solution)/shard_map/ppermute | solution.py:23
  48.6 10.1 %copy-start.6 = (bf16[1,3,128,512]{3,2,1,0:T(8,128)(2,1)}, bf16[1,3,128,512]{3,2,1,0:T(8,128)(2,1)S(1)}, u32[]{:S(2)}) copy-start(bf16[1,3,128,512]{3,2,1,0:T(8,128)(2,1)S(1)} %collective-permute-done.10.refs_1_) | copy-start | bytes 1179652
  48.6 7.1 %copy-start.15 = (f32[1,3,128,512]{3,2,1,0:T(8,128)S(1)}, f32[1,3,128,512]{3,2,1,0:T(8,128)}, u32[]{:S(2)}) copy-start(f32[1,3,128,512]{3,2,1,0:T(8,128)} %get-tuple-element.71.keep) | copy-start | bytes 2359300
  48.8 9.9 %copy-start.2 = (f32[1,3,128,512]{3,2,1,0:T(8,128)}, f32[1,3,128,512]{3,2,1,0:T(8,128)S(1)}, u32[]{:S(2)}) copy-start(f32[1,3,128,512]{3,2,1,0:T(8,128)S(1)} %get-tuple-element.84.refs_2_) | copy-start | bytes 2359300
  48.8 9.9 %collective-permute-start.12 = (bf16[1,3,128,512]{3,2,1,0:T(8,128)(2,1)S(1)}, bf16[1,3,128,512]{3,2,1,0:T(8,128)(2,1)S(1)}, u32[]{:S(2)}, u32[]{:S(2)}) collective-permute-start(bf16[1,3,128,512]{3,2,1,0:T(8,128)(2,1)S(1)} %get-tuple-element.80), channel_id=1, source_target_pairs={{1,5},{3,7},{4,0},{6,2},{9,13},{11,15},{12,8},{14,10},{17,21},{19,... | collective-permute-start | bytes 1179656 | tf_op jit(solution)/shard_map/ppermute | solution.py:23
  55.7 10.8 %copy-start.8 = (bf16[1,3,128,512]{3,2,1,0:T(8,128)(2,1)}, bf16[1,3,128,512]{3,2,1,0:T(8,128)(2,1)S(1)}, u32[]{:S(2)}) copy-start(bf16[1,3,128,512]{3,2,1,0:T(8,128)(2,1)S(1)} %collective-permute-done.11.refs_1_) | copy-start | bytes 1179652
  55.9 10.7 %copy-start.4 = (f32[1,3,128,512]{3,2,1,0:T(8,128)}, f32[1,3,128,512]{3,2,1,0:T(8,128)S(1)}, u32[]{:S(2)}) copy-start(f32[1,3,128,512]{3,2,1,0:T(8,128)S(1)} %get-tuple-element.86.refs_2_) | copy-start | bytes 2359300
  56.0 28.7 %collective-permute-start.19 = (bf16[3,400,512]{2,1,0:T(8,128)(2,1)S(1)}, bf16[3,400,512]{2,1,0:T(8,128)(2,1)S(1)}, u32[]{:S(2)}, u32[]{:S(2)}) collective-permute-start(bf16[3,400,512]{2,1,0:T(8,128)(2,1)S(1)} %pad_maximum_fusion.refs_1_), channel_id=1, source_target_pairs={{0,2},{1,3},{2,0},{3,1},{4,6},{5,7},{6,4},{7,5},{8,10},{9,11},{10,... | collective-permute-start | bytes 3686408 | tf_op jit(solution)/shard_map/ppermute | solution.py:23
  56.9 9.7 %collective-permute-start.13 = (bf16[1,3,128,512]{3,2,1,0:T(8,128)(2,1)S(1)}, bf16[1,3,128,512]{3,2,1,0:T(8,128)(2,1)S(1)}, u32[]{:S(2)}, u32[]{:S(2)}) collective-permute-start(bf16[1,3,128,512]{3,2,1,0:T(8,128)(2,1)S(1)} %get-tuple-element.82), channel_id=1, source_target_pairs={{1,5},{3,7},{4,0},{6,2},{9,13},{11,15},{12,8},{14,10},{17,21},{19,... | collective-permute-start | bytes 1179656 | tf_op jit(solution)/shard_map/ppermute | solution.py:23
  58.2 17.0 %collective-permute-start.15 = (bf16[400,512]{1,0:T(8,128)(2,1)}, bf16[400,512]{1,0:T(8,128)(2,1)}, u32[]{:S(2)}, u32[]{:S(2)}) collective-permute-start(bf16[400,512]{1,0:T(8,128)(2,1)} %get-tuple-element.90.refs_0_), channel_id=1, source_target_pairs={{0,1},{1,0},{2,3},{3,2},{4,5},{5,4},{6,7},{7,6},{8,9},{9,8},{10,11... | collective-permute-start | bytes 1228808 | tf_op jit(solution)/shard_map/ppermute | solution.py:23
  58.3 17.0 %collective-permute-start.16 = (bf16[400,512]{1,0:T(8,128)(2,1)}, bf16[400,512]{1,0:T(8,128)(2,1)}, u32[]{:S(2)}, u32[]{:S(2)}) collective-permute-start(bf16[400,512]{1,0:T(8,128)(2,1)} %collective-permute-done.1.refs_4_), channel_id=1, source_target_pairs={{0,1},{1,0},{2,3},{3,2},{4,5},{5,4},{6,7},{7,6},{8,9},{9,8},{10,11... | collective-permute-start | bytes 1228808 | tf_op jit(solution)/shard_map/ppermute | solution.py:23
  58.7 1.1 copy-start.10
  59.9 19.3 %collective-permute-start.17 = (bf16[1,3,128,512]{3,2,1,0:T(8,128)(2,1)}, bf16[1,3,128,512]{3,2,1,0:T(8,128)(2,1)}, u32[]{:S(2)}, u32[]{:S(2)}) collective-permute-start(bf16[1,3,128,512]{3,2,1,0:T(8,128)(2,1)} %hand_over.2), channel_id=1, source_target_pairs={{0,8},{2,10},{5,13},{7,15},{8,0},{10,2},{13,5},{15,7},{16,24},{18,... | collective-permute-start | bytes 1179656 | tf_op jit(solution)/shard_map/ppermute | solution.py:23
  66.6 1.1 copy-start.12
  67.7 15.8 %collective-permute-start.14 = (bf16[1,3,128,512]{3,2,1,0:T(8,128)(2,1)}, bf16[1,3,128,512]{3,2,1,0:T(8,128)(2,1)}, u32[]{:S(2)}, u32[]{:S(2)}) collective-permute-start(bf16[1,3,128,512]{3,2,1,0:T(8,128)(2,1)} %hand_over.3), channel_id=1, source_target_pairs={{0,8},{2,10},{5,13},{7,15},{8,0},{10,2},{13,5},{15,7},{16,24},{18,... | collective-permute-start | bytes 1179656 | tf_op jit(solution)/shard_map/ppermute | solution.py:23
  71.3 1.4 %copy-start.1 = (f32[1,3,128,512]{3,2,1,0:T(8,128)S(1)}, f32[1,3,128,512]{3,2,1,0:T(8,128)}, u32[]{:S(2)}) copy-start(f32[1,3,128,512]{3,2,1,0:T(8,128)} %copy-done) | copy-start | bytes 2359300
  71.3 1.6 %copy-start.3 = (f32[1,3,128,512]{3,2,1,0:T(8,128)S(1)}, f32[1,3,128,512]{3,2,1,0:T(8,128)}, u32[]{:S(2)}) copy-start(f32[1,3,128,512]{3,2,1,0:T(8,128)} %copy-done.2) | copy-start | bytes 2359300
  72.9 1.0 copy-start.7
  73.9 1.0 copy-start.11
  74.9 1.1 copy-start.5
  74.9 1.2 %copy-start.9 = (bf16[1,3,128,512]{3,2,1,0:T(8,128)(2,1)S(1)}, bf16[1,3,128,512]{3,2,1,0:T(8,128)(2,1)}, u32[]{:S(2)}) copy-start(bf16[1,3,128,512]{3,2,1,0:T(8,128)(2,1)} %copy-done.8) | copy-start | bytes 1179652
  74.9 1.3 %copy-start.13 = (bf16[1,3,128,512]{3,2,1,0:T(8,128)(2,1)S(1)}, bf16[1,3,128,512]{3,2,1,0:T(8,128)(2,1)}, u32[]{:S(2)}) copy-start(bf16[1,3,128,512]{3,2,1,0:T(8,128)(2,1)} %copy-done.12) | copy-start | bytes 1179652
  75.2 4.0 %copy-start.14 = (f32[4]{0:T(128)S(1)}, f32[4]{0:T(128)}, u32[]{:S(2)}) copy-start(f32[4]{0:T(128)} %param.15) | copy-start | bytes 52
  75.2 14.3 %collective-permute-start.18 = (bf16[3,400,512]{2,1,0:T(8,128)(2,1)S(1)}, bf16[3,400,512]{2,1,0:T(8,128)(2,1)S(1)}, u32[]{:S(2)}, u32[]{:S(2)}) collective-permute-start(bf16[3,400,512]{2,1,0:T(8,128)(2,1)S(1)} %pad_maximum_fusion.refs_1_), channel_id=1, source_target_pairs={{0,1},{1,0},{2,3},{3,2},{4,5},{5,4},{6,7},{7,6},{8,9},{9,8},{10,11... | collective-permute-start | bytes 3686408 | tf_op jit(solution)/shard_map/ppermute | solution.py:23
  84.8 4.7 %collective-permute-start.20 = (bf16[3,400,512]{2,1,0:T(8,128)(2,1)S(1)}, bf16[3,400,512]{2,1,0:T(8,128)(2,1)S(1)}, u32[]{:S(2)}, u32[]{:S(2)}) collective-permute-start(bf16[3,400,512]{2,1,0:T(8,128)(2,1)S(1)} %collective-permute-done.19.refs_5_), channel_id=1, source_target_pairs={{0,1},{1,0},{2,3},{3,2},{4,5},{5,4},{6,7},{7,6},{8,9},{9,8},{10,11... | collective-permute-start | bytes 3686408 | tf_op jit(solution)/shard_map/ppermute | solution.py:23
  84.8 13.9 %collective-permute-start.21 = (bf16[2,3,128,512]{3,2,1,0:T(8,128)(2,1)S(1)}, bf16[2,3,128,512]{3,2,1,0:T(8,128)(2,1)S(1)}, u32[]{:S(2)}, u32[]{:S(2)}) collective-permute-start(bf16[2,3,128,512]{3,2,1,0:T(8,128)(2,1)S(1)} %renew_1.1.refs_0_), channel_id=1, source_target_pairs={{0,2},{2,0},{5,7},{7,5},{8,10},{10,8},{13,15},{15,13},{16,18},{18,... | collective-permute-start | bytes 2359304 | tf_op jit(solution)/shard_map/ppermute | solution.py:23
  88.1 11.9 %collective-permute-start.22 = (bf16[2,3,128,512]{3,2,1,0:T(8,128)(2,1)S(1)}, bf16[2,3,128,512]{3,2,1,0:T(8,128)(2,1)S(1)}, u32[]{:S(2)}, u32[]{:S(2)}) collective-permute-start(bf16[2,3,128,512]{3,2,1,0:T(8,128)(2,1)S(1)} %renew_1.1.refs_0_), channel_id=1, source_target_pairs={{0,1},{2,3},{5,4},{7,6},{8,9},{10,11},{13,12},{15,14},{16,17},{18,... | collective-permute-start | bytes 2359304 | tf_op jit(solution)/shard_map/ppermute | solution.py:23
  98.7 3.2 %collective-permute-start.23 = (bf16[2,3,128,512]{3,2,1,0:T(8,128)(2,1)S(1)}, bf16[2,3,128,512]{3,2,1,0:T(8,128)(2,1)S(1)}, u32[]{:S(2)}, u32[]{:S(2)}) collective-permute-start(bf16[2,3,128,512]{3,2,1,0:T(8,128)(2,1)S(1)} %collective-permute-done.21.refs_1_), channel_id=1, source_target_pairs={{0,1},{2,3},{5,4},{7,6},{8,9},{10,11},{13,12},{15,14},{16,17},{18,... | collective-permute-start | bytes 2359304 | tf_op jit(solution)/shard_map/ppermute | solution.py:23
  102.9 12.6 %collective-permute-start.25 = (bf16[128,512]{1,0:T(8,128)(2,1)S(1)}, bf16[128,512]{1,0:T(8,128)(2,1)S(1)}, u32[]{:S(2)}, u32[]{:S(2)}) collective-permute-start(bf16[128,512]{1,0:T(8,128)(2,1)S(1)} %get-tuple-element.96), channel_id=1, source_target_pairs={{0,8},{1,9},{2,10},{3,11},{4,12},{5,13},{6,14},{7,15},{8,0},{9,1},... | collective-permute-start | bytes 393224 | tf_op jit(solution)/shard_map/ppermute | solution.py:23
  104.3 11.2 %collective-permute-start.24 = (bf16[128,512]{1,0:T(8,128)(2,1)S(1)}, bf16[128,512]{1,0:T(8,128)(2,1)S(1)}, u32[]{:S(2)}, u32[]{:S(2)}) collective-permute-start(bf16[128,512]{1,0:T(8,128)(2,1)S(1)} %get-tuple-element.99), channel_id=1, source_target_pairs={{0,4},{1,5},{2,6},{3,7},{4,0},{5,1},{6,2},{7,3},{8,12},{9,13},{10,... | collective-permute-start | bytes 393224 | tf_op jit(solution)/shard_map/ppermute | solution.py:23
  105.9 9.5 %collective-permute-start.26 = (bf16[128,512]{1,0:T(8,128)(2,1)S(1)}, bf16[128,512]{1,0:T(8,128)(2,1)S(1)}, u32[]{:S(2)}, u32[]{:S(2)}) collective-permute-start(bf16[128,512]{1,0:T(8,128)(2,1)S(1)} %get-tuple-element.100), channel_id=1, source_target_pairs={{0,12},{1,13},{2,14},{3,15},{4,8},{5,9},{6,10},{7,11},{8,4},{9,5},... | collective-permute-start | bytes 393224 | tf_op jit(solution)/shard_map/ppermute | solution.py:23
